TPU v7x, 32 devices: a whole 2x2x4 slice. The times are simulated.
32 devices in a mesh: dp: 4 (over y, core), fsdp: 8 (over z, x).
Axes of the slice: x: 2, y: 2, z: 4, core: 2. Of those that a mesh axis runs over, the one named last changes fastest.
Arguments:
- frames: bfloat16 [32, 160, 512], P(('dp', 'fsdp')), may hold values from -6 to 6
- lengths: int32 [32], P(('dp', 'fsdp')), may hold values from 10 to 160, as said below
- cotangent: bfloat16 [32, 160, 512], P(('dp', 'fsdp')), may hold values from -6 to 6
- params: float32 [8210944], P(('dp', 'fsdp')), as said below
- first_moment: float32 [8210944], P(('dp', 'fsdp'))
- second_moment: float32 [8210944], P(('dp', 'fsdp')), as said below
Outputs:
- out: bfloat16 [32, 160, 512], P(('dp', 'fsdp'))
- frames_grad: bfloat16 [32, 160, 512], P(('dp', 'fsdp'))
- new_params: float32 [8210944], P(('dp', 'fsdp'))
- new_first: float32 [8210944], P(('dp', 'fsdp'))
- new_second: float32 [8210944], P(('dp', 'fsdp'))
- weight_norms: float32 [12], replicated
- update_norms: float32 [12], replicated
- trust_ratios: float32 [12], replicated
- gain_grads: float32 [4096], replicated
Inputs may be any that keep to these rules, and one draw needn't show every extreme that they name: `lengths`: in every draw some utterance has exactly 160 valid frames. `params`: the gains are positive. `second_moment`: every entry is positive.
All inputs are finite; a program needn't handle non-finite values.
Results may differ from a plain program's by a relative error of at most 0.02.
Values may be sent and summed in bfloat16 or wider, within the bound.
No kernel may reach another device: no remote copies, remote signals or barrier semaphores. Data moves between devices by JAX's collectives and lax.ppermute only.
A program may use at most 256 MiB of HBM per device.

v0:
```python
import math

import jax
import jax.numpy as jnp
from jax import lax
from jax.sharding import PartitionSpec as P

D = 512
H = 8
HS = 64
FF = 2048
CG = 3072
KER = 31
RELW = 128
STEP = 8


BETA_FIRST = 0.5
BETA_SECOND = 0.5
LEARN_RATE = 0.5
WEIGHT_DECAY = 0.01
ADAM_EPS = 1e-06
NORM_EPS = 1e-05
MASK_FILL = -1000000000.0


def segment_shapes():
    gate_width = CG // 2
    return [
        (D, FF),
        (FF, D),
        (D, 3 * D),
        (D, D),
        (D, CG),
        (gate_width, D),
        (2 * D, D),
        (D, FF),
        (FF, D),
        (5 * D + gate_width,),
        (KER, gate_width + 2 * D),
        (RELW, H),
    ]


def unpack(flat):
    pieces = []
    offset = 0
    for extent in segment_shapes():
        entries = math.prod(extent)
        pieces.append(flat[offset : offset + entries].reshape(extent))
        offset = offset + entries
    return pieces


def segment_ids(positions):
    labels = jnp.zeros(positions.shape, jnp.int32)
    offset = 0
    for extent in segment_shapes()[:-1]:
        offset = offset + math.prod(extent)
        labels = labels + (positions >= offset).astype(jnp.int32)
    return labels


def contract_rows(left, right):
    return lax.dot_general(
        left, right, (((0,), (0,)), ((), ())), preferred_element_type=jnp.float32
    )


def times_transposed(left, right):
    return lax.dot_general(
        left, right, (((1,), (1,)), ((), ())), preferred_element_type=jnp.float32
    )


def layer_norm(values, gain):
    centered = values - jnp.mean(values, axis=-1, keepdims=True)
    variance = jnp.mean(centered * centered, axis=-1, keepdims=True)
    return centered * lax.rsqrt(variance + NORM_EPS) * gain


def norm_backward(values, gain, grad_in):
    return jax.vjp(layer_norm, values, gain)[1](grad_in)


def gelu_exact(values):
    return jax.nn.gelu(values, approximate=False)


def depthwise(values, kernel):
    taps = kernel.shape[0]
    margin = taps // 2
    frame_slots = values.shape[-2]
    padding = [(0, 0)] * (values.ndim - 2) + [(margin, margin), (0, 0)]
    padded = jnp.pad(values, padding)
    result = jnp.zeros_like(values)
    for offset in range(taps):
        result = result + kernel[offset] * lax.slice_in_dim(
            padded, offset, offset + frame_slots, axis=values.ndim - 2
        )
    return result


def ffn_forward(inputs, gain, w_in, w_out):
    normed = layer_norm(inputs, gain).astype(jnp.bfloat16)
    hidden = jnp.dot(normed, w_in, preferred_element_type=jnp.float32)
    active = jax.nn.silu(hidden).astype(jnp.bfloat16)
    output = jnp.dot(active, w_out, preferred_element_type=jnp.float32)
    return (output, (normed, hidden, active))


def ffn_backward(out_grad, saved, inputs, gain, w_in, w_out):
    normed, hidden, active = saved
    active_grad = times_transposed(out_grad, w_out)
    w_out_grad = contract_rows(active, out_grad)
    hidden_grad = jax.vjp(jax.nn.silu, hidden)[1](active_grad)[0].astype(jnp.bfloat16)
    normed_grad = times_transposed(hidden_grad, w_in)
    w_in_grad = contract_rows(normed, hidden_grad)
    input_grad, gain_grad = norm_backward(inputs, gain, normed_grad)
    return (input_grad, gain_grad, w_in_grad, w_out_grad)


def bucket_table(frame_slots):
    distance = lax.iota(jnp.int32, 2 * frame_slots - 1) - (frame_slots - 1)
    buckets = jnp.clip(distance, -(RELW // 2), RELW // 2 - 1) + RELW // 2
    return (buckets[:, None] == lax.iota(jnp.int32, RELW)[None, :]).astype(jnp.float32)


def bias_matrix(expanded, frame_slots):
    tiled = jnp.broadcast_to(expanded, (frame_slots, 2 * frame_slots - 1)).reshape(-1)
    tiled = jnp.concatenate([tiled, jnp.zeros((frame_slots,), tiled.dtype)])
    return tiled.reshape(frame_slots, 2 * frame_slots)[:, :frame_slots][::-1]


def diagonal_sums(grads):
    frame_slots = grads.shape[0]
    flipped = grads[::-1]
    padded = jnp.concatenate([flipped, jnp.zeros_like(flipped)], axis=1).reshape(-1)
    folded = padded[: frame_slots * (2 * frame_slots - 1)].reshape(frame_slots, 2 * frame_slots - 1)
    return jnp.sum(folded.astype(jnp.float32), axis=0)


def head_scores(queries, key_rows, expanded, key_valid):
    frame_slots = queries.shape[0]
    scores = times_transposed(queries, key_rows) * HS ** (-0.5) + bias_matrix(expanded, frame_slots)
    return jnp.where(key_valid[None, :] > 0, scores, MASK_FILL)


def head_forward(operands):
    queries, key_rows, value_rows, expanded, key_valid = operands
    scores = head_scores(queries, key_rows, expanded, key_valid)
    row_max = jnp.max(scores, axis=-1, keepdims=True)
    shifted = jnp.exp(scores - row_max)
    denominator = jnp.sum(shifted, axis=-1, keepdims=True)
    attention = shifted / denominator
    context = jnp.dot(
        attention.astype(jnp.bfloat16), value_rows, preferred_element_type=jnp.float32
    )
    return (context, (row_max + jnp.log(denominator))[:, 0])


def head_backward(operands):
    queries, key_rows, value_rows, expanded, key_valid, log_total, context_grad = operands
    scores = head_scores(queries, key_rows, expanded, key_valid)
    attention = jnp.exp(scores - log_total[:, None])
    value_grad = contract_rows(attention.astype(jnp.bfloat16), context_grad)
    attention_grad = times_transposed(context_grad, value_rows)
    row_dot = jnp.sum(attention * attention_grad, axis=-1, keepdims=True)
    score_grad = (attention * (attention_grad - row_dot)).astype(jnp.bfloat16)
    query_grad = jnp.dot(score_grad, key_rows, preferred_element_type=jnp.float32) * HS ** (-0.5)
    key_grad = contract_rows(score_grad, queries) * HS ** (-0.5)
    return (query_grad, key_grad, value_grad, diagonal_sums(score_grad))


def shards(frames, lengths, cotangent, params, first_moment, second_moment):
    utt_count, frame_slots, model_width = frames.shape
    row_count = utt_count * frame_slots
    gate_width = CG // 2
    shard_size = params.shape[0]
    valid_mask = (lax.iota(jnp.int32, frame_slots)[None, :] < lengths[:, None]).astype(jnp.float32)
    valid_rows = valid_mask.reshape(row_count, 1)
    positions = lax.axis_index(("dp", "fsdp")) * shard_size + lax.iota(jnp.int32, shard_size)
    members = (
        segment_ids(positions)[:, None] == lax.iota(jnp.int32, len(segment_shapes()))[None, :]
    ).astype(jnp.float32)

    def conv_masked(values, kernel):
        shaped = (values * valid_rows).reshape(utt_count, frame_slots, values.shape[1])
        return depthwise(shaped, kernel).reshape(row_count, values.shape[1])

    def split_heads(packed_rows, parts):
        shaped = packed_rows.reshape(utt_count, frame_slots, parts, H, HS).transpose(2, 0, 3, 1, 4)
        return shaped.reshape(parts, utt_count * H, frame_slots, HS)

    def join_heads(per_head, parts):
        shaped = per_head.reshape(parts, utt_count, H, frame_slots, HS).transpose(1, 3, 0, 2, 4)
        return shaped.reshape(row_count, parts * H * HS)

    gathered = lax.all_gather(params.astype(jnp.bfloat16), ("dp", "fsdp"), axis=0, tiled=True)
    (
        ffa_in,
        ffa_out,
        att_qkv,
        att_out,
        cg_in,
        cg_out,
        merge_out,
        ffb_in,
        ffb_out,
        gains,
        kernels,
        rel_table,
    ) = unpack(gathered)
    gains_wide = gains.astype(jnp.float32)
    kernels_wide = kernels.astype(jnp.float32)
    x_zero = frames.reshape(row_count, model_width).astype(jnp.float32)
    ffa_output, ffa_saved = ffn_forward(x_zero, gains_wide[0:D], ffa_in, ffa_out)
    x_one = x_zero + 0.5 * ffa_output
    att_normed = layer_norm(x_one, gains_wide[D : 2 * D]).astype(jnp.bfloat16)
    packed = jnp.dot(att_normed, att_qkv, preferred_element_type=jnp.float32).astype(jnp.bfloat16)
    buckets = bucket_table(frame_slots)
    expanded = jnp.dot(buckets, rel_table.astype(jnp.float32), precision=lax.Precision.HIGHEST)
    head_bias = jnp.tile(expanded.T, (utt_count, 1))
    head_valid = jnp.repeat(valid_mask, H, axis=0)
    per_head = split_heads(packed, 3)
    context_heads, log_totals = lax.map(
        head_forward, (per_head[0], per_head[1], per_head[2], head_bias, head_valid)
    )
    context = join_heads(context_heads[None], 1).astype(jnp.bfloat16)
    att_output = jnp.dot(context, att_out, preferred_element_type=jnp.float32)
    cg_normed = layer_norm(x_one, gains_wide[2 * D : 3 * D]).astype(jnp.bfloat16)
    cg_hidden = jnp.dot(cg_normed, cg_in, preferred_element_type=jnp.float32)
    activated = gelu_exact(cg_hidden)
    left_half = activated[:, :gate_width]
    right_half = activated[:, gate_width:]
    gate_normed = layer_norm(right_half, gains_wide[5 * D :])
    conv_gate = conv_masked(gate_normed, kernels_wide[:, :gate_width])
    gated = (left_half * conv_gate).astype(jnp.bfloat16)
    cg_output = jnp.dot(gated, cg_out, preferred_element_type=jnp.float32)
    joined = jnp.concatenate([att_output, cg_output], axis=1)
    mixed = (joined + conv_masked(joined, kernels_wide[:, gate_width:])).astype(jnp.bfloat16)
    x_two = x_one + jnp.dot(mixed, merge_out, preferred_element_type=jnp.float32)
    ffb_output, ffb_saved = ffn_forward(x_two, gains_wide[3 * D : 4 * D], ffb_in, ffb_out)
    x_three = x_two + 0.5 * ffb_output
    result = (layer_norm(x_three, gains_wide[4 * D : 5 * D]) * valid_rows).astype(jnp.bfloat16)
    again = lax.all_gather(params.astype(jnp.bfloat16), ("dp", "fsdp"), axis=0, tiled=True)
    (
        back_ffa_in,
        back_ffa_out,
        back_qkv,
        back_att_out,
        back_cg_in,
        back_cg_out,
        back_merge,
        back_ffb_in,
        back_ffb_out,
        back_gains,
        back_kernels,
        back_table,
    ) = unpack(again)
    back_gains = back_gains.astype(jnp.float32)
    back_kernels = back_kernels.astype(jnp.float32)
    out_grad = cotangent.reshape(row_count, model_width).astype(jnp.float32) * valid_rows
    x_three_grad, gain_final_grad = norm_backward(x_three, back_gains[4 * D : 5 * D], out_grad)
    x_two_ffn, gain_ffb_grad, ffb_in_grad, ffb_out_grad = ffn_backward(
        (0.5 * x_three_grad).astype(jnp.bfloat16),
        ffb_saved,
        x_two,
        back_gains[3 * D : 4 * D],
        back_ffb_in,
        back_ffb_out,
    )
    x_two_grad = x_three_grad + x_two_ffn
    merged_grad = x_two_grad.astype(jnp.bfloat16)
    mixed_grad = times_transposed(merged_grad, back_merge)
    merge_grad = contract_rows(mixed, merged_grad)
    joined_conv_grad, kernel_merge_grad = jax.vjp(
        conv_masked, joined, back_kernels[:, gate_width:]
    )[1](mixed_grad)
    joined_grad = mixed_grad + joined_conv_grad
    att_output_grad = joined_grad[:, :model_width].astype(jnp.bfloat16)
    cg_output_grad = joined_grad[:, model_width:].astype(jnp.bfloat16)
    gated_grad = times_transposed(cg_output_grad, back_cg_out)
    cg_out_grad = contract_rows(gated, cg_output_grad)
    left_grad = gated_grad * conv_gate
    conv_grad = gated_grad * left_half
    gate_normed_grad, kernel_cgmlp_grad = jax.vjp(
        conv_masked, gate_normed, back_kernels[:, :gate_width]
    )[1](conv_grad)
    right_grad, gain_gate_grad = norm_backward(right_half, back_gains[5 * D :], gate_normed_grad)
    hidden_grad = jax.vjp(gelu_exact, cg_hidden)[1](
        jnp.concatenate([left_grad, right_grad], axis=1)
    )[0].astype(jnp.bfloat16)
    cg_normed_grad = times_transposed(hidden_grad, back_cg_in)
    cg_in_grad = contract_rows(cg_normed, hidden_grad)
    x_one_cg, gain_cgmlp_grad = norm_backward(x_one, back_gains[2 * D : 3 * D], cg_normed_grad)
    context_grad = times_transposed(att_output_grad, back_att_out).astype(jnp.bfloat16)
    att_out_grad = contract_rows(context, att_output_grad)
    context_grad_heads = split_heads(context_grad, 1)[0]
    query_grad, key_grad, value_grad, diagonal_grad = lax.map(
        head_backward,
        (
            per_head[0],
            per_head[1],
            per_head[2],
            head_bias,
            head_valid,
            log_totals,
            context_grad_heads,
        ),
    )
    packed_grad = join_heads(jnp.stack([query_grad, key_grad, value_grad]), 3).astype(jnp.bfloat16)
    att_normed_grad = times_transposed(packed_grad, back_qkv)
    qkv_grad = contract_rows(att_normed, packed_grad)
    x_one_att, gain_att_grad = norm_backward(x_one, back_gains[D : 2 * D], att_normed_grad)
    head_diagonals = jnp.sum(diagonal_grad.reshape(utt_count, H, 2 * frame_slots - 1), axis=0)
    table_grad = lax.dot_general(
        buckets, head_diagonals, (((0,), (1,)), ((), ())), precision=lax.Precision.HIGHEST
    )
    x_one_grad = x_two_grad + x_one_att + x_one_cg
    x_zero_ffn, gain_ffa_grad, ffa_in_grad, ffa_out_grad = ffn_backward(
        (0.5 * x_one_grad).astype(jnp.bfloat16),
        ffa_saved,
        x_zero,
        back_gains[0:D],
        back_ffa_in,
        back_ffa_out,
    )
    frames_grad = (x_one_grad + x_zero_ffn).astype(jnp.bfloat16)
    gains_grad = jnp.concatenate(
        [
            gain_ffa_grad,
            gain_att_grad,
            gain_cgmlp_grad,
            gain_ffb_grad,
            gain_final_grad,
            gain_gate_grad,
        ]
    )
    kernels_grad = jnp.concatenate([kernel_cgmlp_grad, kernel_merge_grad], axis=1)
    flat_grad = jnp.concatenate(
        [
            ffa_in_grad.reshape(-1),
            ffa_out_grad.reshape(-1),
            qkv_grad.reshape(-1),
            att_out_grad.reshape(-1),
            cg_in_grad.reshape(-1),
            cg_out_grad.reshape(-1),
            merge_grad.reshape(-1),
            ffb_in_grad.reshape(-1),
            ffb_out_grad.reshape(-1),
            gains_grad,
            kernels_grad.reshape(-1),
            table_grad.reshape(-1),
        ]
    )
    grad_grid = flat_grad.reshape(lax.axis_size("dp"), lax.axis_size("fsdp"), shard_size)
    received = lax.all_to_all(
        grad_grid.astype(jnp.bfloat16), "fsdp", split_axis=1, concat_axis=1, tiled=True
    ).astype(grad_grid.dtype)
    partial_sum = jnp.sum(received, axis=1)
    grad_shard = (
        lax.psum_scatter(partial_sum.astype(jnp.bfloat16), "dp", scatter_dimension=0, tiled=True)
        .astype(jnp.float32)
        .reshape(shard_size)
    )
    new_first = BETA_FIRST * first_moment + (1.0 - BETA_FIRST) * grad_shard
    new_second = BETA_SECOND * second_moment + (1.0 - BETA_SECOND) * grad_shard * grad_shard
    first_hat = new_first / (1.0 - BETA_FIRST**STEP)
    second_hat = new_second / (1.0 - BETA_SECOND**STEP)
    update = first_hat / (jnp.sqrt(second_hat) + ADAM_EPS) + WEIGHT_DECAY * params
    update_part = jnp.sum(members * (update * update)[:, None], axis=0)
    weight_part = jnp.sum(members * (params * params)[:, None], axis=0)
    weight_squares, update_squares, gain_grads = lax.psum(
        (weight_part, update_part, gains_grad), ("dp", "fsdp")
    )
    weight_norms = jnp.sqrt(weight_squares)
    update_norms = jnp.sqrt(update_squares)
    trust_ratios = weight_norms / (update_norms + ADAM_EPS)
    entry_trust = jnp.sum(members * trust_ratios[None, :], axis=1)
    new_params = params - LEARN_RATE * entry_trust * update
    return (
        result.reshape(utt_count, frame_slots, model_width),
        frames_grad.reshape(utt_count, frame_slots, model_width),
        new_params,
        new_first,
        new_second,
        weight_norms,
        update_norms,
        trust_ratios,
        gain_grads,
    )


def solution(mesh):
    placed = (
        P(("dp", "fsdp"), None, None),
        P(("dp", "fsdp")),
        P(("dp", "fsdp"), None, None),
        P(("dp", "fsdp")),
        P(("dp", "fsdp")),
        P(("dp", "fsdp")),
    )
    return jax.shard_map(
        shards,
        mesh=mesh,
        in_specs=placed,
        out_specs=(
            P(("dp", "fsdp"), None, None),
            P(("dp", "fsdp"), None, None),
            P(("dp", "fsdp")),
            P(("dp", "fsdp")),
            P(("dp", "fsdp")),
            P(),
            P(),
            P(),
            P(),
        ),
        check_vma=False,
    )
```

profile of v0, /device:TPU:0, one launch (start us, length us, event | category | flops | bytes accessed | tf_op | source)
XLA Modules:
  0.0 1284.9 jit_solution(4382521303729498598)
XLA Ops:
  8.5 5.8 broadcast.892
  14.3 8.8 dynamic-update-slice
  24.3 276.3 %all-reduce.135.cloned.1.call-done = bf16[8210944]{0:T(1024)(128)(2,1)} async-done(((bf16[8210944]{0:T(1024)(128)(2,1)}), bf16[8210944]{0:T(1024)(128)(2,1)}) %all-reduce.135.cloned.1.call-update) | async-done | bytes 16421904
  306.0 6.1 fusion.230
  312.1 4.3 slice.731
  316.4 4.2 reshape.1218
  320.6 3.1 slice.894
  323.7 5.9 reshape.1223
  329.6 2.3 fusion.187
  334.3 6.3 multiply_multiply_fusion.5
  341.6 1.8 fusion.231
  343.5 3.7 slice.808
  347.2 4.3 reshape.1220
  351.5 2.7 convolution_convert_fusion.7
  354.1 1.7 reshape.1221
  359.0 1.7 copy.56
  362.9 52.9 %while.28 = (s32[]{:T(128)}, bf16[8,160,64]{1,2,0:T(8,128)(2,1)}, f32[8,160]{1,0:T(8,128)}, f32[8,160]{1,0:T(8,128)}, bf16[8,160,64]{2,1,0:T(8,128)(2,1)}, /*ind...) while((s32[]{:T(128)}, bf16[8,160,64]{1,2,0:T(8,128)(2,1)}, ...), condition=%wide.region_7.8_spmd, body=%wide.region_4.7_spmd.sunk | while | flops 6784002 | bytes 2779705 | solution.py:226
  419.5 4.8 slice.875
  424.3 4.2 reshape.1227
  429.6 4.9 fusion.112
  436.5 2.7 fusion.162
  447.0 2.0 fusion.150
  450.9 2.4 pad_add_fusion.7
  454.9 4.5 fusion.82
  459.4 6.4 multiply_bitcast_fusion.30
  465.8 4.7 multiply_bitcast_fusion.29
  473.6 102.6 %while.29 = (s32[]{:T(128)}, bf16[8,160,64]{1,2,0:T(8,128)(2,1)}, bf16[8,160,64]{1,2,0:T(8,128)(2,1)}, bf16[8,160,64]{1,2,0:T(8,128)(2,1)}, f32[8,319]{1,0:T(8,1...) while((s32[]{:T(128)}, bf16[8,160,64]{1,2,0:T(8,128)(2,1)}, ...), condition=%wide.region_21.22_spmd, body=%wide.region_18.21_spmd.sunk | while | flops 16762243 | bytes 5187479 | solution.py:300
  479.0 1.6 fusion.308
  480.6 1.6 fusion.309
  504.7 1.6 fusion.308
  517.5 1.6 fusion.308
  530.3 1.6 fusion.308
  533.5 1.6 fusion.310
  543.1 1.6 fusion.308
  556.0 1.6 fusion.308
  578.6 9.1 pad_add_fusion
  594.3 1.9 multiply_reduce_fusion.7
  602.7 1.9 convolution_convert_fusion.6
  604.9 2.8 fusion.51
  607.7 1.8 fusion.56
  611.0 2.2 fusion.54
  613.3 2.1 fusion.55
  615.4 2.1 fusion.132
  617.5 1.6 fusion.100
  621.9 2.4 copy.67
  624.3 3.0 reshape.1235
  628.4 4.5 copy.69
  634.8 2.0 copy.72
  637.1 2.4 copy.73
  643.2 3.2 constant_dynamic-update-slice_fusion.9
  649.0 1.8 constant_dynamic-update-slice_fusion.6
  665.6 3.2 dynamic-update-slice.22
  670.3 34.5 %convert_element_type.284 = bf16[4,8,256592]{2,1,0:T(8,128)(2,1)} reshape(bf16[8210944]{0:T(1024)(128)(2,1)} %dynamic-update-slice.23) | data formatting | bytes 32843776 | tf_op jit(solution)/shard_map/convert_element_type | solution.py:359
  704.9 13.4 %copy.62 = bf16[4,8,256592]{2,0,1:T(4,128)(2,1)} copy(bf16[4,8,256592]{2,1,0:T(8,128)(2,1)} %convert_element_type.284) | data formatting | bytes 32843776 | tf_op jit(solution)/shard_map/convert_element_type | solution.py:359
  718.2 5.7 all-to-all-start
  724.0 355.3 %all-to-all-done = bf16[4,8,256592]{2,0,1:T(4,128)(2,1)} async-done(((bf16[4,8,256592]{2,0,1:T(4,128)(2,1)}), bf16[4,8,256592]{2,0,1:T(4,128)(2,1)}, u32[]{:S(2)}, u32[]{:S(2)}) %all-to-all-start) | async-done | bytes 16421920 | tf_op jit(solution)/shard_map/all_to_all | solution.py:358
  1079.2 63.1 %reduce_sum.1015 = bf16[4,256592]{1,0:T(4,128)(2,1)} reduce(bf16[4,8,256592]{2,0,1:T(4,128)(2,1)} %all-to-all-done, bf16[]{:T(256)} %constant.219.clone.1), dimensions={1}, to_apply=%region_100.101 | reduce | flops 7184576 | bytes 18474626 | tf_op jit(solution)/shard_map/reduce_sum | solution.py:361
  1145.0 47.4 %all-reduce.137.cloned.1.call-done = bf16[4,256592]{1,0:T(4,128)(2,1)} async-done(((bf16[4,256592]{1,0:T(4,128)(2,1)}), bf16[4,256592]{1,0:T(4,128)(2,1)}) %all-reduce.137.cloned.1.call-update) | async-done | bytes 2052752
  1192.4 12.6 fusion.79
  1205.0 2.0 fusion.220
  1207.1 10.1 select_reduce_fusion.1
  1217.1 39.5 %all-reduce.131 = (f32[12]{0:T(128)S(1)}, f32[12]{0:T(128)S(1)}, f32[4096]{0:T(1024)}) all-reduce(f32[12]{0:T(128)S(1)} %get-tuple-element.267, f32[12]{0:T(128)S(1)} %get-tuple-element.266, f32[4096]{0:T(1024)S(1)} %get-tuple-element.494), channel_id=1, replica_groups=mesh['dp'=4,'fsdp'=8] {'dp','fsdp'}, use_global_device_ids=true, to_apply=%region_31.32 | all-reduce | flops 4120 | bytes 32960 | tf_op jit(solution)/shard_map/psum | solution.py:374
  1257.2 17.6 %select_reduce_fusion = f32[256592]{0:T(1024)S(1)} fusion(f32[12]{0:T(128)S(1)} %get-tuple-element.354, s32[256592]{0:T(1024)S(1)} %convert_add_fusion), kind=kLoop, calls=%fused_computation.64 | loop fusion | flops 8980720 | bytes 2052784 | tf_op jit(solution)/shard_map/reduce_sum | solution.py:380
  1274.8 3.1 multiply_subtract_fusion
  (885 shorter events, 225.3 us)
Async XLA Ops:
  7.2 293.5 %all-reduce.135.cloned.1.call-start = ((), (), s32[]{:S(2)}) async-start(), calls=%async_computation.1 | async-start | bytes 32845824
  24.0 336.8 %copy-start.197 = (s32[319]{0:T(512)}, s32[319]{0:T(512)S(1)}, u32[]{:S(2)}) copy-start(s32[319]{0:T(512)S(1)} %clamp_add_fusion) | copy-start | bytes 3832
  24.1 305.5 %copy-start.100 = (f32[160]{0:T(256)}, f32[160]{0:T(256)S(1)}, u32[]{:S(2)}) copy-start(f32[160]{0:T(256)S(1)} %broadcast_multiply_fusion.4) | copy-start | bytes 1924
  24.3 277.1 %copy-start.155 = (f32[160]{0:T(256)}, f32[160]{0:T(256)S(1)}, u32[]{:S(2)}) copy-start(f32[160]{0:T(256)S(1)} %fusion.173) | copy-start | bytes 1924
  24.3 305.3 %copy-start.147 = (f32[160]{0:T(256)}, f32[160]{0:T(256)S(1)}, u32[]{:S(2)}) copy-start(f32[160]{0:T(256)S(1)} %fusion.208) | copy-start | bytes 1924
  301.9 31.3 %copy-start.140 = (f32[512]{0:T(512)}, f32[512]{0:T(512)S(1)}, u32[]{:S(2)}) copy-start(f32[512]{0:T(512)S(1)} %get-tuple-element.491) | copy-start | bytes 6148
  301.9 49.5 %copy-start.96 = (f32[512]{0:T(512)}, f32[512]{0:T(512)S(1)}, u32[]{:S(2)}) copy-start(f32[512]{0:T(512)S(1)} %get-tuple-element.492) | copy-start | bytes 6148
  333.0 18.5 %copy-start.98 = (f32[160]{0:T(256)}, f32[160]{0:T(256)S(1)}, u32[]{:S(2)}) copy-start(f32[160]{0:T(256)S(1)} %broadcast_multiply_fusion.3) | copy-start | bytes 1924
  333.2 7.4 copy-start.153
  333.2 18.2 %copy-start.105 = (f32[160]{0:T(256)}, f32[160]{0:T(256)S(1)}, u32[]{:S(2)}) copy-start(f32[160]{0:T(256)S(1)} %fusion.209) | copy-start | bytes 1924
  333.2 8.4 slice-start
  334.3 7.3 slice-start.1
  334.3 7.3 slice-start.2
  334.3 7.3 slice-start.3
  362.9 52.9 %slice-start.4 = ((bf16[8210944]{0:T(1024)(128)(2,1)}), bf16[262144]{0:T(1024)(128)(2,1)S(1)}, s32[]{:S(2)}) async-start(bf16[8210944]{0:T(1024)(128)(2,1)} %all-reduce.135.cloned.1.call-done), calls=%async_computation.7 | async-start | bytes 1048576 | tf_op jit(solution)/shard_map/slice | solution.py:50
  424.3 4.2 copy-start.103
  424.3 4.2 copy-start.145
  429.1 25.9 %copy-start.11 = (f32[1,160,1536]{2,1,0:T(8,128)}, f32[1,160,1536]{2,1,0:T(8,128)S(1)}, u32[]{:S(2)}) copy-start(f32[1,160,1536]{2,1,0:T(8,128)S(1)} %fusion.163) | copy-start | bytes 2949124
  429.6 4.9 copy-start.17
  435.7 3.5 copy-start.26
  436.1 10.8 copy-start.21
  436.5 3.5 copy-start.1
  436.5 3.5 copy-start.94
  439.7 6.8 copy-start.138
  439.9 6.6 copy-start.143
  448.9 4.3 copy-start.8
  454.6 4.8 copy-start.51
  459.4 6.4 copy-start.2
  578.5 9.2 copy-start.31
  578.6 9.2 copy-start.32
  578.6 9.2 copy-start.33
  578.6 9.2 copy-start.34
  578.6 9.2 copy-start.35
  578.6 9.2 copy-start.36
  578.6 9.2 copy-start.104
  597.7 4.1 copy-start.61
  607.7 3.3 copy-start.43
  607.7 3.3 copy-start.95
  607.7 3.3 copy-start.139
  607.7 3.3 copy-start.144
  615.4 3.8 copy-start.156
  628.4 4.5 copy-start.19
  636.9 3.2 copy-start.152
  636.9 3.2 copy-start.182
  636.9 3.2 copy-start.183
  636.9 3.2 copy-start.184
  637.0 3.2 copy-start.185
  637.0 3.2 copy-start.186
  637.0 3.2 copy-start.187
  637.0 3.2 copy-start.188
  637.0 3.2 copy-start.189
  637.0 3.2 copy-start.190
  637.0 3.2 copy-start.191
  637.0 3.2 copy-start.192
  637.0 3.2 copy-start.193
  637.0 5.1 copy-start.149
  643.1 3.2 copy-start.18
  643.2 4.5 copy-start.50
  718.2 361.0 %all-to-all-start = ((bf16[4,8,256592]{2,0,1:T(4,128)(2,1)}), bf16[4,8,256592]{2,0,1:T(4,128)(2,1)}, u32[]{:S(2)}, u32[]{:S(2)}) async-start(bf16[4,8,256592]{2,0,1:T(4,128)(2,1)} %copy.62), calls=%async_computation | async-start | bytes 32849920 | tf_op jit(solution)/shard_map/all_to_all | solution.py:358
  723.9 468.4 %all-reduce.137.cloned.1.call-start = ((), (), s32[]{:S(2)}) async-start(), calls=%async_computation.2 | async-start | bytes 4106240
  1142.4 62.6 %copy-start.10 = (f32[256592]{0:T(1024)S(1)}, f32[256592]{0:T(1024)}, u32[]{:S(2)}) copy-start(f32[256592]{0:T(1024)} %param.13) | copy-start | bytes 3079108
  1192.4 12.7 copy-start.63
  1192.4 12.7 copy-start.64
  1257.2 20.7 %copy-start.196 = (f32[12]{0:T(128)}, f32[12]{0:T(128)S(1)}, u32[]{:S(2)}) copy-start(f32[12]{0:T(128)S(1)} %get-tuple-element.354) | copy-start | bytes 148
  (144 other events, 254.2 us)
Sparse Core Ops, SparseCore 0:
  23.2 277.4 all-reduce.134
  1142.5 49.8 all-reduce.136
where the time goes:
time: 1300 us; the launch traced here: 1280 us
  waiting for transfers between devices  679 us (52%)
  local copies, waits for them, and re-layouts  247 us (19%)
  other arithmetic  175 us (13%)
  matrix products  119 us (9%)
  blocking collectives  39.5 us (3%)
  between operations  17.7 us (1%)
    all_to_all x1, waiting for transfers between devices, shards(): lax.all_to_all(grad_grid.astype(jnp.bfloat16), 'fsdp', split_axis=1, conc...  355 us
    unnamed x4, waiting for transfers between devices  324 us
    unnamed x433, local copies, waits for them, and re-layouts  66.5 us
    reduce_sum x1, other arithmetic, shards(): partial_sum = jnp.sum(received, axis=1)  63.1 us
    convert_element_type x2, local copies, waits for them, and re-layouts, shards(): grad_grid.astype(jnp.bfloat16)  47.9 us
    psum x1, blocking collectives, shards(): lax.psum((weight_part, update_part, gains_grad), ('dp', 'fsdp'))  39.5 us
    dot_general x25, matrix products, contract_rows(): lax.dot_general(left, right, (((0,), (0,)), ((), ())), preferred_element_...  39.4 us
    dot_general x33, matrix products, times_transposed(): lax.dot_general(left, right, (((1,), (1,)), ((), ())), preferred_element_...  38.4 us
  transfers between devices with their start and end apart: 3, of which 3 were waited for; matrix products, arithmetic and copies ran while one was open for 0% of the time, Pallas kernels for 0%

commit v1 on v0

v1 whole, which is shorter than its diff:
```python
import math

import jax
import jax.numpy as jnp
from jax import lax
from jax.experimental import pallas as pl
from jax.experimental.pallas import tpu as pltpu
from jax.sharding import PartitionSpec as P

STEP = 8
BETA_FIRST = 0.5
BETA_SECOND = 0.5
LEARN_RATE = 0.5
WEIGHT_DECAY = 0.01
ADAM_EPS = 1e-06
AXES = ("dp", "fsdp")


def segment_shapes():
    gate_width = CG // 2
    return [
        (D, FF),
        (FF, D),
        (D, 3 * D),
        (D, D),
        (D, CG),
        (gate_width, D),
        (2 * D, D),
        (D, FF),
        (FF, D),
        (5 * D + gate_width,),
        (KER, gate_width + 2 * D),
        (RELW, H),
    ]


D = 512
H = 8
HS = 64
FF = 2048
CG = 3072
KER = 31
RELW = 128
NORM_EPS = 1e-05
MASK_FILL = -1000000000.0
ROW = 512
SLOTS = 160
KEYS = 256
PAD = 16
PADDED = SLOTS + 2 * PAD
GATE = CG // 2
BLOCK = {
    "ffa_in": 0,
    "ffa_out": 4,
    "qkv": 8,
    "att_out": 11,
    "cg_in": 12,
    "cg_out": 18,
    "merge": 21,
    "ffb_in": 23,
    "ffb_out": 27,
    "small": 31,
}
TAPS_AT = 8
REL_AT = 8 + 5 * KER
SMALL = 176
F32, BF16 = jnp.float32, jnp.bfloat16


def dot(left, right):
    return lax.dot_general(left, right, (((1,), (0,)), ((), ())), preferred_element_type=F32)


def dot_t(left, right):
    return lax.dot_general(left, right, (((1,), (1,)), ((), ())), preferred_element_type=F32)


def t_dot(left, right):
    return lax.dot_general(left, right, (((0,), (0,)), ((), ())), preferred_element_type=F32)


def low(values):
    return values.astype(BF16)


def each(count, body):
    def step(at, carry):
        body(at)
        return carry

    lax.fori_loop(0, count, step, 0)


def part(at, size):
    return pl.ds(pl.multiple_of(at * size, size), size)


def normed(values):
    centered = values - jnp.mean(values, axis=-1, keepdims=True)
    variance = jnp.mean(centered * centered, axis=-1, keepdims=True)
    scale = lax.rsqrt(variance + NORM_EPS)
    return centered * scale, scale


def valid_rows(at, size, length):
    return (at * size + lax.broadcasted_iota(jnp.int32, (size, 1), 0) < length).astype(F32)


def norm_back(values, gain, grad):
    hat, scale = normed(values)
    inner = grad * gain
    moved = jnp.mean(inner, axis=-1, keepdims=True) + hat * jnp.mean(inner * hat, axis=-1, keepdims=True)
    return scale * (inner - moved), grad * hat


def erf(values):
    at = jnp.clip(values, -4.0, 4.0)
    square = at * at
    top = jnp.full_like(at, -2.72614225801306e-10)
    for factor in (
        2.77068142495902e-08,
        -2.10102402082508e-06,
        -5.69250639462346e-05,
        -7.34990630326855e-04,
        -2.95459980854025e-03,
        -1.60960333262415e-02,
    ):
        top = top * square + factor
    under = jnp.full_like(at, -1.45660718464996e-05)
    for factor in (
        -2.13374055278905e-04,
        -1.68282697438203e-03,
        -7.37332916720468e-03,
        -1.42647390514189e-02,
    ):
        under = under * square + factor
    return at * top / under


def source_block(coords, at):
    y, c, z, x = coords[0], coords[1], coords[2], coords[3]
    yy, cc, xx, zz = y ^ ((at // 8) % 2), c ^ (at // 16), x ^ ((at // 4) % 2), (z + 4 - at % 4) & 3
    return ((yy * 2 + cc) * 4 + zz) * 2 + xx


def gradient_slot(coords, block):
    y, c, x = coords[0], coords[1], coords[3]
    yy, cc, zz, xx = block // 16, (block // 8) % 2, (block // 2) % 4, block % 2
    return 16 * (c ^ cc) + 8 * (y ^ yy) + 4 * (x ^ xx) + zz


class Loads:
    def __init__(self, coords, sources, wanted, sems):
        self.wanted = wanted
        self.sources = sources
        self.sems = sems
        for at, source in enumerate(sources):
            block = source_block(coords, at)
            first = 0
            for low_block, count, target, rows in wanted:
                here = block - low_block

                @pl.when((here >= 0) & (here < count))
                def _(source=source, target=target, rows=rows, here=here, first=first):
                    pltpu.make_async_copy(
                        source.at[0:rows], target.at[part(here, ROW)] if rows == ROW else target, sems.at[first + here]
                    ).start()

                first = first + count

    def wait(self, which):
        first = sum(count for _, count, _, _ in self.wanted[:which])
        _, count, target, rows = self.wanted[which]
        for at in range(count):
            place = target.at[ROW * at : ROW * at + rows]
            pltpu.make_async_copy(self.sources[0].at[0:rows], place, self.sems.at[first + at]).wait()


class Emits:
    def __init__(self, coords, target, sems):
        self.coords, self.target, self.sems = coords, target, sems
        self.pending = []

    def put(self, block, values):
        copy = pltpu.make_async_copy(
            values, self.target.at[gradient_slot(self.coords, block)], self.sems.at[len(self.pending)]
        )
        copy.start()
        self.pending.append(copy)

    def wait(self):
        for copy in self.pending:
            copy.wait()


def split_columns(raw, target, wide, stage):
    def chunk(k):
        rows = part(k, 128 * wide)
        for lane in range(4):
            stage[lane, 0 : 128 * wide, :] = raw[rows, lane * 128 : lane * 128 + 128].astype(F32)
        for c in range(wide):
            for lane in range(4):
                place = ROW * c + lane * 128
                target[part(k, 128), place : place + 128] = low(stage[lane, pl.ds(c, 128, stride=wide), :])

    each(4, chunk)


def weight_columns(left, grads, wide, stage, target):
    def chunk(k):
        lhs = left[:, part(k, 128)]
        for at in range(2 * wide):
            value = t_dot(lhs, grads[:, 256 * at : 256 * at + 256])
            for half in range(2):
                lane = (at % 2) * 2 + half
                stage[lane, pl.ds(at // 2, 128, stride=wide), :] = value[:, 128 * half : 128 * half + 128]
        rows = part(k, 128 * wide)
        for lane in range(4):
            target[rows, lane * 128 : lane * 128 + 128] = low(stage[lane, 0 : 128 * wide, :])

    each(4, chunk)


def weight_rows(left, grads, count, target):
    def chunk(k):
        lhs = left[:, part(k, 256)]
        for at in range(2):
            target[part(k, 256), 256 * at : 256 * at + 256] = low(t_dot(lhs, grads[:, 256 * at : 256 * at + 256]))

    each(count, chunk)


def norm_rows(source, gain, target):
    def chunk(k):
        hat, _ = normed(source[part(k, 32), :].astype(F32))
        target[part(k, 32), :] = low(hat * gain)

    each(5, chunk)


def norm_rows_back(values, gain, grad, total, add):
    total[...] = jnp.zeros_like(total)

    def chunk(k):
        rows = part(k, 32)
        back, products = norm_back(values[rows, :].astype(F32), gain, grad[rows, :])
        total[...] += jnp.sum(products.reshape(4, 8, products.shape[-1]), axis=0)
        add(rows, back)

    each(5, chunk)
    return jnp.sum(total[...], axis=0, keepdims=True)


def feed_forward(inputs, gain, w_in, w_out, nrm, act, slope, result):
    norm_rows(inputs, gain, nrm)

    def up(j):
        at = part(j, 256)
        hidden = dot(nrm[...], w_in[:, at])
        sig = jax.nn.sigmoid(hidden)
        active = hidden * sig
        act[:, at] = low(active)
        slope[:, at] = low(sig + active * (1.0 - sig))

    each(FF // 256, up)

    def down(j):
        at = part(j, 256)
        result[:, at] = inputs[:, at].astype(F32) + 0.5 * dot(act[...], w_out[:, at])

    each(2, down)


def feed_back(dout, w_in, w_out, nrm, act, slope, dhid, dnrm, stage, g_in, g_out):
    def up(j):
        at = part(j, 256)
        grad = dot_t(dout[...], w_out[at, :])
        dhid[:, at] = low(grad * slope[:, at].astype(F32))

    each(FF // 256, up)
    weight_rows(act, dout, 8, g_out)

    def down(j):
        at = part(j, 256)
        dnrm[:, at] = dot_t(dhid[...], w_in[at, :])

    each(2, down)
    weight_columns(nrm, dhid, 4, stage, g_in)


def first_kernel(coords, frames, *refs):
    sources, refs = refs[:32], refs[32:]
    x1, nrm, act, slope, w_in_out, w_out_out, small, taps, raw, w_in, w_out, stage, low_small, sems, out_sems = refs
    loads = Loads(
        coords,
        sources,
        [(BLOCK["small"], 1, low_small, SMALL), (BLOCK["ffa_in"], 4, raw, ROW), (BLOCK["ffa_out"], 4, w_out, ROW)],
        sems,
    )
    loads.wait(0)
    small[...] = low_small[...].astype(F32)
    taps[...] = jnp.zeros_like(taps)
    for tap in range(KER):
        for c in range(5):
            taps[tap : tap + 1, ROW * c : ROW * c + ROW] = small[TAPS_AT + 5 * tap + c : TAPS_AT + 5 * tap + c + 1, :]
    loads.wait(1)
    split_columns(raw, w_in, 4, stage)
    keep_in = pltpu.make_async_copy(w_in, w_in_out, out_sems.at[0])
    keep_in.start()
    loads.wait(2)
    keep_out = pltpu.make_async_copy(w_out, w_out_out, out_sems.at[1])
    keep_out.start()
    feed_forward(frames, small[0:1, :], w_in, w_out, nrm, act, slope, x1)
    keep_in.wait()
    keep_out.wait()


def bucket_map():
    entry = lax.broadcasted_iota(jnp.int32, (2 * ROW, ROW), 0) // H
    far = lax.broadcasted_iota(jnp.int32, (2 * ROW, ROW), 1)
    far = jnp.where(far >= ROW // 2, far - ROW, far)
    bucket = jnp.clip(far, -(RELW // 2), RELW // 2 - 1) + RELW // 2
    return (entry == bucket).astype(F32)


def own_entries(flat):
    entry = lax.broadcasted_iota(jnp.int32, (H, 2 * ROW), 1)
    head = lax.broadcasted_iota(jnp.int32, (H, 2 * ROW), 0)
    return jnp.where(lax.rem(entry, H) == head, flat, 0.0)


def attention_kernel(coords, length, x1, small, *refs):
    sources, refs = refs[:32], refs[32:]
    a_out, nrm, qkv, probs, ctx, w_qkv_out, w_att_out, raw, w_qkv, w_att, stage, bias, sems, out_sems = refs
    loads = Loads(coords, sources, [(BLOCK["qkv"], 3, raw, ROW), (BLOCK["att_out"], 1, w_att, ROW)], sems)
    norm_rows(x1, small[1:2, :], nrm)
    qkv[SLOTS:KEYS, :] = jnp.zeros((KEYS - SLOTS, 3 * D), BF16)
    flat = jnp.concatenate([small[REL_AT : REL_AT + 1, :], small[REL_AT + 1 : REL_AT + 2, :]], axis=1)
    bias[...] = dot(low(own_entries(jnp.broadcast_to(flat, (H, 2 * ROW)))), low(bucket_map()))
    loads.wait(0)
    split_columns(raw, w_qkv, 3, stage)
    keep_qkv = pltpu.make_async_copy(w_qkv, w_qkv_out, out_sems.at[0])
    keep_qkv.start()
    loads.wait(1)
    keep_att = pltpu.make_async_copy(w_att, w_att_out, out_sems.at[1])
    keep_att.start()

    def project(j):
        at = part(j, 256)
        qkv[0:SLOTS, at] = low(dot(nrm[...], w_qkv[:, at]))

    each(3 * D // 256, project)
    valid = lax.broadcasted_iota(jnp.int32, (1, KEYS), 1) < length[0]
    first_half = lax.broadcasted_iota(jnp.int32, (1, 128), 1) < HS

    def heads(pair):
        queries = qkv[0:SLOTS, part(pair, 128)]
        keys = qkv[:, part(pair + 4, 128)]
        values = qkv[:, part(pair + 8, 128)]
        outs = []
        for odd in range(2):
            head = 2 * pair + odd
            mine = jnp.where(first_half if odd == 0 else jnp.logical_not(first_half), queries, jnp.zeros_like(queries))
            spread = jnp.broadcast_to(bias[pl.ds(head, 1), :], (SLOTS, ROW))
            spread = pltpu.roll(spread, 0, 1, stride=1, stride_axis=0)[:, 0:KEYS]
            scores = jnp.where(valid, dot_t(mine, keys) * HS ** (-0.5) + spread, MASK_FILL)
            shifted = jnp.exp(scores - jnp.max(scores, axis=-1, keepdims=True))
            chances = low(shifted / jnp.sum(shifted, axis=-1, keepdims=True))
            probs[head] = chances
            outs.append(dot(chances, values))
        ctx[:, part(pair, 128)] = low(jnp.where(first_half, outs[0], outs[1]))

    each(H // 2, heads)

    def project_out(j):
        at = part(j, 256)
        a_out[:, at] = dot(ctx[...], w_att[:, at])

    each(2, project_out)
    keep_qkv.wait()
    keep_att.wait()


def convolve(padded, taps, tap_lane, width, finish):
    def chunk(j):
        at = part(j, 128)
        total = jnp.zeros((SLOTS, 128), F32)
        for tap in range(KER):
            total = total + taps[tap : tap + 1, part(j + tap_lane // 128, 128)] * padded[tap + 1 : tap + 1 + SLOTS, at]
        finish(at, total)

    each(width // 128, chunk)


def convolve_back(grads, padded, taps, tap_lane, width, dtaps, finish):
    def chunk(j):
        at = part(j, 128)
        lane = part(j + tap_lane // 128, 128)
        total = jnp.zeros((SLOTS, 128), F32)
        for tap in range(KER):
            total = total + taps[tap : tap + 1, lane] * grads[KER - tap : KER - tap + SLOTS, at]
        finish(at, total)
        own = grads[PAD : PAD + SLOTS, at]
        for tap in range(KER):
            product = own * padded[tap + 1 : tap + 1 + SLOTS, at]
            dtaps[tap : tap + 1, lane] = jnp.sum(product, axis=0, keepdims=True)

    each(width // 128, chunk)


def clear_margins(padded):
    padded[0:PAD, :] = jnp.zeros((PAD, padded.shape[1]), F32)
    padded[PAD + SLOTS : PADDED, :] = jnp.zeros((PAD, padded.shape[1]), F32)


def gating_kernel(coords, length, x1, small, taps, *refs):
    sources, refs = refs[:32], refs[32:]
    c_out, nrm, ug, slope, gpad, cv, gated, w_cg_out, w_co_out, raw, w_cg, w_co, stage, hid, sems, out_sems = refs
    loads = Loads(coords, sources, [(BLOCK["cg_in"], 6, raw, ROW), (BLOCK["cg_out"], 3, w_co, ROW)], sems)
    norm_rows(x1, small[2:3, :], nrm)
    clear_margins(gpad)
    loads.wait(0)
    split_columns(raw, w_cg, 6, stage)
    keep_cg = pltpu.make_async_copy(w_cg, w_cg_out, out_sems.at[0])
    keep_cg.start()

    def up(j):
        at = part(j, 256)
        hid[...] = dot(nrm[...], w_cg[:, at])

        def rows(k):
            row = part(k, 32)
            hidden = hid[row, :]
            half = 0.5 + 0.5 * erf(hidden * (2.0**-0.5))
            ug[row, at] = hidden * half
            slope[row, at] = low(half + hidden * jnp.exp(-0.5 * hidden * hidden) * ((2.0 * math.pi) ** -0.5))

        each(5, rows)

    each(CG // 256, up)

    def gate(k):
        hat, _ = normed(ug[part(k, 16), GATE:])
        valid = valid_rows(k, 16, length[0])
        for c in range(3):
            at = slice(ROW * c, ROW * c + ROW)
            gpad[part(k + 1, 16), at] = hat[:, at] * small[5 + c : 6 + c, :] * valid

    each(SLOTS // 16, gate)

    def finish(at, total):
        cv[:, at] = low(total)
        gated[:, at] = low(ug[:, at] * total)

    convolve(gpad, taps, 0, GATE, finish)
    loads.wait(1)
    keep_co = pltpu.make_async_copy(w_co, w_co_out, out_sems.at[1])
    keep_co.start()

    def down(j):
        at = part(j, 256)
        c_out[:, at] = dot(gated[...], w_co[:, at])

    each(2, down)
    keep_cg.wait()
    keep_co.wait()


def last_kernel(coords, length, a_out, c_out, x1, cot, small, taps, *refs):
    sources, refs = refs[:32], refs[32:]
    out, dx, mixed, mpad, w_merge_out, sgrad, grads = refs[:7]
    (
        raw, w_merge, w_in, w_out, stage, x2, x3, nrm, act, slope, dout, dhid, dnrm, total, g_in, g_out,
        sems, out_sems,
    ) = refs[7:]
    loads = Loads(
        coords,
        sources,
        [(BLOCK["merge"], 2, w_merge, ROW), (BLOCK["ffb_in"], 4, raw, ROW), (BLOCK["ffb_out"], 4, w_out, ROW)],
        sems,
    )
    clear_margins(mpad)

    def join(k):
        row = part(k, 32)
        valid = valid_rows(k, 32, length[0])
        padded = pl.ds(pl.multiple_of(k * 32 + PAD, 16), 32)
        mpad[padded, 0:D] = a_out[row, :] * valid
        mpad[padded, D:] = c_out[row, :] * valid

    each(5, join)

    def finish_with(source, shift):
        def finish(at, value):
            mixed[:, at] = low(source[:, part_of(at, shift)] + value)

        return finish

    def part_of(at, shift):
        return pl.ds(pl.multiple_of(at.start - shift, 128), 128)

    def chunk(j):
        at = part(j, 128)
        value = jnp.zeros((SLOTS, 128), F32)
        for tap in range(KER):
            value = value + taps[tap : tap + 1, part(j + GATE // 128, 128)] * mpad[tap + 1 : tap + 1 + SLOTS, at]

        @pl.when(j < 4)
        def _():
            mixed[:, at] = low(a_out[:, at] + value)

        @pl.when(j >= 4)
        def _():
            mixed[:, at] = low(c_out[:, part(j - 4, 128)] + value)

    each(2 * D // 128, chunk)
    loads.wait(0)
    keep = pltpu.make_async_copy(w_merge, w_merge_out, out_sems.at[8])
    keep.start()

    def merge(j):
        at = part(j, 256)
        x2[:, at] = x1[:, at] + dot(mixed[...], w_merge[:, at])

    each(2, merge)
    loads.wait(1)
    split_columns(raw, w_in, 4, stage)
    loads.wait(2)
    feed_forward(x2, small[3:4, :], w_in, w_out, nrm, act, slope, x3)
    sgrad[...] = jnp.zeros_like(sgrad)
    total[...] = jnp.zeros_like(total)
    gain = small[4:5, :]

    def final(k):
        row = part(k, 32)
        valid = valid_rows(k, 32, length[0])
        values = x3[row, :]
        hat, _ = normed(values)
        out[row, :] = low(hat * gain * valid)
        back, products = norm_back(values, gain, cot[row, :].astype(F32) * valid)
        total[...] += jnp.sum(products.reshape(4, 8, D), axis=0)
        dx[row, :] = back
        dout[row, :] = low(0.5 * back)

    each(5, final)
    sgrad[4:5, :] = jnp.sum(total[...], axis=0, keepdims=True)
    feed_back(dout, w_in, w_out, nrm, act, slope, dhid, dnrm, stage, g_in, g_out)
    emits = Emits(coords, grads, out_sems)
    for at in range(4):
        emits.put(BLOCK["ffb_out"] + at, g_out.at[ROW * at : ROW * at + ROW])
    for at in range(4):
        emits.put(BLOCK["ffb_in"] + at, g_in.at[ROW * at : ROW * at + ROW])

    def add(rows, back):
        dx[rows, :] += back

    sgrad[3:4, :] = norm_rows_back(x2, small[3:4, :], dnrm, total, add)
    keep.wait()
    emits.wait()


def back_gating_kernel(
    coords, length, dx_in, mixed, mpad, x1, nrm, ug, slope, gpad, cv, gated, small, taps, sgrad_in, w_merge, w_co, w_cg,
    grads_in, *refs
):
    dx, datt, sgrad, grads = refs[:4]
    dgrad, djoin, dpad, dgate, dhid, dnrm, dtaps, total, total_gate, stage, g_merge, g_co, g_cg, out_sems = refs[4:]
    emits = Emits(coords, grads, out_sems)
    sgrad[...] = sgrad_in[...]
    clear_margins(dpad)

    def lower(k):
        dgrad[part(k, 32), :] = low(dx_in[part(k, 32), :])

    each(5, lower)

    def merge(j):
        at = part(j, 256)
        dpad[PAD : PAD + SLOTS, at] = dot_t(dgrad[...], w_merge[at, :])

    each(2 * D // 256, merge)
    weight_rows(mixed, dgrad, 4, g_merge)
    for at in range(2):
        emits.put(BLOCK["merge"] + at, g_merge.at[ROW * at : ROW * at + ROW])

    def finish(at, value):
        row_valid = valid_rows(0, SLOTS, length[0])
        djoin[:, at] = low(dpad[PAD : PAD + SLOTS, at] + value * row_valid)

    convolve_back(dpad, mpad, taps, GATE, 2 * D, dtaps, finish)
    datt[...] = djoin[:, 0:D]

    def gate(j):
        at = part(j, 256)
        value = dot_t(djoin[:, D:], w_co[at, :])
        dhid[:, at] = low(value * cv[:, at].astype(F32) * slope[:, at].astype(F32))
        dpad[PAD : PAD + SLOTS, at] = value * ug[:, at]

    each(GATE // 256, gate)

    def co_rows(k):
        lhs = gated[:, part(k, 256)]
        for at in range(2):
            place = slice(256 * at, 256 * at + 256)
            g_co[part(k, 256), place] = low(t_dot(lhs, djoin[:, D + 256 * at : D + 256 * at + 256]))

    each(6, co_rows)
    for at in range(3):
        emits.put(BLOCK["cg_out"] + at, g_co.at[ROW * at : ROW * at + ROW])

    def finish_gate(at, value):
        dgate[:, at] = value * valid_rows(0, SLOTS, length[0])

    convolve_back(dpad, gpad, taps, 0, GATE, dtaps, finish_gate)
    gain = jnp.concatenate([small[5:6, :], small[6:7, :], small[7:8, :]], axis=1)
    total_gate[...] = jnp.zeros_like(total_gate)

    def gate_norm(k):
        row = part(k, 16)
        back, products = norm_back(ug[row, GATE:], gain, dgate[row, :])
        total_gate[...] += products[0:8, :] + products[8:16, :]
        dhid[row, GATE:] = low(back * slope[row, GATE:].astype(F32))

    each(SLOTS // 16, gate_norm)
    gain_grad = jnp.sum(total_gate[...], axis=0, keepdims=True)
    for c in range(3):
        sgrad[5 + c : 6 + c, :] = gain_grad[:, ROW * c : ROW * c + ROW]
    for tap in range(KER):
        for c in range(5):
            at = TAPS_AT + 5 * tap + c
            sgrad[at : at + 1, :] = dtaps[tap : tap + 1, ROW * c : ROW * c + ROW]

    def down(j):
        at = part(j, 256)
        dnrm[:, at] = dot_t(dhid[...], w_cg[at, :])

    each(2, down)
    weight_columns(nrm, dhid, 6, stage, g_cg)
    for at in range(6):
        emits.put(BLOCK["cg_in"] + at, g_cg.at[ROW * at : ROW * at + ROW])

    def add(rows, back):
        dx[rows, :] = dx_in[rows, :] + back

    sgrad[2:3, :] = norm_rows_back(x1, small[2:3, :], dnrm, total, add)
    emits.wait()


def back_attention_kernel(
    coords, dx_in, datt, x1, nrm, qkv, probs, ctx, small, sgrad_in, w_qkv, w_att, grads_in, *refs
):
    dx, sgrad, grads, dctx, dqkv, dnrm, total, stage, sums, g_qkv, g_att, out_sems = refs
    emits = Emits(coords, grads, out_sems)
    sgrad[...] = sgrad_in[...]

    def project(j):
        at = part(j, 256)
        dctx[:, at] = low(dot_t(datt[...], w_att[at, :]))

    each(2, project)
    weight_rows(ctx, datt, 2, g_att)
    emits.put(BLOCK["att_out"], g_att)
    first_half = lax.broadcasted_iota(jnp.int32, (1, 128), 1) < HS
    at_row = lax.broadcasted_iota(jnp.int32, (SLOTS, SLOTS), 0)
    at_column = lax.broadcasted_iota(jnp.int32, (SLOTS, SLOTS), 1)
    flip = low((at_row + at_column == SLOTS - 1).astype(F32))

    def heads(pair):
        queries = qkv[0:SLOTS, part(pair, 128)]
        keys = qkv[:, part(pair + 4, 128)]
        values = qkv[:, part(pair + 8, 128)]
        context = dctx[:, part(pair, 128)]
        q_parts, k_parts, v_parts = [], [], []
        for odd in range(2):
            head = 2 * pair + odd
            half = first_half if odd == 0 else jnp.logical_not(first_half)
            chances = probs[head]
            v_parts.append(t_dot(chances, context)[0:SLOTS])
            wide_chances = chances.astype(F32)
            chance_grad = dot_t(jnp.where(half, context, jnp.zeros_like(context)), values)
            inner = jnp.sum(wide_chances * chance_grad, axis=-1, keepdims=True)
            score_grad = low(wide_chances * (chance_grad - inner))
            q_parts.append(dot(score_grad, keys))
            k_parts.append(t_dot(score_grad, queries)[0:SLOTS])
            wide = jnp.concatenate([dot(flip, score_grad), jnp.zeros((SLOTS, ROW - KEYS), F32)], axis=1)
            wide = pltpu.roll(wide, ROW - SLOTS + 1, 1, stride=1, stride_axis=0)
            sums[pl.ds(head, 1), :] = jnp.sum(wide, axis=0, keepdims=True)
        scale = HS ** (-0.5)
        dqkv[:, part(pair, 128)] = low(jnp.where(first_half, q_parts[0], q_parts[1]) * scale)
        dqkv[:, part(pair + 4, 128)] = low(jnp.where(first_half, k_parts[0], k_parts[1]) * scale)
        dqkv[:, part(pair + 8, 128)] = low(jnp.where(first_half, v_parts[0], v_parts[1]))

    each(H // 2, heads)

    def down(j):
        at = part(j, 256)
        dnrm[:, at] = dot_t(dqkv[...], w_qkv[at, :])

    each(2, down)
    weight_columns(nrm, dqkv, 3, stage, g_qkv)
    for at in range(3):
        emits.put(BLOCK["qkv"] + at, g_qkv.at[ROW * at : ROW * at + ROW])

    def add(rows, back):
        dx[rows, :] = dx_in[rows, :] + back

    sgrad[1:2, :] = norm_rows_back(x1, small[1:2, :], dnrm, total, add)
    by_entry = lax.dot_general(
        sums[...],
        bucket_map(),
        (((1,), (1,)), ((), ())),
        precision=lax.Precision.HIGHEST,
        preferred_element_type=F32,
    )
    flat = jnp.sum(own_entries(by_entry), axis=0, keepdims=True)
    sgrad[REL_AT : REL_AT + 1, :] = flat[:, 0:ROW]
    sgrad[REL_AT + 1 : REL_AT + 2, :] = flat[:, ROW:]
    emits.wait()


def back_first_kernel(coords, dx_in, frames, nrm, act, slope, small, sgrad_in, w_in, w_out, grads_in, *refs):
    fgrad, gains, grads, dout, dhid, dnrm, total, stage, g_in, g_out, g_small, out_sems = refs
    emits = Emits(coords, grads, out_sems)

    def lower(k):
        dout[part(k, 32), :] = low(0.5 * dx_in[part(k, 32), :])

    each(5, lower)
    feed_back(dout, w_in, w_out, nrm, act, slope, dhid, dnrm, stage, g_in, g_out)
    for at in range(4):
        emits.put(BLOCK["ffa_out"] + at, g_out.at[ROW * at : ROW * at + ROW])
    for at in range(4):
        emits.put(BLOCK["ffa_in"] + at, g_in.at[ROW * at : ROW * at + ROW])

    def add(rows, back):
        fgrad[rows, :] = low(dx_in[rows, :] + back)

    gain_grad = norm_rows_back(frames, small[0:1, :], dnrm, total, add)
    gains[...] = sgrad_in[0:8, :]
    gains[0:1, :] = gain_grad
    g_small[0:SMALL, :] = low(sgrad_in[...])
    g_small[0:16, :] = low(jnp.concatenate([gains[...], sgrad_in[8:16, :]], axis=0))
    g_small[SMALL:ROW, :] = jnp.zeros((ROW - SMALL, ROW), BF16)
    emits.put(BLOCK["small"], g_small)
    emits.wait()


VM = pl.BlockSpec(memory_space=pltpu.VMEM)
SM = pl.BlockSpec(memory_space=pltpu.SMEM)
ANY = pl.BlockSpec(memory_space=pl.ANY)
GRADS = ((32, ROW, ROW), BF16)


def call(kernel, name, ins, outs, scratch, aliases=None):
    return pl.pallas_call(
        kernel,
        name=name,
        in_specs=[space for space, _ in ins],
        out_specs=[space for space, _ in outs],
        out_shape=[jax.ShapeDtypeStruct(*kind) for _, kind in outs],
        scratch_shapes=[
            pltpu.SemaphoreType.DMA((each_one,)) if isinstance(each_one, int) else pltpu.VMEM(*each_one)
            for each_one in scratch
        ],
        input_output_aliases=aliases or {},
        compiler_params=pltpu.CompilerParams(vmem_limit_bytes=56 * 2**20),
    )(*[array for _, array in ins])


def layer(coords, length, frames, cot, blocks):
    sources = [(ANY, block) for block in blocks]
    place = (SM, coords)
    wide = ((SLOTS, D), F32)
    thin = ((SLOTS, D), BF16)
    ff = ((SLOTS, FF), BF16)
    x1, nrm_a, act_a, slope_a, w_ffa_in, w_ffa_out, small, taps = call(
        first_kernel,
        "ffa_forward",
        [place, (VM, frames)] + sources,
        [
            (VM, wide),
            (VM, thin),
            (VM, ff),
            (VM, ff),
            (ANY, ((D, FF), BF16)),
            (ANY, ((FF, D), BF16)),
            (VM, ((SMALL, ROW), F32)),
            (VM, ((32, 5 * ROW), F32)),
        ],
        [
            ((FF, D), BF16),
            ((D, FF), BF16),
            ((FF, D), BF16),
            ((4, 128 * 4, 128), F32),
            ((SMALL, ROW), BF16),
            9,
            2,
        ],
    )
    a_out, nrm_t, qkv, probs, ctx, w_qkv, w_att = call(
        attention_kernel,
        "attention_forward",
        [place, (SM, length), (VM, x1), (VM, small)] + sources,
        [
            (VM, wide),
            (VM, thin),
            (VM, ((KEYS, 3 * D), BF16)),
            (VM, ((H, SLOTS, KEYS), BF16)),
            (VM, thin),
            (ANY, ((D, 3 * D), BF16)),
            (ANY, ((D, D), BF16)),
        ],
        [
            ((3 * D, D), BF16),
            ((D, 3 * D), BF16),
            ((D, D), BF16),
            ((4, 128 * 3, 128), F32),
            ((H, ROW), F32),
            4,
            2,
        ],
    )
    c_out, nrm_c, ug, slope_c, gpad, cv, gated, w_cg, w_co = call(
        gating_kernel,
        "gating_forward",
        [place, (SM, length), (VM, x1), (VM, small), (VM, taps)] + sources,
        [
            (VM, wide),
            (VM, thin),
            (VM, ((SLOTS, CG), F32)),
            (VM, ((SLOTS, CG), BF16)),
            (VM, ((PADDED, GATE), F32)),
            (VM, ((SLOTS, GATE), BF16)),
            (VM, ((SLOTS, GATE), BF16)),
            (ANY, ((D, CG), BF16)),
            (ANY, ((GATE, D), BF16)),
        ],
        [
            ((CG, D), BF16),
            ((D, CG), BF16),
            ((GATE, D), BF16),
            ((4, 128 * 6, 128), F32),
            ((SLOTS, 256), F32),
            9,
            2,
        ],
    )
    out, dx2, mixed, mpad, w_merge, sgrad, grads = call(
        last_kernel,
        "merge_ffb",
        [place, (SM, length), (VM, a_out), (VM, c_out), (VM, x1), (VM, cot), (VM, small), (VM, taps)] + sources,
        [
            (VM, thin),
            (VM, wide),
            (VM, ((SLOTS, 2 * D), BF16)),
            (VM, ((PADDED, 2 * D), F32)),
            (ANY, ((2 * D, D), BF16)),
            (VM, ((SMALL, ROW), F32)),
            (ANY, GRADS),
        ],
        [
            ((FF, D), BF16),
            ((2 * D, D), BF16),
            ((D, FF), BF16),
            ((FF, D), BF16),
            ((4, 128 * 4, 128), F32),
            wide,
            wide,
            thin,
            ff,
            ff,
            thin,
            ff,
            wide,
            ((8, D), F32),
            ((FF, D), BF16),
            ((FF, D), BF16),
            10,
            9,
        ],
    )
    dx1, datt, sgrad, grads = call(
        back_gating_kernel,
        "gating_backward",
        [place, (SM, length)]
        + [(VM, a) for a in (dx2, mixed, mpad, x1, nrm_c, ug, slope_c, gpad, cv, gated, small, taps, sgrad)]
        + [(VM, w_merge), (VM, w_co), (VM, w_cg), (ANY, grads)],
        [(VM, wide), (VM, thin), (VM, ((SMALL, ROW), F32)), (ANY, GRADS)],
        [
            thin,
            ((SLOTS, 2 * D), BF16),
            ((PADDED, GATE), F32),
            ((SLOTS, GATE), F32),
            ((SLOTS, CG), BF16),
            wide,
            ((32, 5 * ROW), F32),
            ((8, D), F32),
            ((8, GATE), F32),
            ((4, 128 * 6, 128), F32),
            ((2 * D, D), BF16),
            ((GATE, D), BF16),
            ((CG, D), BF16),
            11,
        ],
        {18: 3},
    )
    dx1, sgrad, grads = call(
        back_attention_kernel,
        "attention_backward",
        [place]
        + [(VM, a) for a in (dx1, datt, x1, nrm_t, qkv, probs, ctx, small, sgrad)]
        + [(VM, w_qkv), (VM, w_att), (ANY, grads)],
        [(VM, wide), (VM, ((SMALL, ROW), F32)), (ANY, GRADS)],
        [
            thin,
            ((SLOTS, 3 * D), BF16),
            wide,
            ((8, D), F32),
            ((4, 128 * 3, 128), F32),
            ((H, ROW), F32),
            ((3 * D, D), BF16),
            ((D, D), BF16),
            4,
        ],
        {12: 2},
    )
    fgrad, gains, grads = call(
        back_first_kernel,
        "ffa_backward",
        [place]
        + [(VM, a) for a in (dx1, frames, nrm_a, act_a, slope_a, small, sgrad)]
        + [(VM, w_ffa_in), (VM, w_ffa_out), (ANY, grads)],
        [(VM, thin), (VM, ((8, ROW), F32)), (ANY, GRADS)],
        [
            thin,
            ff,
            wide,
            ((8, D), F32),
            ((4, 128 * 4, 128), F32),
            ((FF, D), BF16),
            ((FF, D), BF16),
            ((ROW, ROW), BF16),
            9,
        ],
        {10: 2},
    )
    return out, fgrad, gains, grads


def segment_bounds():
    bounds = [0]
    for extent in segment_shapes():
        bounds.append(bounds[-1] + math.prod(extent))
    return bounds


def block_rows(device_count):
    total_rows = -(-segment_bounds()[-1] // ROW)
    step = 16 * device_count
    return -(-total_rows // step) * 16


def align_shard(low_shard, shard_size, rows):
    devices = lax.axis_size("dp") * lax.axis_size("fsdp")
    me = lax.axis_index(AXES)
    block = rows * ROW
    lead = block - shard_size
    pieces = [low_shard]
    have = shard_size
    need = lead * (devices - 1) + block
    hop = 1
    while have < need:
        part = min(shard_size, need - have)
        pairs = [(i, i - hop) for i in range(hop, devices)]
        pieces.append(lax.ppermute(low_shard[:part], AXES, pairs))
        have = have + part
        hop = hop + 1
    return lax.dynamic_slice(jnp.concatenate(pieces), (me * lead,), (block,)).reshape(rows, ROW)


def unalign_block(block_sum, shard_size):
    devices = lax.axis_size("dp") * lax.axis_size("fsdp")
    me = lax.axis_index(AXES)
    rows = block_sum.shape[0]
    block = rows * ROW
    lead = block - shard_size
    flat = block_sum.reshape(-1)
    pieces = [flat]
    have = block
    need = lead * (devices - 1) + block
    hop = 1
    while have < need:
        part = min(block, need - have)
        pairs = [(i, i + hop) for i in range(devices - hop)]
        pieces.insert(0, lax.ppermute(flat[block - part :], AXES, pairs))
        have = have + part
        hop = hop + 1
    start = have - block - me * lead
    return lax.dynamic_slice(jnp.concatenate(pieces), (start,), (shard_size,))


def pair_lists():
    ring = [(i, (i + 2) % 8) for i in range(8)]
    across_x = [(i, i ^ 1) for i in range(8)]
    across_y = [(i, i ^ 2) for i in range(4)]
    across_core = [(i, i ^ 1) for i in range(4)]
    return ring, across_x, across_y, across_core


def fast_mesh():
    return lax.axis_size("dp") == 4 and lax.axis_size("fsdp") == 8


def gather_blocks(block):
    rows = block.shape[0]
    if not fast_mesh():
        whole = lax.all_gather(block, AXES, axis=0, tiled=True).reshape(32, ROW, ROW)
        order = [source_block((0, 0, 0, 0), at) for at in range(32)]
        return [whole[at] for at in order]
    ring, across_x, across_y, across_core = pair_lists()
    own = [block]
    for _ in range(3):
        own.append(lax.ppermute(own[-1], "fsdp", ring))
    by_x = [lax.ppermute(each_one, "fsdp", across_x) for each_one in own]
    by_y = [lax.ppermute(each_one, "dp", across_y) for each_one in own]
    both = [lax.ppermute(each_one, "fsdp", across_x) for each_one in by_y[:2]]
    both = both + [lax.ppermute(each_one, "dp", across_y) for each_one in by_x[2:]]
    near = own + by_x + by_y + both
    far = [lax.ppermute(each_one, "dp", across_core) for each_one in near]
    return near + far


def added(*parts):
    total = parts[0].astype(jnp.float32)
    for part in parts[1:]:
        total = total + part.astype(jnp.float32)
    return total


def scatter_blocks(grads, coords):
    if not fast_mesh():
        devices = lax.axis_size("dp") * lax.axis_size("fsdp")
        order = [gradient_slot((0, 0, 0, 0), block) for block in range(32)]
        rows = jnp.concatenate([grads[at] for at in order]).reshape(devices, -1, ROW)
        return lax.psum_scatter(rows, AXES, scatter_dimension=0).astype(F32)
    ring, across_x, across_y, across_core = pair_lists()
    z = coords[2]

    def core_sum(kind):
        theirs = lax.ppermute(grads[16 + 4 * kind : 20 + 4 * kind], "dp", across_core)
        return low(added(grads[4 * kind : 4 * kind + 4], theirs))

    diagonal = core_sum(3)
    to_x = core_sum(1)
    to_y = core_sum(2)
    mine = core_sum(0)
    from_x = lax.ppermute(diagonal[:2], "fsdp", across_x)
    from_y = lax.ppermute(diagonal[2:], "dp", across_y)
    to_y = jnp.concatenate([low(added(to_y[:2], from_x)), to_y[2:]])
    to_x = jnp.concatenate([to_x[:2], low(added(to_x[2:], from_y))])

    def at(array, back):
        return lax.dynamic_index_in_dim(array, lax.rem(z + 4 - back, 4), 0, keepdims=False)

    running = None
    for back in (1, 2, 3, 0):
        parts = [
            at(mine, back),
            lax.ppermute(at(to_x, back), "fsdp", across_x),
            lax.ppermute(at(to_y, back), "dp", across_y),
        ]
        if running is not None:
            parts.append(lax.ppermute(running, "fsdp", ring))
        running = added(*parts)
        if back:
            running = low(running)
    return running


def sum_everywhere(vector):
    if not fast_mesh():
        return lax.psum(vector, AXES)
    _, across_x, across_y, across_core = pair_lists()
    near_z = [(i, i ^ 2) for i in range(8)]
    far_z = [(i, i ^ 4) for i in range(8)]
    for axis, pairs in (
        ("dp", across_core),
        ("fsdp", across_x),
        ("dp", across_y),
        ("fsdp", near_z),
        ("fsdp", far_z),
    ):
        vector = vector + lax.ppermute(vector, axis, pairs)
    return vector


def most_segments(shard_size, devices):
    bounds = segment_bounds()
    most = 1
    for at in range(devices):
        low, high = at * shard_size, (at + 1) * shard_size
        most = max(most, sum(1 for b in bounds[1:-1] if low < b < high) + 1)
    return most


def shards(frames, lengths, cotangent, params, first_moment, second_moment):
    shard_size = params.shape[0]
    devices = lax.axis_size("dp") * lax.axis_size("fsdp")
    me = lax.axis_index(AXES)
    rows = block_rows(devices)
    if fast_mesh():
        dp, fsdp = lax.axis_index("dp"), lax.axis_index("fsdp")
        coords = jnp.stack([dp // 2, dp % 2, fsdp // 2, fsdp % 2]).astype(jnp.int32)
    else:
        coords = jnp.zeros((4,), jnp.int32)
    blocks = gather_blocks(align_shard(low(params), shard_size, rows))
    result, frames_grad, gains, grads = layer(coords, lengths, frames[0], cotangent[0], blocks)
    block_sum = scatter_blocks(grads, coords)
    grad_shard = unalign_block(low(block_sum), shard_size).astype(F32)
    new_first = BETA_FIRST * first_moment + (1.0 - BETA_FIRST) * grad_shard
    new_second = BETA_SECOND * second_moment + (1.0 - BETA_SECOND) * grad_shard * grad_shard
    first_hat = new_first / (1.0 - BETA_FIRST**STEP)
    second_hat = new_second / (1.0 - BETA_SECOND**STEP)
    update = first_hat / (jnp.sqrt(second_hat) + ADAM_EPS) + WEIGHT_DECAY * params
    count = len(segment_shapes())
    bounds = segment_bounds()
    spans = most_segments(shard_size, devices)
    shard_low = me * shard_size
    first_segment = sum((shard_low >= b).astype(jnp.int32) for b in bounds[1:-1])
    table = jnp.asarray(bounds[1:] + [bounds[-1]] * spans, jnp.int32)
    ends = lax.dynamic_slice(table, (first_segment,), (spans,)) - shard_low
    positions = lax.iota(jnp.int32, shard_size)

    def segment_sums(values):
        total = jnp.zeros((count + spans,), jnp.float32)
        sums = []
        low = jnp.int32(0)
        for at in range(spans):
            inside = (positions >= low) & (positions < ends[at])
            sums.append(jnp.sum(jnp.where(inside, values, 0.0)))
            low = ends[at]
        return lax.dynamic_update_slice(total, jnp.stack(sums), (first_segment,))[:count]

    parts = jnp.concatenate(
        [segment_sums(params * params), segment_sums(update * update), jnp.zeros((8,), jnp.float32)]
    )
    everywhere = sum_everywhere(jnp.concatenate([parts, gains.reshape(-1)]))
    weight_squares = everywhere[:count]
    update_squares = everywhere[count : 2 * count]
    gain_grads = everywhere[parts.shape[0] :]
    weight_norms = jnp.sqrt(weight_squares)
    update_norms = jnp.sqrt(update_squares)
    trust_ratios = weight_norms / (update_norms + ADAM_EPS)
    near_trust = lax.dynamic_slice(
        jnp.concatenate([trust_ratios, jnp.zeros((spans,), jnp.float32)]), (first_segment,), (spans,)
    )
    entry_trust = jnp.broadcast_to(near_trust[spans - 1], (shard_size,))
    for at in range(spans - 2, -1, -1):
        entry_trust = jnp.where(positions < ends[at], near_trust[at], entry_trust)
    new_params = params - LEARN_RATE * entry_trust * update
    return (
        result.reshape(frames.shape),
        frames_grad.reshape(frames.shape),
        new_params,
        new_first,
        new_second,
        weight_norms,
        update_norms,
        trust_ratios,
        gain_grads,
    )


def solution(mesh):
    placed = (
        P(("dp", "fsdp"), None, None),
        P(("dp", "fsdp")),
        P(("dp", "fsdp"), None, None),
        P(("dp", "fsdp")),
        P(("dp", "fsdp")),
        P(("dp", "fsdp")),
    )
    return jax.shard_map(
        shards,
        mesh=mesh,
        in_specs=placed,
        out_specs=(
            P(("dp", "fsdp"), None, None),
            P(("dp", "fsdp"), None, None),
            P(("dp", "fsdp")),
            P(("dp", "fsdp")),
            P(("dp", "fsdp")),
            P(),
            P(),
            P(),
            P(),
        ),
        check_vma=False,
    )
```

time: 1300 us -> 404 us (0.31); the launches traced: 1280 us -> 404 us
  waiting for transfers between devices: 679 us -> 179 us
  local copies, waits for them, and re-layouts: 247 us -> 10.1 us
  other arithmetic: 175 us -> 38.5 us
  Pallas kernels: 0 us -> 121 us
  matrix products: 119 us -> 0 us
  starting transfers between devices: 5.75 us -> 53.5 us
  blocking collectives: 39.5 us -> 0 us
  between operations: 17.7 us -> 1.8 us
    all_to_all x1 -> x0, waiting for transfers between devices: 355 us -> none  [shards(): lax.all_to_all(grad_grid.astype(jnp.bfloat16), 'fsdp', split_axis=1, conc...]
    unnamed x4 -> x0, waiting for transfers between devices: 324 us -> none
    ppermute x0 -> x55, waiting for transfers between devices: none -> 179 us  [the longest x4 28.2 us: scatter_blocks(): lax.ppermute(at(to_y, back), 'dp', across_y)]
    pallas_call x0 -> x7, Pallas kernels: none -> 121 us  [call(): pl.pallas_call(kernel, name=name, in_specs=[space for space, _ in ins], o...]
    dot_general x85 -> x0, matrix products: 119 us -> none  [the longest x25 39.4 us: contract_rows(): lax.dot_general(left, right, (((0,), (0,)), ((), ())), preferred_element_...]
    reduce_sum x36 -> x2, other arithmetic: 103 us -> 13.6 us  [segment_sums(): sums.append(jnp.sum(jnp.where(inside, values, 0.0)))]
    unnamed x433 -> x58, local copies, waits for them, and re-layouts: 66.5 us -> 0.32 us
    ppermute x0 -> x55, starting transfers between devices: none -> 53.5 us  [the longest x4 9.07 us: gather_blocks(): by_x = [lax.ppermute(each_one, 'fsdp', across_x) for each_one in own]]
  transfers between devices with their start and end apart: 3 -> 55, of which waited for: 3 -> 35; matrix products, arithmetic and copies ran while one was open for 0% -> 2% of each run, Pallas kernels for 0% -> 0%
where the time goes in v1:
time: 404 us
  waiting for transfers between devices  179 us (44%)
  Pallas kernels  121 us (30%)
  starting transfers between devices  53.5 us (13%)
  other arithmetic  38.5 us (10%)
  local copies, waits for them, and re-layouts  10.1 us (2%)
    pallas_call x7, Pallas kernels, call(): pl.pallas_call(kernel, name=name, in_specs=[space for space, _ in ins], o...  121 us
    ppermute x4, waiting for transfers between devices, scatter_blocks(): lax.ppermute(at(to_y, back), 'dp', across_y)  28.2 us
    ppermute x1, waiting for transfers between devices, scatter_blocks(): from_x = lax.ppermute(diagonal[:2], 'fsdp', across_x)  23.3 us
    ppermute x2, waiting for transfers between devices, gather_blocks(): lax.ppermute(each_one, 'dp', across_y)  19.2 us
    ppermute x3, waiting for transfers between devices, gather_blocks(): own.append(lax.ppermute(own[-1], 'fsdp', ring))  17.3 us
    ppermute x2, waiting for transfers between devices, gather_blocks(): both = [lax.ppermute(each_one, 'fsdp', across_x) for each_one in by_y[:2]]  16 us
    ppermute x4, waiting for transfers between devices, gather_blocks(): by_x = [lax.ppermute(each_one, 'fsdp', across_x) for each_one in own]  15.8 us
    reduce_sum x2, other arithmetic, segment_sums(): sums.append(jnp.sum(jnp.where(inside, values, 0.0)))  13.6 us
  transfers between devices with their start and end apart: 55, of which 35 were waited for; matrix products, arithmetic and copies ran while one was open for 2% of the time, Pallas kernels for 0%

profile of v1, /device:TPU:0, one launch (start us, length us, event | category | flops | bytes accessed | tf_op | source)
XLA Modules:
  0.0 403.7 jit_solution(8535066058800114254)
XLA Ops:
  2.1 5.4 %select_reduce_fusion.7 = (f32[]{:T(128)}, f32[]{:T(128)}, f32[]{:T(128)}, f32[]{:T(128)}, bf16[256592]{0:T(1024)(128)(2,1)S(1)}) fusion(f32[256592]{0:T(1024)} %param.10, s32[]{:T(128)} %bitcast.8, s32[]{:T(128)} %bitcast.10, s32[]{:T(128)} %bitcast.12, s32[]{:T(128)} %bitcast.14), kind=kLoop, calls=%fused_computation.57 | loop fusion | flops 5131836 | bytes 1539584 | tf_op jit(solution)/shard_map/reduce_sum | solution.py:1140
  8.8 11.9 %collective-permute-done = bf16[177664]{0:T(1024)(128)(2,1)S(1)} collective-permute-done((bf16[177664]{0:T(1024)(128)(2,1)S(1)}, bf16[177664]{0:T(1024)(128)(2,1)S(1)}, u32[]{:S(2)}, u32[]{:S(2)}) %collective-permute-start) | collective-permute-done | bytes 355360 | tf_op jit(solution)/shard_map/ppermute | solution.py:975
  20.7 1.9 fusion.15
  22.9 1.9 collective-permute-start.1
  24.8 2.4 collective-permute-start.4
  27.2 1.5 collective-permute-start.8
  28.7 9.2 %collective-permute-done.1.refs_1_ = bf16[512,512]{1,0:T(8,128)(2,1)S(1)} collective-permute-done((bf16[512,512]{1,0:T(8,128)(2,1)S(1)}, bf16[512,512]{1,0:T(8,128)(2,1)S(1)}, u32[]{:S(2)}, u32[]{:S(2)}) %collective-permute-start.1) | collective-permute-done | bytes 524320 | tf_op jit(solution)/shard_map/ppermute | solution.py:1023
  37.9 2.1 collective-permute-start.5
  40.0 3.2 collective-permute-start.9
  43.2 1.9 collective-permute-start.12
  45.1 6.7 %collective-permute-done.2.refs_2_ = bf16[512,512]{1,0:T(8,128)(2,1)S(1)} collective-permute-done((bf16[512,512]{1,0:T(8,128)(2,1)S(1)}, bf16[512,512]{1,0:T(8,128)(2,1)S(1)}, u32[]{:S(2)}, u32[]{:S(2)}) %collective-permute-start.2) | collective-permute-done | bytes 524320 | tf_op jit(solution)/shard_map/ppermute | solution.py:1023
  51.9 2.4 collective-permute-start.24
  55.6 7.0 %collective-permute-done.12.refs_12_ = bf16[512,512]{1,0:T(8,128)(2,1)S(1)} collective-permute-done((bf16[512,512]{1,0:T(8,128)(2,1)S(1)}, bf16[512,512]{1,0:T(8,128)(2,1)S(1)}, u32[]{:S(2)}, u32[]{:S(2)}) %collective-permute-start.12) | collective-permute-done | bytes 524320 | tf_op jit(solution)/shard_map/ppermute | solution.py:1026
  62.6 2.3 collective-permute-start.6
  65.0 2.8 collective-permute-start.10
  67.8 1.7 collective-permute-start.13
  69.6 1.5 collective-permute-done.3.refs_3_
  71.1 6.3 %collective-permute-done.6.refs_6_ = bf16[512,512]{1,0:T(8,128)(2,1)S(1)} collective-permute-done((bf16[512,512]{1,0:T(8,128)(2,1)S(1)}, bf16[512,512]{1,0:T(8,128)(2,1)S(1)}, u32[]{:S(2)}, u32[]{:S(2)}) %collective-permute-start.6) | collective-permute-done | bytes 524320 | tf_op jit(solution)/shard_map/ppermute | solution.py:1024
  79.7 8.9 %collective-permute-done.13.refs_13_ = bf16[512,512]{1,0:T(8,128)(2,1)} collective-permute-done((bf16[512,512]{1,0:T(8,128)(2,1)S(1)}, bf16[512,512]{1,0:T(8,128)(2,1)}, u32[]{:S(2)}, u32[]{:S(2)}) %collective-permute-start.13) | collective-permute-done | bytes 524320 | tf_op jit(solution)/shard_map/ppermute | solution.py:1026
  88.7 2.2 collective-permute-start.7
  93.7 9.5 %collective-permute-done.7.refs_7_ = bf16[512,512]{1,0:T(8,128)(2,1)} collective-permute-done((bf16[512,512]{1,0:T(8,128)(2,1)S(1)}, bf16[512,512]{1,0:T(8,128)(2,1)}, u32[]{:S(2)}, u32[]{:S(2)}) %collective-permute-start.7) | collective-permute-done | bytes 524320 | tf_op jit(solution)/shard_map/ppermute | solution.py:1024
  103.2 2.7 collective-permute-done.11.refs_11_
  106.8 10.3 %collective-permute-done.14.refs_14_ = bf16[512,512]{1,0:T(8,128)(2,1)} collective-permute-done((bf16[512,512]{1,0:T(8,128)(2,1)S(1)}, bf16[512,512]{1,0:T(8,128)(2,1)}, u32[]{:S(2)}, u32[]{:S(2)}) %collective-permute-start.14) | collective-permute-done | bytes 524320 | tf_op jit(solution)/shard_map/ppermute | solution.py:1027
  118.3 8.9 %collective-permute-done.15.refs_15_ = bf16[512,512]{1,0:T(8,128)(2,1)} collective-permute-done((bf16[512,512]{1,0:T(8,128)(2,1)}, bf16[512,512]{1,0:T(8,128)(2,1)}, u32[]{:S(2)}, u32[]{:S(2)}) %collective-permute-start.15) | collective-permute-done | bytes 524320 | tf_op jit(solution)/shard_map/ppermute | solution.py:1027
  129.6 9.4 %ffa_forward.1 = (f32[160,512]{1,0:T(8,128)}, bf16[160,512]{1,0:T(8,128)(2,1)}, bf16[160,2048]{1,0:T(8,128)(2,1)}, bf16[160,2048]{1,0:T(8,128)(2,1)}, bf16[512,2...) custom-call(s32[4]{0:T(128)} %pad_add_fusion.coords, ...), custom_call_target="tpu_custom_call" | custom-call | tf_op jit(solution)/shard_map/ffa_forward/pallas_call | solution.py:755
  139.0 9.6 %attention_forward.1 = (f32[160,512]{1,0:T(8,128)}, bf16[160,512]{1,0:T(8,128)(2,1)}, bf16[256,1536]{1,0:T(8,128)(2,1)}, bf16[8,160,256]{2,1,0:T(8,128)(2,1)}, b...) custom-call(s32[4]{0:T(128)} %pad_add_fusion.coords, s32[1]{0:T(128)S(6)} %copy.26.length, ...), custom_call_target="tpu_custom_call" | custom-call | tf_op jit(solution)/shard_map/attention_forward/pallas_call | solution.py:755
  148.6 21.6 %gating_forward.1 = (f32[160,512]{1,0:T(8,128)}, bf16[160,512]{1,0:T(8,128)(2,1)}, f32[160,3072]{1,0:T(8,128)}, bf16[160,3072]{1,0:T(8,128)(2,1)}, f32[192,1536]...) custom-call(s32[4]{0:T(128)} %pad_add_fusion.coords, ...), custom_call_target="tpu_custom_call" | custom-call | tf_op jit(solution)/shard_map/gating_forward/pallas_call | solution.py:755
  170.2 20.5 %merge_ffb.1 = (bf16[160,512]{1,0:T(8,128)(2,1)}, f32[160,512]{1,0:T(8,128)}, bf16[160,1024]{1,0:T(8,128)(2,1)}, f32[192,1024]{1,0:T(8,128)}, bf16[1024,512]{1,0...) custom-call(s32[4]{0:T(128)} %pad_add_fusion.coords, s32[1]{0:T(128)S(6)} %copy.26.length, ...), custom_call_target="tpu_custom_call" | custom-call | tf_op jit(solution)/shard_map/merge_ffb/pallas_call | solution.py:755
  190.7 34.7 %gating_backward.1 = (f32[160,512]{1,0:T(8,128)}, bf16[160,512]{1,0:T(8,128)(2,1)}, f32[176,512]{1,0:T(8,128)}, bf16[32,512,512]{2,1,0:T(8,128)(2,1)}) custom-call(s32[4]{0:T(128)} %pad_add_fusion.coords, s32[1]{0:T(128)S(6)} %copy.26.length, f32[160,512]{1,0:T(8,128)} %get-tuple-element.56.dx_in, ...), custom_call_target="tpu_custom_call", output_to_operand_aliasing={{3}: (18, {})} | custom-call | tf_op jit(solution)/shard_map/gating_backward/pallas_call | solution.py:755
  225.4 12.7 %attention_backward.1 = (f32[160,512]{1,0:T(8,128)}, f32[176,512]{1,0:T(8,128)}, bf16[32,512,512]{2,1,0:T(8,128)(2,1)}) custom-call(s32[4]{0:T(128)} %pad_add_fusion.coords, f32[160,512]{1,0:T(8,128)} %get-tuple-element.70.dx_in, bf16[160,512]{1,0:T(8,128)(2,1)} %get-tuple-element.71.datt, ...), custom_call_target="tpu_custom_call", output_to_operand_aliasing={{2}: (12, {})} | custom-call | tf_op jit(solution)/shard_map/attention_backward/pallas_call | solution.py:755
  238.1 12.8 %ffa_backward.1 = (bf16[160,512]{1,0:T(8,128)(2,1)}, f32[8,512]{1,0:T(8,128)}, bf16[32,512,512]{2,1,0:T(8,128)(2,1)}) custom-call(s32[4]{0:T(128)} %pad_add_fusion.coords, f32[160,512]{1,0:T(8,128)} %get-tuple-element.80.dx_in, bf16[160,512]{1,0:T(8,128)(2,1)} %bitcast.62, bf16[160,512]{1,0:T(8,128)(2,1)} %get-tuple-element.81.nrm, ...), custom_call_target="tpu_custom_call", output_to_operand_aliasing={{2}: (10, {})} | custom-call | tf_op jit(solution)/shard_map/ffa_backward/pallas_call | solution.py:755
  250.9 4.1 %fusion.35 = (bf16[4,512,512]{2,1,0:T(8,128)(2,1)S(1)}, bf16[4,512,512]{2,1,0:T(8,128)(2,1)S(1)}, bf16[4,512,512]{2,1,0:T(8,128)(2,1)S(1)}, bf16[4,512,512]{2,1,0:T(8,128)(2,1)S(1)}) fusion(bf16[32,512,512]{2,1,0:T(8,128)(2,1)} %get-tuple-element.89), kind=kLoop, calls=%fused_computation.91 | loop fusion | bytes 16777216 | tf_op jit(solution)/shard_map/slice | solution.py:1050
  256.1 3.1 collective-permute-done.32
  259.2 6.0 %collective-permute-done.37 = bf16[4,512,512]{2,1,0:T(8,128)(2,1)S(1)} collective-permute-done((bf16[4,512,512]{2,1,0:T(8,128)(2,1)S(1)}, bf16[4,512,512]{2,1,0:T(8,128)(2,1)S(1)}, u32[]{:S(2)}, u32[]{:S(2)}) %collective-permute-start.37) | collective-permute-done | bytes 2097184 | tf_op jit(solution)/shard_map/ppermute | solution.py:1050
  265.2 3.0 collective-permute-done.34
  268.2 5.4 %add_convert_fusion.3 = (bf16[4,512,512]{2,1,0:T(8,128)(2,1)}, bf16[4,512,512]{2,1,0:T(8,128)(2,1)}, bf16[4,512,512]{2,1,0:T(8,128)(2,1)S(1)}, bf16[4,512,512]{2,1,0:T(8,128)(2,1)S(1)}) fusion(bf16[4,512,512]{2,1,0:T(8,128)(2,1)S(1)} %collective-permute-done.32, bf16[32,512,512]{2,1,0:T(8,128)(2,1)S(1)} %copy-done, ...), kind=kLoop, calls=%fused_computation.3 | loop fusion | flops 16777216 | bytes 25165824 | tf_op jit(solution)/shard_map/convert_element_type | solution.py:83
  273.6 1.5 fusion.36
  275.9 1.4 slice.135
  277.4 23.3 %collective-permute-done.38 = bf16[2,512,512]{2,1,0:T(8,128)(2,1)} collective-permute-done((bf16[2,512,512]{2,1,0:T(8,128)(2,1)}, bf16[2,512,512]{2,1,0:T(8,128)(2,1)}, u32[]{:S(2)}, u32[]{:S(2)}) %collective-permute-start.38) | collective-permute-done | bytes 1048608 | tf_op jit(solution)/shard_map/ppermute | solution.py:1057
  300.7 1.5 add_convert_fusion.4
  304.9 1.6 collective-permute-start.43
  306.5 1.7 collective-permute-start.42
  308.2 9.7 %collective-permute-done.45 = bf16[512,512]{1,0:T(8,128)(2,1)S(1)} collective-permute-done((bf16[512,512]{1,0:T(8,128)(2,1)S(1)}, bf16[512,512]{1,0:T(8,128)(2,1)S(1)}, u32[]{:S(2)}, u32[]{:S(2)}) %collective-permute-start.45) | collective-permute-done | bytes 524320 | tf_op jit(solution)/shard_map/ppermute | solution.py:1070
  317.9 1.4 collective-permute-done.44
  319.6 1.8 collective-permute-start.41
  321.8 7.4 %collective-permute-done.43 = bf16[512,512]{1,0:T(8,128)(2,1)S(1)} collective-permute-done((bf16[512,512]{1,0:T(8,128)(2,1)S(1)}, bf16[512,512]{1,0:T(8,128)(2,1)S(1)}, u32[]{:S(2)}, u32[]{:S(2)}) %collective-permute-start.43) | collective-permute-done | bytes 524320 | tf_op jit(solution)/shard_map/ppermute | solution.py:1070
  330.5 1.7 collective-permute-done.46
  332.5 1.7 collective-permute-start.39
  334.7 5.7 %collective-permute-done.41 = bf16[512,512]{1,0:T(8,128)(2,1)S(1)} collective-permute-done((bf16[512,512]{1,0:T(8,128)(2,1)S(1)}, bf16[512,512]{1,0:T(8,128)(2,1)S(1)}, u32[]{:S(2)}, u32[]{:S(2)}) %collective-permute-start.41) | collective-permute-done | bytes 524320 | tf_op jit(solution)/shard_map/ppermute | solution.py:1070
  341.7 2.2 collective-permute-done.47
  344.3 5.5 %collective-permute-done.39 = bf16[512,512]{1,0:T(8,128)(2,1)S(1)} collective-permute-done((bf16[512,512]{1,0:T(8,128)(2,1)S(1)}, bf16[512,512]{1,0:T(8,128)(2,1)S(1)}, u32[]{:S(2)}, u32[]{:S(2)}) %collective-permute-start.39) | collective-permute-done | bytes 524320 | tf_op jit(solution)/shard_map/ppermute | solution.py:1070
  351.0 4.3 %collective-permute-done.48 = bf16[512,512]{1,0:T(8,128)(2,1)S(1)} collective-permute-done((bf16[512,512]{1,0:T(8,128)(2,1)S(1)}, bf16[512,512]{1,0:T(8,128)(2,1)S(1)}, u32[]{:S(2)}, u32[]{:S(2)}) %collective-permute-start.48) | collective-permute-done | bytes 524320 | tf_op jit(solution)/shard_map/ppermute | solution.py:1073
  356.0 2.3 collective-permute-start.49
  358.3 2.6 maximum_dynamic-update-slice_fusion
  360.9 2.1 collective-permute-done.49
  363.0 8.2 %select_reduce_fusion.3 = (f32[]{:T(128)}, f32[]{:T(128)}, f32[]{:T(128)}, f32[]{:T(128)}, f32[256592]{0:T(1024)S(1)}, /*index=5*/f32[256592]{0:T(1024)}, f32[256592]{0:T(1024)}) fusion(s32[]{:T(128)} %bitcast.8, s32[]{:T(128)} %bitcast.10, s32[]{:T(128)} %bitcast.12, s32[]{:T(128)} %bitcast.14, f32[256592]{0:T(1024)S(1)} %copy-done.2, s32[]{:T(128)S(6)} %select_n.100, ...), kind=kLoop, calls=%fused_computation.44 | loop fusion | flops 10263676 | bytes 7026756 | tf_op jit(solution)/shard_map/reduce_sum | solution.py:1140
  371.2 2.8 maximum_dynamic-update-slice_fusion.1
  375.9 1.9 collective-permute-start.51
  377.8 1.9 collective-permute-done.51
  379.7 5.9 %collective-permute-start.52 = (f32[4128]{0:T(1024)S(1)}, f32[4128]{0:T(1024)S(1)}, u32[]{:S(2)}, u32[]{:S(2)}) collective-permute-start(f32[4128]{0:T(1024)S(1)} %add.231), channel_id=1, source_target_pairs={{0,16},{8,24},{16,0},{24,8},{1,17},{9,25},{17,1},{25,9},{2,18},{10... | collective-permute-start | bytes 49544 | tf_op jit(solution)/shard_map/ppermute | solution.py:1093
  385.6 1.8 collective-permute-done.52
  387.4 3.8 collective-permute-done.53
  391.2 4.7 %collective-permute-done.54 = f32[4128]{0:T(1024)S(1)} collective-permute-done((f32[4128]{0:T(1024)S(1)}, f32[4128]{0:T(1024)S(1)}, u32[]{:S(2)}, u32[]{:S(2)}) %collective-permute-start.54) | collective-permute-done | bytes 16544 | tf_op jit(solution)/shard_map/ppermute | solution.py:1093
  397.9 5.8 %multiply_subtract_fusion = f32[256592]{0:T(1024)} fusion(f32[256592]{0:T(1024)S(1)} %copy-done.2, f32[256592]{0:T(1024)S(1)} %get-tuple-element.102, f32[]{:T(128)} %bitcast.35, f32[]{:T(128)} %bitcast.34, f32[]{:T(128)} %bitcast.33, f32[]{:T(128)} %bitcast.32, s32[]{:T(128)} %bitcast.12, s32[]{:T(128)} %bitcast.10, s32[]{:T(128)} %bitcast.8), kind=kLoop, calls=%fused_computation.40 | loop fusion | flops 2309328 | bytes 3079132 | tf_op jit(solution)/shard_map/sub | solution.py:1160
  (149 shorter events, 28.3 us)
Async XLA Ops:
  7.5 13.2 %collective-permute-start = (bf16[177664]{0:T(1024)(128)(2,1)S(1)}, bf16[177664]{0:T(1024)(128)(2,1)S(1)}, u32[]{:S(2)}, u32[]{:S(2)}) collective-permute-start(bf16[177664]{0:T(1024)(128)(2,1)S(1)} %slice.129), channel_id=1, source_target_pairs={{1,0},{2,1},{3,2},{4,3},{5,4},{6,5},{7,6},{8,7},{9,8},{10,9},{11,1... | collective-permute-start | bytes 1065992 | tf_op jit(solution)/shard_map/ppermute | solution.py:975
  22.9 106.6 %copy-start.1 = (bf16[512,512]{1,0:T(8,128)(2,1)}, bf16[512,512]{1,0:T(8,128)(2,1)S(1)}, u32[]{:S(2)}) copy-start(bf16[512,512]{1,0:T(8,128)(2,1)S(1)} %reshape.41.refs_0_) | copy-start | bytes 1572868
  22.9 15.0 %collective-permute-start.1 = (bf16[512,512]{1,0:T(8,128)(2,1)S(1)}, bf16[512,512]{1,0:T(8,128)(2,1)S(1)}, u32[]{:S(2)}, u32[]{:S(2)}) collective-permute-start(bf16[512,512]{1,0:T(8,128)(2,1)S(1)} %reshape.41.refs_0_), channel_id=1, source_target_pairs={{0,2},{1,3},{2,4},{3,5},{4,6},{5,7},{6,0},{7,1},{8,10},{9,11},{10,... | collective-permute-start | bytes 1572872 | tf_op jit(solution)/shard_map/ppermute | solution.py:1023
  24.8 15.2 %collective-permute-start.4 = (bf16[512,512]{1,0:T(8,128)(2,1)S(1)}, bf16[512,512]{1,0:T(8,128)(2,1)S(1)}, u32[]{:S(2)}, u32[]{:S(2)}) collective-permute-start(bf16[512,512]{1,0:T(8,128)(2,1)S(1)} %reshape.41.refs_0_), channel_id=1, source_target_pairs={{0,1},{1,0},{2,3},{3,2},{4,5},{5,4},{6,7},{7,6},{8,9},{9,8},{10,11... | collective-permute-start | bytes 1572872 | tf_op jit(solution)/shard_map/ppermute | solution.py:1024
  27.2 16.0 %collective-permute-start.8 = (bf16[512,512]{1,0:T(8,128)(2,1)S(1)}, bf16[512,512]{1,0:T(8,128)(2,1)S(1)}, u32[]{:S(2)}, u32[]{:S(2)}) collective-permute-start(bf16[512,512]{1,0:T(8,128)(2,1)S(1)} %reshape.41.refs_0_), channel_id=1, source_target_pairs={{0,16},{8,24},{16,0},{24,8},{1,17},{9,25},{17,1},{25,9},{2,18},{10... | collective-permute-start | bytes 1572872 | tf_op jit(solution)/shard_map/ppermute | solution.py:1025
  28.7 16.4 %collective-permute-start.16 = (bf16[512,512]{1,0:T(8,128)(2,1)S(1)}, bf16[512,512]{1,0:T(8,128)(2,1)S(1)}, u32[]{:S(2)}, u32[]{:S(2)}) collective-permute-start(bf16[512,512]{1,0:T(8,128)(2,1)S(1)} %reshape.41.refs_0_), channel_id=1, source_target_pairs={{0,8},{8,0},{16,24},{24,16},{1,9},{9,1},{17,25},{25,17},{2,10},{10... | collective-permute-start | bytes 1572872 | tf_op jit(solution)/shard_map/ppermute | solution.py:1029
  37.9 91.7 %copy-start.4 = (bf16[512,512]{1,0:T(8,128)(2,1)}, bf16[512,512]{1,0:T(8,128)(2,1)S(1)}, u32[]{:S(2)}) copy-start(bf16[512,512]{1,0:T(8,128)(2,1)S(1)} %collective-permute-done.1.refs_1_) | copy-start | bytes 1572868
  37.9 14.0 %collective-permute-start.2 = (bf16[512,512]{1,0:T(8,128)(2,1)S(1)}, bf16[512,512]{1,0:T(8,128)(2,1)S(1)}, u32[]{:S(2)}, u32[]{:S(2)}) collective-permute-start(bf16[512,512]{1,0:T(8,128)(2,1)S(1)} %collective-permute-done.1.refs_1_), channel_id=1, source_target_pairs={{0,2},{1,3},{2,4},{3,5},{4,6},{5,7},{6,0},{7,1},{8,10},{9,11},{10,... | collective-permute-start | bytes 1572872 | tf_op jit(solution)/shard_map/ppermute | solution.py:1023
  37.9 14.0 %collective-permute-start.5 = (bf16[512,512]{1,0:T(8,128)(2,1)S(1)}, bf16[512,512]{1,0:T(8,128)(2,1)S(1)}, u32[]{:S(2)}, u32[]{:S(2)}) collective-permute-start(bf16[512,512]{1,0:T(8,128)(2,1)S(1)} %collective-permute-done.1.refs_1_), channel_id=1, source_target_pairs={{0,1},{1,0},{2,3},{3,2},{4,5},{5,4},{6,7},{7,6},{8,9},{9,8},{10,11... | collective-permute-start | bytes 1572872 | tf_op jit(solution)/shard_map/ppermute | solution.py:1024
  40.0 89.5 %copy-start.5 = (bf16[512,512]{1,0:T(8,128)(2,1)}, bf16[512,512]{1,0:T(8,128)(2,1)S(1)}, u32[]{:S(2)}) copy-start(bf16[512,512]{1,0:T(8,128)(2,1)S(1)} %collective-permute-done.4.refs_4_) | copy-start | bytes 1572868
  40.0 15.6 %collective-permute-start.9 = (bf16[512,512]{1,0:T(8,128)(2,1)S(1)}, bf16[512,512]{1,0:T(8,128)(2,1)S(1)}, u32[]{:S(2)}, u32[]{:S(2)}) collective-permute-start(bf16[512,512]{1,0:T(8,128)(2,1)S(1)} %collective-permute-done.1.refs_1_), channel_id=1, source_target_pairs={{0,16},{8,24},{16,0},{24,8},{1,17},{9,25},{17,1},{25,9},{2,18},{10... | collective-permute-start | bytes 1572872 | tf_op jit(solution)/shard_map/ppermute | solution.py:1025
  43.2 86.4 %copy-start.6 = (bf16[512,512]{1,0:T(8,128)(2,1)}, bf16[512,512]{1,0:T(8,128)(2,1)S(1)}, u32[]{:S(2)}) copy-start(bf16[512,512]{1,0:T(8,128)(2,1)S(1)} %collective-permute-done.8.refs_8_) | copy-start | bytes 1572868
  43.2 19.4 %collective-permute-start.12 = (bf16[512,512]{1,0:T(8,128)(2,1)S(1)}, bf16[512,512]{1,0:T(8,128)(2,1)S(1)}, u32[]{:S(2)}, u32[]{:S(2)}) collective-permute-start(bf16[512,512]{1,0:T(8,128)(2,1)S(1)} %collective-permute-done.8.refs_8_), channel_id=1, source_target_pairs={{0,1},{1,0},{2,3},{3,2},{4,5},{5,4},{6,7},{7,6},{8,9},{9,8},{10,11... | collective-permute-start | bytes 1572872 | tf_op jit(solution)/shard_map/ppermute | solution.py:1026
  45.1 84.4 %copy-start.7 = (bf16[512,512]{1,0:T(8,128)(2,1)}, bf16[512,512]{1,0:T(8,128)(2,1)S(1)}, u32[]{:S(2)}) copy-start(bf16[512,512]{1,0:T(8,128)(2,1)S(1)} %collective-permute-done.16.refs_16_) | copy-start | bytes 1572868
  45.1 19.8 %collective-permute-start.17 = (bf16[512,512]{1,0:T(8,128)(2,1)S(1)}, bf16[512,512]{1,0:T(8,128)(2,1)S(1)}, u32[]{:S(2)}, u32[]{:S(2)}) collective-permute-start(bf16[512,512]{1,0:T(8,128)(2,1)S(1)} %collective-permute-done.1.refs_1_), channel_id=1, source_target_pairs={{0,8},{8,0},{16,24},{24,16},{1,9},{9,1},{17,25},{25,17},{2,10},{10... | collective-permute-start | bytes 1572872 | tf_op jit(solution)/shard_map/ppermute | solution.py:1029
  51.9 77.7 %copy-start.8 = (bf16[512,512]{1,0:T(8,128)(2,1)}, bf16[512,512]{1,0:T(8,128)(2,1)S(1)}, u32[]{:S(2)}) copy-start(bf16[512,512]{1,0:T(8,128)(2,1)S(1)} %collective-permute-done.2.refs_2_) | copy-start | bytes 1572868
  51.9 16.0 %collective-permute-start.20 = (bf16[512,512]{1,0:T(8,128)(2,1)S(1)}, bf16[512,512]{1,0:T(8,128)(2,1)S(1)}, u32[]{:S(2)}, u32[]{:S(2)}) collective-permute-start(bf16[512,512]{1,0:T(8,128)(2,1)S(1)} %collective-permute-done.4.refs_4_), channel_id=1, source_target_pairs={{0,8},{8,0},{16,24},{24,16},{1,9},{9,1},{17,25},{25,17},{2,10},{10... | collective-permute-start | bytes 1572872 | tf_op jit(solution)/shard_map/ppermute | solution.py:1029
  51.9 39.0 %copy-start.9 = (bf16[512,512]{1,0:T(8,128)(2,1)}, bf16[512,512]{1,0:T(8,128)(2,1)S(1)}, u32[]{:S(2)}) copy-start(bf16[512,512]{1,0:T(8,128)(2,1)S(1)} %collective-permute-done.5.refs_5_) | copy-start | bytes 1572868
  51.9 17.7 %collective-permute-start.24 = (bf16[512,512]{1,0:T(8,128)(2,1)S(1)}, bf16[512,512]{1,0:T(8,128)(2,1)S(1)}, u32[]{:S(2)}, u32[]{:S(2)}) collective-permute-start(bf16[512,512]{1,0:T(8,128)(2,1)S(1)} %collective-permute-done.8.refs_8_), channel_id=1, source_target_pairs={{0,8},{8,0},{16,24},{24,16},{1,9},{9,1},{17,25},{25,17},{2,10},{10... | collective-permute-start | bytes 1572872 | tf_op jit(solution)/shard_map/ppermute | solution.py:1029
  55.6 15.5 %collective-permute-start.3 = (bf16[512,512]{1,0:T(8,128)(2,1)S(1)}, bf16[512,512]{1,0:T(8,128)(2,1)S(1)}, u32[]{:S(2)}, u32[]{:S(2)}) collective-permute-start(bf16[512,512]{1,0:T(8,128)(2,1)S(1)} %collective-permute-done.2.refs_2_), channel_id=1, source_target_pairs={{0,2},{1,3},{2,4},{3,5},{4,6},{5,7},{6,0},{7,1},{8,10},{9,11},{10,... | collective-permute-start | bytes 1572872 | tf_op jit(solution)/shard_map/ppermute | solution.py:1023
  62.6 14.7 %collective-permute-start.6 = (bf16[512,512]{1,0:T(8,128)(2,1)S(1)}, bf16[512,512]{1,0:T(8,128)(2,1)S(1)}, u32[]{:S(2)}, u32[]{:S(2)}) collective-permute-start(bf16[512,512]{1,0:T(8,128)(2,1)S(1)} %collective-permute-done.2.refs_2_), channel_id=1, source_target_pairs={{0,1},{1,0},{2,3},{3,2},{4,5},{5,4},{6,7},{7,6},{8,9},{9,8},{10,11... | collective-permute-start | bytes 1572872 | tf_op jit(solution)/shard_map/ppermute | solution.py:1024
  65.0 14.7 %collective-permute-start.10 = (bf16[512,512]{1,0:T(8,128)(2,1)S(1)}, bf16[512,512]{1,0:T(8,128)(2,1)S(1)}, u32[]{:S(2)}, u32[]{:S(2)}) collective-permute-start(bf16[512,512]{1,0:T(8,128)(2,1)S(1)} %collective-permute-done.2.refs_2_), channel_id=1, source_target_pairs={{0,16},{8,24},{16,0},{24,8},{1,17},{9,25},{17,1},{25,9},{2,18},{10... | collective-permute-start | bytes 1572872 | tf_op jit(solution)/shard_map/ppermute | solution.py:1025
  67.8 20.8 %collective-permute-start.13 = (bf16[512,512]{1,0:T(8,128)(2,1)S(1)}, bf16[512,512]{1,0:T(8,128)(2,1)}, u32[]{:S(2)}, u32[]{:S(2)}) collective-permute-start(bf16[512,512]{1,0:T(8,128)(2,1)S(1)} %collective-permute-done.9.refs_9_), channel_id=1, source_target_pairs={{0,1},{1,0},{2,3},{3,2},{4,5},{5,4},{6,7},{7,6},{8,9},{9,8},{10,11... | collective-permute-start | bytes 1572872 | tf_op jit(solution)/shard_map/ppermute | solution.py:1026
  69.6 21.3 %collective-permute-start.18 = (bf16[512,512]{1,0:T(8,128)(2,1)S(1)}, bf16[512,512]{1,0:T(8,128)(2,1)S(1)}, u32[]{:S(2)}, u32[]{:S(2)}) collective-permute-start(bf16[512,512]{1,0:T(8,128)(2,1)S(1)} %collective-permute-done.2.refs_2_), channel_id=1, source_target_pairs={{0,8},{8,0},{16,24},{24,16},{1,9},{9,1},{17,25},{25,17},{2,10},{10... | collective-permute-start | bytes 1572872 | tf_op jit(solution)/shard_map/ppermute | solution.py:1029
  71.1 20.8 %collective-permute-start.21 = (bf16[512,512]{1,0:T(8,128)(2,1)S(1)}, bf16[512,512]{1,0:T(8,128)(2,1)S(1)}, u32[]{:S(2)}, u32[]{:S(2)}) collective-permute-start(bf16[512,512]{1,0:T(8,128)(2,1)S(1)} %collective-permute-done.5.refs_5_), channel_id=1, source_target_pairs={{0,8},{8,0},{16,24},{24,16},{1,9},{9,1},{17,25},{25,17},{2,10},{10... | collective-permute-start | bytes 1572872 | tf_op jit(solution)/shard_map/ppermute | solution.py:1029
  77.3 39.8 %copy-start.16 = (bf16[512,512]{1,0:T(8,128)(2,1)}, bf16[512,512]{1,0:T(8,128)(2,1)S(1)}, u32[]{:S(2)}) copy-start(bf16[512,512]{1,0:T(8,128)(2,1)S(1)} %collective-permute-done.6.refs_6_) | copy-start | bytes 1572868
  77.3 15.7 %collective-permute-start.25 = (bf16[512,512]{1,0:T(8,128)(2,1)S(1)}, bf16[512,512]{1,0:T(8,128)(2,1)S(1)}, u32[]{:S(2)}, u32[]{:S(2)}) collective-permute-start(bf16[512,512]{1,0:T(8,128)(2,1)S(1)} %collective-permute-done.9.refs_9_), channel_id=1, source_target_pairs={{0,8},{8,0},{16,24},{24,16},{1,9},{9,1},{17,25},{25,17},{2,10},{10... | collective-permute-start | bytes 1572872 | tf_op jit(solution)/shard_map/ppermute | solution.py:1029
  79.7 38.0 %copy-start.17 = (bf16[512,512]{1,0:T(8,128)(2,1)}, bf16[512,512]{1,0:T(8,128)(2,1)S(1)}, u32[]{:S(2)}) copy-start(bf16[512,512]{1,0:T(8,128)(2,1)S(1)} %collective-permute-done.10.refs_10_) | copy-start | bytes 1572868
  79.7 13.4 %collective-permute-start.28 = (bf16[512,512]{1,0:T(8,128)(2,1)S(1)}, bf16[512,512]{1,0:T(8,128)(2,1)S(1)}, u32[]{:S(2)}, u32[]{:S(2)}) collective-permute-start(bf16[512,512]{1,0:T(8,128)(2,1)S(1)} %collective-permute-done.12.refs_12_), channel_id=1, source_target_pairs={{0,8},{8,0},{16,24},{24,16},{1,9},{9,1},{17,25},{25,17},{2,10},{10... | collective-permute-start | bytes 1572872 | tf_op jit(solution)/shard_map/ppermute | solution.py:1029
  88.7 14.5 %collective-permute-start.7 = (bf16[512,512]{1,0:T(8,128)(2,1)S(1)}, bf16[512,512]{1,0:T(8,128)(2,1)}, u32[]{:S(2)}, u32[]{:S(2)}) collective-permute-start(bf16[512,512]{1,0:T(8,128)(2,1)S(1)} %collective-permute-done.3.refs_3_), channel_id=1, source_target_pairs={{0,1},{1,0},{2,3},{3,2},{4,5},{5,4},{6,7},{7,6},{8,9},{9,8},{10,11... | collective-permute-start | bytes 1572872 | tf_op jit(solution)/shard_map/ppermute | solution.py:1024
  90.9 15.0 %collective-permute-start.11 = (bf16[512,512]{1,0:T(8,128)(2,1)S(1)}, bf16[512,512]{1,0:T(8,128)(2,1)}, u32[]{:S(2)}, u32[]{:S(2)}) collective-permute-start(bf16[512,512]{1,0:T(8,128)(2,1)S(1)} %collective-permute-done.3.refs_3_), channel_id=1, source_target_pairs={{0,16},{8,24},{16,0},{24,8},{1,17},{9,25},{17,1},{25,9},{2,18},{10... | collective-permute-start | bytes 1572872 | tf_op jit(solution)/shard_map/ppermute | solution.py:1025
  91.8 25.3 %collective-permute-start.14 = (bf16[512,512]{1,0:T(8,128)(2,1)S(1)}, bf16[512,512]{1,0:T(8,128)(2,1)}, u32[]{:S(2)}, u32[]{:S(2)}) collective-permute-start(bf16[512,512]{1,0:T(8,128)(2,1)S(1)} %collective-permute-done.6.refs_6_), channel_id=1, source_target_pairs={{0,16},{8,24},{16,0},{24,8},{1,17},{9,25},{17,1},{25,9},{2,18},{10... | collective-permute-start | bytes 1572872 | tf_op jit(solution)/shard_map/ppermute | solution.py:1027
  93.1 24.1 %collective-permute-start.19 = (bf16[512,512]{1,0:T(8,128)(2,1)S(1)}, bf16[512,512]{1,0:T(8,128)(2,1)S(1)}, u32[]{:S(2)}, u32[]{:S(2)}) collective-permute-start(bf16[512,512]{1,0:T(8,128)(2,1)S(1)} %collective-permute-done.3.refs_3_), channel_id=1, source_target_pairs={{0,8},{8,0},{16,24},{24,16},{1,9},{9,1},{17,25},{25,17},{2,10},{10... | collective-permute-start | bytes 1572872 | tf_op jit(solution)/shard_map/ppermute | solution.py:1029
  93.2 24.5 %collective-permute-start.22 = (bf16[512,512]{1,0:T(8,128)(2,1)S(1)}, bf16[512,512]{1,0:T(8,128)(2,1)S(1)}, u32[]{:S(2)}, u32[]{:S(2)}) collective-permute-start(bf16[512,512]{1,0:T(8,128)(2,1)S(1)} %collective-permute-done.6.refs_6_), channel_id=1, source_target_pairs={{0,8},{8,0},{16,24},{24,16},{1,9},{9,1},{17,25},{25,17},{2,10},{10... | collective-permute-start | bytes 1572872 | tf_op jit(solution)/shard_map/ppermute | solution.py:1029
  103.2 14.6 %collective-permute-start.26 = (bf16[512,512]{1,0:T(8,128)(2,1)S(1)}, bf16[512,512]{1,0:T(8,128)(2,1)S(1)}, u32[]{:S(2)}, u32[]{:S(2)}) collective-permute-start(bf16[512,512]{1,0:T(8,128)(2,1)S(1)} %collective-permute-done.10.refs_10_), channel_id=1, source_target_pairs={{0,8},{8,0},{16,24},{24,16},{1,9},{9,1},{17,25},{25,17},{2,10},{10... | collective-permute-start | bytes 1572872 | tf_op jit(solution)/shard_map/ppermute | solution.py:1029
  105.9 21.3 %collective-permute-start.15 = (bf16[512,512]{1,0:T(8,128)(2,1)}, bf16[512,512]{1,0:T(8,128)(2,1)}, u32[]{:S(2)}, u32[]{:S(2)}) collective-permute-start(bf16[512,512]{1,0:T(8,128)(2,1)} %collective-permute-done.7.refs_7_), channel_id=1, source_target_pairs={{0,16},{8,24},{16,0},{24,8},{1,17},{9,25},{17,1},{25,9},{2,18},{10... | collective-permute-start | bytes 1572872 | tf_op jit(solution)/shard_map/ppermute | solution.py:1027
  117.1 11.5 %collective-permute-start.29 = (bf16[512,512]{1,0:T(8,128)(2,1)}, bf16[512,512]{1,0:T(8,128)(2,1)}, u32[]{:S(2)}, u32[]{:S(2)}) collective-permute-start(bf16[512,512]{1,0:T(8,128)(2,1)} %collective-permute-done.13.refs_13_), channel_id=1, source_target_pairs={{0,8},{8,0},{16,24},{24,16},{1,9},{9,1},{17,25},{25,17},{2,10},{10... | collective-permute-start | bytes 1572872 | tf_op jit(solution)/shard_map/ppermute | solution.py:1029
  117.1 11.5 %collective-permute-start.23 = (bf16[512,512]{1,0:T(8,128)(2,1)}, bf16[512,512]{1,0:T(8,128)(2,1)}, u32[]{:S(2)}, u32[]{:S(2)}) collective-permute-start(bf16[512,512]{1,0:T(8,128)(2,1)} %collective-permute-done.7.refs_7_), channel_id=1, source_target_pairs={{0,8},{8,0},{16,24},{24,16},{1,9},{9,1},{17,25},{25,17},{2,10},{10... | collective-permute-start | bytes 1572872 | tf_op jit(solution)/shard_map/ppermute | solution.py:1029
  117.7 10.9 %collective-permute-start.27 = (bf16[512,512]{1,0:T(8,128)(2,1)}, bf16[512,512]{1,0:T(8,128)(2,1)}, u32[]{:S(2)}, u32[]{:S(2)}) collective-permute-start(bf16[512,512]{1,0:T(8,128)(2,1)} %collective-permute-done.11.refs_11_), channel_id=1, source_target_pairs={{0,8},{8,0},{16,24},{24,16},{1,9},{9,1},{17,25},{25,17},{2,10},{10... | collective-permute-start | bytes 1572872 | tf_op jit(solution)/shard_map/ppermute | solution.py:1029
  117.8 10.8 %collective-permute-start.30 = (bf16[512,512]{1,0:T(8,128)(2,1)}, bf16[512,512]{1,0:T(8,128)(2,1)}, u32[]{:S(2)}, u32[]{:S(2)}) collective-permute-start(bf16[512,512]{1,0:T(8,128)(2,1)} %collective-permute-done.14.refs_14_), channel_id=1, source_target_pairs={{0,8},{8,0},{16,24},{24,16},{1,9},{9,1},{17,25},{25,17},{2,10},{10... | collective-permute-start | bytes 1572872 | tf_op jit(solution)/shard_map/ppermute | solution.py:1029
  127.2 2.3 collective-permute-start.31
  255.0 4.2 %collective-permute-start.32 = (bf16[4,512,512]{2,1,0:T(8,128)(2,1)S(1)}, bf16[4,512,512]{2,1,0:T(8,128)(2,1)S(1)}, u32[]{:S(2)}, u32[]{:S(2)}) collective-permute-start(bf16[4,512,512]{2,1,0:T(8,128)(2,1)S(1)} %get-tuple-element.109), channel_id=1, source_target_pairs={{0,8},{8,0},{16,24},{24,16},{1,9},{9,1},{17,25},{25,17},{2,10},{10... | collective-permute-start | bytes 6291464 | tf_op jit(solution)/shard_map/ppermute | solution.py:1050
  255.1 10.1 %collective-permute-start.37 = (bf16[4,512,512]{2,1,0:T(8,128)(2,1)S(1)}, bf16[4,512,512]{2,1,0:T(8,128)(2,1)S(1)}, u32[]{:S(2)}, u32[]{:S(2)}) collective-permute-start(bf16[4,512,512]{2,1,0:T(8,128)(2,1)S(1)} %get-tuple-element.110), channel_id=1, source_target_pairs={{0,8},{8,0},{16,24},{24,16},{1,9},{9,1},{17,25},{25,17},{2,10},{10... | collective-permute-start | bytes 6291464 | tf_op jit(solution)/shard_map/ppermute | solution.py:1050
  255.6 12.6 %collective-permute-start.34 = (bf16[4,512,512]{2,1,0:T(8,128)(2,1)S(1)}, bf16[4,512,512]{2,1,0:T(8,128)(2,1)S(1)}, u32[]{:S(2)}, u32[]{:S(2)}) collective-permute-start(bf16[4,512,512]{2,1,0:T(8,128)(2,1)S(1)} %get-tuple-element.111), channel_id=1, source_target_pairs={{0,8},{8,0},{16,24},{24,16},{1,9},{9,1},{17,25},{25,17},{2,10},{10... | collective-permute-start | bytes 6291464 | tf_op jit(solution)/shard_map/ppermute | solution.py:1050
  255.7 12.6 %collective-permute-start.33 = (bf16[4,512,512]{2,1,0:T(8,128)(2,1)S(1)}, bf16[4,512,512]{2,1,0:T(8,128)(2,1)}, u32[]{:S(2)}, u32[]{:S(2)}) collective-permute-start(bf16[4,512,512]{2,1,0:T(8,128)(2,1)S(1)} %get-tuple-element.112), channel_id=1, source_target_pairs={{0,8},{8,0},{16,24},{24,16},{1,9},{9,1},{17,25},{25,17},{2,10},{10... | collective-permute-start | bytes 6291464 | tf_op jit(solution)/shard_map/ppermute | solution.py:1050
  275.1 25.5 %collective-permute-start.38 = (bf16[2,512,512]{2,1,0:T(8,128)(2,1)}, bf16[2,512,512]{2,1,0:T(8,128)(2,1)}, u32[]{:S(2)}, u32[]{:S(2)}) collective-permute-start(bf16[2,512,512]{2,1,0:T(8,128)(2,1)} %get-tuple-element.122), channel_id=1, source_target_pairs={{0,1},{1,0},{2,3},{3,2},{4,5},{5,4},{6,7},{7,6},{8,9},{9,8},{10,11... | collective-permute-start | bytes 3145736 | tf_op jit(solution)/shard_map/ppermute | solution.py:1057
  275.5 27.8 %collective-permute-start.35 = (bf16[2,512,512]{2,1,0:T(8,128)(2,1)}, bf16[2,512,512]{2,1,0:T(8,128)(2,1)S(1)}, u32[]{:S(2)}, u32[]{:S(2)}) collective-permute-start(bf16[2,512,512]{2,1,0:T(8,128)(2,1)} %get-tuple-element.121), channel_id=1, source_target_pairs={{0,16},{8,24},{16,0},{24,8},{1,17},{9,25},{17,1},{25,9},{2,18},{10... | collective-permute-start | bytes 3145736 | tf_op jit(solution)/shard_map/ppermute | solution.py:1058
  303.0 14.9 %collective-permute-start.45 = (bf16[512,512]{1,0:T(8,128)(2,1)S(1)}, bf16[512,512]{1,0:T(8,128)(2,1)S(1)}, u32[]{:S(2)}, u32[]{:S(2)}) collective-permute-start(bf16[512,512]{1,0:T(8,128)(2,1)S(1)} %get-tuple-element.120), channel_id=1, source_target_pairs={{0,16},{8,24},{16,0},{24,8},{1,17},{9,25},{17,1},{25,9},{2,18},{10... | collective-permute-start | bytes 1572872 | tf_op jit(solution)/shard_map/ppermute | solution.py:1070
  304.4 14.9 %collective-permute-start.44 = (bf16[512,512]{1,0:T(8,128)(2,1)S(1)}, bf16[512,512]{1,0:T(8,128)(2,1)S(1)}, u32[]{:S(2)}, u32[]{:S(2)}) collective-permute-start(bf16[512,512]{1,0:T(8,128)(2,1)S(1)} %get-tuple-element.116), channel_id=1, source_target_pairs={{0,1},{1,0},{2,3},{3,2},{4,5},{5,4},{6,7},{7,6},{8,9},{9,8},{10,11... | collective-permute-start | bytes 1572872 | tf_op jit(solution)/shard_map/ppermute | solution.py:1069
  304.9 24.2 %collective-permute-start.43 = (bf16[512,512]{1,0:T(8,128)(2,1)S(1)}, bf16[512,512]{1,0:T(8,128)(2,1)S(1)}, u32[]{:S(2)}, u32[]{:S(2)}) collective-permute-start(bf16[512,512]{1,0:T(8,128)(2,1)S(1)} %get-tuple-element.119), channel_id=1, source_target_pairs={{0,16},{8,24},{16,0},{24,8},{1,17},{9,25},{17,1},{25,9},{2,18},{10... | collective-permute-start | bytes 1572872 | tf_op jit(solution)/shard_map/ppermute | solution.py:1070
  306.5 24.0 %collective-permute-start.42 = (bf16[512,512]{1,0:T(8,128)(2,1)S(1)}, bf16[512,512]{1,0:T(8,128)(2,1)S(1)}, u32[]{:S(2)}, u32[]{:S(2)}) collective-permute-start(bf16[512,512]{1,0:T(8,128)(2,1)S(1)} %get-tuple-element.115), channel_id=1, source_target_pairs={{0,1},{1,0},{2,3},{3,2},{4,5},{5,4},{6,7},{7,6},{8,9},{9,8},{10,11... | collective-permute-start | bytes 1572872 | tf_op jit(solution)/shard_map/ppermute | solution.py:1069
  319.5 12.7 %collective-permute-start.46 = (bf16[512,512]{1,0:T(8,128)(2,1)S(1)}, bf16[512,512]{1,0:T(8,128)(2,1)S(1)}, u32[]{:S(2)}, u32[]{:S(2)}) collective-permute-start(bf16[512,512]{1,0:T(8,128)(2,1)S(1)} %fusion.1), channel_id=1, source_target_pairs={{0,2},{1,3},{2,4},{3,5},{4,6},{5,7},{6,0},{7,1},{8,10},{9,11},{10,... | collective-permute-start | bytes 1572872 | tf_op jit(solution)/shard_map/ppermute | solution.py:1073
  319.6 20.8 %collective-permute-start.41 = (bf16[512,512]{1,0:T(8,128)(2,1)S(1)}, bf16[512,512]{1,0:T(8,128)(2,1)S(1)}, u32[]{:S(2)}, u32[]{:S(2)}) collective-permute-start(bf16[512,512]{1,0:T(8,128)(2,1)S(1)} %get-tuple-element.118), channel_id=1, source_target_pairs={{0,16},{8,24},{16,0},{24,8},{1,17},{9,25},{17,1},{25,9},{2,18},{10... | collective-permute-start | bytes 1572872 | tf_op jit(solution)/shard_map/ppermute | solution.py:1070
  321.4 20.3 %collective-permute-start.40 = (bf16[512,512]{1,0:T(8,128)(2,1)S(1)}, bf16[512,512]{1,0:T(8,128)(2,1)S(1)}, u32[]{:S(2)}, u32[]{:S(2)}) collective-permute-start(bf16[512,512]{1,0:T(8,128)(2,1)S(1)} %get-tuple-element.114), channel_id=1, source_target_pairs={{0,1},{1,0},{2,3},{3,2},{4,5},{5,4},{6,7},{7,6},{8,9},{9,8},{10,11... | collective-permute-start | bytes 1572872 | tf_op jit(solution)/shard_map/ppermute | solution.py:1069
  332.5 11.5 %collective-permute-start.47 = (bf16[512,512]{1,0:T(8,128)(2,1)S(1)}, bf16[512,512]{1,0:T(8,128)(2,1)S(1)}, u32[]{:S(2)}, u32[]{:S(2)}) collective-permute-start(bf16[512,512]{1,0:T(8,128)(2,1)S(1)} %fusion.4), channel_id=1, source_target_pairs={{0,2},{1,3},{2,4},{3,5},{4,6},{5,7},{6,0},{7,1},{8,10},{9,11},{10,... | collective-permute-start | bytes 1572872 | tf_op jit(solution)/shard_map/ppermute | solution.py:1073
  332.5 17.3 %collective-permute-start.39 = (bf16[512,512]{1,0:T(8,128)(2,1)S(1)}, bf16[512,512]{1,0:T(8,128)(2,1)S(1)}, u32[]{:S(2)}, u32[]{:S(2)}) collective-permute-start(bf16[512,512]{1,0:T(8,128)(2,1)S(1)} %get-tuple-element.117), channel_id=1, source_target_pairs={{0,16},{8,24},{16,0},{24,8},{1,17},{9,25},{17,1},{25,9},{2,18},{10... | collective-permute-start | bytes 1572872 | tf_op jit(solution)/shard_map/ppermute | solution.py:1070
  334.3 16.8 %collective-permute-start.36 = (bf16[512,512]{1,0:T(8,128)(2,1)S(1)}, bf16[512,512]{1,0:T(8,128)(2,1)S(1)}, u32[]{:S(2)}, u32[]{:S(2)}) collective-permute-start(bf16[512,512]{1,0:T(8,128)(2,1)S(1)} %get-tuple-element.113), channel_id=1, source_target_pairs={{0,1},{1,0},{2,3},{3,2},{4,5},{5,4},{6,7},{7,6},{8,9},{9,8},{10,11... | collective-permute-start | bytes 1572872 | tf_op jit(solution)/shard_map/ppermute | solution.py:1069
  344.3 11.0 %collective-permute-start.48 = (bf16[512,512]{1,0:T(8,128)(2,1)S(1)}, bf16[512,512]{1,0:T(8,128)(2,1)S(1)}, u32[]{:S(2)}, u32[]{:S(2)}) collective-permute-start(bf16[512,512]{1,0:T(8,128)(2,1)S(1)} %fusion.7), channel_id=1, source_target_pairs={{0,2},{1,3},{2,4},{3,5},{4,6},{5,7},{6,0},{7,1},{8,10},{9,11},{10,... | collective-permute-start | bytes 1572872 | tf_op jit(solution)/shard_map/ppermute | solution.py:1073
  356.0 7.0 %collective-permute-start.49 = (bf16[172112]{0:T(1024)(128)(2,1)S(1)}, bf16[172112]{0:T(1024)(128)(2,1)S(1)}, u32[]{:S(2)}, u32[]{:S(2)}) collective-permute-start(bf16[172112]{0:T(1024)(128)(2,1)S(1)} %slice.136), channel_id=1, source_target_pairs={{0,1},{1,2},{2,3},{3,4},{4,5},{5,6},{6,7},{7,8},{8,9},{9,10},{10,1... | collective-permute-start | bytes 1032680 | tf_op jit(solution)/shard_map/ppermute | solution.py:995
  374.1 1.9 collective-permute-start.50
  375.9 3.8 collective-permute-start.51
  379.7 7.7 %collective-permute-start.52 = (f32[4128]{0:T(1024)S(1)}, f32[4128]{0:T(1024)S(1)}, u32[]{:S(2)}, u32[]{:S(2)}) collective-permute-start(f32[4128]{0:T(1024)S(1)} %add.231), channel_id=1, source_target_pairs={{0,16},{8,24},{16,0},{24,8},{1,17},{9,25},{17,1},{25,9},{2,18},{10... | collective-permute-start | bytes 49544 | tf_op jit(solution)/shard_map/ppermute | solution.py:1093
  387.4 3.8 collective-permute-start.53
  391.2 4.7 %collective-permute-start.54 = (f32[4128]{0:T(1024)S(1)}, f32[4128]{0:T(1024)S(1)}, u32[]{:S(2)}, u32[]{:S(2)}) collective-permute-start(f32[4128]{0:T(1024)S(1)} %add.233), channel_id=1, source_target_pairs={{0,4},{1,5},{2,6},{3,7},{4,0},{5,1},{6,2},{7,3},{8,12},{9,13},{10,... | collective-permute-start | bytes 49544 | tf_op jit(solution)/shard_map/ppermute | solution.py:1093
  (19 other events, 437.6 us)

commit v2 on v1

--- a/solution.py
+++ b/solution.py
@@ -44,6 +44,7 @@
 NORM_EPS = 1e-05
 MASK_FILL = -1000000000.0
 ROW = 512
+HALF = ROW // 2
 SLOTS = 160
 KEYS = 256
 PAD = 16
@@ -137,9 +138,17 @@
     return at * top / under
 
 
-def source_block(coords, at):
+PIECES = []
+for far_core in range(2):
+    for kind in ((0, 0), (0, 1), (1, 0)):
+        PIECES += [(far_core, *kind, back, 0, ROW) for back in range(4)]
+    for first_row in (0, ROW // 2):
+        PIECES += [(far_core, 1, 1, back, first_row, ROW // 2) for back in range(4)]
+
+
+def source_block(coords, piece):
     y, c, z, x = coords[0], coords[1], coords[2], coords[3]
-    yy, cc, xx, zz = y ^ ((at // 8) % 2), c ^ (at // 16), x ^ ((at // 4) % 2), (z + 4 - at % 4) & 3
+    yy, cc, xx, zz = y ^ piece[1], c ^ piece[0], x ^ piece[2], (z + 4 - piece[3]) & 3
     return ((yy * 2 + cc) * 4 + zz) * 2 + xx
 
 
@@ -152,28 +161,38 @@
 class Loads:
     def __init__(self, coords, sources, wanted, sems):
         self.wanted = wanted
-        self.sources = sources
+        self.source = sources[0]
         self.sems = sems
-        for at, source in enumerate(sources):
-            block = source_block(coords, at)
+        for piece, source in zip(PIECES, sources):
+            block = source_block(coords, piece)
             first = 0
             for low_block, count, target, rows in wanted:
                 here = block - low_block
 
                 @pl.when((here >= 0) & (here < count))
-                def _(source=source, target=target, rows=rows, here=here, first=first):
-                    pltpu.make_async_copy(
-                        source.at[0:rows], target.at[part(here, ROW)] if rows == ROW else target, sems.at[first + here]
-                    ).start()
-
-                first = first + count
+                def _(piece=piece, source=source, target=target, rows=rows, here=here, first=first):
+                    for half in range(2):
+                        inside = HALF * half - piece[4]
+                        size = min(HALF, rows - HALF * half)
+                        if 0 <= inside < piece[5] and size > 0:
+                            place = pl.ds(pl.multiple_of(here * ROW + HALF * half, 16), size)
+                            pltpu.make_async_copy(
+                                source.at[inside : inside + size], target.at[place], sems.at[first + 2 * here + half]
+                            ).start()
+
+                first = first + 2 * count
 
     def wait(self, which):
-        first = sum(count for _, count, _, _ in self.wanted[:which])
+        first = 2 * sum(count for _, count, _, _ in self.wanted[:which])
         _, count, target, rows = self.wanted[which]
         for at in range(count):
-            place = target.at[ROW * at : ROW * at + rows]
-            pltpu.make_async_copy(self.sources[0].at[0:rows], place, self.sems.at[first + at]).wait()
+            for half in range(2):
+                size = min(HALF, rows - HALF * half)
+                if size > 0:
+                    start = ROW * at + HALF * half
+                    pltpu.make_async_copy(
+                        self.source.at[0:size], target.at[start : start + size], self.sems.at[first + 2 * at + half]
+                    ).wait()
 
 
 class Emits:
@@ -289,7 +308,7 @@
 
 
 def first_kernel(coords, frames, *refs):
-    sources, refs = refs[:32], refs[32:]
+    sources, refs = refs[: len(PIECES)], refs[len(PIECES) :]
     x1, nrm, act, slope, w_in_out, w_out_out, small, taps, raw, w_in, w_out, stage, low_small, sems, out_sems = refs
     loads = Loads(
         coords,
@@ -330,7 +349,7 @@
 
 
 def attention_kernel(coords, length, x1, small, *refs):
-    sources, refs = refs[:32], refs[32:]
+    sources, refs = refs[: len(PIECES)], refs[len(PIECES) :]
     a_out, nrm, qkv, probs, ctx, w_qkv_out, w_att_out, raw, w_qkv, w_att, stage, bias, sems, out_sems = refs
     loads = Loads(coords, sources, [(BLOCK["qkv"], 3, raw, ROW), (BLOCK["att_out"], 1, w_att, ROW)], sems)
     norm_rows(x1, small[1:2, :], nrm)
@@ -414,7 +433,7 @@
 
 
 def gating_kernel(coords, length, x1, small, taps, *refs):
-    sources, refs = refs[:32], refs[32:]
+    sources, refs = refs[: len(PIECES)], refs[len(PIECES) :]
     c_out, nrm, ug, slope, gpad, cv, gated, w_cg_out, w_co_out, raw, w_cg, w_co, stage, hid, sems, out_sems = refs
     loads = Loads(coords, sources, [(BLOCK["cg_in"], 6, raw, ROW), (BLOCK["cg_out"], 3, w_co, ROW)], sems)
     norm_rows(x1, small[2:3, :], nrm)
@@ -467,7 +486,7 @@
 
 
 def last_kernel(coords, length, a_out, c_out, x1, cot, small, taps, *refs):
-    sources, refs = refs[:32], refs[32:]
+    sources, refs = refs[: len(PIECES)], refs[len(PIECES) :]
     out, dx, mixed, mpad, w_merge_out, sgrad, grads = refs[:7]
     (
         raw, w_merge, w_in, w_out, stage, x2, x3, nrm, act, slope, dout, dhid, dnrm, total, g_in, g_out,
@@ -793,7 +812,7 @@
             ((FF, D), BF16),
             ((4, 128 * 4, 128), F32),
             ((SMALL, ROW), BF16),
-            9,
+            18,
             2,
         ],
     )
@@ -816,7 +835,7 @@
             ((D, D), BF16),
             ((4, 128 * 3, 128), F32),
             ((H, ROW), F32),
-            4,
+            8,
             2,
         ],
     )
@@ -841,7 +860,7 @@
             ((GATE, D), BF16),
             ((4, 128 * 6, 128), F32),
             ((SLOTS, 256), F32),
-            9,
+            18,
             2,
         ],
     )
@@ -875,7 +894,7 @@
             ((8, D), F32),
             ((FF, D), BF16),
             ((FF, D), BF16),
-            10,
+            20,
             9,
         ],
     )
@@ -978,7 +997,7 @@
     return lax.dynamic_slice(jnp.concatenate(pieces), (me * lead,), (block,)).reshape(rows, ROW)
 
 
-def unalign_block(block_sum, shard_size):
+def unalign_block(block_sum, shard_size, padded):
     devices = lax.axis_size("dp") * lax.axis_size("fsdp")
     me = lax.axis_index(AXES)
     rows = block_sum.shape[0]
@@ -996,7 +1015,8 @@
         have = have + part
         hop = hop + 1
     start = have - block - me * lead
-    return lax.dynamic_slice(jnp.concatenate(pieces), (start,), (shard_size,))
+    pieces.append(jnp.zeros((max(0, padded - block),), flat.dtype))
+    return lax.dynamic_slice(jnp.concatenate(pieces), (start,), (padded,))
 
 
 def pair_lists():
@@ -1012,20 +1032,18 @@
 
 
 def gather_blocks(block):
-    rows = block.shape[0]
     if not fast_mesh():
         whole = lax.all_gather(block, AXES, axis=0, tiled=True).reshape(32, ROW, ROW)
-        order = [source_block((0, 0, 0, 0), at) for at in range(32)]
-        return [whole[at] for at in order]
+        return [whole[source_block((0, 0, 0, 0), piece)][piece[4] : piece[4] + piece[5]] for piece in PIECES]
     ring, across_x, across_y, across_core = pair_lists()
     own = [block]
     for _ in range(3):
         own.append(lax.ppermute(own[-1], "fsdp", ring))
     by_x = [lax.ppermute(each_one, "fsdp", across_x) for each_one in own]
     by_y = [lax.ppermute(each_one, "dp", across_y) for each_one in own]
-    both = [lax.ppermute(each_one, "fsdp", across_x) for each_one in by_y[:2]]
-    both = both + [lax.ppermute(each_one, "dp", across_y) for each_one in by_x[2:]]
-    near = own + by_x + by_y + both
+    top = [lax.ppermute(each_one[:HALF], "fsdp", across_x) for each_one in by_y]
+    bottom = [lax.ppermute(each_one[HALF:], "dp", across_y) for each_one in by_x]
+    near = own + by_x + by_y + top + bottom
     far = [lax.ppermute(each_one, "dp", across_core) for each_one in near]
     return near + far
 
@@ -1098,9 +1116,63 @@
     bounds = segment_bounds()
     most = 1
     for at in range(devices):
-        low, high = at * shard_size, (at + 1) * shard_size
-        most = max(most, sum(1 for b in bounds[1:-1] if low < b < high) + 1)
+        low_end, high_end = at * shard_size, (at + 1) * shard_size
+        most = max(most, sum(1 for b in bounds[1:-1] if low_end < b < high_end) + 1)
     return most
+
+
+LANES = 128
+CHUNK = 256
+
+
+def entry_places(step):
+    row = step * CHUNK + lax.broadcasted_iota(jnp.int32, (CHUNK, LANES), 0)
+    return row * LANES + lax.broadcasted_iota(jnp.int32, (CHUNK, LANES), 1)
+
+
+def update_kernel(segments, params, first, second, grad, new_first, new_second, update, sums):
+    step = pl.program_id(0)
+    spans = segments.shape[0] - 2
+
+    @pl.when(step == 0)
+    def _():
+        sums[...] = jnp.zeros_like(sums)
+
+    grads = grad[...]
+    firsts = BETA_FIRST * first[...] + (1.0 - BETA_FIRST) * grads
+    seconds = BETA_SECOND * second[...] + (1.0 - BETA_SECOND) * grads * grads
+    new_first[...] = firsts
+    new_second[...] = seconds
+    first_hat = firsts * (1.0 / (1.0 - BETA_FIRST**STEP))
+    second_hat = seconds * (1.0 / (1.0 - BETA_SECOND**STEP))
+    values = params[...]
+    change = first_hat / (jnp.sqrt(second_hat) + ADAM_EPS) + WEIGHT_DECAY * values
+    update[...] = change
+    places = entry_places(step)
+    lane = lax.broadcasted_iota(jnp.int32, (1, LANES), 1)
+    for at in range(spans):
+        inside = (places >= segments[1 + at]) & (places < segments[2 + at])
+        mine = lane == segments[0] + at
+        for row, entries in enumerate((values, change)):
+            squares = jnp.where(inside, entries * entries, 0.0)
+            total = jnp.sum(jnp.sum(squares, axis=0, keepdims=True), axis=1, keepdims=True)
+            sums[row : row + 1, :] += jnp.where(mine, total, 0.0)
+
+
+def apply_kernel(segments, sums, params, update, new_params, norms):
+    step = pl.program_id(0)
+    spans = segments.shape[0] - 2
+    roots = jnp.sqrt(sums[0:2, :])
+    trust = roots[0:1, :] / (roots[1:2, :] + ADAM_EPS)
+    norms[0:2, :] = roots
+    norms[2:3, :] = trust
+    places = entry_places(step)
+    lane = lax.broadcasted_iota(jnp.int32, (1, LANES), 1)
+    scale = jnp.zeros((CHUNK, LANES), F32)
+    for at in range(spans):
+        own = jnp.sum(jnp.where(lane == segments[0] + at, trust, 0.0), axis=1, keepdims=True)
+        scale = jnp.where(places >= segments[1 + at], own, scale)
+    new_params[...] = params[...] - LEARN_RATE * scale * update[...]
 
 
 def shards(frames, lengths, cotangent, params, first_moment, second_moment):
@@ -1116,57 +1188,53 @@
     blocks = gather_blocks(align_shard(low(params), shard_size, rows))
     result, frames_grad, gains, grads = layer(coords, lengths, frames[0], cotangent[0], blocks)
     block_sum = scatter_blocks(grads, coords)
-    grad_shard = unalign_block(low(block_sum), shard_size).astype(F32)
-    new_first = BETA_FIRST * first_moment + (1.0 - BETA_FIRST) * grad_shard
-    new_second = BETA_SECOND * second_moment + (1.0 - BETA_SECOND) * grad_shard * grad_shard
-    first_hat = new_first / (1.0 - BETA_FIRST**STEP)
-    second_hat = new_second / (1.0 - BETA_SECOND**STEP)
-    update = first_hat / (jnp.sqrt(second_hat) + ADAM_EPS) + WEIGHT_DECAY * params
-    count = len(segment_shapes())
+    steps = -(-shard_size // (LANES * CHUNK))
+    padded = steps * LANES * CHUNK
+    grad_shard = unalign_block(low(block_sum), shard_size, padded).astype(F32)
+
+    def square(flat):
+        return jnp.pad(flat, (0, padded - flat.shape[0])).reshape(-1, LANES)
+
     bounds = segment_bounds()
     spans = most_segments(shard_size, devices)
     shard_low = me * shard_size
     first_segment = sum((shard_low >= b).astype(jnp.int32) for b in bounds[1:-1])
     table = jnp.asarray(bounds[1:] + [bounds[-1]] * spans, jnp.int32)
-    ends = lax.dynamic_slice(table, (first_segment,), (spans,)) - shard_low
-    positions = lax.iota(jnp.int32, shard_size)
-
-    def segment_sums(values):
-        total = jnp.zeros((count + spans,), jnp.float32)
-        sums = []
-        low = jnp.int32(0)
-        for at in range(spans):
-            inside = (positions >= low) & (positions < ends[at])
-            sums.append(jnp.sum(jnp.where(inside, values, 0.0)))
-            low = ends[at]
-        return lax.dynamic_update_slice(total, jnp.stack(sums), (first_segment,))[:count]
-
-    parts = jnp.concatenate(
-        [segment_sums(params * params), segment_sums(update * update), jnp.zeros((8,), jnp.float32)]
-    )
-    everywhere = sum_everywhere(jnp.concatenate([parts, gains.reshape(-1)]))
-    weight_squares = everywhere[:count]
-    update_squares = everywhere[count : 2 * count]
-    gain_grads = everywhere[parts.shape[0] :]
-    weight_norms = jnp.sqrt(weight_squares)
-    update_norms = jnp.sqrt(update_squares)
-    trust_ratios = weight_norms / (update_norms + ADAM_EPS)
-    near_trust = lax.dynamic_slice(
-        jnp.concatenate([trust_ratios, jnp.zeros((spans,), jnp.float32)]), (first_segment,), (spans,)
-    )
-    entry_trust = jnp.broadcast_to(near_trust[spans - 1], (shard_size,))
-    for at in range(spans - 2, -1, -1):
-        entry_trust = jnp.where(positions < ends[at], near_trust[at], entry_trust)
-    new_params = params - LEARN_RATE * entry_trust * update
+    ends = jnp.clip(lax.dynamic_slice(table, (first_segment,), (spans,)) - shard_low, 0, shard_size)
+    segments = jnp.concatenate([first_segment[None], jnp.zeros((1,), jnp.int32), ends]).astype(jnp.int32)
+    grid = pl.BlockSpec((CHUNK, LANES), lambda step: (step, 0))
+    whole = pl.BlockSpec((8, LANES), lambda step: (0, 0))
+    flat_kind = jax.ShapeDtypeStruct((padded // LANES, LANES), F32)
+    tile_kind = jax.ShapeDtypeStruct((8, LANES), F32)
+    params_square = square(params)
+    new_first, new_second, update, sums = pl.pallas_call(
+        update_kernel,
+        name="update",
+        grid=(steps,),
+        in_specs=[SM] + [grid] * 4,
+        out_specs=[grid] * 3 + [whole],
+        out_shape=[flat_kind] * 3 + [tile_kind],
+    )(segments, params_square, square(first_moment), square(second_moment), grad_shard.reshape(-1, LANES))
+    gain_grads = sum_everywhere(gains).reshape(-1)
+    sums = sum_everywhere(sums)
+    new_params, norms = pl.pallas_call(
+        apply_kernel,
+        name="apply",
+        grid=(steps,),
+        in_specs=[SM, whole, grid, grid],
+        out_specs=[grid, whole],
+        out_shape=[flat_kind, tile_kind],
+    )(segments, sums, params_square, update)
+    count = len(segment_shapes())
     return (
         result.reshape(frames.shape),
         frames_grad.reshape(frames.shape),
-        new_params,
-        new_first,
-        new_second,
-        weight_norms,
-        update_norms,
-        trust_ratios,
+        new_params.reshape(-1)[:shard_size],
+        new_first.reshape(-1)[:shard_size],
+        new_second.reshape(-1)[:shard_size],
+        norms[0, :count],
+        norms[1, :count],
+        norms[2, :count],
         gain_grads,
     )
 

time: 404 us -> 394 us (0.975)
  other arithmetic: 38.5 us -> 18.1 us
  Pallas kernels: 121 us -> 135 us
  waiting for transfers between devices: 179 us -> 165 us
  local copies, waits for them, and re-layouts: 10.1 us -> 22.1 us
    ppermute x4 -> x8, waiting for transfers between devices: 35.2 us -> 52.7 us  [the longest x4 43.1 us: gather_blocks(): top = [lax.ppermute(each_one[:HALF], 'fsdp', across_x) for each_one in by_y]]
    ppermute x4, waiting for transfers between devices: 15.8 us -> 0.86 us  [gather_blocks(): by_x = [lax.ppermute(each_one, 'fsdp', across_x) for each_one in own]]
    reduce_sum x2 -> x0, other arithmetic: 13.6 us -> none  [segment_sums(): sums.append(jnp.sum(jnp.where(inside, values, 0.0)))]
    pallas_call x0 -> x2, Pallas kernels: none -> 13.4 us  [the longest x1 7.42 us: shards(): pl.pallas_call(update_kernel, name='update', grid=(steps,), in_specs=[SM]...]
    ppermute x3, waiting for transfers between devices: 17.3 us -> 9.18 us  [gather_blocks(): own.append(lax.ppermute(own[-1], 'fsdp', ring))]
    sub x2 -> x0, other arithmetic: 6.58 us -> none  [the longest x1 5.84 us: shards(): new_params = params - LEARN_RATE * entry_trust * update]
    slice x3 -> x11, local copies, waits for them, and re-layouts: 2.01 us -> 8.5 us  [the longest x1 2.24 us: shards(): new_first.reshape(-1)[:shard_size]]
    dynamic_update_slice x2 -> x0, other arithmetic: 5.34 us -> none  [segment_sums(): lax.dynamic_update_slice(total, jnp.stack(sums), (first_segment,))[:count]]
  transfers between devices with their start and end apart: 55 -> 68, of which waited for: 35 -> 32; matrix products, arithmetic and copies ran while one was open for 2% -> 5% of each run, Pallas kernels for 0% -> 2%
where the time goes in v2:
time: 394 us; the launch traced here: 393 us
  waiting for transfers between devices  165 us (42%)
  Pallas kernels  135 us (34%)
  starting transfers between devices  50 us (13%)
  local copies, waits for them, and re-layouts  22.1 us (6%)
  other arithmetic  18.1 us (5%)
    pallas_call x7, Pallas kernels, call(): pl.pallas_call(kernel, name=name, in_specs=[space for space, _ in ins], o...  122 us
    ppermute x4, waiting for transfers between devices, gather_blocks(): top = [lax.ppermute(each_one[:HALF], 'fsdp', across_x) for each_one in by_y]  43.1 us
    ppermute x4, waiting for transfers between devices, scatter_blocks(): lax.ppermute(at(to_y, back), 'dp', across_y)  25.3 us
    ppermute x1, waiting for transfers between devices, scatter_blocks(): from_x = lax.ppermute(diagonal[:2], 'fsdp', across_x)  21.4 us
    ppermute x10, waiting for transfers between devices, sum_everywhere(): vector = vector + lax.ppermute(vector, axis, pairs)  16.3 us
    ppermute x4, waiting for transfers between devices, core_sum(): theirs = lax.ppermute(grads[16 + 4 * kind:20 + 4 * kind], 'dp', across_core)  12.1 us
    ppermute x1, waiting for transfers between devices, align_shard(): pieces.append(lax.ppermute(low_shard[:part], AXES, pairs))  11.9 us
    ppermute x4, waiting for transfers between devices, scatter_blocks(): lax.ppermute(at(to_x, back), 'fsdp', across_x)  10.5 us
  transfers between devices with their start and end apart: 68, of which 32 were waited for; matrix products, arithmetic and copies ran while one was open for 5% of the time, Pallas kernels for 2%

profile of v2, /device:TPU:0, one launch (start us, length us, event | category | flops | bytes accessed | tf_op | source)
XLA Modules:
  0.0 393.0 jit_solution(15222998353542025343)
XLA Ops:
  1.9 1.3 collective-permute-start
  3.3 11.9 %collective-permute-done = bf16[177664]{0:T(1024)(128)(2,1)S(1)} collective-permute-done((bf16[177664]{0:T(1024)(128)(2,1)S(1)}, bf16[177664]{0:T(1024)(128)(2,1)S(1)}, u32[]{:S(2)}, u32[]{:S(2)}) %collective-permute-start) | collective-permute-done | bytes 355360 | tf_op jit(solution)/shard_map/ppermute | solution.py:994
  15.1 1.9 fusion.14
  17.4 1.9 collective-permute-start.1
  19.2 2.5 collective-permute-start.8
  21.8 1.4 collective-permute-start.4
  23.1 9.2 %collective-permute-done.1.refs_1_ = bf16[512,512]{1,0:T(8,128)(2,1)S(1)} collective-permute-done((bf16[512,512]{1,0:T(8,128)(2,1)S(1)}, bf16[512,512]{1,0:T(8,128)(2,1)S(1)}, u32[]{:S(2)}, u32[]{:S(2)}) %collective-permute-start.1) | collective-permute-done | bytes 524320 | tf_op jit(solution)/shard_map/ppermute | solution.py:1041
  32.3 5.2 %collective-permute-start.9 = (bf16[512,512]{1,0:T(8,128)(2,1)S(1)}, bf16[512,512]{1,0:T(8,128)(2,1)S(1)}, u32[]{:S(2)}, u32[]{:S(2)}) collective-permute-start(bf16[512,512]{1,0:T(8,128)(2,1)S(1)} %collective-permute-done.1.refs_1_), channel_id=1, source_target_pairs={{0,16},{8,24},{16,0},{24,8},{1,17},{9,25},{17,1},{25,9},{2,18},{10... | collective-permute-start | bytes 1572872 | tf_op jit(solution)/shard_map/ppermute | solution.py:1043
  38.0 1.9 collective-permute-start.5
  39.9 7.0 %collective-permute-done.12.refs_12_ = bf16[256,512]{1,0:T(8,128)(2,1)S(1)} collective-permute-done((bf16[256,512]{1,0:T(8,128)(2,1)S(1)}, bf16[256,512]{1,0:T(8,128)(2,1)S(1)}, u32[]{:S(2)}, u32[]{:S(2)}) %collective-permute-start.12) | collective-permute-done | bytes 262176 | tf_op jit(solution)/shard_map/ppermute | solution.py:1044
  46.9 7.7 %collective-permute-done.16.refs_16_ = bf16[256,512]{1,0:T(8,128)(2,1)S(1)} collective-permute-done((bf16[256,512]{1,0:T(8,128)(2,1)S(1)}, bf16[256,512]{1,0:T(8,128)(2,1)S(1)}, u32[]{:S(2)}, u32[]{:S(2)}) %collective-permute-start.16) | collective-permute-done | bytes 262176 | tf_op jit(solution)/shard_map/ppermute | solution.py:1045
  56.5 1.7 collective-permute-start.10
  61.1 15.0 %collective-permute-done.13.refs_13_ = bf16[256,512]{1,0:T(8,128)(2,1)S(1)} collective-permute-done((bf16[256,512]{1,0:T(8,128)(2,1)S(1)}, bf16[256,512]{1,0:T(8,128)(2,1)S(1)}, u32[]{:S(2)}, u32[]{:S(2)}) %collective-permute-start.13) | collective-permute-done | bytes 262176 | tf_op jit(solution)/shard_map/ppermute | solution.py:1044
  78.2 1.4 collective-permute-start.7
  82.4 15.3 %collective-permute-done.14.refs_14_ = bf16[256,512]{1,0:T(8,128)(2,1)S(1)} collective-permute-done((bf16[256,512]{1,0:T(8,128)(2,1)S(1)}, bf16[256,512]{1,0:T(8,128)(2,1)S(1)}, u32[]{:S(2)}, u32[]{:S(2)}) %collective-permute-start.14) | collective-permute-done | bytes 262176 | tf_op jit(solution)/shard_map/ppermute | solution.py:1044
  97.8 1.4 collective-permute-done.18.refs_18_
  102.9 1.4 collective-permute-start.19
  104.9 5.8 %collective-permute-done.15.refs_15_ = bf16[256,512]{1,0:T(8,128)(2,1)} collective-permute-done((bf16[256,512]{1,0:T(8,128)(2,1)S(1)}, bf16[256,512]{1,0:T(8,128)(2,1)}, u32[]{:S(2)}, u32[]{:S(2)}) %collective-permute-start.15) | collective-permute-done | bytes 262176 | tf_op jit(solution)/shard_map/ppermute | solution.py:1044
  113.9 9.4 %ffa_forward.1 = (f32[160,512]{1,0:T(8,128)}, bf16[160,512]{1,0:T(8,128)(2,1)}, bf16[160,2048]{1,0:T(8,128)(2,1)}, bf16[160,2048]{1,0:T(8,128)(2,1)}, bf16[512,2...) custom-call(s32[4]{0:T(128)} %pad_add_fusion.coords, ...), custom_call_target="tpu_custom_call" | custom-call | tf_op jit(solution)/shard_map/ffa_forward/pallas_call | solution.py:774
  123.4 9.7 %attention_forward.1 = (f32[160,512]{1,0:T(8,128)}, bf16[160,512]{1,0:T(8,128)(2,1)}, bf16[256,1536]{1,0:T(8,128)(2,1)}, bf16[8,160,256]{2,1,0:T(8,128)(2,1)}, b...) custom-call(s32[4]{0:T(128)} %pad_add_fusion.coords, s32[1]{0:T(128)S(6)} %copy.24.length, ...), custom_call_target="tpu_custom_call" | custom-call | tf_op jit(solution)/shard_map/attention_forward/pallas_call | solution.py:774
  133.1 21.7 %gating_forward.1 = (f32[160,512]{1,0:T(8,128)}, bf16[160,512]{1,0:T(8,128)(2,1)}, f32[160,3072]{1,0:T(8,128)}, bf16[160,3072]{1,0:T(8,128)(2,1)}, f32[192,1536]...) custom-call(s32[4]{0:T(128)} %pad_add_fusion.coords, ...), custom_call_target="tpu_custom_call" | custom-call | tf_op jit(solution)/shard_map/gating_forward/pallas_call | solution.py:774
  154.8 20.8 %merge_ffb.1 = (bf16[160,512]{1,0:T(8,128)(2,1)}, f32[160,512]{1,0:T(8,128)}, bf16[160,1024]{1,0:T(8,128)(2,1)}, f32[192,1024]{1,0:T(8,128)}, bf16[1024,512]{1,0...) custom-call(s32[4]{0:T(128)} %pad_add_fusion.coords, s32[1]{0:T(128)S(6)} %copy.24.length, ...), custom_call_target="tpu_custom_call" | custom-call | tf_op jit(solution)/shard_map/merge_ffb/pallas_call | solution.py:774
  175.6 34.7 %gating_backward.1 = (f32[160,512]{1,0:T(8,128)}, bf16[160,512]{1,0:T(8,128)(2,1)}, f32[176,512]{1,0:T(8,128)}, bf16[32,512,512]{2,1,0:T(8,128)(2,1)}) custom-call(s32[4]{0:T(128)} %pad_add_fusion.coords, s32[1]{0:T(128)S(6)} %copy.24.length, f32[160,512]{1,0:T(8,128)} %get-tuple-element.62.dx_in, ...), custom_call_target="tpu_custom_call", output_to_operand_aliasing={{3}: (18, {})} | custom-call | tf_op jit(solution)/shard_map/gating_backward/pallas_call | solution.py:774
  210.3 12.7 %attention_backward.1 = (f32[160,512]{1,0:T(8,128)}, f32[176,512]{1,0:T(8,128)}, bf16[32,512,512]{2,1,0:T(8,128)(2,1)}) custom-call(s32[4]{0:T(128)} %pad_add_fusion.coords, f32[160,512]{1,0:T(8,128)} %get-tuple-element.76.dx_in, bf16[160,512]{1,0:T(8,128)(2,1)} %get-tuple-element.77.datt, ...), custom_call_target="tpu_custom_call", output_to_operand_aliasing={{2}: (12, {})} | custom-call | tf_op jit(solution)/shard_map/attention_backward/pallas_call | solution.py:774
  223.0 12.8 %ffa_backward.1 = (bf16[160,512]{1,0:T(8,128)(2,1)}, f32[8,512]{1,0:T(8,128)}, bf16[32,512,512]{2,1,0:T(8,128)(2,1)}) custom-call(s32[4]{0:T(128)} %pad_add_fusion.coords, f32[160,512]{1,0:T(8,128)} %get-tuple-element.86.dx_in, bf16[160,512]{1,0:T(8,128)(2,1)} %bitcast.69, bf16[160,512]{1,0:T(8,128)(2,1)} %get-tuple-element.87.nrm, ...), custom_call_target="tpu_custom_call", output_to_operand_aliasing={{2}: (10, {})} | custom-call | tf_op jit(solution)/shard_map/ffa_backward/pallas_call | solution.py:774
  235.9 3.9 %fusion.32 = (bf16[4,512,512]{2,1,0:T(8,128)(2,1)S(1)}, bf16[4,512,512]{2,1,0:T(8,128)(2,1)S(1)}, bf16[4,512,512]{2,1,0:T(8,128)(2,1)S(1)}, bf16[4,512,512]{2,1,0:T(8,128)(2,1)S(1)}) fusion(bf16[32,512,512]{2,1,0:T(8,128)(2,1)} %get-tuple-element.95), kind=kLoop, calls=%fused_computation.72 | loop fusion | bytes 16777216 | tf_op jit(solution)/shard_map/slice | solution.py:1068
  240.9 3.1 collective-permute-done.40
  244.0 6.0 %collective-permute-done.45 = bf16[4,512,512]{2,1,0:T(8,128)(2,1)S(1)} collective-permute-done((bf16[4,512,512]{2,1,0:T(8,128)(2,1)S(1)}, bf16[4,512,512]{2,1,0:T(8,128)(2,1)S(1)}, u32[]{:S(2)}, u32[]{:S(2)}) %collective-permute-start.45) | collective-permute-done | bytes 2097184 | tf_op jit(solution)/shard_map/ppermute | solution.py:1068
  250.0 3.0 collective-permute-done.42
  253.0 5.4 %add_convert_fusion.3 = (bf16[4,512,512]{2,1,0:T(8,128)(2,1)}, bf16[4,512,512]{2,1,0:T(8,128)(2,1)}, bf16[4,512,512]{2,1,0:T(8,128)(2,1)S(1)}, bf16[4,512,512]{2,1,0:T(8,128)(2,1)S(1)}) fusion(bf16[4,512,512]{2,1,0:T(8,128)(2,1)S(1)} %collective-permute-done.40, bf16[32,512,512]{2,1,0:T(8,128)(2,1)S(1)} %copy-done, ...), kind=kLoop, calls=%fused_computation.3 | loop fusion | flops 16777216 | bytes 25165824 | tf_op jit(solution)/shard_map/convert_element_type | solution.py:84
  258.5 1.5 fusion.33
  259.9 1.5 collective-permute-start.46
  262.5 1.4 slice.134
  264.0 21.4 %collective-permute-done.46 = bf16[2,512,512]{2,1,0:T(8,128)(2,1)} collective-permute-done((bf16[2,512,512]{2,1,0:T(8,128)(2,1)}, bf16[2,512,512]{2,1,0:T(8,128)(2,1)}, u32[]{:S(2)}, u32[]{:S(2)}) %collective-permute-start.46) | collective-permute-done | bytes 1048608 | tf_op jit(solution)/shard_map/ppermute | solution.py:1075
  285.4 1.5 add_convert_fusion.4
  287.8 1.6 collective-permute-start.53
  293.0 9.7 %collective-permute-done.53 = bf16[512,512]{1,0:T(8,128)(2,1)S(1)} collective-permute-done((bf16[512,512]{1,0:T(8,128)(2,1)S(1)}, bf16[512,512]{1,0:T(8,128)(2,1)S(1)}, u32[]{:S(2)}, u32[]{:S(2)}) %collective-permute-start.53) | collective-permute-done | bytes 524320 | tf_op jit(solution)/shard_map/ppermute | solution.py:1088
  302.7 2.7 collective-permute-done.52
  306.2 1.5 collective-permute-start.48
  307.7 6.2 %collective-permute-done.51 = bf16[512,512]{1,0:T(8,128)(2,1)S(1)} collective-permute-done((bf16[512,512]{1,0:T(8,128)(2,1)S(1)}, bf16[512,512]{1,0:T(8,128)(2,1)S(1)}, u32[]{:S(2)}, u32[]{:S(2)}) %collective-permute-start.51) | collective-permute-done | bytes 524320 | tf_op jit(solution)/shard_map/ppermute | solution.py:1088
  313.9 2.7 collective-permute-done.50
  318.3 1.5 collective-permute-start.44
  319.8 5.4 %collective-permute-done.49 = bf16[512,512]{1,0:T(8,128)(2,1)S(1)} collective-permute-done((bf16[512,512]{1,0:T(8,128)(2,1)S(1)}, bf16[512,512]{1,0:T(8,128)(2,1)S(1)}, u32[]{:S(2)}, u32[]{:S(2)}) %collective-permute-start.49) | collective-permute-done | bytes 524320 | tf_op jit(solution)/shard_map/ppermute | solution.py:1088
  325.1 2.7 collective-permute-done.48
  329.1 1.5 pad_bitcast_fusion
  330.6 4.1 %collective-permute-done.47 = bf16[512,512]{1,0:T(8,128)(2,1)S(1)} collective-permute-done((bf16[512,512]{1,0:T(8,128)(2,1)S(1)}, bf16[512,512]{1,0:T(8,128)(2,1)S(1)}, u32[]{:S(2)}, u32[]{:S(2)}) %collective-permute-start.47) | collective-permute-done | bytes 524320 | tf_op jit(solution)/shard_map/ppermute | solution.py:1088
  334.7 2.4 collective-permute-done.44
  337.1 2.9 collective-permute-done.56
  340.7 2.9 collective-permute-start.57
  344.9 5.7 %collective-permute-done.64 = f32[8,512]{1,0:T(8,128)S(1)} collective-permute-done((f32[8,512]{1,0:T(8,128)S(1)}, f32[8,512]{1,0:T(8,128)S(1)}, u32[]{:S(2)}, u32[]{:S(2)}) %collective-permute-start.64) | collective-permute-done | bytes 16416 | tf_op jit(solution)/shard_map/ppermute | solution.py:1111
  351.2 3.1 collective-permute-done.65
  354.4 2.5 fusion.13.grad
  356.9 7.4 %update.1 = (f32[2048,128]{1,0:T(8,128)}, f32[2048,128]{1,0:T(8,128)}, f32[2048,128]{1,0:T(8,128)}, f32[8,128]{1,0:T(8,128)}) custom-call(s32[6]{0:T(128)} %pad_add_fusion.1.segments, f32[2048,128]{1,0:T(8,128)} %pad_bitcast_fusion.2.params, f32[2048,128]{1,0:T(8,128)} %get-tuple-element.125.first, f32[2048,128]{1,0:T(8,128)} %get-tuple-element.124.second, ...), custom_call_target="tpu_custom_call" | custom-call | tf_op jit(solution)/shard_map/update/pallas_call | solution.py:1210
  364.4 1.6 collective-permute-start.67
  366.9 3.4 collective-permute-done.59
  370.3 1.5 collective-permute-start.60
  371.9 2.1 collective-permute-done.60
  373.9 1.7 collective-permute-start.61
  375.7 1.9 collective-permute-done.61
  377.6 1.4 collective-permute-start.62
  379.6 2.2 slice.137
  383.4 6.0 %apply.1 = (f32[2048,128]{1,0:T(8,128)}, f32[8,128]{1,0:T(8,128)}) custom-call(s32[6]{0:T(128)} %pad_add_fusion.1.segments, f32[8,128]{1,0:T(8,128)} %add.227.sums, f32[2048,128]{1,0:T(8,128)} %pad_bitcast_fusion.2.params, f32[2048,128]{1,0:T(8,128)} %get-tuple-element.97.update), custom_call_target="tpu_custom_call" | custom-call | tf_op jit(solution)/shard_map/apply/pallas_call | solution.py:1220
  389.5 2.2 slice.136
  391.7 1.3 slice_bitcast_fusion
  (207 shorter events, 34.3 us)
Async XLA Ops:
  1.9 13.2 %collective-permute-start = (bf16[177664]{0:T(1024)(128)(2,1)S(1)}, bf16[177664]{0:T(1024)(128)(2,1)S(1)}, u32[]{:S(2)}, u32[]{:S(2)}) collective-permute-start(bf16[177664]{0:T(1024)(128)(2,1)S(1)} %slice.120), channel_id=1, source_target_pairs={{1,0},{2,1},{3,2},{4,3},{5,4},{6,5},{7,6},{8,7},{9,8},{10,9},{11,1... | collective-permute-start | bytes 1065992 | tf_op jit(solution)/shard_map/ppermute | solution.py:994
  17.4 15.0 %collective-permute-start.1 = (bf16[512,512]{1,0:T(8,128)(2,1)S(1)}, bf16[512,512]{1,0:T(8,128)(2,1)S(1)}, u32[]{:S(2)}, u32[]{:S(2)}) collective-permute-start(bf16[512,512]{1,0:T(8,128)(2,1)S(1)} %reshape.64.refs_0_), channel_id=1, source_target_pairs={{0,2},{1,3},{2,4},{3,5},{4,6},{5,7},{6,0},{7,1},{8,10},{9,11},{10,... | collective-permute-start | bytes 1572872 | tf_op jit(solution)/shard_map/ppermute | solution.py:1041
  19.2 18.3 %collective-permute-start.8 = (bf16[512,512]{1,0:T(8,128)(2,1)S(1)}, bf16[512,512]{1,0:T(8,128)(2,1)S(1)}, u32[]{:S(2)}, u32[]{:S(2)}) collective-permute-start(bf16[512,512]{1,0:T(8,128)(2,1)S(1)} %reshape.64.refs_0_), channel_id=1, source_target_pairs={{0,16},{8,24},{16,0},{24,8},{1,17},{9,25},{17,1},{25,9},{2,18},{10... | collective-permute-start | bytes 1572872 | tf_op jit(solution)/shard_map/ppermute | solution.py:1043
  21.8 15.9 %collective-permute-start.4 = (bf16[512,512]{1,0:T(8,128)(2,1)S(1)}, bf16[512,512]{1,0:T(8,128)(2,1)S(1)}, u32[]{:S(2)}, u32[]{:S(2)}) collective-permute-start(bf16[512,512]{1,0:T(8,128)(2,1)S(1)} %reshape.64.refs_0_), channel_id=1, source_target_pairs={{0,1},{1,0},{2,3},{3,2},{4,5},{5,4},{6,7},{7,6},{8,9},{9,8},{10,11... | collective-permute-start | bytes 1572872 | tf_op jit(solution)/shard_map/ppermute | solution.py:1042
  23.1 14.9 %collective-permute-start.20 = (bf16[512,512]{1,0:T(8,128)(2,1)S(1)}, bf16[512,512]{1,0:T(8,128)(2,1)}, u32[]{:S(2)}, u32[]{:S(2)}) collective-permute-start(bf16[512,512]{1,0:T(8,128)(2,1)S(1)} %reshape.64.refs_0_), channel_id=1, source_target_pairs={{0,8},{8,0},{16,24},{24,16},{1,9},{9,1},{17,25},{25,17},{2,10},{10... | collective-permute-start | bytes 1572872 | tf_op jit(solution)/shard_map/ppermute | solution.py:1047
  32.3 22.3 %collective-permute-start.9 = (bf16[512,512]{1,0:T(8,128)(2,1)S(1)}, bf16[512,512]{1,0:T(8,128)(2,1)S(1)}, u32[]{:S(2)}, u32[]{:S(2)}) collective-permute-start(bf16[512,512]{1,0:T(8,128)(2,1)S(1)} %collective-permute-done.1.refs_1_), channel_id=1, source_target_pairs={{0,16},{8,24},{16,0},{24,8},{1,17},{9,25},{17,1},{25,9},{2,18},{10... | collective-permute-start | bytes 1572872 | tf_op jit(solution)/shard_map/ppermute | solution.py:1043
  37.6 9.3 %collective-permute-start.12 = (bf16[256,512]{1,0:T(8,128)(2,1)S(1)}, bf16[256,512]{1,0:T(8,128)(2,1)S(1)}, u32[]{:S(2)}, u32[]{:S(2)}) collective-permute-start(bf16[256,512]{1,0:T(8,128)(2,1)S(1)} %slice.121), channel_id=1, source_target_pairs={{0,1},{1,0},{2,3},{3,2},{4,5},{5,4},{6,7},{7,6},{8,9},{9,8},{10,11... | collective-permute-start | bytes 786440 | tf_op jit(solution)/shard_map/ppermute | solution.py:1044
  37.7 16.9 %collective-permute-start.16 = (bf16[256,512]{1,0:T(8,128)(2,1)S(1)}, bf16[256,512]{1,0:T(8,128)(2,1)S(1)}, u32[]{:S(2)}, u32[]{:S(2)}) collective-permute-start(bf16[256,512]{1,0:T(8,128)(2,1)S(1)} %slice.125), channel_id=1, source_target_pairs={{0,16},{8,24},{16,0},{24,8},{1,17},{9,25},{17,1},{25,9},{2,18},{10... | collective-permute-start | bytes 786440 | tf_op jit(solution)/shard_map/ppermute | solution.py:1045
  37.8 17.4 %collective-permute-start.2 = (bf16[512,512]{1,0:T(8,128)(2,1)S(1)}, bf16[512,512]{1,0:T(8,128)(2,1)S(1)}, u32[]{:S(2)}, u32[]{:S(2)}) collective-permute-start(bf16[512,512]{1,0:T(8,128)(2,1)S(1)} %collective-permute-done.1.refs_1_), channel_id=1, source_target_pairs={{0,2},{1,3},{2,4},{3,5},{4,6},{5,7},{6,0},{7,1},{8,10},{9,11},{10,... | collective-permute-start | bytes 1572872 | tf_op jit(solution)/shard_map/ppermute | solution.py:1041
  38.0 18.1 %collective-permute-start.5 = (bf16[512,512]{1,0:T(8,128)(2,1)S(1)}, bf16[512,512]{1,0:T(8,128)(2,1)S(1)}, u32[]{:S(2)}, u32[]{:S(2)}) collective-permute-start(bf16[512,512]{1,0:T(8,128)(2,1)S(1)} %collective-permute-done.1.refs_1_), channel_id=1, source_target_pairs={{0,1},{1,0},{2,3},{3,2},{4,5},{5,4},{6,7},{7,6},{8,9},{9,8},{10,11... | collective-permute-start | bytes 1572872 | tf_op jit(solution)/shard_map/ppermute | solution.py:1042
  46.9 9.3 %collective-permute-start.21 = (bf16[512,512]{1,0:T(8,128)(2,1)S(1)}, bf16[512,512]{1,0:T(8,128)(2,1)}, u32[]{:S(2)}, u32[]{:S(2)}) collective-permute-start(bf16[512,512]{1,0:T(8,128)(2,1)S(1)} %collective-permute-done.1.refs_1_), channel_id=1, source_target_pairs={{0,8},{8,0},{16,24},{24,16},{1,9},{9,1},{17,25},{25,17},{2,10},{10... | collective-permute-start | bytes 1572872 | tf_op jit(solution)/shard_map/ppermute | solution.py:1047
  54.6 3.6 collective-permute-start.28
  55.2 4.4 %collective-permute-start.32 = (bf16[256,512]{1,0:T(8,128)(2,1)S(1)}, bf16[256,512]{1,0:T(8,128)(2,1)S(1)}, u32[]{:S(2)}, u32[]{:S(2)}) collective-permute-start(bf16[256,512]{1,0:T(8,128)(2,1)S(1)} %collective-permute-done.12.refs_12_), channel_id=1, source_target_pairs={{0,8},{8,0},{16,24},{24,16},{1,9},{9,1},{17,25},{25,17},{2,10},{10... | collective-permute-start | bytes 786440 | tf_op jit(solution)/shard_map/ppermute | solution.py:1047
  56.2 4.3 %collective-permute-start.36 = (bf16[256,512]{1,0:T(8,128)(2,1)S(1)}, bf16[256,512]{1,0:T(8,128)(2,1)S(1)}, u32[]{:S(2)}, u32[]{:S(2)}) collective-permute-start(bf16[256,512]{1,0:T(8,128)(2,1)S(1)} %collective-permute-done.16.refs_16_), channel_id=1, source_target_pairs={{0,8},{8,0},{16,24},{24,16},{1,9},{9,1},{17,25},{25,17},{2,10},{10... | collective-permute-start | bytes 786440 | tf_op jit(solution)/shard_map/ppermute | solution.py:1047
  56.2 20.5 %collective-permute-start.6 = (bf16[512,512]{1,0:T(8,128)(2,1)S(1)}, bf16[512,512]{1,0:T(8,128)(2,1)S(1)}, u32[]{:S(2)}, u32[]{:S(2)}) collective-permute-start(bf16[512,512]{1,0:T(8,128)(2,1)S(1)} %collective-permute-done.2.refs_2_), channel_id=1, source_target_pairs={{0,1},{1,0},{2,3},{3,2},{4,5},{5,4},{6,7},{7,6},{8,9},{9,8},{10,11... | collective-permute-start | bytes 1572872 | tf_op jit(solution)/shard_map/ppermute | solution.py:1042
  56.5 20.2 %collective-permute-start.10 = (bf16[512,512]{1,0:T(8,128)(2,1)S(1)}, bf16[512,512]{1,0:T(8,128)(2,1)}, u32[]{:S(2)}, u32[]{:S(2)}) collective-permute-start(bf16[512,512]{1,0:T(8,128)(2,1)S(1)} %collective-permute-done.2.refs_2_), channel_id=1, source_target_pairs={{0,16},{8,24},{16,0},{24,8},{1,17},{9,25},{17,1},{25,9},{2,18},{10... | collective-permute-start | bytes 1572872 | tf_op jit(solution)/shard_map/ppermute | solution.py:1043
  58.3 17.9 %collective-permute-start.13 = (bf16[256,512]{1,0:T(8,128)(2,1)S(1)}, bf16[256,512]{1,0:T(8,128)(2,1)S(1)}, u32[]{:S(2)}, u32[]{:S(2)}) collective-permute-start(bf16[256,512]{1,0:T(8,128)(2,1)S(1)} %slice.122), channel_id=1, source_target_pairs={{0,1},{1,0},{2,3},{3,2},{4,5},{5,4},{6,7},{7,6},{8,9},{9,8},{10,11... | collective-permute-start | bytes 786440 | tf_op jit(solution)/shard_map/ppermute | solution.py:1044
  59.6 16.6 %collective-permute-start.17 = (bf16[256,512]{1,0:T(8,128)(2,1)S(1)}, bf16[256,512]{1,0:T(8,128)(2,1)S(1)}, u32[]{:S(2)}, u32[]{:S(2)}) collective-permute-start(bf16[256,512]{1,0:T(8,128)(2,1)S(1)} %slice.126), channel_id=1, source_target_pairs={{0,16},{8,24},{16,0},{24,8},{1,17},{9,25},{17,1},{25,9},{2,18},{10... | collective-permute-start | bytes 786440 | tf_op jit(solution)/shard_map/ppermute | solution.py:1045
  60.4 17.7 %collective-permute-start.3 = (bf16[512,512]{1,0:T(8,128)(2,1)S(1)}, bf16[512,512]{1,0:T(8,128)(2,1)S(1)}, u32[]{:S(2)}, u32[]{:S(2)}) collective-permute-start(bf16[512,512]{1,0:T(8,128)(2,1)S(1)} %collective-permute-done.2.refs_2_), channel_id=1, source_target_pairs={{0,2},{1,3},{2,4},{3,5},{4,6},{5,7},{6,0},{7,1},{8,10},{9,11},{10,... | collective-permute-start | bytes 1572872 | tf_op jit(solution)/shard_map/ppermute | solution.py:1041
  76.1 5.4 %collective-permute-start.22 = (bf16[512,512]{1,0:T(8,128)(2,1)S(1)}, bf16[512,512]{1,0:T(8,128)(2,1)S(1)}, u32[]{:S(2)}, u32[]{:S(2)}) collective-permute-start(bf16[512,512]{1,0:T(8,128)(2,1)S(1)} %collective-permute-done.2.refs_2_), channel_id=1, source_target_pairs={{0,8},{8,0},{16,24},{24,16},{1,9},{9,1},{17,25},{25,17},{2,10},{10... | collective-permute-start | bytes 1572872 | tf_op jit(solution)/shard_map/ppermute | solution.py:1047
  76.2 6.1 %collective-permute-start.25 = (bf16[512,512]{1,0:T(8,128)(2,1)S(1)}, bf16[512,512]{1,0:T(8,128)(2,1)S(1)}, u32[]{:S(2)}, u32[]{:S(2)}) collective-permute-start(bf16[512,512]{1,0:T(8,128)(2,1)S(1)} %collective-permute-done.5.refs_5_), channel_id=1, source_target_pairs={{0,8},{8,0},{16,24},{24,16},{1,9},{9,1},{17,25},{25,17},{2,10},{10... | collective-permute-start | bytes 1572872 | tf_op jit(solution)/shard_map/ppermute | solution.py:1047
  76.6 2.9 collective-permute-start.33
  76.7 3.7 collective-permute-start.37
  78.2 21.0 %collective-permute-start.7 = (bf16[512,512]{1,0:T(8,128)(2,1)S(1)}, bf16[512,512]{1,0:T(8,128)(2,1)}, u32[]{:S(2)}, u32[]{:S(2)}) collective-permute-start(bf16[512,512]{1,0:T(8,128)(2,1)S(1)} %collective-permute-done.3.refs_3_), channel_id=1, source_target_pairs={{0,1},{1,0},{2,3},{3,2},{4,5},{5,4},{6,7},{7,6},{8,9},{9,8},{10,11... | collective-permute-start | bytes 1572872 | tf_op jit(solution)/shard_map/ppermute | solution.py:1042
  79.6 20.1 %collective-permute-start.11 = (bf16[512,512]{1,0:T(8,128)(2,1)S(1)}, bf16[512,512]{1,0:T(8,128)(2,1)}, u32[]{:S(2)}, u32[]{:S(2)}) collective-permute-start(bf16[512,512]{1,0:T(8,128)(2,1)S(1)} %collective-permute-done.3.refs_3_), channel_id=1, source_target_pairs={{0,16},{8,24},{16,0},{24,8},{1,17},{9,25},{17,1},{25,9},{2,18},{10... | collective-permute-start | bytes 1572872 | tf_op jit(solution)/shard_map/ppermute | solution.py:1043
  80.5 17.3 %collective-permute-start.14 = (bf16[256,512]{1,0:T(8,128)(2,1)S(1)}, bf16[256,512]{1,0:T(8,128)(2,1)S(1)}, u32[]{:S(2)}, u32[]{:S(2)}) collective-permute-start(bf16[256,512]{1,0:T(8,128)(2,1)S(1)} %slice.123), channel_id=1, source_target_pairs={{0,1},{1,0},{2,3},{3,2},{4,5},{5,4},{6,7},{7,6},{8,9},{9,8},{10,11... | collective-permute-start | bytes 786440 | tf_op jit(solution)/shard_map/ppermute | solution.py:1044
  81.6 17.6 %collective-permute-start.18 = (bf16[256,512]{1,0:T(8,128)(2,1)S(1)}, bf16[256,512]{1,0:T(8,128)(2,1)S(1)}, u32[]{:S(2)}, u32[]{:S(2)}) collective-permute-start(bf16[256,512]{1,0:T(8,128)(2,1)S(1)} %slice.127), channel_id=1, source_target_pairs={{0,16},{8,24},{16,0},{24,8},{1,17},{9,25},{17,1},{25,9},{2,18},{10... | collective-permute-start | bytes 786440 | tf_op jit(solution)/shard_map/ppermute | solution.py:1045
  82.3 19.4 %collective-permute-start.29 = (bf16[512,512]{1,0:T(8,128)(2,1)S(1)}, bf16[512,512]{1,0:T(8,128)(2,1)S(1)}, u32[]{:S(2)}, u32[]{:S(2)}) collective-permute-start(bf16[512,512]{1,0:T(8,128)(2,1)S(1)} %collective-permute-done.9.refs_9_), channel_id=1, source_target_pairs={{0,8},{8,0},{16,24},{24,16},{1,9},{9,1},{17,25},{25,17},{2,10},{10... | collective-permute-start | bytes 1572872 | tf_op jit(solution)/shard_map/ppermute | solution.py:1047
  97.8 6.5 %collective-permute-start.23 = (bf16[512,512]{1,0:T(8,128)(2,1)S(1)}, bf16[512,512]{1,0:T(8,128)(2,1)S(1)}, u32[]{:S(2)}, u32[]{:S(2)}) collective-permute-start(bf16[512,512]{1,0:T(8,128)(2,1)S(1)} %collective-permute-done.3.refs_3_), channel_id=1, source_target_pairs={{0,8},{8,0},{16,24},{24,16},{1,9},{9,1},{17,25},{25,17},{2,10},{10... | collective-permute-start | bytes 1572872 | tf_op jit(solution)/shard_map/ppermute | solution.py:1047
  99.2 5.1 %collective-permute-start.26 = (bf16[512,512]{1,0:T(8,128)(2,1)S(1)}, bf16[512,512]{1,0:T(8,128)(2,1)S(1)}, u32[]{:S(2)}, u32[]{:S(2)}) collective-permute-start(bf16[512,512]{1,0:T(8,128)(2,1)S(1)} %collective-permute-done.6.refs_6_), channel_id=1, source_target_pairs={{0,8},{8,0},{16,24},{24,16},{1,9},{9,1},{17,25},{25,17},{2,10},{10... | collective-permute-start | bytes 1572872 | tf_op jit(solution)/shard_map/ppermute | solution.py:1047
  99.2 3.1 collective-permute-start.34
  99.7 3.1 collective-permute-start.38
  101.8 10.8 %collective-permute-start.30 = (bf16[512,512]{1,0:T(8,128)(2,1)}, bf16[512,512]{1,0:T(8,128)(2,1)S(1)}, u32[]{:S(2)}, u32[]{:S(2)}) collective-permute-start(bf16[512,512]{1,0:T(8,128)(2,1)} %collective-permute-done.10.refs_10_), channel_id=1, source_target_pairs={{0,8},{8,0},{16,24},{24,16},{1,9},{9,1},{17,25},{25,17},{2,10},{10... | collective-permute-start | bytes 1572872 | tf_op jit(solution)/shard_map/ppermute | solution.py:1047
  102.3 8.4 %collective-permute-start.15 = (bf16[256,512]{1,0:T(8,128)(2,1)S(1)}, bf16[256,512]{1,0:T(8,128)(2,1)}, u32[]{:S(2)}, u32[]{:S(2)}) collective-permute-start(bf16[256,512]{1,0:T(8,128)(2,1)S(1)} %slice.124), channel_id=1, source_target_pairs={{0,1},{1,0},{2,3},{3,2},{4,5},{5,4},{6,7},{7,6},{8,9},{9,8},{10,11... | collective-permute-start | bytes 786440 | tf_op jit(solution)/shard_map/ppermute | solution.py:1044
  102.9 8.3 %collective-permute-start.19 = (bf16[256,512]{1,0:T(8,128)(2,1)S(1)}, bf16[256,512]{1,0:T(8,128)(2,1)}, u32[]{:S(2)}, u32[]{:S(2)}) collective-permute-start(bf16[256,512]{1,0:T(8,128)(2,1)S(1)} %slice.128), channel_id=1, source_target_pairs={{0,16},{8,24},{16,0},{24,8},{1,17},{9,25},{17,1},{25,9},{2,18},{10... | collective-permute-start | bytes 786440 | tf_op jit(solution)/shard_map/ppermute | solution.py:1045
  104.3 8.8 %collective-permute-start.27 = (bf16[512,512]{1,0:T(8,128)(2,1)}, bf16[512,512]{1,0:T(8,128)(2,1)S(1)}, u32[]{:S(2)}, u32[]{:S(2)}) collective-permute-start(bf16[512,512]{1,0:T(8,128)(2,1)} %collective-permute-done.7.refs_7_), channel_id=1, source_target_pairs={{0,8},{8,0},{16,24},{24,16},{1,9},{9,1},{17,25},{25,17},{2,10},{10... | collective-permute-start | bytes 1572872 | tf_op jit(solution)/shard_map/ppermute | solution.py:1047
  104.3 8.8 %collective-permute-start.31 = (bf16[512,512]{1,0:T(8,128)(2,1)}, bf16[512,512]{1,0:T(8,128)(2,1)}, u32[]{:S(2)}, u32[]{:S(2)}) collective-permute-start(bf16[512,512]{1,0:T(8,128)(2,1)} %collective-permute-done.11.refs_11_), channel_id=1, source_target_pairs={{0,8},{8,0},{16,24},{24,16},{1,9},{9,1},{17,25},{25,17},{2,10},{10... | collective-permute-start | bytes 1572872 | tf_op jit(solution)/shard_map/ppermute | solution.py:1047
  239.8 4.2 %collective-permute-start.40 = (bf16[4,512,512]{2,1,0:T(8,128)(2,1)S(1)}, bf16[4,512,512]{2,1,0:T(8,128)(2,1)S(1)}, u32[]{:S(2)}, u32[]{:S(2)}) collective-permute-start(bf16[4,512,512]{2,1,0:T(8,128)(2,1)S(1)} %get-tuple-element.107), channel_id=1, source_target_pairs={{0,8},{8,0},{16,24},{24,16},{1,9},{9,1},{17,25},{25,17},{2,10},{10... | collective-permute-start | bytes 6291464 | tf_op jit(solution)/shard_map/ppermute | solution.py:1068
  239.9 10.1 %collective-permute-start.45 = (bf16[4,512,512]{2,1,0:T(8,128)(2,1)S(1)}, bf16[4,512,512]{2,1,0:T(8,128)(2,1)S(1)}, u32[]{:S(2)}, u32[]{:S(2)}) collective-permute-start(bf16[4,512,512]{2,1,0:T(8,128)(2,1)S(1)} %get-tuple-element.108), channel_id=1, source_target_pairs={{0,8},{8,0},{16,24},{24,16},{1,9},{9,1},{17,25},{25,17},{2,10},{10... | collective-permute-start | bytes 6291464 | tf_op jit(solution)/shard_map/ppermute | solution.py:1068
  240.4 12.6 %collective-permute-start.42 = (bf16[4,512,512]{2,1,0:T(8,128)(2,1)S(1)}, bf16[4,512,512]{2,1,0:T(8,128)(2,1)S(1)}, u32[]{:S(2)}, u32[]{:S(2)}) collective-permute-start(bf16[4,512,512]{2,1,0:T(8,128)(2,1)S(1)} %get-tuple-element.109), channel_id=1, source_target_pairs={{0,8},{8,0},{16,24},{24,16},{1,9},{9,1},{17,25},{25,17},{2,10},{10... | collective-permute-start | bytes 6291464 | tf_op jit(solution)/shard_map/ppermute | solution.py:1068
  240.5 12.6 %collective-permute-start.41 = (bf16[4,512,512]{2,1,0:T(8,128)(2,1)S(1)}, bf16[4,512,512]{2,1,0:T(8,128)(2,1)}, u32[]{:S(2)}, u32[]{:S(2)}) collective-permute-start(bf16[4,512,512]{2,1,0:T(8,128)(2,1)S(1)} %get-tuple-element.110), channel_id=1, source_target_pairs={{0,8},{8,0},{16,24},{24,16},{1,9},{9,1},{17,25},{25,17},{2,10},{10... | collective-permute-start | bytes 6291464 | tf_op jit(solution)/shard_map/ppermute | solution.py:1068
  259.9 25.5 %collective-permute-start.46 = (bf16[2,512,512]{2,1,0:T(8,128)(2,1)}, bf16[2,512,512]{2,1,0:T(8,128)(2,1)}, u32[]{:S(2)}, u32[]{:S(2)}) collective-permute-start(bf16[2,512,512]{2,1,0:T(8,128)(2,1)} %get-tuple-element.120), channel_id=1, source_target_pairs={{0,1},{1,0},{2,3},{3,2},{4,5},{5,4},{6,7},{7,6},{8,9},{9,8},{10,11... | collective-permute-start | bytes 3145736 | tf_op jit(solution)/shard_map/ppermute | solution.py:1075
  261.4 27.9 %collective-permute-start.43 = (bf16[2,512,512]{2,1,0:T(8,128)(2,1)}, bf16[2,512,512]{2,1,0:T(8,128)(2,1)S(1)}, u32[]{:S(2)}, u32[]{:S(2)}) collective-permute-start(bf16[2,512,512]{2,1,0:T(8,128)(2,1)} %get-tuple-element.119), channel_id=1, source_target_pairs={{0,16},{8,24},{16,0},{24,8},{1,17},{9,25},{17,1},{25,9},{2,18},{10... | collective-permute-start | bytes 3145736 | tf_op jit(solution)/shard_map/ppermute | solution.py:1076
  287.8 14.9 %collective-permute-start.53 = (bf16[512,512]{1,0:T(8,128)(2,1)S(1)}, bf16[512,512]{1,0:T(8,128)(2,1)S(1)}, u32[]{:S(2)}, u32[]{:S(2)}) collective-permute-start(bf16[512,512]{1,0:T(8,128)(2,1)S(1)} %get-tuple-element.118), channel_id=1, source_target_pairs={{0,16},{8,24},{16,0},{24,8},{1,17},{9,25},{17,1},{25,9},{2,18},{10... | collective-permute-start | bytes 1572872 | tf_op jit(solution)/shard_map/ppermute | solution.py:1088
  290.4 14.9 %collective-permute-start.52 = (bf16[512,512]{1,0:T(8,128)(2,1)S(1)}, bf16[512,512]{1,0:T(8,128)(2,1)S(1)}, u32[]{:S(2)}, u32[]{:S(2)}) collective-permute-start(bf16[512,512]{1,0:T(8,128)(2,1)S(1)} %get-tuple-element.114), channel_id=1, source_target_pairs={{0,1},{1,0},{2,3},{3,2},{4,5},{5,4},{6,7},{7,6},{8,9},{9,8},{10,11... | collective-permute-start | bytes 1572872 | tf_op jit(solution)/shard_map/ppermute | solution.py:1087
  291.5 22.4 %collective-permute-start.51 = (bf16[512,512]{1,0:T(8,128)(2,1)S(1)}, bf16[512,512]{1,0:T(8,128)(2,1)S(1)}, u32[]{:S(2)}, u32[]{:S(2)}) collective-permute-start(bf16[512,512]{1,0:T(8,128)(2,1)S(1)} %get-tuple-element.117), channel_id=1, source_target_pairs={{0,16},{8,24},{16,0},{24,8},{1,17},{9,25},{17,1},{25,9},{2,18},{10... | collective-permute-start | bytes 1572872 | tf_op jit(solution)/shard_map/ppermute | solution.py:1088
  292.5 24.1 %collective-permute-start.50 = (bf16[512,512]{1,0:T(8,128)(2,1)S(1)}, bf16[512,512]{1,0:T(8,128)(2,1)S(1)}, u32[]{:S(2)}, u32[]{:S(2)}) collective-permute-start(bf16[512,512]{1,0:T(8,128)(2,1)S(1)} %get-tuple-element.113), channel_id=1, source_target_pairs={{0,1},{1,0},{2,3},{3,2},{4,5},{5,4},{6,7},{7,6},{8,9},{9,8},{10,11... | collective-permute-start | bytes 1572872 | tf_op jit(solution)/shard_map/ppermute | solution.py:1087
  305.6 11.8 %collective-permute-start.54 = (bf16[512,512]{1,0:T(8,128)(2,1)S(1)}, bf16[512,512]{1,0:T(8,128)(2,1)S(1)}, u32[]{:S(2)}, u32[]{:S(2)}) collective-permute-start(bf16[512,512]{1,0:T(8,128)(2,1)S(1)} %fusion.1), channel_id=1, source_target_pairs={{0,2},{1,3},{2,4},{3,5},{4,6},{5,7},{6,0},{7,1},{8,10},{9,11},{10,... | collective-permute-start | bytes 1572872 | tf_op jit(solution)/shard_map/ppermute | solution.py:1091
  305.6 19.5 %collective-permute-start.49 = (bf16[512,512]{1,0:T(8,128)(2,1)S(1)}, bf16[512,512]{1,0:T(8,128)(2,1)S(1)}, u32[]{:S(2)}, u32[]{:S(2)}) collective-permute-start(bf16[512,512]{1,0:T(8,128)(2,1)S(1)} %get-tuple-element.116), channel_id=1, source_target_pairs={{0,16},{8,24},{16,0},{24,8},{1,17},{9,25},{17,1},{25,9},{2,18},{10... | collective-permute-start | bytes 1572872 | tf_op jit(solution)/shard_map/ppermute | solution.py:1088
  306.2 21.6 %collective-permute-start.48 = (bf16[512,512]{1,0:T(8,128)(2,1)S(1)}, bf16[512,512]{1,0:T(8,128)(2,1)S(1)}, u32[]{:S(2)}, u32[]{:S(2)}) collective-permute-start(bf16[512,512]{1,0:T(8,128)(2,1)S(1)} %get-tuple-element.112), channel_id=1, source_target_pairs={{0,1},{1,0},{2,3},{3,2},{4,5},{5,4},{6,7},{7,6},{8,9},{9,8},{10,11... | collective-permute-start | bytes 1572872 | tf_op jit(solution)/shard_map/ppermute | solution.py:1087
  317.6 11.0 %collective-permute-start.55 = (bf16[512,512]{1,0:T(8,128)(2,1)S(1)}, bf16[512,512]{1,0:T(8,128)(2,1)S(1)}, u32[]{:S(2)}, u32[]{:S(2)}) collective-permute-start(bf16[512,512]{1,0:T(8,128)(2,1)S(1)} %fusion.4), channel_id=1, source_target_pairs={{0,2},{1,3},{2,4},{3,5},{4,6},{5,7},{6,0},{7,1},{8,10},{9,11},{10,... | collective-permute-start | bytes 1572872 | tf_op jit(solution)/shard_map/ppermute | solution.py:1091
  317.7 16.9 %collective-permute-start.47 = (bf16[512,512]{1,0:T(8,128)(2,1)S(1)}, bf16[512,512]{1,0:T(8,128)(2,1)S(1)}, u32[]{:S(2)}, u32[]{:S(2)}) collective-permute-start(bf16[512,512]{1,0:T(8,128)(2,1)S(1)} %get-tuple-element.115), channel_id=1, source_target_pairs={{0,16},{8,24},{16,0},{24,8},{1,17},{9,25},{17,1},{25,9},{2,18},{10... | collective-permute-start | bytes 1572872 | tf_op jit(solution)/shard_map/ppermute | solution.py:1088
  318.3 18.8 %collective-permute-start.44 = (bf16[512,512]{1,0:T(8,128)(2,1)S(1)}, bf16[512,512]{1,0:T(8,128)(2,1)S(1)}, u32[]{:S(2)}, u32[]{:S(2)}) collective-permute-start(bf16[512,512]{1,0:T(8,128)(2,1)S(1)} %get-tuple-element.111), channel_id=1, source_target_pairs={{0,1},{1,0},{2,3},{3,2},{4,5},{5,4},{6,7},{7,6},{8,9},{9,8},{10,11... | collective-permute-start | bytes 1572872 | tf_op jit(solution)/shard_map/ppermute | solution.py:1087
  329.0 11.0 %collective-permute-start.56 = (bf16[512,512]{1,0:T(8,128)(2,1)S(1)}, bf16[512,512]{1,0:T(8,128)(2,1)S(1)}, u32[]{:S(2)}, u32[]{:S(2)}) collective-permute-start(bf16[512,512]{1,0:T(8,128)(2,1)S(1)} %fusion.7), channel_id=1, source_target_pairs={{0,2},{1,3},{2,4},{3,5},{4,6},{5,7},{6,0},{7,1},{8,10},{9,11},{10,... | collective-permute-start | bytes 1572872 | tf_op jit(solution)/shard_map/ppermute | solution.py:1091
  330.5 14.2 %collective-permute-start.63 = (f32[8,512]{1,0:T(8,128)S(1)}, f32[8,512]{1,0:T(8,128)S(1)}, u32[]{:S(2)}, u32[]{:S(2)}) collective-permute-start(f32[8,512]{1,0:T(8,128)S(1)} %copy-done.37), channel_id=1, source_target_pairs={{0,8},{8,0},{16,24},{24,16},{1,9},{9,1},{17,25},{25,17},{2,10},{10... | collective-permute-start | bytes 49160 | tf_op jit(solution)/shard_map/ppermute | solution.py:1111
  340.7 13.7 %collective-permute-start.57 = (bf16[172112]{0:T(1024)(128)(2,1)S(1)}, bf16[172112]{0:T(1024)(128)(2,1)S(1)}, u32[]{:S(2)}, u32[]{:S(2)}) collective-permute-start(bf16[172112]{0:T(1024)(128)(2,1)S(1)} %slice.135), channel_id=1, source_target_pairs={{0,1},{1,2},{2,3},{3,4},{4,5},{5,6},{6,7},{7,8},{8,9},{9,10},{10,1... | collective-permute-start | bytes 1032680 | tf_op jit(solution)/shard_map/ppermute | solution.py:1014
  344.7 5.9 %collective-permute-start.64 = (f32[8,512]{1,0:T(8,128)S(1)}, f32[8,512]{1,0:T(8,128)S(1)}, u32[]{:S(2)}, u32[]{:S(2)}) collective-permute-start(f32[8,512]{1,0:T(8,128)S(1)} %add.228), channel_id=1, source_target_pairs={{0,1},{1,0},{2,3},{3,2},{4,5},{5,4},{6,7},{7,6},{8,9},{9,8},{10,11... | collective-permute-start | bytes 49160 | tf_op jit(solution)/shard_map/ppermute | solution.py:1111
  350.6 3.7 collective-permute-start.65
  354.4 10.0 %collective-permute-start.66 = (f32[8,512]{1,0:T(8,128)S(1)}, f32[8,512]{1,0:T(8,128)S(1)}, u32[]{:S(2)}, u32[]{:S(2)}) collective-permute-start(f32[8,512]{1,0:T(8,128)S(1)} %add.230), channel_id=1, source_target_pairs={{0,2},{1,3},{2,0},{3,1},{4,6},{5,7},{6,4},{7,5},{8,10},{9,11},{10,... | collective-permute-start | bytes 49160 | tf_op jit(solution)/shard_map/ppermute | solution.py:1111
  364.4 14.5 %collective-permute-start.67 = (f32[8,512]{1,0:T(8,128)S(1)}, f32[8,512]{1,0:T(8,128)S(1)}, u32[]{:S(2)}, u32[]{:S(2)}) collective-permute-start(f32[8,512]{1,0:T(8,128)S(1)} %add.231), channel_id=1, source_target_pairs={{0,4},{1,5},{2,6},{3,7},{4,0},{5,1},{6,2},{7,3},{8,12},{9,13},{10,... | collective-permute-start | bytes 49160 | tf_op jit(solution)/shard_map/ppermute | solution.py:1111
  366.7 3.6 collective-permute-start.59
  370.3 3.6 collective-permute-start.60
  373.9 3.6 collective-permute-start.61
  377.6 5.3 %collective-permute-start.62 = (f32[8,128]{1,0:T(8,128)S(1)}, f32[8,128]{1,0:T(8,128)S(1)}, u32[]{:S(2)}, u32[]{:S(2)}) collective-permute-start(f32[8,128]{1,0:T(8,128)S(1)} %add.226), channel_id=1, source_target_pairs={{0,4},{1,5},{2,6},{3,7},{4,0},{5,1},{6,2},{7,3},{8,12},{9,13},{10,... | collective-permute-start | bytes 12296 | tf_op jit(solution)/shard_map/ppermute | solution.py:1111
  (43 other events, 990.0 us)

commit v3 on v2

v3 whole, which is shorter than its diff:
```python
import math
from types import SimpleNamespace

import jax
import jax.numpy as jnp
from jax import lax
from jax.experimental import pallas as pl
from jax.experimental.pallas import tpu as pltpu
from jax.sharding import PartitionSpec as P

STEP = 8
BETA_FIRST = 0.5
BETA_SECOND = 0.5
LEARN_RATE = 0.5
WEIGHT_DECAY = 0.01
ADAM_EPS = 1e-06
AXES = ("dp", "fsdp")


def segment_shapes():
    gate_width = CG // 2
    return [
        (D, FF),
        (FF, D),
        (D, 3 * D),
        (D, D),
        (D, CG),
        (gate_width, D),
        (2 * D, D),
        (D, FF),
        (FF, D),
        (5 * D + gate_width,),
        (KER, gate_width + 2 * D),
        (RELW, H),
    ]


D = 512
H = 8
HS = 64
FF = 2048
CG = 3072
KER = 31
RELW = 128
NORM_EPS = 1e-05
MASK_FILL = -1000000000.0
ROW = 512
HALF = ROW // 2
SLOTS = 160
KEYS = 256
PAD = 16
PADDED = SLOTS + 2 * PAD
GATE = CG // 2
BLOCK = {
    "ffa_in": (0, 4),
    "ffa_out": (4, 4),
    "qkv": (8, 3),
    "att_out": (11, 1),
    "cg_in": (12, 6),
    "cg_out": (18, 3),
    "merge": (21, 2),
    "ffb_in": (23, 4),
    "ffb_out": (27, 4),
    "small": (31, 1),
}
TAPS_AT = 8
REL_AT = 8 + 5 * KER
SMALL = 176
F32, BF16 = jnp.float32, jnp.bfloat16


def dot(left, right):
    return lax.dot_general(left, right, (((1,), (0,)), ((), ())), preferred_element_type=F32)


def dot_t(left, right):
    return lax.dot_general(left, right, (((1,), (1,)), ((), ())), preferred_element_type=F32)


def t_dot(left, right):
    return lax.dot_general(left, right, (((0,), (0,)), ((), ())), preferred_element_type=F32)


def low(values):
    return values.astype(BF16)


def each(count, body):
    def step(at, carry):
        body(at)
        return carry

    lax.fori_loop(0, count, step, 0)


def part(at, size):
    if isinstance(at, int):
        return slice(at * size, at * size + size)
    return pl.ds(pl.multiple_of(at * size, size), size)


def rows_of(name):
    first, count = BLOCK[name]
    return slice(ROW * first, ROW * (first + count))


def lane_mean(values, width):
    return jnp.sum(values, axis=-1, keepdims=True) * (1.0 / width)


def normed(values):
    centered = values - lane_mean(values, values.shape[-1])
    scale = lax.rsqrt(lane_mean(centered * centered, values.shape[-1]) + NORM_EPS)
    return centered * scale, scale


def valid_rows(length):
    return (lax.broadcasted_iota(jnp.int32, (SLOTS, 1), 0) < length).astype(F32)


def fold_rows(values):
    return jnp.sum(values, axis=0, keepdims=True)


def norm_rows(source, gain, target):
    for k in range(2):
        hat, _ = normed(source[part(k, 80), :].astype(F32))
        target[part(k, 80), :] = low(hat * gain)


def norm_rows_back(values, gain, grad, add):
    total = jnp.zeros((1, values.shape[1]), F32)
    for k in range(2):
        rows = part(k, 80)
        hat, scale = normed(values[rows, :].astype(F32))
        mine = grad[rows, :]
        total = total + fold_rows(mine * hat)
        inner = mine * gain
        width = values.shape[1]
        moved = lane_mean(inner, width) + hat * lane_mean(inner * hat, width)
        add(rows, scale * (inner - moved))
    return total


PIECES = []
for far_core in range(2):
    for kind in ((0, 0), (0, 1), (1, 0)):
        PIECES += [(far_core, *kind, back, 0, ROW) for back in range(4)]
    for first_row in (0, HALF):
        PIECES += [(far_core, 1, 1, back, first_row, HALF) for back in range(4)]


def source_block(coords, piece):
    y, c, z, x = coords[0], coords[1], coords[2], coords[3]
    yy, cc, xx, zz = y ^ piece[1], c ^ piece[0], x ^ piece[2], (z + 4 - piece[3]) & 3
    return ((yy * 2 + cc) * 4 + zz) * 2 + xx


class Loads:
    def __init__(self, coords, sources, target, sems):
        self.source, self.target, self.sems = sources[0], target, sems
        for piece, source in zip(PIECES, sources):
            block = source_block(coords, piece)
            for half in range(2):
                inside = HALF * half - piece[4]
                if 0 <= inside < piece[5]:
                    place = pl.ds(pl.multiple_of(block * ROW + HALF * half, HALF), HALF)
                    pltpu.make_async_copy(
                        source.at[inside : inside + HALF], target.at[place], sems.at[2 * block + half]
                    ).start()

    def wait(self, name):
        first, count = BLOCK[name]
        for at in range(2 * first, 2 * (first + count)):
            pltpu.make_async_copy(
                self.source.at[0:HALF], self.target.at[HALF * at : HALF * at + HALF], self.sems.at[at]
            ).wait()


class Emits:
    def __init__(self, coords, kept, sent, sems):
        self.coords, self.kept, self.sent, self.sems = coords, kept, sent, sems
        self.pending = []

    def put(self, block, values):
        core, z, x = (block // 8) % 2, (block // 2) % 4, block % 2
        slot = 4 * (self.coords[3] ^ x) + ((self.coords[2] + 3 - z) & 3)
        sem = self.sems.at[len(self.pending)]


        @pl.when(self.coords[1] == core)
        def _():
            pltpu.make_async_copy(values, self.kept.at[slot], sem).start()

        @pl.when(self.coords[1] != core)
        def _():
            pltpu.make_async_copy(values, self.sent.at[slot], sem).start()

        self.pending.append(pltpu.make_async_copy(values, self.kept.at[slot], sem))

    def put_tensor(self, name, rows):
        first, count = BLOCK[name]
        for at in range(count):
            self.put(first + at, rows.at[ROW * at : ROW * at + ROW])

    def wait(self):
        for copy in self.pending:
            copy.wait()


def split_columns(raw, target, wide, stage):
    def chunk(k):
        rows = part(k, 128 * wide)
        for lane in range(4):
            stage[lane, 0 : 128 * wide, :] = raw[rows, lane * 128 : lane * 128 + 128].astype(F32)
        for c in range(wide):
            for lane in range(4):
                place = ROW * c + lane * 128
                target[part(k, 128), place : place + 128] = low(stage[lane, pl.ds(c, 128, stride=wide), :])

    each(4, chunk)


def weight_columns(left, grads, wide, stage, left_t, target):
    left_t[...] = left[...].T

    def chunk(j):
        value = dot(left_t[...], grads[:, part(j, 256)])
        c, pair = j // 2, (j % 2) * 2
        for half in range(2):
            stage[pair + half, pl.ds(c, ROW, stride=wide), :] = value[:, 128 * half : 128 * half + 128]

    each(2 * wide, chunk)

    def lower(k):
        rows = part(k, ROW)
        for lane in range(4):
            target[rows, lane * 128 : lane * 128 + 128] = low(stage[lane, rows, :])

    each(wide, lower)


def weight_rows(left, grads, count, left_t, target):
    def chunk(k):
        left_t[...] = left[:, part(k, ROW)].T
        for at in range(2):
            target[part(k, ROW), 256 * at : 256 * at + 256] = low(dot(left_t[...], grads[:, 256 * at : 256 * at + 256]))

    each(count, chunk)


def feed_forward(inputs, gain, w_in, w_out, nrm, act, slope, result):
    norm_rows(inputs, gain, nrm)

    def up(j):
        at = part(j, 256)
        hidden = dot(nrm[...], w_in[:, at])
        sig = jax.nn.sigmoid(hidden)
        active = hidden * sig
        act[:, at] = low(active)
        slope[:, at] = low(sig + active * (1.0 - sig))

    each(FF // 256, up)

    def down(j):
        at = part(j, 256)
        result[:, at] = inputs[:, at].astype(F32) + 0.5 * dot(act[...], w_out[:, at])

    each(2, down)


def feed_back(dout, w_in, w_out, nrm, act, slope, dhid, dnrm, stage, left_t, g_in, g_out, emits, name):
    def up(j):
        at = part(j, 256)
        grad = dot_t(dout[...], w_out[at, :])
        dhid[:, at] = low(grad * slope[:, at].astype(F32))

    each(FF // 256, up)
    weight_rows(act, dout, 4, left_t, g_out)
    emits.put_tensor(name + "_out", g_out)

    def down(j):
        at = part(j, 256)
        dnrm[:, at] = dot_t(dhid[:, 0:FF], w_in[at, :])

    each(2, down)
    weight_columns(nrm, dhid, 4, stage, left_t, g_in)
    emits.put_tensor(name + "_in", g_in)


def bucket_map():
    entry = lax.broadcasted_iota(jnp.int32, (2 * ROW, ROW), 0) // H
    far = lax.broadcasted_iota(jnp.int32, (2 * ROW, ROW), 1)
    far = jnp.where(far >= ROW // 2, far - ROW, far)
    bucket = jnp.clip(far, -(RELW // 2), RELW // 2 - 1) + RELW // 2
    return (entry == bucket).astype(F32)


def own_entries(flat):
    entry = lax.broadcasted_iota(jnp.int32, (H, 2 * ROW), 1)
    head = lax.broadcasted_iota(jnp.int32, (H, 2 * ROW), 0)
    return jnp.where(lax.rem(entry, H) == head, flat, 0.0)


def tap_row(small, tap, row, lane):
    return small[lane, pl.ds(TAPS_AT + 5 * tap + row, 1), :]


def shifted_sum(padded, at, factor):
    total = None
    for low_part in range(8):
        slab = padded[low_part : low_part + SLOTS + 24, at]
        inner = None
        for high_part in range(4):
            offset = 8 * high_part + low_part
            if offset:
                term = factor(offset) * slab[8 * high_part : 8 * high_part + SLOTS]
                inner = term if inner is None else inner + term
        total = inner if total is None else total + inner
    return total


def convolve(padded, small, first_row, width, finish):

    def chunk(j):
        at = part(j, 128)
        row, lane = first_row + j // 4, j % 4
        finish(j, at, shifted_sum(padded, at, lambda offset: tap_row(small, offset - 1, row, lane)))

    each(width // 128, chunk)


def convolve_back(grads, padded, small, first_row, width, sgrad, finish):

    def chunk(j):
        at = part(j, 128)
        row, lane = first_row + j // 4, j % 4
        finish(j, at, shifted_sum(grads, at, lambda offset: tap_row(small, KER - offset, row, lane)))
        own = grads[PAD : PAD + SLOTS, at]
        for low_part in range(8):
            slab = padded[low_part : low_part + SLOTS + 24, at]
            for high_part in range(4):
                offset = 8 * high_part + low_part
                if offset:
                    tile = slab[8 * high_part : 8 * high_part + SLOTS]
                    sgrad[lane, pl.ds(TAPS_AT + 5 * (offset - 1) + row, 1), :] = fold_rows(own * tile)

    each(width // 128, chunk)


def clear_margins(padded):
    padded[0:PAD, :] = jnp.zeros((PAD, padded.shape[1]), F32)
    padded[PAD + SLOTS : PADDED, :] = jnp.zeros((PAD, padded.shape[1]), F32)


def gelu_parts(hidden):
    bell = jnp.exp(-0.5 * hidden * hidden)
    spread = 1.0 + (0.3275911 * 2.0**-0.5) * jnp.abs(hidden)
    near = pl.reciprocal(spread, approx=True)
    near = near * (2.0 - spread * near)
    tail = jnp.full_like(near, 0.5 * 1.061405429)
    for factor in (-1.453152027, 1.421413741, -0.284496736, 0.254829592):
        tail = tail * near + 0.5 * factor
    tail = tail * near * bell
    below = jnp.where(hidden >= 0.0, 1.0 - tail, tail)
    return hidden * below, below + hidden * bell * ((2.0 * math.pi) ** -0.5)


def attention_forward(r, length):
    norm_rows(r.x1, r.small[1:2, :], r.nrm_t)
    r.qkv[SLOTS:KEYS, :] = jnp.zeros((KEYS - SLOTS, 3 * D), BF16)
    flat = jnp.concatenate([r.small[REL_AT : REL_AT + 1, :], r.small[REL_AT + 1 : REL_AT + 2, :]], axis=1)
    r.bias[...] = dot(low(own_entries(jnp.broadcast_to(flat, (H, 2 * ROW)))), low(bucket_map()))

    def project(j):
        at = part(j, 256)
        r.qkv[0:SLOTS, at] = low(dot(r.nrm_t[...], r.w_qkv[:, at]))

    each(3 * D // 256, project)
    valid = lax.broadcasted_iota(jnp.int32, (1, KEYS), 1) < length
    first_half = lax.broadcasted_iota(jnp.int32, (1, 128), 1) < HS

    def heads(pair):
        queries = r.qkv[0:SLOTS, part(pair, 128)]
        keys = r.qkv[:, part(pair + 4, 128)]
        values = r.qkv[:, part(pair + 8, 128)]
        outs = []
        for odd in range(2):
            head = 2 * pair + odd
            half = first_half if odd == 0 else jnp.logical_not(first_half)
            mine = jnp.where(half, queries, jnp.zeros_like(queries))
            spread = jnp.broadcast_to(r.bias[pl.ds(head, 1), :], (SLOTS, ROW))
            spread = pltpu.roll(spread, 0, 1, stride=1, stride_axis=0)[:, 0:KEYS]
            scores = jnp.where(valid, dot_t(mine, keys) * HS ** (-0.5) + spread, MASK_FILL)
            shifted = jnp.exp(scores - jnp.max(scores, axis=-1, keepdims=True))
            chances = low(shifted / jnp.sum(shifted, axis=-1, keepdims=True))
            r.probs[head] = chances
            outs.append(dot(chances, values))
        r.ctx[:, part(pair, 128)] = low(jnp.where(first_half, outs[0], outs[1]))

    each(H // 2, heads)

    def project_out(j):
        at = part(j, 256)
        r.cat[:, at] = dot(r.ctx[...], r.w[rows_of("att_out"), at])

    each(2, project_out)


def gating_forward(r, length):
    norm_rows(r.x1, r.small[2:3, :], r.nrm_c)

    def up(j):
        at = part(j, 256)
        r.hid[...] = dot(r.nrm_c[...], r.w_cg[:, at])
        for k in range(5):
            rows = part(k, 32)
            active, slope = gelu_parts(r.hid[rows, :])
            r.ug[rows, at] = active
            r.slope_c[rows, at] = low(slope)

    each(CG // 256, up)
    tiles = [slice(GATE + 128 * j, GATE + 128 * j + 128) for j in range(GATE // 128)]
    total = jnp.zeros((SLOTS, 128), F32)
    for at in tiles:
        total = total + r.ug[:, at]
    mean = lane_mean(total, GATE)
    total = jnp.zeros((SLOTS, 128), F32)
    for at in tiles:
        centered = r.ug[:, at] - mean
        total = total + centered * centered
    scale = lax.rsqrt(lane_mean(total, GATE) + NORM_EPS)
    r.gmean[...] = jnp.broadcast_to(mean, (SLOTS, 128))
    r.gscale[...] = jnp.broadcast_to(scale, (SLOTS, 128))
    scale = scale * valid_rows(length)
    for j, at in enumerate(tiles):
        gain = r.small[5 + j // 4 : 6 + j // 4, part(j % 4, 128)]
        r.gpad[PAD : PAD + SLOTS, part(j, 128)] = (r.ug[:, at] - mean) * scale * gain

    def finish(j, at, value):
        r.cv[:, at] = low(value)
        r.gated[:, at] = low(r.ug[:, at] * value)

    convolve(r.gpad, r.tiles, 0, GATE, finish)

    def down(j):
        r.cat[:, part(j + 2, 256)] = dot(r.gated[...], r.w[rows_of("cg_out"), part(j, 256)])

    each(2, down)


def merge_forward(r, length):
    valid = valid_rows(length)
    for j in range(8):
        at = part(j, 128)
        r.mpad[PAD : PAD + SLOTS, at] = r.cat[:, at] * valid

    def finish(j, at, value):
        r.mixed[:, at] = low(r.cat[:, at] + value)

    convolve(r.mpad, r.tiles, 3, 2 * D, finish)

    def merge(j):
        at = part(j, 256)
        r.x2[:, at] = r.x1[:, at] + dot(r.mixed[...], r.w[rows_of("merge"), at])

    each(2, merge)


def final_norm(r, length):
    gain = r.small[4:5, :]
    valid = valid_rows(length)
    total = jnp.zeros((1, D), F32)
    for k in range(2):
        rows = part(k, 80)
        hat, scale = normed(r.x3[rows, :])
        r.out[rows, :] = low(hat * gain * valid[80 * k : 80 * k + 80])
        mine = r.cot[rows, :].astype(F32) * valid[80 * k : 80 * k + 80]
        total = total + fold_rows(mine * hat)
        inner = mine * gain
        back = scale * (inner - (lane_mean(inner, D) + hat * lane_mean(inner * hat, D)))
        r.dx[rows, :] = back
        r.dout[rows, :] = low(0.5 * back)
    r.gains[4:5, :] = total


def merge_back(r, length, emits):
    for k in range(2):
        r.dout[part(k, 80), :] = low(r.dx[part(k, 80), :])
    w_merge = r.w.at[rows_of("merge")]

    def merge(j):
        at = part(j, 256)
        r.dpad[PAD : PAD + SLOTS, at] = dot_t(r.dout[...], w_merge[at, :])

    each(2 * D // 256, merge)
    weight_rows(r.mixed, r.dout, 2, r.left_t, w_merge)
    emits.put_tensor("merge", w_merge)

    def finish(j, at, value):
        r.djoin[:, at] = low(r.dpad[PAD : PAD + SLOTS, at] + value * valid_rows(length))

    convolve_back(r.dpad, r.mpad, r.tiles, 3, 2 * D, r.tgrad, finish)


def gating_back(r, length, emits):
    w_co = r.w.at[rows_of("cg_out")]

    def gate(j):
        at = part(j, 256)
        value = dot_t(r.djoin[:, D:], w_co[at, :])
        r.dhid[:, at] = low(value * r.cv[:, at].astype(F32) * r.slope_c[:, at].astype(F32))
        r.dpad[PAD : PAD + SLOTS, at] = value * r.ug[:, at]

    each(GATE // 256, gate)
    r.dout[...] = r.djoin[:, D:]
    weight_rows(r.gated, r.dout, 3, r.left_t, w_co)
    emits.put_tensor("cg_out", w_co)

    def finish(j, at, value):
        r.dgate[:, at] = value * valid_rows(length)

    convolve_back(r.dpad, r.gpad, r.tiles, 0, GATE, r.tgrad, finish)
    r.sum_inner[...] = jnp.zeros_like(r.sum_inner)
    r.sum_hat[...] = jnp.zeros_like(r.sum_hat)

    def gate_sums(j):
        row, lane = 5 + j // 4, j % 4
        hat = (r.ug[:, part(j + GATE // 128, 128)] - r.gmean[...]) * r.gscale[...]
        grad = r.dgate[:, part(j, 128)]
        r.tgrad[lane, pl.ds(row, 1), :] = fold_rows(grad * hat)
        inner = grad * r.tiles[lane, pl.ds(row, 1), :]
        r.sum_inner[...] += inner
        r.sum_hat[...] += inner * hat

    def gate_back(j):
        row, lane = 5 + j // 4, j % 4
        far = part(j + GATE // 128, 128)
        hat = (r.ug[:, far] - r.gmean[...]) * r.gscale[...]
        inner = r.dgate[:, part(j, 128)] * r.tiles[lane, pl.ds(row, 1), :]
        back = r.gscale[...] * (inner - r.sum_inner[...] - hat * r.sum_hat[...])
        r.dhid[:, far] = low(back * r.slope_c[:, far].astype(F32))

    each(GATE // 128, gate_sums)
    for sums in (r.sum_inner, r.sum_hat):
        sums[...] = jnp.broadcast_to(lane_mean(sums[...], GATE), (SLOTS, 128))
    each(GATE // 128, gate_back)

    def down(j):
        at = part(j, 256)
        r.dnrm[:, at] = dot_t(r.dhid[...], r.w_cg[at, :])

    each(2, down)
    g_cg = r.w.at[rows_of("cg_in")]
    weight_columns(r.nrm_c, r.dhid, 6, r.stage, r.left_t, g_cg)
    emits.put_tensor("cg_in", g_cg)

    def add(rows, back):
        r.dx[rows, :] += back

    r.gains[2:3, :] = norm_rows_back(r.x1, r.small[2:3, :], r.dnrm, add)


def forward_kernel(names, coords, length_ref, frames, cot, *refs):
    sources, refs = refs[: len(PIECES)], refs[len(PIECES) :]
    r = SimpleNamespace(**dict(zip(names, refs)))
    r.cot = cot
    length = length_ref[0]
    loads = Loads(coords, sources, r.w, r.load_sems)
    kept = []

    def keep(source, target):
        copy = pltpu.make_async_copy(source, target, r.keep_sems.at[len(kept)])
        copy.start()
        kept.append(copy)

    for padded in (r.gpad, r.mpad, r.dpad):
        clear_margins(padded)
    r.tgrad[...] = jnp.zeros_like(r.tgrad)
    r.gains[...] = jnp.zeros_like(r.gains)
    loads.wait("small")
    r.small[...] = r.w[ROW * 31 : ROW * 31 + SMALL, :].astype(F32)
    for lane in range(4):
        r.tiles[lane] = r.small[:, part(lane, 128)]
    loads.wait("ffa_in")
    split_columns(r.w.at[rows_of("ffa_in")], r.w_ffa_in, 4, r.stage)
    keep(r.w_ffa_in, r.keep_ffa_in)
    loads.wait("ffa_out")
    keep(r.w.at[rows_of("ffa_out")], r.keep_ffa_out)
    feed_forward(frames, r.small[0:1, :], r.w_ffa_in, r.w.at[rows_of("ffa_out")], r.nrm, r.act, r.slope, r.x1)
    keep(r.nrm, r.keep_nrm)
    keep(r.act, r.keep_act)
    keep(r.slope, r.keep_slope)
    keep(r.x1, r.keep_x1)
    loads.wait("qkv")
    split_columns(r.w.at[rows_of("qkv")], r.w_qkv, 3, r.stage)
    keep(r.w_qkv, r.keep_qkv)
    loads.wait("att_out")
    keep(r.w.at[rows_of("att_out")], r.keep_att)
    attention_forward(r, length)
    keep(r.nrm_t, r.keep_nrm_t)
    keep(r.qkv, r.keep_heads)
    keep(r.probs, r.keep_probs)
    keep(r.ctx, r.keep_ctx)
    loads.wait("cg_in")
    split_columns(r.w.at[rows_of("cg_in")], r.w_cg, 6, r.stage)
    loads.wait("cg_out")
    gating_forward(r, length)
    loads.wait("merge")
    merge_forward(r, length)
    loads.wait("ffb_in")
    split_columns(r.w.at[rows_of("ffb_in")], r.w_ffb_in, 4, r.stage)
    loads.wait("ffb_out")
    w_out = r.w.at[rows_of("ffb_out")]
    feed_forward(r.x2, r.small[3:4, :], r.w_ffb_in, w_out, r.nrm_b, r.act_b, r.slope_b, r.x3)
    final_norm(r, length)
    high = Emits(coords, r.high_kept, r.high_sent, r.high_sems)
    every = Emits(coords, r.low_kept, r.low_sent, r.low_sems)

    def put(block, values):
        (high if block >= 16 else every).put(block, values)

    emits = SimpleNamespace(
        put_tensor=lambda name, rows: [
            put(BLOCK[name][0] + at, rows.at[ROW * at : ROW * at + ROW]) for at in range(BLOCK[name][1])
        ]
    )
    feed_back(
        r.dout, r.w_ffb_in, w_out, r.nrm_b, r.act_b, r.slope_b, r.dhid, r.dnrm, r.stage, r.left_t,
        r.w.at[rows_of("ffb_in")], w_out, emits, "ffb",
    )

    def add(rows, back):
        r.dx[rows, :] += back

    r.gains[3:4, :] = norm_rows_back(r.x2, r.small[3:4, :], r.dnrm, add)
    merge_back(r, length, emits)
    keep(r.djoin, r.keep_djoin)
    gating_back(r, length, emits)
    keep(r.dx, r.keep_dx)
    for lane in range(4):
        at = part(lane, 128)
        r.gains[5:8, at] = r.tgrad[lane, 5:8, :]
        r.w[ROW * 31 : ROW * 31 + SMALL, at] = low(r.tgrad[lane])
    r.w[ROW * 31 : ROW * 31 + 16, :] = low(
        jnp.concatenate(
            [
                jnp.zeros((8, ROW), F32),
                jnp.concatenate([r.tgrad[lane, 8:16, :] for lane in range(4)], axis=1),
            ],
            axis=0,
        )
    )
    r.w[ROW * 31 + SMALL : ROW * 32, :] = jnp.zeros((ROW - SMALL, ROW), BF16)
    put(31, r.w.at[ROW * 31 : ROW * 32])
    for copy in kept:
        copy.wait()
    high.wait()
    every.wait()


def attention_back(r, emits):
    def project(j):
        at = part(j, 256)
        r.dctx[:, at] = low(dot_t(r.datt[...], r.w_att[at, :]))

    each(2, project)
    weight_rows(r.ctx, r.datt, 1, r.left_t, r.w_att)
    emits.put_tensor("att_out", r.w_att)
    first_half = lax.broadcasted_iota(jnp.int32, (1, 128), 1) < HS
    at_row = lax.broadcasted_iota(jnp.int32, (SLOTS, SLOTS), 0)
    at_column = lax.broadcasted_iota(jnp.int32, (SLOTS, SLOTS), 1)
    flip = low((at_row + at_column == SLOTS - 1).astype(F32))

    def heads(pair):
        queries = r.qkv[0:SLOTS, part(pair, 128)]
        keys = r.qkv[:, part(pair + 4, 128)]
        values = r.qkv[:, part(pair + 8, 128)]
        context = r.dctx[:, part(pair, 128)]
        q_parts, k_parts, v_parts = [], [], []
        for odd in range(2):
            head = 2 * pair + odd
            half = first_half if odd == 0 else jnp.logical_not(first_half)
            chances = r.probs[head]
            v_parts.append(t_dot(chances, context)[0:SLOTS])
            wide_chances = chances.astype(F32)
            chance_grad = dot_t(jnp.where(half, context, jnp.zeros_like(context)), values)
            inner = jnp.sum(wide_chances * chance_grad, axis=-1, keepdims=True)
            score_grad = low(wide_chances * (chance_grad - inner))
            q_parts.append(dot(score_grad, keys))
            k_parts.append(t_dot(score_grad, queries)[0:SLOTS])
            wide = jnp.concatenate([dot(flip, score_grad), jnp.zeros((SLOTS, ROW - KEYS), F32)], axis=1)
            wide = pltpu.roll(wide, ROW - SLOTS + 1, 1, stride=1, stride_axis=0)
            r.sums[pl.ds(head, 1), :] = fold_rows(wide)
        scale = HS ** (-0.5)
        r.dhid[:, part(pair, 128)] = low(jnp.where(first_half, q_parts[0], q_parts[1]) * scale)
        r.dhid[:, part(pair + 4, 128)] = low(jnp.where(first_half, k_parts[0], k_parts[1]) * scale)
        r.dhid[:, part(pair + 8, 128)] = low(jnp.where(first_half, v_parts[0], v_parts[1]))

    each(H // 2, heads)

    def down(j):
        at = part(j, 256)
        r.dnrm[:, at] = dot_t(r.dhid[:, 0 : 3 * D], r.w_qkv[at, :])

    each(2, down)

    def add(rows, back):
        r.dx[rows, :] += back
        r.dout[rows, :] = low(0.5 * r.dx[rows, :])

    r.late[1:2, :] = norm_rows_back(r.x1, r.gain_rows[1:2, :], r.dnrm, add)


def attention_weights_back(r, emits):
    weight_columns(r.nrm_t, r.dhid, 3, r.stage, r.left_t, r.g_qkv)
    emits.put_tensor("qkv", r.g_qkv)
    by_entry = lax.dot_general(
        r.sums[...],
        bucket_map(),
        (((1,), (1,)), ((), ())),
        precision=lax.Precision.HIGHEST,
        preferred_element_type=F32,
    )
    flat = fold_rows(own_entries(by_entry))
    r.late[8:9, :] = flat[:, 0:ROW]
    r.late[9:10, :] = flat[:, ROW:]


def backward_kernel(names, coords, frames, gains, gain_rows, *refs):
    r = SimpleNamespace(**dict(zip(names, refs)))
    r.gain_rows = gain_rows
    waits = {}
    for at, (name, source, target) in enumerate(
        (
            ("att", r.in_att, r.w_att),
            ("djoin", r.in_djoin.at[:, 0:D], r.datt),
            ("ctx", r.in_ctx, r.ctx),
            ("heads", r.in_heads, r.qkv),
            ("probs", r.in_probs, r.probs),
            ("qkv", r.in_qkv, r.w_qkv),
            ("x1", r.in_x1, r.x1),
            ("dx", r.in_dx, r.dx),
            ("nrm_t", r.in_nrm_t, r.nrm_t),
            ("ffa_out", r.in_ffa_out, r.w_ffa_out),
            ("slope", r.in_slope, r.slope),
            ("act", r.in_act, r.act),
            ("ffa_in", r.in_ffa_in, r.w_ffa_in),
            ("nrm", r.in_nrm, r.nrm),
        )
    ):
        waits[name] = pltpu.make_async_copy(source, target, r.load_sems.at[at])
        waits[name].start()
    r.late[...] = jnp.zeros_like(r.late)
    emits = Emits(coords, r.low_kept, r.low_sent, r.low_sems)
    for name in ("att", "djoin", "ctx", "heads", "probs", "qkv", "x1", "dx"):
        waits[name].wait()
    attention_back(r, emits)
    waits["nrm_t"].wait()
    attention_weights_back(r, emits)
    for name in ("ffa_out", "slope", "act", "ffa_in", "nrm"):
        waits[name].wait()
    feed_back(
        r.dout, r.w_ffa_in, r.w_ffa_out, r.nrm, r.act, r.slope, r.dhid, r.dnrm, r.stage, r.left_t, r.g_ffa_in,
        r.w_ffa_out, emits, "ffa",
    )

    def add(rows, back):
        r.fgrad[rows, :] = low(r.dx[rows, :] + back)

    r.late[0:1, :] = norm_rows_back(frames, gain_rows[0:1, :], r.dnrm, add)
    r.late[2:8, :] = gains[2:8, :]
    emits.wait()


VM = pl.BlockSpec(memory_space=pltpu.VMEM)
SM = pl.BlockSpec(memory_space=pltpu.SMEM)
ANY = pl.BlockSpec(memory_space=pl.ANY)
WIDE, THIN = ((SLOTS, D), F32), ((SLOTS, D), BF16)
FULL = ((SLOTS, FF), BF16)
HALF_GRADS = ((8, ROW, ROW), BF16)

FORWARD_OUT = {
    "out": (VM, THIN),
    "gains": (VM, ((8, ROW), F32)),
    "small": (VM, ((SMALL, ROW), F32)),
    "high_kept": (ANY, HALF_GRADS),
    "high_sent": (ANY, HALF_GRADS),
    "low_kept": (ANY, HALF_GRADS),
    "low_sent": (ANY, HALF_GRADS),
    "keep_ffa_in": (ANY, ((D, FF), BF16)),
    "keep_ffa_out": (ANY, ((FF, D), BF16)),
    "keep_qkv": (ANY, ((D, 3 * D), BF16)),
    "keep_att": (ANY, ((D, D), BF16)),
    "keep_nrm": (ANY, THIN),
    "keep_act": (ANY, FULL),
    "keep_slope": (ANY, FULL),
    "keep_x1": (ANY, WIDE),
    "keep_nrm_t": (ANY, THIN),
    "keep_heads": (ANY, ((KEYS, 3 * D), BF16)),
    "keep_probs": (ANY, ((H, SLOTS, KEYS), BF16)),
    "keep_ctx": (ANY, THIN),
    "keep_djoin": (ANY, ((SLOTS, 2 * D), BF16)),
    "keep_dx": (ANY, WIDE),
}
FORWARD_SCRATCH = {
    "w": ((32 * ROW, ROW), BF16),
    "w_ffa_in": ((D, FF), BF16),
    "w_qkv": ((D, 3 * D), BF16),
    "w_cg": ((D, CG), BF16),
    "w_ffb_in": ((D, FF), BF16),
    "stage": ((4, 6 * ROW, 128), F32),
    "left_t": ((ROW, SLOTS), BF16),
    "tiles": ((4, SMALL, 128), F32),
    "tgrad": ((4, SMALL, 128), F32),
    "bias": ((H, ROW), F32),
    "nrm": THIN,
    "act": FULL,
    "slope": FULL,
    "nrm_t": THIN,
    "qkv": ((KEYS, 3 * D), BF16),
    "probs": ((H, SLOTS, KEYS), BF16),
    "ctx": THIN,
    "nrm_c": THIN,
    "hid": ((SLOTS, 256), F32),
    "ug": ((SLOTS, CG), F32),
    "slope_c": ((SLOTS, CG), BF16),
    "gmean": ((SLOTS, 128), F32),
    "gscale": ((SLOTS, 128), F32),
    "sum_inner": ((SLOTS, 128), F32),
    "sum_hat": ((SLOTS, 128), F32),
    "gpad": ((PADDED, GATE), F32),
    "cv": ((SLOTS, GATE), BF16),
    "gated": ((SLOTS, GATE), BF16),
    "cat": ((SLOTS, 2 * D), F32),
    "mpad": ((PADDED, 2 * D), F32),
    "mixed": ((SLOTS, 2 * D), BF16),
    "nrm_b": THIN,
    "act_b": FULL,
    "slope_b": FULL,
    "dpad": ((PADDED, GATE), F32),
    "djoin": ((SLOTS, 2 * D), BF16),
    "dgate": ((SLOTS, GATE), F32),
    "dhid": ((SLOTS, CG), BF16),
    "dnrm": WIDE,
    "dout": THIN,
    "dx": WIDE,
    "x1": WIDE,
    "x2": WIDE,
    "x3": WIDE,
    "load_sems": 64,
    "keep_sems": 16,
    "high_sems": 16,
    "low_sems": 4,
}
BACKWARD_IN = (
    "ffa_in", "ffa_out", "qkv", "att", "nrm", "act", "slope", "x1", "nrm_t", "heads", "probs", "ctx", "djoin", "dx",
)
BACKWARD_OUT = {
    "fgrad": (VM, THIN),
    "late": (VM, ((16, ROW), F32)),
    "low_kept": (ANY, HALF_GRADS),
    "low_sent": (ANY, HALF_GRADS),
}
BACKWARD_SCRATCH = {
    "w_ffa_in": ((D, FF), BF16),
    "w_ffa_out": ((FF, D), BF16),
    "w_qkv": ((D, 3 * D), BF16),
    "w_att": ((D, D), BF16),
    "g_ffa_in": ((FF, D), BF16),
    "g_qkv": ((3 * D, D), BF16),
    "stage": ((4, 4 * ROW, 128), F32),
    "left_t": ((ROW, SLOTS), BF16),
    "sums": ((H, ROW), F32),
    "nrm": THIN,
    "act": FULL,
    "slope": FULL,
    "nrm_t": THIN,
    "qkv": ((KEYS, 3 * D), BF16),
    "probs": ((H, SLOTS, KEYS), BF16),
    "ctx": THIN,
    "datt": THIN,
    "dctx": THIN,
    "dhid": FULL,
    "dnrm": WIDE,
    "dout": THIN,
    "dx": WIDE,
    "x1": WIDE,
    "load_sems": 14,
    "low_sems": 12,
}


def call(kernel, name, ins, outs, scratch, limit, aliases=None):
    return pl.pallas_call(
        kernel,
        name=name,
        in_specs=[space for space, _ in ins],
        out_specs=[space for space, _ in outs],
        out_shape=[jax.ShapeDtypeStruct(*kind) for _, kind in outs],
        scratch_shapes=[
            pltpu.SemaphoreType.DMA((each_one,)) if isinstance(each_one, int) else pltpu.VMEM(*each_one)
            for each_one in scratch
        ],
        input_output_aliases=aliases or {},
        compiler_params=pltpu.CompilerParams(vmem_limit_bytes=limit * 2**20),
    )(*[array for _, array in ins])


def forward(coords, length, frames, cot, blocks):
    def kernel(*refs):
        forward_kernel([*FORWARD_OUT, *FORWARD_SCRATCH], *refs)

    outs = call(
        kernel,
        "forward",
        [(SM, coords), (SM, length), (VM, frames), (VM, cot)] + [(ANY, block) for block in blocks],
        list(FORWARD_OUT.values()),
        list(FORWARD_SCRATCH.values()),
        58,
    )
    return dict(zip(FORWARD_OUT, outs))


def backward(coords, frames, state):
    def kernel(*refs):
        names = ["in_" + name for name in BACKWARD_IN] + ["in_low_kept", "in_low_sent"]
        backward_kernel([*names, *BACKWARD_OUT, *BACKWARD_SCRATCH], *refs)

    ins = [(SM, coords), (VM, frames), (VM, state["gains"]), (VM, state["small"])]
    ins += [(ANY, state["keep_" + name]) for name in BACKWARD_IN]
    ins += [(ANY, state["low_kept"]), (ANY, state["low_sent"])]
    outs = call(
        kernel,
        "backward",
        ins,
        list(BACKWARD_OUT.values()),
        list(BACKWARD_SCRATCH.values()),
        58,
        {len(ins) - 2: 2, len(ins) - 1: 3},
    )
    return dict(zip(BACKWARD_OUT, outs))


def segment_bounds():
    bounds = [0]
    for extent in segment_shapes():
        bounds.append(bounds[-1] + math.prod(extent))
    return bounds


def block_rows(device_count):
    total_rows = -(-segment_bounds()[-1] // ROW)
    step = 16 * device_count
    return -(-total_rows // step) * 16


def align_shard(low_shard, shard_size, rows):
    devices = lax.axis_size("dp") * lax.axis_size("fsdp")
    me = lax.axis_index(AXES)
    block = rows * ROW
    lead = block - shard_size
    pieces = [low_shard]
    have = shard_size
    need = lead * (devices - 1) + block
    hop = 1
    while have < need:
        part = min(shard_size, need - have)
        pairs = [(i, i - hop) for i in range(hop, devices)]
        pieces.append(lax.ppermute(low_shard[:part], AXES, pairs))
        have = have + part
        hop = hop + 1
    return lax.dynamic_slice(jnp.concatenate(pieces), (me * lead,), (block,)).reshape(rows, ROW)


def unalign_block(block_sum, shard_size, padded):
    devices = lax.axis_size("dp") * lax.axis_size("fsdp")
    me = lax.axis_index(AXES)
    rows = block_sum.shape[0]
    block = rows * ROW
    lead = block - shard_size
    flat = block_sum.reshape(-1)
    pieces = [flat]
    have = block
    need = lead * (devices - 1) + block
    hop = 1
    while have < need:
        part = min(block, need - have)
        pairs = [(i, i + hop) for i in range(devices - hop)]
        pieces.insert(0, lax.ppermute(flat[block - part :], AXES, pairs))
        have = have + part
        hop = hop + 1
    start = have - block - me * lead
    pieces.append(jnp.zeros((max(0, padded - block),), flat.dtype))
    return lax.dynamic_slice(jnp.concatenate(pieces), (start,), (padded,))


def pair_lists():
    ring = [(i, (i + 2) % 8) for i in range(8)]
    across_x = [(i, i ^ 1) for i in range(8)]
    across_y = [(i, i ^ 2) for i in range(4)]
    across_core = [(i, i ^ 1) for i in range(4)]
    return ring, across_x, across_y, across_core


def fast_mesh():
    return lax.axis_size("dp") == 4 and lax.axis_size("fsdp") == 8


def after(value, *others):
    return lax.optimization_barrier((value, *others))[0]


def gather_blocks(block):
    if not fast_mesh():
        whole = lax.all_gather(block, AXES, axis=0, tiled=True).reshape(32, ROW, ROW)
        return [whole[source_block((0, 0, 0, 0), piece)][piece[4] : piece[4] + piece[5]] for piece in PIECES]
    ring, across_x, across_y, across_core = pair_lists()

    def over_x(value):
        return lax.ppermute(value, "fsdp", across_x)

    def over_y(value):
        return lax.ppermute(value, "dp", across_y)

    def over_core(value, *others):
        return lax.ppermute(after(value, *others), "dp", across_core)

    own = [block]
    for _ in range(3):
        own.append(lax.ppermute(own[-1], "fsdp", ring))
    by_x = [over_x(each_one) for each_one in own]
    by_y = [over_y(each_one) for each_one in own]
    top = [over_x(each_one[:HALF]) for each_one in by_y]
    bottom = [over_y(each_one[HALF:]) for each_one in by_x]
    near = own + by_x + by_y + top + bottom
    later = [own[2], own[3], by_x[3], by_y[3]]
    far = [over_core(each_one) for each_one in own]
    far += [over_core(by_x[at], later[at]) for at in range(3)] + [over_core(by_x[3])]
    far += [over_core(by_y[at], later[at]) for at in range(3)] + [over_core(by_y[3])]
    ends = [own[3], by_x[2], by_x[3], top[3]]
    far += [over_core(top[at], ends[at]) for at in range(3)] + [over_core(top[3])]
    far += [over_core(bottom[at], ends[at]) for at in range(3)] + [over_core(bottom[3])]
    return near + far


def added(*parts):
    total = parts[0].astype(F32)
    for each_one in parts[1:]:
        total = total + each_one.astype(F32)
    return total


def placed_late(late, rows, me):
    block = jnp.concatenate(
        [
            jnp.zeros((rows, ROW), F32),
            late[0:8],
            jnp.zeros((REL_AT - 8, ROW), F32),
            late[8:10],
            jnp.zeros((ROW - REL_AT - 2 + rows, ROW), F32),
        ]
    )
    start = jnp.clip(me * rows - ROW * BLOCK["small"][0] + rows, 0, ROW + rows)
    return lax.dynamic_slice(block, (start, 0), (rows, ROW))


def scatter_blocks(state, back, coords, rows, me):
    late = back["late"]
    if not fast_mesh():
        late = lax.psum(late, AXES)
        blocks = []
        for half in ((back["low_kept"], back["low_sent"]), (state["high_kept"], state["high_sent"])):
            for core in half:
                blocks += [core[4 * x + (3 - z) % 4] for z in range(4) for x in range(2)]
        own = lax.psum_scatter(jnp.concatenate(blocks), AXES, scatter_dimension=0, tiled=True)
        return own.astype(F32) + placed_late(late, rows, me), late[0:8]
    ring, across_x, across_y, across_core = pair_lists()
    high = coords[0] == 1
    high_kept, low_kept = state["high_kept"], back["low_kept"]
    high_got = lax.ppermute(state["high_sent"], "dp", across_core)
    low_got = [lax.ppermute(back["low_sent"][4:], "dp", across_core)]
    low_got.insert(0, lax.ppermute(back["low_sent"][:4], "dp", across_core))

    def chip_sum(own_half, x, first, last):
        here = slice(4 * x + first, 4 * x + last)
        of_high = added(high_kept[here], high_got[here])
        of_low = added(low_kept[here], low_got[x][first:last])
        return low(jnp.where(high == own_half, of_high, of_low))

    def over_x(value):
        return lax.ppermute(value, "fsdp", across_x)

    def over_y(value):
        return lax.ppermute(value, "dp", across_y)

    from_y = over_y(chip_sum(False, 1, 0, 2))
    from_x = over_x(chip_sum(False, 1, 2, 4))
    to_y = chip_sum(False, 0, 0, 2)
    to_x_late = chip_sum(True, 1, 2, 4)
    sent_y = [over_y(to_y[0]), over_y(to_y[1])]
    to_x = low(added(chip_sum(True, 1, 0, 2), from_y))
    sent_x = [over_x(to_x[0]), over_x(to_x[1])]
    to_y_late = low(added(chip_sum(False, 0, 2, 4), from_x))
    sent_x += [over_x(to_x_late[0]), over_x(to_x_late[1])]
    sent_y += [over_y(to_y_late[0]), over_y(to_y_late[1])]
    mine = chip_sum(True, 0, 0, 4)
    late = late + lax.ppermute(late, "dp", across_core)
    late = late + over_x(late)
    late = late + over_y(late)
    running = low(added(mine[0], sent_x[0], sent_y[0]))
    running = low(added(mine[1], sent_x[1], sent_y[1], lax.ppermute(running, "fsdp", ring)))
    late = late + lax.ppermute(late, "fsdp", [(i, i ^ 2) for i in range(8)])
    running = low(added(mine[2], sent_x[2], sent_y[2], lax.ppermute(running, "fsdp", ring)))
    late = late + lax.ppermute(after(late, running), "fsdp", [(i, i ^ 4) for i in range(8)])
    total = added(mine[3], sent_x[3], sent_y[3], lax.ppermute(after(running, late), "fsdp", ring))
    return total + placed_late(late, rows, me), late[0:8]


def sum_everywhere(vector):
    if not fast_mesh():
        return lax.psum(vector, AXES)
    _, across_x, across_y, across_core = pair_lists()
    near_z = [(i, i ^ 2) for i in range(8)]
    far_z = [(i, i ^ 4) for i in range(8)]
    for axis, pairs in (
        ("dp", across_core),
        ("fsdp", across_x),
        ("dp", across_y),
        ("fsdp", near_z),
        ("fsdp", far_z),
    ):
        vector = vector + lax.ppermute(vector, axis, pairs)
    return vector


def most_segments(shard_size, devices):
    bounds = segment_bounds()
    most = 1
    for at in range(devices):
        low_end, high_end = at * shard_size, (at + 1) * shard_size
        most = max(most, sum(1 for b in bounds[1:-1] if low_end < b < high_end) + 1)
    return most


LANES = 128
CHUNK = 256


def entry_places(step):
    row = step * CHUNK + lax.broadcasted_iota(jnp.int32, (CHUNK, LANES), 0)
    return row * LANES + lax.broadcasted_iota(jnp.int32, (CHUNK, LANES), 1)


def update_kernel(segments, params, first, second, grad, new_first, new_second, update, sums):
    step = pl.program_id(0)
    spans = segments.shape[0] - 2

    @pl.when(step == 0)
    def _():
        sums[...] = jnp.zeros_like(sums)

    grads = grad[...]
    firsts = BETA_FIRST * first[...] + (1.0 - BETA_FIRST) * grads
    seconds = BETA_SECOND * second[...] + (1.0 - BETA_SECOND) * grads * grads
    new_first[...] = firsts
    new_second[...] = seconds
    first_hat = firsts * (1.0 / (1.0 - BETA_FIRST**STEP))
    second_hat = seconds * (1.0 / (1.0 - BETA_SECOND**STEP))
    values = params[...]
    change = first_hat / (jnp.sqrt(second_hat) + ADAM_EPS) + WEIGHT_DECAY * values
    update[...] = change
    places = entry_places(step)
    lane = lax.broadcasted_iota(jnp.int32, (1, LANES), 1)
    for at in range(spans):
        inside = (places >= segments[1 + at]) & (places < segments[2 + at])
        mine = lane == segments[0] + at
        for row, entries in enumerate((values, change)):
            squares = jnp.where(inside, entries * entries, 0.0)
            total = jnp.sum(jnp.sum(squares, axis=0, keepdims=True), axis=1, keepdims=True)
            sums[row : row + 1, :] += jnp.where(mine, total, 0.0)


def apply_kernel(segments, sums, params, update, new_params, norms):
    step = pl.program_id(0)
    spans = segments.shape[0] - 2
    roots = jnp.sqrt(sums[0:2, :])
    trust = roots[0:1, :] / (roots[1:2, :] + ADAM_EPS)
    norms[0:2, :] = roots
    norms[2:3, :] = trust
    places = entry_places(step)
    lane = lax.broadcasted_iota(jnp.int32, (1, LANES), 1)
    scale = jnp.zeros((CHUNK, LANES), F32)
    for at in range(spans):
        own = jnp.sum(jnp.where(lane == segments[0] + at, trust, 0.0), axis=1, keepdims=True)
        scale = jnp.where(places >= segments[1 + at], own, scale)
    new_params[...] = params[...] - LEARN_RATE * scale * update[...]


def shards(frames, lengths, cotangent, params, first_moment, second_moment):
    shard_size = params.shape[0]
    devices = lax.axis_size("dp") * lax.axis_size("fsdp")
    me = lax.axis_index(AXES)
    rows = block_rows(devices)
    if fast_mesh():
        dp, fsdp = lax.axis_index("dp"), lax.axis_index("fsdp")
        coords = jnp.stack([dp // 2, dp % 2, fsdp // 2, fsdp % 2]).astype(jnp.int32)
    else:
        coords = jnp.zeros((4,), jnp.int32)
    blocks = gather_blocks(align_shard(low(params), shard_size, rows))
    state = forward(coords, lengths, frames[0], cotangent[0], blocks)
    back = backward(coords, frames[0], state)
    block_sum, gain_grads = scatter_blocks(state, back, coords, rows, me)
    steps = -(-shard_size // (LANES * CHUNK))
    padded = steps * LANES * CHUNK
    grad_shard = unalign_block(low(block_sum), shard_size, padded).astype(F32)

    def square(flat):
        return jnp.pad(flat, (0, padded - flat.shape[0])).reshape(-1, LANES)

    bounds = segment_bounds()
    spans = most_segments(shard_size, devices)
    shard_low = me * shard_size
    first_segment = sum((shard_low >= b).astype(jnp.int32) for b in bounds[1:-1])
    table = jnp.asarray(bounds[1:] + [bounds[-1]] * spans, jnp.int32)
    ends = jnp.clip(lax.dynamic_slice(table, (first_segment,), (spans,)) - shard_low, 0, shard_size)
    segments = jnp.concatenate([first_segment[None], jnp.zeros((1,), jnp.int32), ends]).astype(jnp.int32)
    grid = pl.BlockSpec((CHUNK, LANES), lambda step: (step, 0))
    whole = pl.BlockSpec((8, LANES), lambda step: (0, 0))
    flat_kind = jax.ShapeDtypeStruct((padded // LANES, LANES), F32)
    tile_kind = jax.ShapeDtypeStruct((8, LANES), F32)
    params_square = square(params)
    new_first, new_second, update, sums = pl.pallas_call(
        update_kernel,
        name="update",
        grid=(steps,),
        in_specs=[SM] + [grid] * 4,
        out_specs=[grid] * 3 + [whole],
        out_shape=[flat_kind] * 3 + [tile_kind],
    )(segments, params_square, square(first_moment), square(second_moment), grad_shard.reshape(-1, LANES))
    sums = sum_everywhere(sums)
    new_params, norms = pl.pallas_call(
        apply_kernel,
        name="apply",
        grid=(steps,),
        in_specs=[SM, whole, grid, grid],
        out_specs=[grid, whole],
        out_shape=[flat_kind, tile_kind],
    )(segments, sums, params_square, update)
    count = len(segment_shapes())
    return (
        state["out"].reshape(frames.shape),
        back["fgrad"].reshape(frames.shape),
        new_params.reshape(-1)[:shard_size],
        new_first.reshape(-1)[:shard_size],
        new_second.reshape(-1)[:shard_size],
        norms[0, :count],
        norms[1, :count],
        norms[2, :count],
        gain_grads.reshape(-1),
    )


def solution(mesh):
    placed = (
        P(("dp", "fsdp"), None, None),
        P(("dp", "fsdp")),
        P(("dp", "fsdp"), None, None),
        P(("dp", "fsdp")),
        P(("dp", "fsdp")),
        P(("dp", "fsdp")),
    )
    return jax.shard_map(
        shards,
        mesh=mesh,
        in_specs=placed,
        out_specs=(
            P(("dp", "fsdp"), None, None),
            P(("dp", "fsdp"), None, None),
            P(("dp", "fsdp")),
            P(("dp", "fsdp")),
            P(("dp", "fsdp")),
            P(),
            P(),
            P(),
            P(),
        ),
        check_vma=False,
    )
```

time: 394 us -> 369 us (0.937)
  Pallas kernels: 135 us -> 95.9 us
  waiting for transfers between devices: 165 us -> 148 us
  starting transfers between devices: 50 us -> 66.5 us
  local copies, waits for them, and re-layouts: 22.1 us -> 32.1 us
  other arithmetic: 18.1 us -> 22.7 us
    pallas_call x7 -> x2, Pallas kernels: 122 us -> 82.5 us  [call(): pl.pallas_call(kernel, name=name, in_specs=[space for space, _ in ins], o...]
    ppermute x53 -> x57, waiting for transfers between devices: 128 us -> 108 us  [the longest x14 74.9 us: over_x(): return lax.ppermute(value, 'fsdp', across_x)]
    ppermute x53 -> x57, starting transfers between devices: 37 us -> 46.3 us  [the longest x14 19.7 us: over_x(): return lax.ppermute(value, 'fsdp', across_x)]
    concatenate x0 -> x1, local copies, waits for them, and re-layouts: none -> 9.19 us  [placed_late(): jnp.concatenate([jnp.zeros((rows, ROW), F32), late[0:8], jnp.zeros((REL_A...]
    ppermute x3, waiting for transfers between devices: 9.18 us -> 15.8 us  [gather_blocks(): own.append(lax.ppermute(own[-1], 'fsdp', ring))]
    ppermute x10 -> x5, waiting for transfers between devices: 16.3 us -> 10.4 us  [sum_everywhere(): vector = vector + lax.ppermute(vector, axis, pairs)]
    ppermute x1, starting transfers between devices: 2.94 us -> 8.2 us  [unalign_block(): pieces.insert(0, lax.ppermute(flat[block - part:], AXES, pairs))]
    convert_element_type x7, other arithmetic: 9.26 us -> 13.2 us  [low(): return values.astype(BF16)]
  transfers between devices with their start and end apart: 68 -> 67, of which waited for: 32 -> 33; matrix products, arithmetic and copies ran while one was open for 5% -> 9% of each run, Pallas kernels for 2% -> 6%
where the time goes in v3:
time: 369 us; the launch traced here: 368 us
  waiting for transfers between devices  148 us (40%)
  Pallas kernels  95.9 us (26%)
  starting transfers between devices  66.5 us (18%)
  local copies, waits for them, and re-layouts  32.1 us (9%)
  other arithmetic  22.7 us (6%)
    pallas_call x2, Pallas kernels, call(): pl.pallas_call(kernel, name=name, in_specs=[space for space, _ in ins], o...  82.5 us
    ppermute x14, waiting for transfers between devices, over_x(): return lax.ppermute(value, 'fsdp', across_x)  74.9 us
    ppermute x14, starting transfers between devices, over_x(): return lax.ppermute(value, 'fsdp', across_x)  19.7 us
    ppermute x14, starting transfers between devices, over_y(): return lax.ppermute(value, 'dp', across_y)  19.5 us
    ppermute x14, waiting for transfers between devices, over_y(): return lax.ppermute(value, 'dp', across_y)  18.1 us
    ppermute x3, waiting for transfers between devices, gather_blocks(): own.append(lax.ppermute(own[-1], 'fsdp', ring))  15.8 us
    convert_element_type x7, other arithmetic, low(): return values.astype(BF16)  13.2 us
    ppermute x1, waiting for transfers between devices, align_shard(): pieces.append(lax.ppermute(low_shard[:part], AXES, pairs))  11.9 us
  transfers between devices with their start and end apart: 67, of which 33 were waited for; matrix products, arithmetic and copies ran while one was open for 9% of the time, Pallas kernels for 6%

profile of v3, /device:TPU:0, one launch (start us, length us, event | category | flops | bytes accessed | tf_op | source)
XLA Modules:
  0.0 367.5 jit_solution(12970686374746040913)
XLA Ops:
  0.6 1.3 convert_element_type.217
  1.9 1.3 collective-permute-start
  3.3 11.9 %collective-permute-done = bf16[177664]{0:T(1024)(128)(2,1)S(1)} collective-permute-done((bf16[177664]{0:T(1024)(128)(2,1)S(1)}, bf16[177664]{0:T(1024)(128)(2,1)S(1)}, u32[]{:S(2)}, u32[]{:S(2)}) %collective-permute-start) | collective-permute-done | bytes 355360 | tf_op jit(solution)/shard_map/ppermute | solution.py:970
  15.1 1.9 fusion.15
  17.4 1.9 collective-permute-start.1
  19.2 2.5 collective-permute-start.8
  21.8 1.4 collective-permute-start.4
  23.1 9.2 %collective-permute-done.1.refs_5_ = bf16[512,512]{1,0:T(8,128)(2,1)S(1)} collective-permute-done((bf16[512,512]{1,0:T(8,128)(2,1)S(1)}, bf16[512,512]{1,0:T(8,128)(2,1)S(1)}, u32[]{:S(2)}, u32[]{:S(2)}) %collective-permute-start.1) | collective-permute-done | bytes 524320 | tf_op jit(solution)/shard_map/ppermute | solution.py:1031
  32.3 5.2 %collective-permute-start.9 = (bf16[512,512]{1,0:T(8,128)(2,1)S(1)}, bf16[512,512]{1,0:T(8,128)(2,1)S(1)}, u32[]{:S(2)}, u32[]{:S(2)}) collective-permute-start(bf16[512,512]{1,0:T(8,128)(2,1)S(1)} %collective-permute-done.1.refs_5_), channel_id=1, source_target_pairs={{0,16},{8,24},{16,0},{24,8},{1,17},{9,25},{17,1},{25,9},{2,18},{10... | collective-permute-start | bytes 1572872 | tf_op jit(solution)/shard_map/ppermute | solution.py:1024
  37.7 2.0 collective-permute-start.12
  39.7 6.6 %collective-permute-done.2.refs_6_ = bf16[512,512]{1,0:T(8,128)(2,1)S(1)} collective-permute-done((bf16[512,512]{1,0:T(8,128)(2,1)S(1)}, bf16[512,512]{1,0:T(8,128)(2,1)S(1)}, u32[]{:S(2)}, u32[]{:S(2)}) %collective-permute-start.2) | collective-permute-done | bytes 524320 | tf_op jit(solution)/shard_map/ppermute | solution.py:1031
  46.3 3.7 %collective-permute-start.6 = (bf16[512,512]{1,0:T(8,128)(2,1)S(1)}, bf16[512,512]{1,0:T(8,128)(2,1)S(1)}, u32[]{:S(2)}, u32[]{:S(2)}) collective-permute-start(bf16[512,512]{1,0:T(8,128)(2,1)S(1)} %collective-permute-done.2.refs_6_), channel_id=1, source_target_pairs={{0,1},{1,0},{2,3},{3,2},{4,5},{5,4},{6,7},{7,6},{8,9},{9,8},{10,11... | collective-permute-start | bytes 1572872 | tf_op jit(solution)/shard_map/ppermute | solution.py:1021
  50.0 2.6 collective-permute-start.16
  52.7 2.1 collective-permute-start.13
  54.8 3.2 collective-permute-done.12.refs_16_
  58.1 1.7 collective-permute-done.16.refs_20_
  59.8 1.2 collective-permute-start.10
  61.0 12.0 %collective-permute-done.13.refs_17_ = bf16[256,512]{1,0:T(8,128)(2,1)S(1)} collective-permute-done((bf16[256,512]{1,0:T(8,128)(2,1)S(1)}, bf16[256,512]{1,0:T(8,128)(2,1)S(1)}, u32[]{:S(2)}, u32[]{:S(2)}) %collective-permute-start.13) | collective-permute-done | bytes 262176 | tf_op jit(solution)/shard_map/ppermute | solution.py:1021
  73.6 2.3 collective-permute-done.10.refs_14_
  77.3 1.8 collective-permute-start.14
  79.4 1.7 collective-permute-start.11
  81.1 1.2 collective-permute-done.18.refs_22_
  82.3 4.3 %collective-permute-done.14.refs_18_ = bf16[256,512]{1,0:T(8,128)(2,1)S(1)} collective-permute-done((bf16[256,512]{1,0:T(8,128)(2,1)S(1)}, bf16[256,512]{1,0:T(8,128)(2,1)S(1)}, u32[]{:S(2)}, u32[]{:S(2)}) %collective-permute-start.14) | collective-permute-done | bytes 262176 | tf_op jit(solution)/shard_map/ppermute | solution.py:1021
  88.8 7.0 %collective-permute-done.7.refs_11_ = bf16[512,512]{1,0:T(8,128)(2,1)} collective-permute-done((bf16[512,512]{1,0:T(8,128)(2,1)S(1)}, bf16[512,512]{1,0:T(8,128)(2,1)}, u32[]{:S(2)}, u32[]{:S(2)}) %collective-permute-start.7) | collective-permute-done | bytes 524320 | tf_op jit(solution)/shard_map/ppermute | solution.py:1021
  99.1 6.5 %collective-permute-done.19.refs_23_ = bf16[256,512]{1,0:T(8,128)(2,1)S(1)} collective-permute-done((bf16[256,512]{1,0:T(8,128)(2,1)S(1)}, bf16[256,512]{1,0:T(8,128)(2,1)S(1)}, u32[]{:S(2)}, u32[]{:S(2)}) %collective-permute-start.19) | collective-permute-done | bytes 262176 | tf_op jit(solution)/shard_map/ppermute | solution.py:1024
  105.6 1.7 collective-permute-start.15
  108.7 5.0 %collective-permute-done.15.refs_19_ = bf16[256,512]{1,0:T(8,128)(2,1)} collective-permute-done((bf16[256,512]{1,0:T(8,128)(2,1)S(1)}, bf16[256,512]{1,0:T(8,128)(2,1)}, u32[]{:S(2)}, u32[]{:S(2)}) %collective-permute-start.15) | collective-permute-done | bytes 262176 | tf_op jit(solution)/shard_map/ppermute | solution.py:1021
  117.6 61.8 %forward.1 = (bf16[160,512]{1,0:T(8,128)(2,1)}, f32[8,512]{1,0:T(8,128)}, f32[176,512]{1,0:T(8,128)}, bf16[8,512,512]{2,1,0:T(8,128)(2,1)}, bf16[8,512,512]{2,1,...) custom-call(s32[4]{0:T(128)} %pad_add_fusion.refs_0_, ...), custom_call_target="tpu_custom_call" | custom-call | tf_op jit(solution)/shard_map/forward/pallas_call | solution.py:895
  179.5 20.7 %backward.1 = (bf16[160,512]{1,0:T(8,128)(2,1)}, f32[16,512]{1,0:T(8,128)}, bf16[8,512,512]{2,1,0:T(8,128)(2,1)}, bf16[8,512,512]{2,1,0:T(8,128)(2,1)}) custom-call(s32[4]{0:T(128)} %pad_add_fusion.refs_0_, bf16[160,512]{1,0:T(8,128)(2,1)} %bitcast.77, f32[8,512]{1,0:T(8,128)} %get-tuple-element.67.refs_2_, ...), custom_call_target="tpu_custom_call", output_to_operand_aliasing={{2}: (18, {}), {3}: (19, {})} | custom-call | tf_op jit(solution)/shard_map/backward/pallas_call | solution.py:895
  200.2 4.5 %fusion.17 = (bf16[4,512,512]{2,1,0:T(8,128)(2,1)}, bf16[4,512,512]{2,1,0:T(8,128)(2,1)}) fusion(bf16[8,512,512]{2,1,0:T(8,128)(2,1)} %get-tuple-element.89), kind=kLoop, calls=%fused_computation.60 | loop fusion | bytes 8388608 | tf_op jit(solution)/shard_map/slice | solution.py:1082
  205.2 6.8 %collective-permute-done.42 = bf16[4,512,512]{2,1,0:T(8,128)(2,1)} collective-permute-done((bf16[4,512,512]{2,1,0:T(8,128)(2,1)}, bf16[4,512,512]{2,1,0:T(8,128)(2,1)}, u32[]{:S(2)}, u32[]{:S(2)}) %collective-permute-start.42) | collective-permute-done | bytes 2097184 | tf_op jit(solution)/shard_map/ppermute | solution.py:1082
  212.0 4.2 %select_convert_fusion.6 = (bf16[2,512,512]{2,1,0:T(8,128)(2,1)S(1)}, bf16[2,512,512]{2,1,0:T(8,128)(2,1)S(1)}, bf16[2,512,512]{2,1,0:T(8,128)(2,1)S(1)}) fusion(pred[]{:T(512)S(6)} %eq.12, bf16[4,512,512]{2,1,0:T(8,128)(2,1)} %collective-permute-done.42, bf16[8,512,512]{2,1,0:T(8,128)(2,1)} %collective-permute-done.40, ...), kind=kLoop, calls=%fused_computation.10 | loop fusion | flops 9437184 | bytes 11534338 | tf_op jit(solution)/shard_map/convert_element_type | solution.py:85
  216.2 1.3 collective-permute-start.44
  218.3 23.4 %collective-permute-done.44 = bf16[2,512,512]{2,1,0:T(8,128)(2,1)S(1)} collective-permute-done((bf16[2,512,512]{2,1,0:T(8,128)(2,1)S(1)}, bf16[2,512,512]{2,1,0:T(8,128)(2,1)S(1)}, u32[]{:S(2)}, u32[]{:S(2)}) %collective-permute-start.44) | collective-permute-done | bytes 1048608 | tf_op jit(solution)/shard_map/ppermute | solution.py:1092
  242.7 3.5 add_convert_fusion.1
  247.7 2.8 select_convert_fusion
  250.4 1.5 collective-permute-start.49
  251.9 1.5 collective-permute-start.50
  253.4 7.8 %collective-permute-done.51 = bf16[512,512]{1,0:T(8,128)(2,1)S(1)} collective-permute-done((bf16[512,512]{1,0:T(8,128)(2,1)S(1)}, bf16[512,512]{1,0:T(8,128)(2,1)S(1)}, u32[]{:S(2)}, u32[]{:S(2)}) %collective-permute-start.51) | collective-permute-done | bytes 524320 | tf_op jit(solution)/shard_map/ppermute | solution.py:1092
  263.2 1.3 collective-permute-start.46
  265.9 6.5 %collective-permute-done.49 = bf16[512,512]{1,0:T(8,128)(2,1)S(1)} collective-permute-done((bf16[512,512]{1,0:T(8,128)(2,1)S(1)}, bf16[512,512]{1,0:T(8,128)(2,1)S(1)}, u32[]{:S(2)}, u32[]{:S(2)}) %collective-permute-start.49) | collective-permute-done | bytes 524320 | tf_op jit(solution)/shard_map/ppermute | solution.py:1092
  274.4 1.2 collective-permute-done.55
  275.6 1.3 collective-permute-start.56
  276.9 5.7 %collective-permute-done.56 = f32[16,512]{1,0:T(8,128)S(1)} collective-permute-done((f32[16,512]{1,0:T(8,128)S(1)}, f32[16,512]{1,0:T(8,128)S(1)}, u32[]{:S(2)}, u32[]{:S(2)}) %collective-permute-start.56) | collective-permute-done | bytes 32800 | tf_op jit(solution)/shard_map/ppermute | solution.py:1092
  282.9 3.6 collective-permute-done.57
  286.5 3.9 %collective-permute-done.58 = f32[16,512]{1,0:T(8,128)S(1)} collective-permute-done((f32[16,512]{1,0:T(8,128)S(1)}, f32[16,512]{1,0:T(8,128)S(1)}, u32[]{:S(2)}, u32[]{:S(2)}) %collective-permute-start.58) | collective-permute-done | bytes 32800 | tf_op jit(solution)/shard_map/ppermute | solution.py:1113
  291.5 1.9 collective-permute-start.59
  294.0 1.5 collective-permute-start.45
  298.6 9.2 %concatenate.14 = f32[1536,512]{1,0:T(8,128)} concatenate(f32[512,512]{1,0:T(8,128)S(1)} %broadcast_in_dim.13, f32[8,512]{1,0:T(8,128)S(1)} %get-tuple-element.116, f32[155,512]{1,0:T(8,128)S(1)} %broadcast_in_dim.14, f32[2,512]{1,0:T(2,128)S(1)} %slice.244, f32[859,512]{1,0:T(8,128)S(1)} %broadcast_in_dim.15), dimensions={0} | concatenate | bytes 6291456 | tf_op jit(solution)/shard_map/concatenate | solution.py:1055
  307.8 2.4 fusion.16
  310.6 8.2 %collective-permute-start.61 = (bf16[172112]{0:T(1024)(128)(2,1)S(1)}, bf16[172112]{0:T(1024)(128)(2,1)S(1)}, u32[]{:S(2)}, u32[]{:S(2)}) collective-permute-start(bf16[172112]{0:T(1024)(128)(2,1)S(1)} %slice.245), channel_id=1, source_target_pairs={{0,1},{1,2},{2,3},{3,4},{4,5},{5,6},{6,7},{7,8},{8,9},{9,10},{10,1... | collective-permute-start | bytes 1032680 | tf_op jit(solution)/shard_map/ppermute | solution.py:990
  319.4 1.5 pad_bitcast_fusion
  320.9 2.7 collective-permute-done.61
  323.6 2.5 fusion.14.grad
  326.1 7.4 %update.1 = (f32[2048,128]{1,0:T(8,128)}, f32[2048,128]{1,0:T(8,128)}, f32[2048,128]{1,0:T(8,128)}, f32[8,128]{1,0:T(8,128)}) custom-call(s32[6]{0:T(128)} %pad_add_fusion.1.segments, f32[2048,128]{1,0:T(8,128)} %pad_bitcast_fusion.2.params, f32[2048,128]{1,0:T(8,128)} %get-tuple-element.121.first, f32[2048,128]{1,0:T(8,128)} %get-tuple-element.120.second, ...), custom_call_target="tpu_custom_call" | custom-call | tf_op jit(solution)/shard_map/update/pallas_call | solution.py:1233
  333.5 6.4 %collective-permute-start.62 = (f32[8,128]{1,0:T(8,128)}, f32[8,128]{1,0:T(8,128)S(1)}, u32[]{:S(2)}, u32[]{:S(2)}) collective-permute-start(f32[8,128]{1,0:T(8,128)} %get-tuple-element.93), channel_id=1, source_target_pairs={{0,8},{8,0},{16,24},{24,16},{1,9},{9,1},{17,25},{25,17},{2,10},{10... | collective-permute-start | bytes 12296 | tf_op jit(solution)/shard_map/ppermute | solution.py:1133
  341.7 3.6 collective-permute-done.63
  345.3 2.4 collective-permute-start.64
  347.7 1.6 collective-permute-done.64
  349.3 3.6 collective-permute-done.65
  353.5 2.2 slice.247
  358.0 6.0 %apply.1 = (f32[2048,128]{1,0:T(8,128)}, f32[8,128]{1,0:T(8,128)}) custom-call(s32[6]{0:T(128)} %pad_add_fusion.1.segments, f32[8,128]{1,0:T(8,128)} %add.223.sums, f32[2048,128]{1,0:T(8,128)} %pad_bitcast_fusion.2.params, f32[2048,128]{1,0:T(8,128)} %get-tuple-element.94.update), custom_call_target="tpu_custom_call" | custom-call | tf_op jit(solution)/shard_map/apply/pallas_call | solution.py:1242
  364.0 2.2 slice.246
  366.2 1.3 slice_bitcast_fusion.12
  (205 shorter events, 32.6 us)
Async XLA Ops:
  1.9 13.2 %collective-permute-start = (bf16[177664]{0:T(1024)(128)(2,1)S(1)}, bf16[177664]{0:T(1024)(128)(2,1)S(1)}, u32[]{:S(2)}, u32[]{:S(2)}) collective-permute-start(bf16[177664]{0:T(1024)(128)(2,1)S(1)} %slice.213), channel_id=1, source_target_pairs={{1,0},{2,1},{3,2},{4,3},{5,4},{6,5},{7,6},{8,7},{9,8},{10,9},{11,1... | collective-permute-start | bytes 1065992 | tf_op jit(solution)/shard_map/ppermute | solution.py:970
  17.4 15.0 %collective-permute-start.1 = (bf16[512,512]{1,0:T(8,128)(2,1)S(1)}, bf16[512,512]{1,0:T(8,128)(2,1)S(1)}, u32[]{:S(2)}, u32[]{:S(2)}) collective-permute-start(bf16[512,512]{1,0:T(8,128)(2,1)S(1)} %reshape.64.refs_4_), channel_id=1, source_target_pairs={{0,2},{1,3},{2,4},{3,5},{4,6},{5,7},{6,0},{7,1},{8,10},{9,11},{10,... | collective-permute-start | bytes 1572872 | tf_op jit(solution)/shard_map/ppermute | solution.py:1031
  19.2 18.3 %collective-permute-start.8 = (bf16[512,512]{1,0:T(8,128)(2,1)S(1)}, bf16[512,512]{1,0:T(8,128)(2,1)S(1)}, u32[]{:S(2)}, u32[]{:S(2)}) collective-permute-start(bf16[512,512]{1,0:T(8,128)(2,1)S(1)} %reshape.64.refs_4_), channel_id=1, source_target_pairs={{0,16},{8,24},{16,0},{24,8},{1,17},{9,25},{17,1},{25,9},{2,18},{10... | collective-permute-start | bytes 1572872 | tf_op jit(solution)/shard_map/ppermute | solution.py:1024
  21.8 15.8 %collective-permute-start.4 = (bf16[512,512]{1,0:T(8,128)(2,1)S(1)}, bf16[512,512]{1,0:T(8,128)(2,1)S(1)}, u32[]{:S(2)}, u32[]{:S(2)}) collective-permute-start(bf16[512,512]{1,0:T(8,128)(2,1)S(1)} %reshape.64.refs_4_), channel_id=1, source_target_pairs={{0,1},{1,0},{2,3},{3,2},{4,5},{5,4},{6,7},{7,6},{8,9},{9,8},{10,11... | collective-permute-start | bytes 1572872 | tf_op jit(solution)/shard_map/ppermute | solution.py:1021
  23.1 14.5 %collective-permute-start.20 = (bf16[512,512]{1,0:T(8,128)(2,1)S(1)}, bf16[512,512]{1,0:T(8,128)(2,1)S(1)}, u32[]{:S(2)}, u32[]{:S(2)}) collective-permute-start(bf16[512,512]{1,0:T(8,128)(2,1)S(1)} %reshape.64.refs_4_), channel_id=1, source_target_pairs={{0,8},{8,0},{16,24},{24,16},{1,9},{9,1},{17,25},{25,17},{2,10},{10... | collective-permute-start | bytes 1572872 | tf_op jit(solution)/shard_map/ppermute | solution.py:1027
  32.3 14.0 %collective-permute-start.2 = (bf16[512,512]{1,0:T(8,128)(2,1)S(1)}, bf16[512,512]{1,0:T(8,128)(2,1)S(1)}, u32[]{:S(2)}, u32[]{:S(2)}) collective-permute-start(bf16[512,512]{1,0:T(8,128)(2,1)S(1)} %collective-permute-done.1.refs_5_), channel_id=1, source_target_pairs={{0,2},{1,3},{2,4},{3,5},{4,6},{5,7},{6,0},{7,1},{8,10},{9,11},{10,... | collective-permute-start | bytes 1572872 | tf_op jit(solution)/shard_map/ppermute | solution.py:1031
  32.3 17.7 %collective-permute-start.9 = (bf16[512,512]{1,0:T(8,128)(2,1)S(1)}, bf16[512,512]{1,0:T(8,128)(2,1)S(1)}, u32[]{:S(2)}, u32[]{:S(2)}) collective-permute-start(bf16[512,512]{1,0:T(8,128)(2,1)S(1)} %collective-permute-done.1.refs_5_), channel_id=1, source_target_pairs={{0,16},{8,24},{16,0},{24,8},{1,17},{9,25},{17,1},{25,9},{2,18},{10... | collective-permute-start | bytes 1572872 | tf_op jit(solution)/shard_map/ppermute | solution.py:1024
  37.5 15.1 %collective-permute-start.5 = (bf16[512,512]{1,0:T(8,128)(2,1)S(1)}, bf16[512,512]{1,0:T(8,128)(2,1)S(1)}, u32[]{:S(2)}, u32[]{:S(2)}) collective-permute-start(bf16[512,512]{1,0:T(8,128)(2,1)S(1)} %collective-permute-done.1.refs_5_), channel_id=1, source_target_pairs={{0,1},{1,0},{2,3},{3,2},{4,5},{5,4},{6,7},{7,6},{8,9},{9,8},{10,11... | collective-permute-start | bytes 1572872 | tf_op jit(solution)/shard_map/ppermute | solution.py:1021
  37.6 23.4 %collective-permute-start.21 = (bf16[512,512]{1,0:T(8,128)(2,1)S(1)}, bf16[512,512]{1,0:T(8,128)(2,1)S(1)}, u32[]{:S(2)}, u32[]{:S(2)}) collective-permute-start(bf16[512,512]{1,0:T(8,128)(2,1)S(1)} %collective-permute-done.1.refs_5_), channel_id=1, source_target_pairs={{0,8},{8,0},{16,24},{24,16},{1,9},{9,1},{17,25},{25,17},{2,10},{10... | collective-permute-start | bytes 1572872 | tf_op jit(solution)/shard_map/ppermute | solution.py:1027
  37.7 20.3 %collective-permute-start.12 = (bf16[256,512]{1,0:T(8,128)(2,1)S(1)}, bf16[256,512]{1,0:T(8,128)(2,1)S(1)}, u32[]{:S(2)}, u32[]{:S(2)}) collective-permute-start(bf16[256,512]{1,0:T(8,128)(2,1)S(1)} %slice.214), channel_id=1, source_target_pairs={{0,1},{1,0},{2,3},{3,2},{4,5},{5,4},{6,7},{7,6},{8,9},{9,8},{10,11... | collective-permute-start | bytes 786440 | tf_op jit(solution)/shard_map/ppermute | solution.py:1021
  46.3 27.2 %collective-permute-start.6 = (bf16[512,512]{1,0:T(8,128)(2,1)S(1)}, bf16[512,512]{1,0:T(8,128)(2,1)S(1)}, u32[]{:S(2)}, u32[]{:S(2)}) collective-permute-start(bf16[512,512]{1,0:T(8,128)(2,1)S(1)} %collective-permute-done.2.refs_6_), channel_id=1, source_target_pairs={{0,1},{1,0},{2,3},{3,2},{4,5},{5,4},{6,7},{7,6},{8,9},{9,8},{10,11... | collective-permute-start | bytes 1572872 | tf_op jit(solution)/shard_map/ppermute | solution.py:1021
  50.0 9.8 %collective-permute-start.16 = (bf16[256,512]{1,0:T(8,128)(2,1)S(1)}, bf16[256,512]{1,0:T(8,128)(2,1)S(1)}, u32[]{:S(2)}, u32[]{:S(2)}) collective-permute-start(bf16[256,512]{1,0:T(8,128)(2,1)S(1)} %slice.218), channel_id=1, source_target_pairs={{0,16},{8,24},{16,0},{24,8},{1,17},{9,25},{17,1},{25,9},{2,18},{10... | collective-permute-start | bytes 786440 | tf_op jit(solution)/shard_map/ppermute | solution.py:1024
  52.7 20.2 %collective-permute-start.13 = (bf16[256,512]{1,0:T(8,128)(2,1)S(1)}, bf16[256,512]{1,0:T(8,128)(2,1)S(1)}, u32[]{:S(2)}, u32[]{:S(2)}) collective-permute-start(bf16[256,512]{1,0:T(8,128)(2,1)S(1)} %slice.215), channel_id=1, source_target_pairs={{0,1},{1,0},{2,3},{3,2},{4,5},{5,4},{6,7},{7,6},{8,9},{9,8},{10,11... | collective-permute-start | bytes 786440 | tf_op jit(solution)/shard_map/ppermute | solution.py:1021
  58.0 14.9 %collective-permute-start.17 = (bf16[256,512]{1,0:T(8,128)(2,1)S(1)}, bf16[256,512]{1,0:T(8,128)(2,1)S(1)}, u32[]{:S(2)}, u32[]{:S(2)}) collective-permute-start(bf16[256,512]{1,0:T(8,128)(2,1)S(1)} %slice.219), channel_id=1, source_target_pairs={{0,16},{8,24},{16,0},{24,8},{1,17},{9,25},{17,1},{25,9},{2,18},{10... | collective-permute-start | bytes 786440 | tf_op jit(solution)/shard_map/ppermute | solution.py:1024
  59.8 16.1 %collective-permute-start.10 = (bf16[512,512]{1,0:T(8,128)(2,1)S(1)}, bf16[512,512]{1,0:T(8,128)(2,1)}, u32[]{:S(2)}, u32[]{:S(2)}) collective-permute-start(bf16[512,512]{1,0:T(8,128)(2,1)S(1)} %collective-permute-done.2.refs_6_), channel_id=1, source_target_pairs={{0,16},{8,24},{16,0},{24,8},{1,17},{9,25},{17,1},{25,9},{2,18},{10... | collective-permute-start | bytes 1572872 | tf_op jit(solution)/shard_map/ppermute | solution.py:1024
  60.9 16.3 %collective-permute-start.3 = (bf16[512,512]{1,0:T(8,128)(2,1)S(1)}, bf16[512,512]{1,0:T(8,128)(2,1)S(1)}, u32[]{:S(2)}, u32[]{:S(2)}) collective-permute-start(bf16[512,512]{1,0:T(8,128)(2,1)S(1)} %collective-permute-done.2.refs_6_), channel_id=1, source_target_pairs={{0,2},{1,3},{2,4},{3,5},{4,6},{5,7},{6,0},{7,1},{8,10},{9,11},{10,... | collective-permute-start | bytes 1572872 | tf_op jit(solution)/shard_map/ppermute | solution.py:1031
  72.9 6.1 %collective-permute-start.24 = (bf16[512,512]{1,0:T(8,128)(2,1)S(1)}, bf16[512,512]{1,0:T(8,128)(2,1)S(1)}, u32[]{:S(2)}, u32[]{:S(2)}) collective-permute-start(bf16[512,512]{1,0:T(8,128)(2,1)S(1)} %collective-permute-done.4.refs_8_), channel_id=1, source_target_pairs={{0,8},{8,0},{16,24},{24,16},{1,9},{9,1},{17,25},{25,17},{2,10},{10... | collective-permute-start | bytes 1572872 | tf_op jit(solution)/shard_map/ppermute | solution.py:1027
  73.0 6.4 %collective-permute-start.28 = (bf16[512,512]{1,0:T(8,128)(2,1)S(1)}, bf16[512,512]{1,0:T(8,128)(2,1)S(1)}, u32[]{:S(2)}, u32[]{:S(2)}) collective-permute-start(bf16[512,512]{1,0:T(8,128)(2,1)S(1)} %collective-permute-done.8.refs_12_), channel_id=1, source_target_pairs={{0,8},{8,0},{16,24},{24,16},{1,9},{9,1},{17,25},{25,17},{2,10},{10... | collective-permute-start | bytes 1572872 | tf_op jit(solution)/shard_map/ppermute | solution.py:1027
  73.5 5.9 %collective-permute-start.22 = (bf16[512,512]{1,0:T(8,128)(2,1)S(1)}, bf16[512,512]{1,0:T(8,128)(2,1)S(1)}, u32[]{:S(2)}, u32[]{:S(2)}) collective-permute-start(bf16[512,512]{1,0:T(8,128)(2,1)S(1)} %collective-permute-done.2.refs_6_), channel_id=1, source_target_pairs={{0,8},{8,0},{16,24},{24,16},{1,9},{9,1},{17,25},{25,17},{2,10},{10... | collective-permute-start | bytes 1572872 | tf_op jit(solution)/shard_map/ppermute | solution.py:1027
  75.9 6.4 %collective-permute-start.18 = (bf16[256,512]{1,0:T(8,128)(2,1)S(1)}, bf16[256,512]{1,0:T(8,128)(2,1)S(1)}, u32[]{:S(2)}, u32[]{:S(2)}) collective-permute-start(bf16[256,512]{1,0:T(8,128)(2,1)S(1)} %slice.220), channel_id=1, source_target_pairs={{0,16},{8,24},{16,0},{24,8},{1,17},{9,25},{17,1},{25,9},{2,18},{10... | collective-permute-start | bytes 786440 | tf_op jit(solution)/shard_map/ppermute | solution.py:1024
  77.3 9.3 %collective-permute-start.14 = (bf16[256,512]{1,0:T(8,128)(2,1)S(1)}, bf16[256,512]{1,0:T(8,128)(2,1)S(1)}, u32[]{:S(2)}, u32[]{:S(2)}) collective-permute-start(bf16[256,512]{1,0:T(8,128)(2,1)S(1)} %slice.216), channel_id=1, source_target_pairs={{0,1},{1,0},{2,3},{3,2},{4,5},{5,4},{6,7},{7,6},{8,9},{9,8},{10,11... | collective-permute-start | bytes 786440 | tf_op jit(solution)/shard_map/ppermute | solution.py:1021
  79.1 16.7 %collective-permute-start.7 = (bf16[512,512]{1,0:T(8,128)(2,1)S(1)}, bf16[512,512]{1,0:T(8,128)(2,1)}, u32[]{:S(2)}, u32[]{:S(2)}) collective-permute-start(bf16[512,512]{1,0:T(8,128)(2,1)S(1)} %collective-permute-done.3.refs_7_), channel_id=1, source_target_pairs={{0,1},{1,0},{2,3},{3,2},{4,5},{5,4},{6,7},{7,6},{8,9},{9,8},{10,11... | collective-permute-start | bytes 1572872 | tf_op jit(solution)/shard_map/ppermute | solution.py:1021
  79.4 7.2 %collective-permute-start.33 = (bf16[256,512]{1,0:T(8,128)(2,1)S(1)}, bf16[256,512]{1,0:T(8,128)(2,1)}, u32[]{:S(2)}, u32[]{:S(2)}) collective-permute-start(bf16[256,512]{1,0:T(8,128)(2,1)S(1)} %collective-permute-done.13.refs_17_), channel_id=1, source_target_pairs={{0,8},{8,0},{16,24},{24,16},{1,9},{9,1},{17,25},{25,17},{2,10},{10... | collective-permute-start | bytes 786440 | tf_op jit(solution)/shard_map/ppermute | solution.py:1027
  79.4 17.4 %collective-permute-start.11 = (bf16[512,512]{1,0:T(8,128)(2,1)S(1)}, bf16[512,512]{1,0:T(8,128)(2,1)}, u32[]{:S(2)}, u32[]{:S(2)}) collective-permute-start(bf16[512,512]{1,0:T(8,128)(2,1)S(1)} %collective-permute-done.3.refs_7_), channel_id=1, source_target_pairs={{0,16},{8,24},{16,0},{24,8},{1,17},{9,25},{17,1},{25,9},{2,18},{10... | collective-permute-start | bytes 1572872 | tf_op jit(solution)/shard_map/ppermute | solution.py:1024
  82.3 4.8 %collective-permute-start.37 = (bf16[256,512]{1,0:T(8,128)(2,1)S(1)}, bf16[256,512]{1,0:T(8,128)(2,1)}, u32[]{:S(2)}, u32[]{:S(2)}) collective-permute-start(bf16[256,512]{1,0:T(8,128)(2,1)S(1)} %collective-permute-done.17.refs_21_), channel_id=1, source_target_pairs={{0,8},{8,0},{16,24},{24,16},{1,9},{9,1},{17,25},{25,17},{2,10},{10... | collective-permute-start | bytes 786440 | tf_op jit(solution)/shard_map/ppermute | solution.py:1027
  86.6 12.2 %collective-permute-start.25 = (bf16[512,512]{1,0:T(8,128)(2,1)S(1)}, bf16[512,512]{1,0:T(8,128)(2,1)S(1)}, u32[]{:S(2)}, u32[]{:S(2)}) collective-permute-start(bf16[512,512]{1,0:T(8,128)(2,1)S(1)} %collective-permute-done.5.refs_9_), channel_id=1, source_target_pairs={{0,8},{8,0},{16,24},{24,16},{1,9},{9,1},{17,25},{25,17},{2,10},{10... | collective-permute-start | bytes 1572872 | tf_op jit(solution)/shard_map/ppermute | solution.py:1027
  87.1 20.2 %collective-permute-start.29 = (bf16[512,512]{1,0:T(8,128)(2,1)S(1)}, bf16[512,512]{1,0:T(8,128)(2,1)S(1)}, u32[]{:S(2)}, u32[]{:S(2)}) collective-permute-start(bf16[512,512]{1,0:T(8,128)(2,1)S(1)} %collective-permute-done.9.refs_13_), channel_id=1, source_target_pairs={{0,8},{8,0},{16,24},{24,16},{1,9},{9,1},{17,25},{25,17},{2,10},{10... | collective-permute-start | bytes 1572872 | tf_op jit(solution)/shard_map/ppermute | solution.py:1027
  88.1 10.4 %collective-permute-start.36 = (bf16[256,512]{1,0:T(8,128)(2,1)S(1)}, bf16[256,512]{1,0:T(8,128)(2,1)S(1)}, u32[]{:S(2)}, u32[]{:S(2)}) collective-permute-start(bf16[256,512]{1,0:T(8,128)(2,1)S(1)} %collective-permute-done.16.refs_20_), channel_id=1, source_target_pairs={{0,8},{8,0},{16,24},{24,16},{1,9},{9,1},{17,25},{25,17},{2,10},{10... | collective-permute-start | bytes 786440 | tf_op jit(solution)/shard_map/ppermute | solution.py:1027
  95.8 11.6 %collective-permute-start.23 = (bf16[512,512]{1,0:T(8,128)(2,1)S(1)}, bf16[512,512]{1,0:T(8,128)(2,1)S(1)}, u32[]{:S(2)}, u32[]{:S(2)}) collective-permute-start(bf16[512,512]{1,0:T(8,128)(2,1)S(1)} %collective-permute-done.3.refs_7_), channel_id=1, source_target_pairs={{0,8},{8,0},{16,24},{24,16},{1,9},{9,1},{17,25},{25,17},{2,10},{10... | collective-permute-start | bytes 1572872 | tf_op jit(solution)/shard_map/ppermute | solution.py:1027
  96.8 8.8 %collective-permute-start.19 = (bf16[256,512]{1,0:T(8,128)(2,1)S(1)}, bf16[256,512]{1,0:T(8,128)(2,1)S(1)}, u32[]{:S(2)}, u32[]{:S(2)}) collective-permute-start(bf16[256,512]{1,0:T(8,128)(2,1)S(1)} %slice.221), channel_id=1, source_target_pairs={{0,16},{8,24},{16,0},{24,8},{1,17},{9,25},{17,1},{25,9},{2,18},{10... | collective-permute-start | bytes 786440 | tf_op jit(solution)/shard_map/ppermute | solution.py:1024
  98.5 9.5 %collective-permute-start.38 = (bf16[256,512]{1,0:T(8,128)(2,1)S(1)}, bf16[256,512]{1,0:T(8,128)(2,1)}, u32[]{:S(2)}, u32[]{:S(2)}) collective-permute-start(bf16[256,512]{1,0:T(8,128)(2,1)S(1)} %collective-permute-done.18.refs_22_), channel_id=1, source_target_pairs={{0,8},{8,0},{16,24},{24,16},{1,9},{9,1},{17,25},{25,17},{2,10},{10... | collective-permute-start | bytes 786440 | tf_op jit(solution)/shard_map/ppermute | solution.py:1027
  98.8 9.3 %collective-permute-start.34 = (bf16[256,512]{1,0:T(8,128)(2,1)S(1)}, bf16[256,512]{1,0:T(8,128)(2,1)}, u32[]{:S(2)}, u32[]{:S(2)}) collective-permute-start(bf16[256,512]{1,0:T(8,128)(2,1)S(1)} %collective-permute-done.14.refs_18_), channel_id=1, source_target_pairs={{0,8},{8,0},{16,24},{24,16},{1,9},{9,1},{17,25},{25,17},{2,10},{10... | collective-permute-start | bytes 786440 | tf_op jit(solution)/shard_map/ppermute | solution.py:1027
  105.6 8.0 %collective-permute-start.15 = (bf16[256,512]{1,0:T(8,128)(2,1)S(1)}, bf16[256,512]{1,0:T(8,128)(2,1)}, u32[]{:S(2)}, u32[]{:S(2)}) collective-permute-start(bf16[256,512]{1,0:T(8,128)(2,1)S(1)} %slice.217), channel_id=1, source_target_pairs={{0,1},{1,0},{2,3},{3,2},{4,5},{5,4},{6,7},{7,6},{8,9},{9,8},{10,11... | collective-permute-start | bytes 786440 | tf_op jit(solution)/shard_map/ppermute | solution.py:1021
  107.3 9.1 %collective-permute-start.26 = (bf16[512,512]{1,0:T(8,128)(2,1)S(1)}, bf16[512,512]{1,0:T(8,128)(2,1)S(1)}, u32[]{:S(2)}, u32[]{:S(2)}) collective-permute-start(bf16[512,512]{1,0:T(8,128)(2,1)S(1)} %collective-permute-done.6.refs_10_), channel_id=1, source_target_pairs={{0,8},{8,0},{16,24},{24,16},{1,9},{9,1},{17,25},{25,17},{2,10},{10... | collective-permute-start | bytes 1572872 | tf_op jit(solution)/shard_map/ppermute | solution.py:1027
  107.4 6.2 %collective-permute-start.39 = (bf16[256,512]{1,0:T(8,128)(2,1)S(1)}, bf16[256,512]{1,0:T(8,128)(2,1)S(1)}, u32[]{:S(2)}, u32[]{:S(2)}) collective-permute-start(bf16[256,512]{1,0:T(8,128)(2,1)S(1)} %collective-permute-done.19.refs_23_), channel_id=1, source_target_pairs={{0,8},{8,0},{16,24},{24,16},{1,9},{9,1},{17,25},{25,17},{2,10},{10... | collective-permute-start | bytes 786440 | tf_op jit(solution)/shard_map/ppermute | solution.py:1027
  108.0 8.4 %collective-permute-start.30 = (bf16[512,512]{1,0:T(8,128)(2,1)}, bf16[512,512]{1,0:T(8,128)(2,1)S(1)}, u32[]{:S(2)}, u32[]{:S(2)}) collective-permute-start(bf16[512,512]{1,0:T(8,128)(2,1)} %collective-permute-done.10.refs_14_), channel_id=1, source_target_pairs={{0,8},{8,0},{16,24},{24,16},{1,9},{9,1},{17,25},{25,17},{2,10},{10... | collective-permute-start | bytes 1572872 | tf_op jit(solution)/shard_map/ppermute | solution.py:1027
  108.1 8.3 %collective-permute-start.27 = (bf16[512,512]{1,0:T(8,128)(2,1)}, bf16[512,512]{1,0:T(8,128)(2,1)S(1)}, u32[]{:S(2)}, u32[]{:S(2)}) collective-permute-start(bf16[512,512]{1,0:T(8,128)(2,1)} %collective-permute-done.7.refs_11_), channel_id=1, source_target_pairs={{0,8},{8,0},{16,24},{24,16},{1,9},{9,1},{17,25},{25,17},{2,10},{10... | collective-permute-start | bytes 1572872 | tf_op jit(solution)/shard_map/ppermute | solution.py:1027
  113.6 2.8 collective-permute-start.31
  179.4 32.6 %collective-permute-start.40 = (bf16[8,512,512]{2,1,0:T(8,128)(2,1)}, bf16[8,512,512]{2,1,0:T(8,128)(2,1)}, u32[]{:S(2)}, u32[]{:S(2)}) collective-permute-start(bf16[8,512,512]{2,1,0:T(8,128)(2,1)} %get-tuple-element.87), channel_id=1, source_target_pairs={{0,8},{8,0},{16,24},{24,16},{1,9},{9,1},{17,25},{25,17},{2,10},{10... | collective-permute-start | bytes 12582920 | tf_op jit(solution)/shard_map/ppermute | solution.py:1081
  204.7 7.3 %collective-permute-start.42 = (bf16[4,512,512]{2,1,0:T(8,128)(2,1)}, bf16[4,512,512]{2,1,0:T(8,128)(2,1)}, u32[]{:S(2)}, u32[]{:S(2)}) collective-permute-start(bf16[4,512,512]{2,1,0:T(8,128)(2,1)} %get-tuple-element.105), channel_id=1, source_target_pairs={{0,8},{8,0},{16,24},{24,16},{1,9},{9,1},{17,25},{25,17},{2,10},{10... | collective-permute-start | bytes 6291464 | tf_op jit(solution)/shard_map/ppermute | solution.py:1082
  205.2 13.1 %collective-permute-start.41 = (bf16[4,512,512]{2,1,0:T(8,128)(2,1)}, bf16[4,512,512]{2,1,0:T(8,128)(2,1)S(1)}, u32[]{:S(2)}, u32[]{:S(2)}) collective-permute-start(bf16[4,512,512]{2,1,0:T(8,128)(2,1)} %get-tuple-element.106), channel_id=1, source_target_pairs={{0,8},{8,0},{16,24},{24,16},{1,9},{9,1},{17,25},{25,17},{2,10},{10... | collective-permute-start | bytes 6291464 | tf_op jit(solution)/shard_map/ppermute | solution.py:1083
  216.2 25.5 %collective-permute-start.44 = (bf16[2,512,512]{2,1,0:T(8,128)(2,1)S(1)}, bf16[2,512,512]{2,1,0:T(8,128)(2,1)S(1)}, u32[]{:S(2)}, u32[]{:S(2)}) collective-permute-start(bf16[2,512,512]{2,1,0:T(8,128)(2,1)S(1)} %get-tuple-element.100), channel_id=1, source_target_pairs={{0,1},{1,0},{2,3},{3,2},{4,5},{5,4},{6,7},{7,6},{8,9},{9,8},{10,11... | collective-permute-start | bytes 3145736 | tf_op jit(solution)/shard_map/ppermute | solution.py:1092
  217.5 25.1 %collective-permute-start.48 = (bf16[2,512,512]{2,1,0:T(8,128)(2,1)S(1)}, bf16[2,512,512]{2,1,0:T(8,128)(2,1)S(1)}, u32[]{:S(2)}, u32[]{:S(2)}) collective-permute-start(bf16[2,512,512]{2,1,0:T(8,128)(2,1)S(1)} %get-tuple-element.101), channel_id=1, source_target_pairs={{0,16},{8,24},{16,0},{24,8},{1,17},{9,25},{17,1},{25,9},{2,18},{10... | collective-permute-start | bytes 3145736 | tf_op jit(solution)/shard_map/ppermute | solution.py:1095
  246.3 14.9 %collective-permute-start.51 = (bf16[512,512]{1,0:T(8,128)(2,1)S(1)}, bf16[512,512]{1,0:T(8,128)(2,1)S(1)}, u32[]{:S(2)}, u32[]{:S(2)}) collective-permute-start(bf16[512,512]{1,0:T(8,128)(2,1)S(1)} %get-tuple-element.112), channel_id=1, source_target_pairs={{0,1},{1,0},{2,3},{3,2},{4,5},{5,4},{6,7},{7,6},{8,9},{9,8},{10,11... | collective-permute-start | bytes 1572872 | tf_op jit(solution)/shard_map/ppermute | solution.py:1092
  247.2 14.9 %collective-permute-start.52 = (bf16[512,512]{1,0:T(8,128)(2,1)S(1)}, bf16[512,512]{1,0:T(8,128)(2,1)S(1)}, u32[]{:S(2)}, u32[]{:S(2)}) collective-permute-start(bf16[512,512]{1,0:T(8,128)(2,1)S(1)} %get-tuple-element.114), channel_id=1, source_target_pairs={{0,16},{8,24},{16,0},{24,8},{1,17},{9,25},{17,1},{25,9},{2,18},{10... | collective-permute-start | bytes 1572872 | tf_op jit(solution)/shard_map/ppermute | solution.py:1095
  250.4 22.0 %collective-permute-start.49 = (bf16[512,512]{1,0:T(8,128)(2,1)S(1)}, bf16[512,512]{1,0:T(8,128)(2,1)S(1)}, u32[]{:S(2)}, u32[]{:S(2)}) collective-permute-start(bf16[512,512]{1,0:T(8,128)(2,1)S(1)} %get-tuple-element.111), channel_id=1, source_target_pairs={{0,1},{1,0},{2,3},{3,2},{4,5},{5,4},{6,7},{7,6},{8,9},{9,8},{10,11... | collective-permute-start | bytes 1572872 | tf_op jit(solution)/shard_map/ppermute | solution.py:1092
  251.9 21.4 %collective-permute-start.50 = (bf16[512,512]{1,0:T(8,128)(2,1)S(1)}, bf16[512,512]{1,0:T(8,128)(2,1)S(1)}, u32[]{:S(2)}, u32[]{:S(2)}) collective-permute-start(bf16[512,512]{1,0:T(8,128)(2,1)S(1)} %get-tuple-element.113), channel_id=1, source_target_pairs={{0,16},{8,24},{16,0},{24,8},{1,17},{9,25},{17,1},{25,9},{2,18},{10... | collective-permute-start | bytes 1572872 | tf_op jit(solution)/shard_map/ppermute | solution.py:1095
  262.3 11.7 %collective-permute-start.53 = (bf16[512,512]{1,0:T(8,128)(2,1)S(1)}, bf16[512,512]{1,0:T(8,128)(2,1)S(1)}, u32[]{:S(2)}, u32[]{:S(2)}) collective-permute-start(bf16[512,512]{1,0:T(8,128)(2,1)S(1)} %fusion.1), channel_id=1, source_target_pairs={{0,2},{1,3},{2,4},{3,5},{4,6},{5,7},{6,0},{7,1},{8,10},{9,11},{10,... | collective-permute-start | bytes 1572872 | tf_op jit(solution)/shard_map/ppermute | solution.py:1112
  263.2 27.2 %collective-permute-start.46 = (bf16[512,512]{1,0:T(8,128)(2,1)S(1)}, bf16[512,512]{1,0:T(8,128)(2,1)S(1)}, u32[]{:S(2)}, u32[]{:S(2)}) collective-permute-start(bf16[512,512]{1,0:T(8,128)(2,1)S(1)} %get-tuple-element.108), channel_id=1, source_target_pairs={{0,1},{1,0},{2,3},{3,2},{4,5},{5,4},{6,7},{7,6},{8,9},{9,8},{10,11... | collective-permute-start | bytes 1572872 | tf_op jit(solution)/shard_map/ppermute | solution.py:1092
  265.4 25.1 %collective-permute-start.47 = (bf16[512,512]{1,0:T(8,128)(2,1)S(1)}, bf16[512,512]{1,0:T(8,128)(2,1)S(1)}, u32[]{:S(2)}, u32[]{:S(2)}) collective-permute-start(bf16[512,512]{1,0:T(8,128)(2,1)S(1)} %get-tuple-element.110), channel_id=1, source_target_pairs={{0,16},{8,24},{16,0},{24,8},{1,17},{9,25},{17,1},{25,9},{2,18},{10... | collective-permute-start | bytes 1572872 | tf_op jit(solution)/shard_map/ppermute | solution.py:1095
  274.3 16.2 %collective-permute-start.54 = (bf16[512,512]{1,0:T(8,128)(2,1)S(1)}, bf16[512,512]{1,0:T(8,128)(2,1)S(1)}, u32[]{:S(2)}, u32[]{:S(2)}) collective-permute-start(bf16[512,512]{1,0:T(8,128)(2,1)S(1)} %fusion.4), channel_id=1, source_target_pairs={{0,2},{1,3},{2,4},{3,5},{4,6},{5,7},{6,0},{7,1},{8,10},{9,11},{10,... | collective-permute-start | bytes 1572872 | tf_op jit(solution)/shard_map/ppermute | solution.py:1114
  275.6 7.0 %collective-permute-start.56 = (f32[16,512]{1,0:T(8,128)S(1)}, f32[16,512]{1,0:T(8,128)S(1)}, u32[]{:S(2)}, u32[]{:S(2)}) collective-permute-start(f32[16,512]{1,0:T(8,128)S(1)} %add.210), channel_id=1, source_target_pairs={{0,1},{1,0},{2,3},{3,2},{4,5},{5,4},{6,7},{7,6},{8,9},{9,8},{10,11... | collective-permute-start | bytes 98312 | tf_op jit(solution)/shard_map/ppermute | solution.py:1092
  282.6 3.9 %collective-permute-start.57 = (f32[16,512]{1,0:T(8,128)S(1)}, f32[16,512]{1,0:T(8,128)S(1)}, u32[]{:S(2)}, u32[]{:S(2)}) collective-permute-start(f32[16,512]{1,0:T(8,128)S(1)} %add.211), channel_id=1, source_target_pairs={{0,16},{8,24},{16,0},{24,8},{1,17},{9,25},{17,1},{25,9},{2,18},{10... | collective-permute-start | bytes 98312 | tf_op jit(solution)/shard_map/ppermute | solution.py:1095
  286.5 3.9 %collective-permute-start.58 = (f32[16,512]{1,0:T(8,128)S(1)}, f32[16,512]{1,0:T(8,128)S(1)}, u32[]{:S(2)}, u32[]{:S(2)}) collective-permute-start(f32[16,512]{1,0:T(8,128)S(1)} %add.212), channel_id=1, source_target_pairs={{0,2},{1,3},{2,0},{3,1},{4,6},{5,7},{6,4},{7,5},{8,10},{9,11},{10,... | collective-permute-start | bytes 98312 | tf_op jit(solution)/shard_map/ppermute | solution.py:1113
  291.5 4.8 %collective-permute-start.59 = (f32[16,512]{1,0:T(8,128)S(1)}, f32[16,512]{1,0:T(8,128)S(1)}, u32[]{:S(2)}, u32[]{:S(2)}) collective-permute-start(f32[16,512]{1,0:T(8,128)S(1)} %add.213), channel_id=1, source_target_pairs={{0,4},{1,5},{2,6},{3,7},{4,0},{5,1},{6,2},{7,3},{8,12},{9,13},{10,... | collective-permute-start | bytes 98312 | tf_op jit(solution)/shard_map/ppermute | solution.py:1115
  293.5 14.3 %collective-permute-start.43 = (bf16[512,512]{1,0:T(8,128)(2,1)}, bf16[512,512]{1,0:T(8,128)(2,1)}, u32[]{:S(2)}, u32[]{:S(2)}) collective-permute-start(bf16[512,512]{1,0:T(8,128)(2,1)} %get-tuple-element.107), channel_id=1, source_target_pairs={{0,1},{1,0},{2,3},{3,2},{4,5},{5,4},{6,7},{7,6},{8,9},{9,8},{10,11... | collective-permute-start | bytes 1572872 | tf_op jit(solution)/shard_map/ppermute | solution.py:1092
  294.0 13.8 %collective-permute-start.45 = (bf16[512,512]{1,0:T(8,128)(2,1)}, bf16[512,512]{1,0:T(8,128)(2,1)}, u32[]{:S(2)}, u32[]{:S(2)}) collective-permute-start(bf16[512,512]{1,0:T(8,128)(2,1)} %get-tuple-element.109), channel_id=1, source_target_pairs={{0,16},{8,24},{16,0},{24,8},{1,17},{9,25},{17,1},{25,9},{2,18},{10... | collective-permute-start | bytes 1572872 | tf_op jit(solution)/shard_map/ppermute | solution.py:1095
  296.4 11.4 %collective-permute-start.60 = (bf16[512,512]{1,0:T(8,128)(2,1)}, bf16[512,512]{1,0:T(8,128)(2,1)}, u32[]{:S(2)}, u32[]{:S(2)}) collective-permute-start(bf16[512,512]{1,0:T(8,128)(2,1)} %fusion.7), channel_id=1, source_target_pairs={{0,2},{1,3},{2,4},{3,5},{4,6},{5,7},{6,0},{7,1},{8,10},{9,11},{10,... | collective-permute-start | bytes 1572872 | tf_op jit(solution)/shard_map/ppermute | solution.py:1116
  310.6 13.0 %collective-permute-start.61 = (bf16[172112]{0:T(1024)(128)(2,1)S(1)}, bf16[172112]{0:T(1024)(128)(2,1)S(1)}, u32[]{:S(2)}, u32[]{:S(2)}) collective-permute-start(bf16[172112]{0:T(1024)(128)(2,1)S(1)} %slice.245), channel_id=1, source_target_pairs={{0,1},{1,2},{2,3},{3,4},{4,5},{5,6},{6,7},{7,8},{8,9},{9,10},{10,1... | collective-permute-start | bytes 1032680 | tf_op jit(solution)/shard_map/ppermute | solution.py:990
  333.5 7.5 %collective-permute-start.62 = (f32[8,128]{1,0:T(8,128)}, f32[8,128]{1,0:T(8,128)S(1)}, u32[]{:S(2)}, u32[]{:S(2)}) collective-permute-start(f32[8,128]{1,0:T(8,128)} %get-tuple-element.93), channel_id=1, source_target_pairs={{0,8},{8,0},{16,24},{24,16},{1,9},{9,1},{17,25},{25,17},{2,10},{10... | collective-permute-start | bytes 12296 | tf_op jit(solution)/shard_map/ppermute | solution.py:1133
  341.7 3.6 collective-permute-start.63
  345.3 4.0 %collective-permute-start.64 = (f32[8,128]{1,0:T(8,128)S(1)}, f32[8,128]{1,0:T(8,128)S(1)}, u32[]{:S(2)}, u32[]{:S(2)}) collective-permute-start(f32[8,128]{1,0:T(8,128)S(1)} %add.220), channel_id=1, source_target_pairs={{0,16},{8,24},{16,0},{24,8},{1,17},{9,25},{17,1},{25,9},{2,18},{10... | collective-permute-start | bytes 12296 | tf_op jit(solution)/shard_map/ppermute | solution.py:1133
  349.3 3.6 collective-permute-start.65
  352.9 4.5 %collective-permute-start.66 = (f32[8,128]{1,0:T(8,128)S(1)}, f32[8,128]{1,0:T(8,128)S(1)}, u32[]{:S(2)}, u32[]{:S(2)}) collective-permute-start(f32[8,128]{1,0:T(8,128)S(1)} %add.222), channel_id=1, source_target_pairs={{0,4},{1,5},{2,6},{3,7},{4,0},{5,1},{6,2},{7,3},{8,12},{9,13},{10,... | collective-permute-start | bytes 12296 | tf_op jit(solution)/shard_map/ppermute | solution.py:1133
  (42 other events, 1192.6 us)

commit v4 on v3

--- a/solution.py
+++ b/solution.py
@@ -142,66 +142,128 @@
     return total
 
 
-PIECES = []
-for far_core in range(2):
-    for kind in ((0, 0), (0, 1), (1, 0)):
-        PIECES += [(far_core, *kind, back, 0, ROW) for back in range(4)]
-    for first_row in (0, HALF):
-        PIECES += [(far_core, 1, 1, back, first_row, HALF) for back in range(4)]
-
-
-def source_block(coords, piece):
+TOTAL_ROWS = 16037
+PARTS = 32
+TILE = 16
+SPAN = 528
+STARTS = [TILE * (TOTAL_ROWS * d // (PARTS * TILE)) for d in range(PARTS + 1)]
+SHORTEST = min(high - first for first, high in zip(STARTS, STARTS[1:]))
+
+
+def start_of(d):
+    return ((TOTAL_ROWS * d) >> 9) * TILE
+
+
+def gathered_layout():
+    layout = []
+    for core in range(2):
+        layout += [[(core, 0, 0, back, 0, SPAN, 0)] for back in range(4)]
+        for y, x, first, last in ((0, 1, 0, HALF), (1, 0, HALF, SPAN)):
+            whole = [(core, y, x, back, 0, SPAN, 0) for back in range(4)]
+            diagonal = [(core, 1, 1, back, first, last) for back in range(4)]
+            layout += [[whole[0]], [whole[1]]]
+            layout += [[whole[2], (*diagonal[0], SPAN)], [whole[3], (*diagonal[1], SPAN)]]
+            layout += [[(*diagonal[2], 0)], [(*diagonal[3], 0)]]
+    return layout
+
+
+LAYOUT = gathered_layout()
+
+
+def source_part(coords, piece):
     y, c, z, x = coords[0], coords[1], coords[2], coords[3]
     yy, cc, xx, zz = y ^ piece[1], c ^ piece[0], x ^ piece[2], (z + 4 - piece[3]) & 3
     return ((yy * 2 + cc) * 4 + zz) * 2 + xx
 
 
 class Loads:
-    def __init__(self, coords, sources, target, sems):
-        self.source, self.target, self.sems = sources[0], target, sems
-        for piece, source in zip(PIECES, sources):
-            block = source_block(coords, piece)
-            for half in range(2):
-                inside = HALF * half - piece[4]
-                if 0 <= inside < piece[5]:
-                    place = pl.ds(pl.multiple_of(block * ROW + HALF * half, HALF), HALF)
-                    pltpu.make_async_copy(
-                        source.at[inside : inside + HALF], target.at[place], sems.at[2 * block + half]
-                    ).start()
+    def __init__(self, coords, sources, target, seams, sems):
+        self.source, self.target, self.seams, self.sems = sources[0], target, seams, sems
+        self.here, self.joined = set(), set()
+        seams[0, 0] = jnp.zeros((TILE, ROW), BF16)
+        seams[PARTS, 1] = jnp.zeros((TILE, ROW), BF16)
+
+        def rows(at, size):
+            return pl.ds(pl.multiple_of(at, TILE), size)
+
+        for pieces, source in zip(LAYOUT, sources):
+            for piece in pieces:
+                first, last, offset = piece[4:]
+                offset = offset - first
+                d = source_part(coords, piece)
+                start = start_of(d)
+                length = start_of(d + 1) - start
+                inner, outer = max(first, TILE), min(last, SHORTEST)
+                sem = sems.at[d]
+                pltpu.make_async_copy(
+                    source.at[offset + inner : offset + outer], target.at[rows(start + inner, outer - inner)], sem
+                ).start()
+                if first == 0:
+                    pltpu.make_async_copy(source.at[offset : offset + TILE], seams.at[d, 1], sem).start()
+                if last == SPAN:
+
+                    @pl.when(length > SHORTEST)
+                    def _(source=source, offset=offset, start=start, sem=sem):
+                        pltpu.make_async_copy(
+                            source.at[offset + SHORTEST : offset + SHORTEST + TILE],
+                            target.at[rows(start + SHORTEST, TILE)],
+                            sem,
+                        ).start()
+
+                    pltpu.make_async_copy(source.at[rows(offset + length, TILE)], seams.at[d + 1, 0], sem).start()
+
+    def wait_part(self, d):
+        if d in self.here or not 0 <= d < PARTS:
+            return
+        self.here.add(d)
+        size = STARTS[d + 1] - STARTS[d] + TILE
+        pltpu.make_async_copy(self.source.at[0:size], self.target.at[0:size], self.sems.at[d]).wait()
 
     def wait(self, name):
-        first, count = BLOCK[name]
-        for at in range(2 * first, 2 * (first + count)):
-            pltpu.make_async_copy(
-                self.source.at[0:HALF], self.target.at[HALF * at : HALF * at + HALF], self.sems.at[at]
-            ).wait()
+        rows = rows_of(name)
+        last = min(rows.stop, STARTS[-1] + TILE)
+        for d in range(PARTS + 1):
+            if STARTS[d] < last and STARTS[d] + TILE > rows.start and d not in self.joined:
+                self.wait_part(d - 1)
+                self.wait_part(d)
+                self.joined.add(d)
+                self.target[STARTS[d] : STARTS[d] + TILE, :] = self.seams[d, 0] + self.seams[d, 1]
+            if d < PARTS and STARTS[d] + TILE < last and STARTS[d + 1] > rows.start:
+                self.wait_part(d)
 
 
 class Emits:
-    def __init__(self, coords, kept, sent, sems):
-        self.coords, self.kept, self.sent, self.sems = coords, kept, sent, sems
+    def __init__(self, coords, halves, sems):
+        self.coords, self.halves, self.sems = coords, halves, sems
         self.pending = []
 
-    def put(self, block, values):
-        core, z, x = (block // 8) % 2, (block // 2) % 4, block % 2
-        slot = 4 * (self.coords[3] ^ x) + ((self.coords[2] + 3 - z) & 3)
+    def put(self, d, values, rows):
+        core, z, x = (d // 8) % 2, (d // 2) % 4, d % 2
+        kept, sent = self.halves[d // 16]
+        far_x = self.coords[3] ^ x
+        place = (self.coords[2] + 3 - z) & 3
         sem = self.sems.at[len(self.pending)]
-
 
         @pl.when(self.coords[1] == core)
         def _():
-            pltpu.make_async_copy(values, self.kept.at[slot], sem).start()
-
-        @pl.when(self.coords[1] != core)
+            pltpu.make_async_copy(values, kept.at[4 * far_x + place, rows], sem).start()
+
+        @pl.when((self.coords[1] != core) & (far_x == 0))
         def _():
-            pltpu.make_async_copy(values, self.sent.at[slot], sem).start()
-
-        self.pending.append(pltpu.make_async_copy(values, self.kept.at[slot], sem))
-
-    def put_tensor(self, name, rows):
-        first, count = BLOCK[name]
-        for at in range(count):
-            self.put(first + at, rows.at[ROW * at : ROW * at + ROW])
+            pltpu.make_async_copy(values, sent[0].at[place, rows], sem).start()
+
+        @pl.when((self.coords[1] != core) & (far_x == 1))
+        def _():
+            pltpu.make_async_copy(values, sent[1].at[place, rows], sem).start()
+
+        self.pending.append(pltpu.make_async_copy(values, kept.at[0, rows], sem))
+
+    def put_tensor(self, name, values):
+        rows = rows_of(name)
+        for d in range(PARTS):
+            first, last = max(rows.start, STARTS[d]), min(rows.stop, STARTS[d] + SPAN)
+            if first < last:
+                self.put(d, values.at[first - rows.start : last - rows.start], slice(first - STARTS[d], last - STARTS[d]))
 
     def wait(self):
         for copy in self.pending:
@@ -562,11 +624,11 @@
 
 
 def forward_kernel(names, coords, length_ref, frames, cot, *refs):
-    sources, refs = refs[: len(PIECES)], refs[len(PIECES) :]
+    sources, refs = refs[: len(LAYOUT)], refs[len(LAYOUT) :]
     r = SimpleNamespace(**dict(zip(names, refs)))
     r.cot = cot
     length = length_ref[0]
-    loads = Loads(coords, sources, r.w, r.load_sems)
+    loads = Loads(coords, sources, r.w, r.seams, r.load_sems)
     kept = []
 
     def keep(source, target):
@@ -614,16 +676,10 @@
     w_out = r.w.at[rows_of("ffb_out")]
     feed_forward(r.x2, r.small[3:4, :], r.w_ffb_in, w_out, r.nrm_b, r.act_b, r.slope_b, r.x3)
     final_norm(r, length)
-    high = Emits(coords, r.high_kept, r.high_sent, r.high_sems)
-    every = Emits(coords, r.low_kept, r.low_sent, r.low_sems)
-
-    def put(block, values):
-        (high if block >= 16 else every).put(block, values)
-
-    emits = SimpleNamespace(
-        put_tensor=lambda name, rows: [
-            put(BLOCK[name][0] + at, rows.at[ROW * at : ROW * at + ROW]) for at in range(BLOCK[name][1])
-        ]
+    emits = Emits(
+        coords,
+        ((r.low_kept, (r.low_near, r.low_far)), (r.high_kept, (r.high_near, r.high_far))),
+        r.emit_sems,
     )
     feed_back(
         r.dout, r.w_ffb_in, w_out, r.nrm_b, r.act_b, r.slope_b, r.dhid, r.dnrm, r.stage, r.left_t,
@@ -652,11 +708,10 @@
         )
     )
     r.w[ROW * 31 + SMALL : ROW * 32, :] = jnp.zeros((ROW - SMALL, ROW), BF16)
-    put(31, r.w.at[ROW * 31 : ROW * 32])
+    emits.put_tensor("small", r.w.at[rows_of("small")])
     for copy in kept:
         copy.wait()
-    high.wait()
-    every.wait()
+    emits.wait()
 
 
 def attention_back(r, emits):
@@ -752,7 +807,7 @@
         waits[name] = pltpu.make_async_copy(source, target, r.load_sems.at[at])
         waits[name].start()
     r.late[...] = jnp.zeros_like(r.late)
-    emits = Emits(coords, r.low_kept, r.low_sent, r.low_sems)
+    emits = Emits(coords, ((r.low_kept, (r.low_near, r.low_far)),), r.emit_sems)
     for name in ("att", "djoin", "ctx", "heads", "probs", "qkv", "x1", "dx"):
         waits[name].wait()
     attention_back(r, emits)
@@ -778,16 +833,18 @@
 ANY = pl.BlockSpec(memory_space=pl.ANY)
 WIDE, THIN = ((SLOTS, D), F32), ((SLOTS, D), BF16)
 FULL = ((SLOTS, FF), BF16)
-HALF_GRADS = ((8, ROW, ROW), BF16)
+KEPT, SENT = ((8, SPAN, ROW), BF16), ((4, SPAN, ROW), BF16)
 
 FORWARD_OUT = {
     "out": (VM, THIN),
     "gains": (VM, ((8, ROW), F32)),
     "small": (VM, ((SMALL, ROW), F32)),
-    "high_kept": (ANY, HALF_GRADS),
-    "high_sent": (ANY, HALF_GRADS),
-    "low_kept": (ANY, HALF_GRADS),
-    "low_sent": (ANY, HALF_GRADS),
+    "high_kept": (ANY, KEPT),
+    "high_near": (ANY, SENT),
+    "high_far": (ANY, SENT),
+    "low_kept": (ANY, KEPT),
+    "low_near": (ANY, SENT),
+    "low_far": (ANY, SENT),
     "keep_ffa_in": (ANY, ((D, FF), BF16)),
     "keep_ffa_out": (ANY, ((FF, D), BF16)),
     "keep_qkv": (ANY, ((D, 3 * D), BF16)),
@@ -848,19 +905,21 @@
     "x1": WIDE,
     "x2": WIDE,
     "x3": WIDE,
-    "load_sems": 64,
+    "seams": ((PARTS + 1, 2, TILE, ROW), BF16),
+    "load_sems": PARTS,
     "keep_sems": 16,
-    "high_sems": 16,
-    "low_sems": 4,
+    "emit_sems": 40,
 }
 BACKWARD_IN = (
     "ffa_in", "ffa_out", "qkv", "att", "nrm", "act", "slope", "x1", "nrm_t", "heads", "probs", "ctx", "djoin", "dx",
 )
+PASSED = ("low_kept", "low_near", "low_far")
 BACKWARD_OUT = {
     "fgrad": (VM, THIN),
     "late": (VM, ((16, ROW), F32)),
-    "low_kept": (ANY, HALF_GRADS),
-    "low_sent": (ANY, HALF_GRADS),
+    "low_kept": (ANY, KEPT),
+    "low_near": (ANY, SENT),
+    "low_far": (ANY, SENT),
 }
 BACKWARD_SCRATCH = {
     "w_ffa_in": ((D, FF), BF16),
@@ -887,7 +946,7 @@
     "dx": WIDE,
     "x1": WIDE,
     "load_sems": 14,
-    "low_sems": 12,
+    "emit_sems": 24,
 }
 
 
@@ -924,12 +983,12 @@
 
 def backward(coords, frames, state):
     def kernel(*refs):
-        names = ["in_" + name for name in BACKWARD_IN] + ["in_low_kept", "in_low_sent"]
+        names = ["in_" + name for name in BACKWARD_IN + PASSED]
         backward_kernel([*names, *BACKWARD_OUT, *BACKWARD_SCRATCH], *refs)
 
     ins = [(SM, coords), (VM, frames), (VM, state["gains"]), (VM, state["small"])]
     ins += [(ANY, state["keep_" + name]) for name in BACKWARD_IN]
-    ins += [(ANY, state["low_kept"]), (ANY, state["low_sent"])]
+    ins += [(ANY, state[name]) for name in PASSED]
     outs = call(
         kernel,
         "backward",
@@ -937,7 +996,7 @@
         list(BACKWARD_OUT.values()),
         list(BACKWARD_SCRATCH.values()),
         58,
-        {len(ins) - 2: 2, len(ins) - 1: 3},
+        {len(ins) - 3 + at: 2 + at for at in range(3)},
     )
     return dict(zip(BACKWARD_OUT, outs))
 
@@ -949,99 +1008,71 @@
     return bounds
 
 
-def block_rows(device_count):
-    total_rows = -(-segment_bounds()[-1] // ROW)
-    step = 16 * device_count
-    return -(-total_rows // step) * 16
-
-
-def align_shard(low_shard, shard_size, rows):
-    devices = lax.axis_size("dp") * lax.axis_size("fsdp")
-    me = lax.axis_index(AXES)
-    block = rows * ROW
-    lead = block - shard_size
-    pieces = [low_shard]
-    have = shard_size
-    need = lead * (devices - 1) + block
-    hop = 1
-    while have < need:
-        part = min(shard_size, need - have)
-        pairs = [(i, i - hop) for i in range(hop, devices)]
-        pieces.append(lax.ppermute(low_shard[:part], AXES, pairs))
-        have = have + part
-        hop = hop + 1
-    return lax.dynamic_slice(jnp.concatenate(pieces), (me * lead,), (block,)).reshape(rows, ROW)
-
-
-def unalign_block(block_sum, shard_size, padded):
-    devices = lax.axis_size("dp") * lax.axis_size("fsdp")
-    me = lax.axis_index(AXES)
-    rows = block_sum.shape[0]
-    block = rows * ROW
-    lead = block - shard_size
-    flat = block_sum.reshape(-1)
-    pieces = [flat]
-    have = block
-    need = lead * (devices - 1) + block
-    hop = 1
-    while have < need:
-        part = min(block, need - have)
-        pairs = [(i, i + hop) for i in range(devices - hop)]
-        pieces.insert(0, lax.ppermute(flat[block - part :], AXES, pairs))
-        have = have + part
-        hop = hop + 1
-    start = have - block - me * lead
-    pieces.append(jnp.zeros((max(0, padded - block),), flat.dtype))
-    return lax.dynamic_slice(jnp.concatenate(pieces), (start,), (padded,))
-
-
-def pair_lists():
-    ring = [(i, (i + 2) % 8) for i in range(8)]
-    across_x = [(i, i ^ 1) for i in range(8)]
-    across_y = [(i, i ^ 2) for i in range(4)]
-    across_core = [(i, i ^ 1) for i in range(4)]
-    return ring, across_x, across_y, across_core
-
-
 def fast_mesh():
     return lax.axis_size("dp") == 4 and lax.axis_size("fsdp") == 8
 
 
+def over_x(value):
+    return lax.ppermute(value, "fsdp", [(i, i ^ 1) for i in range(8)])
+
+
+def over_y(value):
+    return lax.ppermute(value, "dp", [(i, i ^ 2) for i in range(4)])
+
+
+def over_core(value):
+    return lax.ppermute(value, "dp", [(i, i ^ 1) for i in range(4)])
+
+
+def round_z(value):
+    return lax.ppermute(value, "fsdp", [(i, (i + 2) % 8) for i in range(8)])
+
+
+def over_z(value, step):
+    return lax.ppermute(value, "fsdp", [(i, i ^ (2 * step)) for i in range(8)])
+
+
 def after(value, *others):
     return lax.optimization_barrier((value, *others))[0]
 
 
-def gather_blocks(block):
+def shard_offset(me, shard_size):
+    return me * shard_size - start_of(me) * ROW
+
+
+def gather_shards(shard, me):
+    shard_size = shard.shape[0]
     if not fast_mesh():
-        whole = lax.all_gather(block, AXES, axis=0, tiled=True).reshape(32, ROW, ROW)
-        return [whole[source_block((0, 0, 0, 0), piece)][piece[4] : piece[4] + piece[5]] for piece in PIECES]
-    ring, across_x, across_y, across_core = pair_lists()
-
-    def over_x(value):
-        return lax.ppermute(value, "fsdp", across_x)
-
-    def over_y(value):
-        return lax.ppermute(value, "dp", across_y)
-
-    def over_core(value, *others):
-        return lax.ppermute(after(value, *others), "dp", across_core)
-
-    own = [block]
-    for _ in range(3):
-        own.append(lax.ppermute(own[-1], "fsdp", ring))
-    by_x = [over_x(each_one) for each_one in own]
-    by_y = [over_y(each_one) for each_one in own]
-    top = [over_x(each_one[:HALF]) for each_one in by_y]
-    bottom = [over_y(each_one[HALF:]) for each_one in by_x]
-    near = own + by_x + by_y + top + bottom
-    later = [own[2], own[3], by_x[3], by_y[3]]
-    far = [over_core(each_one) for each_one in own]
-    far += [over_core(by_x[at], later[at]) for at in range(3)] + [over_core(by_x[3])]
-    far += [over_core(by_y[at], later[at]) for at in range(3)] + [over_core(by_y[3])]
-    ends = [own[3], by_x[2], by_x[3], top[3]]
-    far += [over_core(top[at], ends[at]) for at in range(3)] + [over_core(top[3])]
-    far += [over_core(bottom[at], ends[at]) for at in range(3)] + [over_core(bottom[3])]
-    return near + far
+        whole = lax.all_gather(shard, AXES, axis=0, tiled=True)
+        whole = jnp.pad(whole, (0, (STARTS[-1] + SPAN) * ROW - whole.shape[0])).reshape(-1, ROW)
+        spans = [whole[start : start + SPAN] for start in STARTS[:-1]]
+        spans = spans[:1] + [jnp.concatenate([jnp.zeros((TILE, ROW), BF16), span[TILE:]]) for span in spans[1:]]
+        return [
+            jnp.concatenate([spans[source_part((0, 0, 0, 0), piece)][piece[4] : piece[5]] for piece in pieces])
+            for pieces in LAYOUT
+        ]
+    most = TILE * ROW
+    padded = jnp.pad(shard, (most, SPAN * ROW - shard_size))
+    span = lax.dynamic_slice(padded, (most - shard_offset(me, shard_size),), (SPAN * ROW,)).reshape(SPAN, ROW)
+    own, by_x, by_y = [span], [], []
+    for back in range(4):
+        if back < 3:
+            own.append(round_z(own[back]))
+        if back < 2:
+            by_x.append(over_x(own[back]))
+            by_y.append(over_y(own[back]))
+        else:
+            by_x.append(over_x(jnp.concatenate([own[back], by_y[back - 2][:HALF]])))
+            by_y.append(over_y(jnp.concatenate([own[back], by_x[back - 2][HALF:SPAN]])))
+    for back in (2, 3):
+        by_x.append(over_x(by_y[back][:HALF]))
+        by_y.append(over_y(by_x[back][HALF:SPAN]))
+    far_own = [over_core(after(own[0], own[1])), over_core(after(own[1], own[2])), over_core(after(own[2], own[3]))]
+    far_own.append(over_core(after(own[3], by_x[1])))
+    until = [own[3], by_x[2], by_x[3], by_x[4], by_x[5]]
+    far_x = [over_core(after(each_one, until[at])) for at, each_one in enumerate(by_x[:5])] + [over_core(by_x[5])]
+    far_y = [over_core(after(each_one, until[at])) for at, each_one in enumerate(by_y[:5])] + [over_core(by_y[5])]
+    return own + by_x + by_y + far_own + far_x + far_y
 
 
 def added(*parts):
@@ -1051,87 +1082,82 @@
     return total
 
 
-def placed_late(late, rows, me):
-    block = jnp.concatenate(
-        [
-            jnp.zeros((rows, ROW), F32),
-            late[0:8],
-            jnp.zeros((REL_AT - 8, ROW), F32),
-            late[8:10],
-            jnp.zeros((ROW - REL_AT - 2 + rows, ROW), F32),
-        ]
-    )
-    start = jnp.clip(me * rows - ROW * BLOCK["small"][0] + rows, 0, ROW + rows)
-    return lax.dynamic_slice(block, (start, 0), (rows, ROW))
-
-
-def scatter_blocks(state, back, coords, rows, me):
+def late_rows(late, above, below):
+    gains = jnp.pad(late[0:8], ((above, below - 8), (0, 0)))
+    return gains + jnp.pad(late[8:10], ((above + REL_AT, below - REL_AT - 2), (0, 0)))
+
+
+def scatter_slow(state, back, shard_size, padded):
     late = back["late"]
+    pieces = []
+    for source, half in ((back, "low"), (state, "high")):
+        for core in range(2):
+            for at in range(8):
+                z, x = at // 2, at % 2
+                if core == 0:
+                    span = source[half + "_kept"][4 * x + 3 - z]
+                else:
+                    span = source[half + ("_near", "_far")[x]][3 - z]
+                d = len(pieces)
+                pieces.append(span[: STARTS[d + 1] - STARTS[d] if d < PARTS - 1 else SPAN])
+    rows = jnp.concatenate(pieces)
+    first = ROW * BLOCK["small"][0]
+    rows = low(rows.astype(F32) + late_rows(late, first, rows.shape[0] - first))
+    flat = rows.reshape(-1)[: segment_bounds()[-1]]
+    shard = lax.psum_scatter(flat, AXES, scatter_dimension=0, tiled=True)
+    return jnp.pad(shard, (0, padded - shard_size)).astype(F32), lax.psum(late[0:8], AXES)
+
+
+def scatter_grads(state, back, coords, me, shard_size, padded):
     if not fast_mesh():
-        late = lax.psum(late, AXES)
-        blocks = []
-        for half in ((back["low_kept"], back["low_sent"]), (state["high_kept"], state["high_sent"])):
-            for core in half:
-                blocks += [core[4 * x + (3 - z) % 4] for z in range(4) for x in range(2)]
-        own = lax.psum_scatter(jnp.concatenate(blocks), AXES, scatter_dimension=0, tiled=True)
-        return own.astype(F32) + placed_late(late, rows, me), late[0:8]
-    ring, across_x, across_y, across_core = pair_lists()
+        return scatter_slow(state, back, shard_size, padded)
     high = coords[0] == 1
     high_kept, low_kept = state["high_kept"], back["low_kept"]
-    high_got = lax.ppermute(state["high_sent"], "dp", across_core)
-    low_got = [lax.ppermute(back["low_sent"][4:], "dp", across_core)]
-    low_got.insert(0, lax.ppermute(back["low_sent"][:4], "dp", across_core))
+    high_got = [over_core(state["high_near"]), over_core(state["high_far"])]
+    low_far = over_core(back["low_far"])
+    low_got = [over_core(after(back["low_near"], low_far)), low_far]
 
     def chip_sum(own_half, x, first, last):
         here = slice(4 * x + first, 4 * x + last)
-        of_high = added(high_kept[here], high_got[here])
+        of_high = added(high_kept[here], high_got[x][first:last])
         of_low = added(low_kept[here], low_got[x][first:last])
         return low(jnp.where(high == own_half, of_high, of_low))
-
-    def over_x(value):
-        return lax.ppermute(value, "fsdp", across_x)
-
-    def over_y(value):
-        return lax.ppermute(value, "dp", across_y)
 
     from_y = over_y(chip_sum(False, 1, 0, 2))
     from_x = over_x(chip_sum(False, 1, 2, 4))
     to_y = chip_sum(False, 0, 0, 2)
+    sent_y = [over_y(to_y[0]), over_y(to_y[1])]
     to_x_late = chip_sum(True, 1, 2, 4)
-    sent_y = [over_y(to_y[0]), over_y(to_y[1])]
     to_x = low(added(chip_sum(True, 1, 0, 2), from_y))
     sent_x = [over_x(to_x[0]), over_x(to_x[1])]
     to_y_late = low(added(chip_sum(False, 0, 2, 4), from_x))
     sent_x += [over_x(to_x_late[0]), over_x(to_x_late[1])]
     sent_y += [over_y(to_y_late[0]), over_y(to_y_late[1])]
     mine = chip_sum(True, 0, 0, 4)
-    late = late + lax.ppermute(late, "dp", across_core)
-    late = late + over_x(late)
-    late = late + over_y(late)
+    late = back["late"]
+    late = late + over_core(late)
+    late = late + over_x(after(late, from_x))
+    late = late + over_y(after(late, sent_x[0]))
     running = low(added(mine[0], sent_x[0], sent_y[0]))
-    running = low(added(mine[1], sent_x[1], sent_y[1], lax.ppermute(running, "fsdp", ring)))
-    late = late + lax.ppermute(late, "fsdp", [(i, i ^ 2) for i in range(8)])
-    running = low(added(mine[2], sent_x[2], sent_y[2], lax.ppermute(running, "fsdp", ring)))
-    late = late + lax.ppermute(after(late, running), "fsdp", [(i, i ^ 4) for i in range(8)])
-    total = added(mine[3], sent_x[3], sent_y[3], lax.ppermute(after(running, late), "fsdp", ring))
-    return total + placed_late(late, rows, me), late[0:8]
+    running = low(added(mine[1], sent_x[1], sent_y[1], round_z(running)))
+    late = late + over_z(after(late, sent_x[1]), 1)
+    running = low(added(mine[2], sent_x[2], sent_y[2], round_z(running)))
+    late = late + over_z(after(late, sent_x[2]), 2)
+    total = added(mine[3], sent_x[3], sent_y[3], round_z(running))
+    first = ROW * BLOCK["small"][0] - STARTS[PARTS - 1]
+    total = total + jnp.where(me == PARTS - 1, 1.0, 0.0) * late_rows(late, first, SPAN - first)
+    flat = jnp.pad(total.reshape(-1), (0, max(0, TILE * ROW + padded - SPAN * ROW)))
+    return lax.dynamic_slice(flat, (shard_offset(me, shard_size),), (padded,)), late[0:8]
 
 
 def sum_everywhere(vector):
     if not fast_mesh():
         return lax.psum(vector, AXES)
-    _, across_x, across_y, across_core = pair_lists()
-    near_z = [(i, i ^ 2) for i in range(8)]
-    far_z = [(i, i ^ 4) for i in range(8)]
-    for axis, pairs in (
-        ("dp", across_core),
-        ("fsdp", across_x),
-        ("dp", across_y),
-        ("fsdp", near_z),
-        ("fsdp", far_z),
-    ):
-        vector = vector + lax.ppermute(vector, axis, pairs)
-    return vector
+    vector = vector + over_core(vector)
+    vector = vector + over_x(vector)
+    vector = vector + over_y(vector)
+    vector = vector + over_z(vector, 1)
+    return vector + over_z(vector, 2)
 
 
 def most_segments(shard_size, devices):
@@ -1144,17 +1170,26 @@
 
 
 LANES = 128
-CHUNK = 256
-
-
-def entry_places(step):
-    row = step * CHUNK + lax.broadcasted_iota(jnp.int32, (CHUNK, LANES), 0)
-    return row * LANES + lax.broadcasted_iota(jnp.int32, (CHUNK, LANES), 1)
+CHUNK = 512
+
+
+def chunk_spans(segments, step):
+    first, last = step * (CHUNK * LANES), (step + 1) * (CHUNK * LANES)
+    for at in range(segments.shape[0] - 2):
+        start, end = segments[1 + at], segments[2 + at]
+        whole = (start <= first) & (last <= end)
+        some = (start < last) & (end > first) & jnp.logical_not(whole)
+
+        def inside(first=first, start=start, end=end):
+            row = lax.broadcasted_iota(jnp.int32, (CHUNK, LANES), 0)
+            place = first + row * LANES + lax.broadcasted_iota(jnp.int32, (CHUNK, LANES), 1)
+            return (place >= start) & (place < end)
+
+        yield at, whole, some, inside
 
 
 def update_kernel(segments, params, first, second, grad, new_first, new_second, update, sums):
     step = pl.program_id(0)
-    spans = segments.shape[0] - 2
 
     @pl.when(step == 0)
     def _():
@@ -1167,53 +1202,64 @@
     new_second[...] = seconds
     first_hat = firsts * (1.0 / (1.0 - BETA_FIRST**STEP))
     second_hat = seconds * (1.0 / (1.0 - BETA_SECOND**STEP))
-    values = params[...]
-    change = first_hat / (jnp.sqrt(second_hat) + ADAM_EPS) + WEIGHT_DECAY * values
-    update[...] = change
-    places = entry_places(step)
+    update[...] = first_hat / (jnp.sqrt(second_hat) + ADAM_EPS) + WEIGHT_DECAY * params[...]
     lane = lax.broadcasted_iota(jnp.int32, (1, LANES), 1)
-    for at in range(spans):
-        inside = (places >= segments[1 + at]) & (places < segments[2 + at])
-        mine = lane == segments[0] + at
-        for row, entries in enumerate((values, change)):
-            squares = jnp.where(inside, entries * entries, 0.0)
-            total = jnp.sum(jnp.sum(squares, axis=0, keepdims=True), axis=1, keepdims=True)
-            sums[row : row + 1, :] += jnp.where(mine, total, 0.0)
+
+    def add_squares(at, pick):
+        for row, entries in enumerate((params, update)):
+            values = entries[...]
+            total = jnp.sum(pick(values * values), axis=0, keepdims=True)
+            total = jnp.sum(total, axis=1, keepdims=True)
+            sums[row : row + 1, :] += jnp.where(lane == segments[0] + at, total, 0.0)
+
+    for at, whole, some, inside in chunk_spans(segments, step):
+
+        @pl.when(whole)
+        def _(at=at):
+            add_squares(at, lambda squares: squares)
+
+        @pl.when(some)
+        def _(at=at, inside=inside):
+            add_squares(at, lambda squares: jnp.where(inside(), squares, 0.0))
 
 
 def apply_kernel(segments, sums, params, update, new_params, norms):
     step = pl.program_id(0)
-    spans = segments.shape[0] - 2
     roots = jnp.sqrt(sums[0:2, :])
     trust = roots[0:1, :] / (roots[1:2, :] + ADAM_EPS)
     norms[0:2, :] = roots
     norms[2:3, :] = trust
-    places = entry_places(step)
+    norms[3:8, :] = jnp.zeros((5, LANES), F32)
     lane = lax.broadcasted_iota(jnp.int32, (1, LANES), 1)
-    scale = jnp.zeros((CHUNK, LANES), F32)
-    for at in range(spans):
-        own = jnp.sum(jnp.where(lane == segments[0] + at, trust, 0.0), axis=1, keepdims=True)
-        scale = jnp.where(places >= segments[1 + at], own, scale)
-    new_params[...] = params[...] - LEARN_RATE * scale * update[...]
+    for at, whole, some, inside in chunk_spans(segments, step):
+
+        def moved(at=at):
+            scale = LEARN_RATE * jnp.sum(jnp.where(lane == segments[0] + at, trust, 0.0), axis=1, keepdims=True)
+            return params[...] - scale * update[...]
+
+        @pl.when(whole)
+        def _(moved=moved):
+            new_params[...] = moved()
+
+        @pl.when(some)
+        def _(moved=moved, inside=inside):
+            new_params[...] = jnp.where(inside(), moved(), new_params[...])
 
 
 def shards(frames, lengths, cotangent, params, first_moment, second_moment):
     shard_size = params.shape[0]
     devices = lax.axis_size("dp") * lax.axis_size("fsdp")
     me = lax.axis_index(AXES)
-    rows = block_rows(devices)
     if fast_mesh():
         dp, fsdp = lax.axis_index("dp"), lax.axis_index("fsdp")
         coords = jnp.stack([dp // 2, dp % 2, fsdp // 2, fsdp % 2]).astype(jnp.int32)
     else:
         coords = jnp.zeros((4,), jnp.int32)
-    blocks = gather_blocks(align_shard(low(params), shard_size, rows))
-    state = forward(coords, lengths, frames[0], cotangent[0], blocks)
+    state = forward(coords, lengths, frames[0], cotangent[0], gather_shards(low(params), me))
     back = backward(coords, frames[0], state)
-    block_sum, gain_grads = scatter_blocks(state, back, coords, rows, me)
     steps = -(-shard_size // (LANES * CHUNK))
     padded = steps * LANES * CHUNK
-    grad_shard = unalign_block(low(block_sum), shard_size, padded).astype(F32)
+    grad_shard, gain_grads = scatter_grads(state, back, coords, me, shard_size, padded)
 
     def square(flat):
         return jnp.pad(flat, (0, padded - flat.shape[0])).reshape(-1, LANES)

time: 369 us -> 338 us (0.916)
  starting transfers between devices: 66.5 us -> 45.1 us
  waiting for transfers between devices: 148 us -> 163 us
  local copies, waits for them, and re-layouts: 32.1 us -> 17.5 us
  other arithmetic: 22.7 us -> 17.1 us
    ppermute x67 -> x58, starting transfers between devices: 66.5 us -> 45.1 us  [the longest x13 16.8 us: over_y(): return lax.ppermute(value, 'dp', [(i, i ^ 2) for i in range(4)])]
    ppermute x67 -> x58, waiting for transfers between devices: 148 us -> 163 us  [the longest x13 81.1 us: over_x(): return lax.ppermute(value, 'fsdp', [(i, i ^ 1) for i in range(8)])]
    concatenate x1 -> x0, local copies, waits for them, and re-layouts: 9.19 us -> none  [placed_late(): jnp.concatenate([jnp.zeros((rows, ROW), F32), late[0:8], jnp.zeros((REL_A...]
    slice x12 -> x9, local copies, waits for them, and re-layouts: 7.68 us -> 2.05 us  [the longest x2 1.93 us: gather_shards(): by_x.append(over_x(by_y[back][:HALF]))]
  transfers between devices with their start and end apart: 67 -> 58, of which waited for: 33 -> 29; matrix products, arithmetic and copies ran while one was open for 9% -> 5% of each run, Pallas kernels for 6% -> 0%
where the time goes in v4:
time: 338 us
  waiting for transfers between devices  163 us (48%)
  Pallas kernels  93 us (28%)
  starting transfers between devices  45.1 us (13%)
  local copies, waits for them, and re-layouts  17.5 us (5%)
  other arithmetic  17.1 us (5%)
    pallas_call x2, Pallas kernels, call(): pl.pallas_call(kernel, name=name, in_specs=[space for space, _ in ins], o...  82.8 us
    ppermute x13, waiting for transfers between devices, over_x(): return lax.ppermute(value, 'fsdp', [(i, i ^ 1) for i in range(8)])  81.1 us
    ppermute x13, waiting for transfers between devices, over_y(): return lax.ppermute(value, 'dp', [(i, i ^ 2) for i in range(4)])  31 us
    ppermute x6, waiting for transfers between devices, round_z(): return lax.ppermute(value, 'fsdp', [(i, (i + 2) % 8) for i in range(8)])  26.9 us
    ppermute x13, starting transfers between devices, over_y(): return lax.ppermute(value, 'dp', [(i, i ^ 2) for i in range(4)])  16.8 us
    ppermute x22, waiting for transfers between devices, over_core(): return lax.ppermute(value, 'dp', [(i, i ^ 1) for i in range(4)])  15.7 us
    ppermute x13, starting transfers between devices, over_x(): return lax.ppermute(value, 'fsdp', [(i, i ^ 1) for i in range(8)])  14.2 us
    convert_element_type x7, other arithmetic, low(): return values.astype(BF16)  13 us
  transfers between devices with their start and end apart: 58, of which 29 were waited for; matrix products, arithmetic and copies ran while one was open for 5% of the time, Pallas kernels for 0%

profile of v4, /device:TPU:0, one launch (start us, length us, event | category | flops | bytes accessed | tf_op | source)
XLA Modules:
  0.0 337.6 jit_solution(17339700136650159922)
XLA Ops:
  0.7 1.3 convert_element_type.219
  2.8 3.1 collective-permute-start
  5.8 1.5 collective-permute-start.5
  7.3 12.8 %collective-permute-done.refs_5_ = bf16[528,512]{1,0:T(8,128)(2,1)S(1)} collective-permute-done((bf16[528,512]{1,0:T(8,128)(2,1)S(1)}, bf16[528,512]{1,0:T(8,128)(2,1)S(1)}, u32[]{:S(2)}, u32[]{:S(2)}) %collective-permute-start) | collective-permute-done | bytes 540704 | tf_op jit(solution)/shard_map/ppermute | solution.py:1028
  20.1 1.5 collective-permute-start.3
  22.2 1.5 collective-permute-start.7
  23.7 11.7 %collective-permute-done.1.refs_6_ = bf16[528,512]{1,0:T(8,128)(2,1)S(1)} collective-permute-done((bf16[528,512]{1,0:T(8,128)(2,1)S(1)}, bf16[528,512]{1,0:T(8,128)(2,1)S(1)}, u32[]{:S(2)}, u32[]{:S(2)}) %collective-permute-start.1) | collective-permute-done | bytes 540704 | tf_op jit(solution)/shard_map/ppermute | solution.py:1028
  35.5 1.3 collective-permute-start.6
  36.9 1.6 collective-permute-start.9
  38.4 8.5 %collective-permute-done.4.refs_9_ = bf16[528,512]{1,0:T(8,128)(2,1)S(1)} collective-permute-done((bf16[528,512]{1,0:T(8,128)(2,1)S(1)}, bf16[528,512]{1,0:T(8,128)(2,1)S(1)}, u32[]{:S(2)}, u32[]{:S(2)}) %collective-permute-start.4) | collective-permute-done | bytes 540704 | tf_op jit(solution)/shard_map/ppermute | solution.py:1016
  47.6 2.2 collective-permute-done.2.refs_7_
  49.8 1.1 collective-permute-start.11
  50.9 11.4 %collective-permute-done.6.refs_10_ = bf16[784,512]{1,0:T(8,128)(2,1)S(1)} collective-permute-done((bf16[784,512]{1,0:T(8,128)(2,1)S(1)}, bf16[784,512]{1,0:T(8,128)(2,1)S(1)}, u32[]{:S(2)}, u32[]{:S(2)}) %collective-permute-start.6) | collective-permute-done | bytes 802848 | tf_op jit(solution)/shard_map/ppermute | solution.py:1016
  62.4 1.2 collective-permute-start.8
  63.7 1.6 collective-permute-start.13
  66.8 11.6 %collective-permute-done.13.refs_18_ = bf16[272,512]{1,0:T(8,128)(2,1)S(1)} collective-permute-done((bf16[272,512]{1,0:T(8,128)(2,1)S(1)}, bf16[272,512]{1,0:T(8,128)(2,1)S(1)}, u32[]{:S(2)}, u32[]{:S(2)}) %collective-permute-start.13) | collective-permute-done | bytes 278560 | tf_op jit(solution)/shard_map/ppermute | solution.py:1020
  78.4 1.0 collective-permute-start.10
  79.5 6.8 %collective-permute-done.10.refs_12_ = bf16[256,512]{1,0:T(8,128)(2,1)S(1)} collective-permute-done((bf16[256,512]{1,0:T(8,128)(2,1)S(1)}, bf16[256,512]{1,0:T(8,128)(2,1)S(1)}, u32[]{:S(2)}, u32[]{:S(2)}) %collective-permute-start.10) | collective-permute-done | bytes 262176 | tf_op jit(solution)/shard_map/ppermute | solution.py:1016
  88.4 1.1 collective-permute-start.12
  89.5 7.3 %collective-permute-done.12.refs_13_ = bf16[256,512]{1,0:T(8,128)(2,1)S(1)} collective-permute-done((bf16[256,512]{1,0:T(8,128)(2,1)S(1)}, bf16[256,512]{1,0:T(8,128)(2,1)S(1)}, u32[]{:S(2)}, u32[]{:S(2)}) %collective-permute-start.12) | collective-permute-done | bytes 262176 | tf_op jit(solution)/shard_map/ppermute | solution.py:1016
  98.9 5.8 %collective-permute-done.14.refs_19_ = bf16[272,512]{1,0:T(8,128)(2,1)} collective-permute-done((bf16[272,512]{1,0:T(8,128)(2,1)S(1)}, bf16[272,512]{1,0:T(8,128)(2,1)}, u32[]{:S(2)}, u32[]{:S(2)}) %collective-permute-start.14) | collective-permute-done | bytes 278560 | tf_op jit(solution)/shard_map/ppermute | solution.py:1020
  105.4 2.6 collective-permute-done.29.refs_34_
  111.8 62.0 %forward.1 = (bf16[160,512]{1,0:T(8,128)(2,1)}, f32[8,512]{1,0:T(8,128)}, f32[176,512]{1,0:T(8,128)}, bf16[8,528,512]{2,1,0:T(8,128)(2,1)}, bf16[4,528,512]{2,1,...) custom-call(s32[4]{0:T(128)} %pad_add_fusion.refs_0_, ...), custom_call_target="tpu_custom_call" | custom-call | tf_op jit(solution)/shard_map/forward/pallas_call | solution.py:954
  173.8 20.8 %backward.1 = (bf16[160,512]{1,0:T(8,128)(2,1)}, f32[16,512]{1,0:T(8,128)}, bf16[8,528,512]{2,1,0:T(8,128)(2,1)}, bf16[4,528,512]{2,1,0:T(8,128)(2,1)}, bf16[4,528,512]{2,1,0:T(8,128)(2,1)}) custom-call(s32[4]{0:T(128)} %pad_add_fusion.refs_0_, bf16[160,512]{1,0:T(8,128)(2,1)} %bitcast.75, ...), custom_call_target="tpu_custom_call", output_to_operand_aliasing={{2}: (18, {}), {3}: (19, {}), {4}: (20, {})} | custom-call | tf_op jit(solution)/shard_map/backward/pallas_call | solution.py:954
  195.3 4.0 %collective-permute-done.32 = bf16[4,528,512]{2,1,0:T(8,128)(2,1)} collective-permute-done((bf16[4,528,512]{2,1,0:T(8,128)(2,1)}, bf16[4,528,512]{2,1,0:T(8,128)(2,1)}, u32[]{:S(2)}, u32[]{:S(2)}) %collective-permute-start.32) | collective-permute-done | bytes 2162720 | tf_op jit(solution)/shard_map/ppermute | solution.py:1024
  199.4 6.0 %collective-permute-done.34 = bf16[4,528,512]{2,1,0:T(8,128)(2,1)} collective-permute-done((bf16[4,528,512]{2,1,0:T(8,128)(2,1)}, bf16[4,528,512]{2,1,0:T(8,128)(2,1)}, u32[]{:S(2)}, u32[]{:S(2)}) %collective-permute-start.34) | collective-permute-done | bytes 2162720 | tf_op jit(solution)/shard_map/ppermute | solution.py:1024
  205.5 4.4 %select_convert_fusion.6 = (bf16[2,528,512]{2,1,0:T(8,128)(2,1)S(1)}, bf16[2,528,512]{2,1,0:T(8,128)(2,1)S(1)}, bf16[2,528,512]{2,1,0:T(8,128)(2,1)S(1)}) fusion(pred[]{:T(512)S(6)} %eq.15, bf16[4,528,512]{2,1,0:T(8,128)(2,1)} %collective-permute-done.32, bf16[4,528,512]{2,1,0:T(8,128)(2,1)} %collective-permute-done.34, ...), kind=kLoop, calls=%fused_computation.10 | loop fusion | flops 9732096 | bytes 11894786 | tf_op jit(solution)/shard_map/convert_element_type | solution.py:85
  210.4 1.9 collective-permute-start.40
  212.3 23.5 %collective-permute-done.36 = bf16[2,528,512]{2,1,0:T(8,128)(2,1)S(1)} collective-permute-done((bf16[2,528,512]{2,1,0:T(8,128)(2,1)S(1)}, bf16[2,528,512]{2,1,0:T(8,128)(2,1)S(1)}, u32[]{:S(2)}, u32[]{:S(2)}) %collective-permute-start.36) | collective-permute-done | bytes 1081376 | tf_op jit(solution)/shard_map/ppermute | solution.py:1016
  236.4 3.7 %add_convert_fusion.1 = (bf16[2,528,512]{2,1,0:T(8,128)(2,1)S(1)}, bf16[2,528,512]{2,1,0:T(8,128)(2,1)S(1)}, bf16[2,528,512]{2,1,0:T(8,128)(2,1)S(1)}) fusion(bf16[2,528,512]{2,1,0:T(8,128)(2,1)S(1)} %collective-permute-done.36, bf16[4,528,512]{2,1,0:T(8,128)(2,1)} %collective-permute-done.33, bf16[4,528,512]{2,1,0:T(8,128)(2,1)S(1)} %collective-permute-done.31, ...), kind=kLoop, calls=%fused_computation.7 | loop fusion | flops 17301504 | bytes 18382850 | tf_op jit(solution)/shard_map/convert_element_type | solution.py:85
  240.2 1.2 collective-permute-start.43
  241.5 1.0 collective-permute-start.44
  242.6 1.6 collective-permute-start.41
  244.5 2.8 select_convert_fusion
  247.4 8.2 %collective-permute-done.43 = bf16[528,512]{1,0:T(8,128)(2,1)S(1)} collective-permute-done((bf16[528,512]{1,0:T(8,128)(2,1)S(1)}, bf16[528,512]{1,0:T(8,128)(2,1)S(1)}, u32[]{:S(2)}, u32[]{:S(2)}) %collective-permute-start.43) | collective-permute-done | bytes 540704 | tf_op jit(solution)/shard_map/ppermute | solution.py:1016
  255.5 1.3 collective-permute-done.44
  257.4 1.2 collective-permute-start.38
  258.6 1.8 collective-permute-start.39
  260.4 6.7 %collective-permute-done.41 = bf16[528,512]{1,0:T(8,128)(2,1)S(1)} collective-permute-done((bf16[528,512]{1,0:T(8,128)(2,1)S(1)}, bf16[528,512]{1,0:T(8,128)(2,1)S(1)}, u32[]{:S(2)}, u32[]{:S(2)}) %collective-permute-start.41) | collective-permute-done | bytes 540704 | tf_op jit(solution)/shard_map/ppermute | solution.py:1016
  267.1 1.3 collective-permute-done.42
  269.1 1.2 collective-permute-done.48
  270.3 1.6 collective-permute-start.49
  271.9 1.0 pad_bitcast_fusion.2.params
  273.4 6.0 %collective-permute-done.49 = f32[16,512]{1,0:T(8,128)S(1)} collective-permute-done((f32[16,512]{1,0:T(8,128)S(1)}, f32[16,512]{1,0:T(8,128)S(1)}, u32[]{:S(2)}, u32[]{:S(2)}) %collective-permute-start.49) | collective-permute-done | bytes 32800 | tf_op jit(solution)/shard_map/ppermute | solution.py:1016
  279.4 1.7 collective-permute-start.37
  281.8 1.1 pad_bitcast_fusion.1.first
  282.9 8.2 %collective-permute-done.50 = f32[16,512]{1,0:T(8,128)S(1)} collective-permute-done((f32[16,512]{1,0:T(8,128)S(1)}, f32[16,512]{1,0:T(8,128)S(1)}, u32[]{:S(2)}, u32[]{:S(2)}) %collective-permute-start.50) | collective-permute-done | bytes 32800 | tf_op jit(solution)/shard_map/ppermute | solution.py:1020
  291.3 3.7 %collective-permute-done.51 = f32[16,512]{1,0:T(8,128)S(1)} collective-permute-done((f32[16,512]{1,0:T(8,128)S(1)}, f32[16,512]{1,0:T(8,128)S(1)}, u32[]{:S(2)}, u32[]{:S(2)}) %collective-permute-start.51) | collective-permute-done | bytes 32800 | tf_op jit(solution)/shard_map/ppermute | solution.py:1032
  295.0 2.1 collective-permute-start.52
  297.7 2.1 collective-permute-done.52
  299.9 1.3 fusion.11
  302.5 1.7 dynamic-slice_bitcast_fusion
  304.2 5.9 %update.1 = (f32[2048,128]{1,0:T(8,128)}, f32[2048,128]{1,0:T(8,128)}, f32[2048,128]{1,0:T(8,128)}, f32[8,128]{1,0:T(8,128)}) custom-call(s32[6]{0:T(128)} %pad_add_fusion.1.segments, f32[2048,128]{1,0:T(8,128)} %pad_bitcast_fusion.2.params, f32[2048,128]{1,0:T(8,128)} %pad_bitcast_fusion.1.first, f32[2048,128]{1,0:T(8,128)} %get-tuple-element.135.second, ...), custom_call_target="tpu_custom_call" | custom-call | tf_op jit(solution)/shard_map/update/pallas_call | solution.py:1279
  310.1 1.4 collective-permute-done.53
  313.1 2.7 collective-permute-done.54
  315.8 1.4 collective-permute-start.55
  317.2 2.2 collective-permute-done.55
  319.4 1.3 collective-permute-start.56
  320.7 2.3 collective-permute-done.56
  323.0 2.2 collective-permute-start.57
  325.8 2.2 slice.224
  329.7 4.4 %apply.1 = (f32[2048,128]{1,0:T(8,128)}, f32[8,128]{1,0:T(8,128)}) custom-call(s32[6]{0:T(128)} %pad_add_fusion.1.segments, f32[8,128]{1,0:T(8,128)} %add.223.sums, f32[2048,128]{1,0:T(8,128)} %pad_bitcast_fusion.2.params, f32[2048,128]{1,0:T(8,128)} %get-tuple-element.110.update), custom_call_target="tpu_custom_call" | custom-call | tf_op jit(solution)/shard_map/apply/pallas_call | solution.py:1288
  334.1 2.2 slice.223
  336.3 1.3 slice_bitcast_fusion.12
  (179 shorter events, 22.5 us)
Async XLA Ops:
  2.7 44.2 %copy-start.5 = (bf16[528,512]{1,0:T(8,128)(2,1)}, bf16[528,512]{1,0:T(8,128)(2,1)S(1)}, u32[]{:S(2)}) copy-start(bf16[528,512]{1,0:T(8,128)(2,1)S(1)} %reshape.62.refs_4_) | copy-start | bytes 1622020
  2.8 17.4 %collective-permute-start = (bf16[528,512]{1,0:T(8,128)(2,1)S(1)}, bf16[528,512]{1,0:T(8,128)(2,1)S(1)}, u32[]{:S(2)}, u32[]{:S(2)}) collective-permute-start(bf16[528,512]{1,0:T(8,128)(2,1)S(1)} %reshape.62.refs_4_), channel_id=1, source_target_pairs={{0,2},{1,3},{2,4},{3,5},{4,6},{5,7},{6,0},{7,1},{8,10},{9,11},{10,... | collective-permute-start | bytes 1622024 | tf_op jit(solution)/shard_map/ppermute | solution.py:1028
  5.8 17.9 %collective-permute-start.5 = (bf16[528,512]{1,0:T(8,128)(2,1)S(1)}, bf16[528,512]{1,0:T(8,128)(2,1)S(1)}, u32[]{:S(2)}, u32[]{:S(2)}) collective-permute-start(bf16[528,512]{1,0:T(8,128)(2,1)S(1)} %reshape.62.refs_4_), channel_id=1, source_target_pairs={{0,16},{8,24},{16,0},{24,8},{1,17},{9,25},{17,1},{25,9},{2,18},{10... | collective-permute-start | bytes 1622024 | tf_op jit(solution)/shard_map/ppermute | solution.py:1020
  20.1 15.3 %collective-permute-start.1 = (bf16[528,512]{1,0:T(8,128)(2,1)S(1)}, bf16[528,512]{1,0:T(8,128)(2,1)S(1)}, u32[]{:S(2)}, u32[]{:S(2)}) collective-permute-start(bf16[528,512]{1,0:T(8,128)(2,1)S(1)} %collective-permute-done.refs_5_), channel_id=1, source_target_pairs={{0,2},{1,3},{2,4},{3,5},{4,6},{5,7},{6,0},{7,1},{8,10},{9,11},{10,... | collective-permute-start | bytes 1622024 | tf_op jit(solution)/shard_map/ppermute | solution.py:1028
  20.1 16.6 %collective-permute-start.3 = (bf16[528,512]{1,0:T(8,128)(2,1)S(1)}, bf16[528,512]{1,0:T(8,128)(2,1)S(1)}, u32[]{:S(2)}, u32[]{:S(2)}) collective-permute-start(bf16[528,512]{1,0:T(8,128)(2,1)S(1)} %reshape.62.refs_4_), channel_id=1, source_target_pairs={{0,1},{1,0},{2,3},{3,2},{4,5},{5,4},{6,7},{7,6},{8,9},{9,8},{10,11... | collective-permute-start | bytes 1622024 | tf_op jit(solution)/shard_map/ppermute | solution.py:1016
  21.6 25.3 %collective-permute-start.4 = (bf16[528,512]{1,0:T(8,128)(2,1)S(1)}, bf16[528,512]{1,0:T(8,128)(2,1)S(1)}, u32[]{:S(2)}, u32[]{:S(2)}) collective-permute-start(bf16[528,512]{1,0:T(8,128)(2,1)S(1)} %collective-permute-done.refs_5_), channel_id=1, source_target_pairs={{0,1},{1,0},{2,3},{3,2},{4,5},{5,4},{6,7},{7,6},{8,9},{9,8},{10,11... | collective-permute-start | bytes 1622024 | tf_op jit(solution)/shard_map/ppermute | solution.py:1016
  22.2 24.8 %collective-permute-start.7 = (bf16[528,512]{1,0:T(8,128)(2,1)S(1)}, bf16[528,512]{1,0:T(8,128)(2,1)S(1)}, u32[]{:S(2)}, u32[]{:S(2)}) collective-permute-start(bf16[528,512]{1,0:T(8,128)(2,1)S(1)} %collective-permute-done.refs_5_), channel_id=1, source_target_pairs={{0,16},{8,24},{16,0},{24,8},{1,17},{9,25},{17,1},{25,9},{2,18},{10... | collective-permute-start | bytes 1622024 | tf_op jit(solution)/shard_map/ppermute | solution.py:1020
  23.7 62.6 %copy-start.10 = (bf16[528,512]{1,0:T(8,128)(2,1)}, bf16[528,512]{1,0:T(8,128)(2,1)S(1)}, u32[]{:S(2)}) copy-start(bf16[528,512]{1,0:T(8,128)(2,1)S(1)} %collective-permute-done.5.refs_14_) | copy-start | bytes 1622020
  35.4 14.3 %collective-permute-start.2 = (bf16[528,512]{1,0:T(8,128)(2,1)S(1)}, bf16[528,512]{1,0:T(8,128)(2,1)S(1)}, u32[]{:S(2)}, u32[]{:S(2)}) collective-permute-start(bf16[528,512]{1,0:T(8,128)(2,1)S(1)} %collective-permute-done.1.refs_6_), channel_id=1, source_target_pairs={{0,2},{1,3},{2,4},{3,5},{4,6},{5,7},{6,0},{7,1},{8,10},{9,11},{10,... | collective-permute-start | bytes 1622024 | tf_op jit(solution)/shard_map/ppermute | solution.py:1028
  35.5 26.9 %collective-permute-start.6 = (bf16[784,512]{1,0:T(8,128)(2,1)S(1)}, bf16[784,512]{1,0:T(8,128)(2,1)S(1)}, u32[]{:S(2)}, u32[]{:S(2)}) collective-permute-start(bf16[784,512]{1,0:T(8,128)(2,1)S(1)} %pad_maximum_fusion.2), channel_id=1, source_target_pairs={{0,1},{1,0},{2,3},{3,2},{4,5},{5,4},{6,7},{7,6},{8,9},{9,8},{10,11... | collective-permute-start | bytes 2408456 | tf_op jit(solution)/shard_map/ppermute | solution.py:1016
  36.8 49.5 %copy-start.8 = (bf16[528,512]{1,0:T(8,128)(2,1)}, bf16[528,512]{1,0:T(8,128)(2,1)S(1)}, u32[]{:S(2)}) copy-start(bf16[528,512]{1,0:T(8,128)(2,1)S(1)} %collective-permute-done.3.refs_8_) | copy-start | bytes 1622020
  36.9 28.5 %collective-permute-start.9 = (bf16[800,512]{1,0:T(8,128)(2,1)S(1)}, bf16[800,512]{1,0:T(8,128)(2,1)}, u32[]{:S(2)}, u32[]{:S(2)}) collective-permute-start(bf16[800,512]{1,0:T(8,128)(2,1)S(1)} %pad_maximum_fusion), channel_id=1, source_target_pairs={{0,16},{8,24},{16,0},{24,8},{1,17},{9,25},{17,1},{25,9},{2,18},{10... | collective-permute-start | bytes 2457608 | tf_op jit(solution)/shard_map/ppermute | solution.py:1020
  46.9 16.7 %collective-permute-start.15 = (bf16[528,512]{1,0:T(8,128)(2,1)S(1)}, bf16[528,512]{1,0:T(8,128)(2,1)S(1)}, u32[]{:S(2)}, u32[]{:S(2)}) collective-permute-start(bf16[528,512]{1,0:T(8,128)(2,1)S(1)} %reshape.62.refs_4_), channel_id=1, source_target_pairs={{0,8},{8,0},{16,24},{24,16},{1,9},{9,1},{17,25},{25,17},{2,10},{10... | collective-permute-start | bytes 1622024 | tf_op jit(solution)/shard_map/ppermute | solution.py:1024
  47.0 40.0 %copy-start.11 = (bf16[528,512]{1,0:T(8,128)(2,1)}, bf16[528,512]{1,0:T(8,128)(2,1)S(1)}, u32[]{:S(2)}) copy-start(bf16[528,512]{1,0:T(8,128)(2,1)S(1)} %collective-permute-done.7.refs_15_) | copy-start | bytes 1622020
  47.0 18.3 %collective-permute-start.16 = (bf16[528,512]{1,0:T(8,128)(2,1)S(1)}, bf16[528,512]{1,0:T(8,128)(2,1)S(1)}, u32[]{:S(2)}, u32[]{:S(2)}) collective-permute-start(bf16[528,512]{1,0:T(8,128)(2,1)S(1)} %collective-permute-done.refs_5_), channel_id=1, source_target_pairs={{0,8},{8,0},{16,24},{24,16},{1,9},{9,1},{17,25},{25,17},{2,10},{10... | collective-permute-start | bytes 1622024 | tf_op jit(solution)/shard_map/ppermute | solution.py:1024
  49.8 37.2 %collective-permute-start.11 = (bf16[800,512]{1,0:T(8,128)(2,1)S(1)}, bf16[800,512]{1,0:T(8,128)(2,1)}, u32[]{:S(2)}, u32[]{:S(2)}) collective-permute-start(bf16[800,512]{1,0:T(8,128)(2,1)S(1)} %pad_maximum_fusion.1), channel_id=1, source_target_pairs={{0,16},{8,24},{16,0},{24,8},{1,17},{9,25},{17,1},{25,9},{2,18},{10... | collective-permute-start | bytes 2457608 | tf_op jit(solution)/shard_map/ppermute | solution.py:1020
  62.4 48.3 %copy-start.6 = (bf16[784,512]{1,0:T(8,128)(2,1)}, bf16[784,512]{1,0:T(8,128)(2,1)S(1)}, u32[]{:S(2)}) copy-start(bf16[784,512]{1,0:T(8,128)(2,1)S(1)} %collective-permute-done.6.refs_10_) | copy-start | bytes 2408452
  62.4 26.0 %collective-permute-start.8 = (bf16[784,512]{1,0:T(8,128)(2,1)S(1)}, bf16[784,512]{1,0:T(8,128)(2,1)S(1)}, u32[]{:S(2)}, u32[]{:S(2)}) collective-permute-start(bf16[784,512]{1,0:T(8,128)(2,1)S(1)} %pad_maximum_fusion.3), channel_id=1, source_target_pairs={{0,1},{1,0},{2,3},{3,2},{4,5},{5,4},{6,7},{7,6},{8,9},{9,8},{10,11... | collective-permute-start | bytes 2408456 | tf_op jit(solution)/shard_map/ppermute | solution.py:1016
  63.7 41.1 %copy-start.18 = (bf16[528,512]{1,0:T(8,128)(2,1)}, bf16[528,512]{1,0:T(8,128)(2,1)S(1)}, u32[]{:S(2)}) copy-start(bf16[528,512]{1,0:T(8,128)(2,1)S(1)} %collective-permute-done.15.refs_20_) | copy-start | bytes 1622020
  63.7 14.7 %collective-permute-start.13 = (bf16[272,512]{1,0:T(8,128)(2,1)S(1)}, bf16[272,512]{1,0:T(8,128)(2,1)S(1)}, u32[]{:S(2)}, u32[]{:S(2)}) collective-permute-start(bf16[272,512]{1,0:T(8,128)(2,1)S(1)} %slice.199), channel_id=1, source_target_pairs={{0,16},{8,24},{16,0},{24,8},{1,17},{9,25},{17,1},{25,9},{2,18},{10... | collective-permute-start | bytes 835592 | tf_op jit(solution)/shard_map/ppermute | solution.py:1020
  65.3 21.0 %collective-permute-start.17 = (bf16[528,512]{1,0:T(8,128)(2,1)S(1)}, bf16[528,512]{1,0:T(8,128)(2,1)S(1)}, u32[]{:S(2)}, u32[]{:S(2)}) collective-permute-start(bf16[528,512]{1,0:T(8,128)(2,1)S(1)} %collective-permute-done.1.refs_6_), channel_id=1, source_target_pairs={{0,8},{8,0},{16,24},{24,16},{1,9},{9,1},{17,25},{25,17},{2,10},{10... | collective-permute-start | bytes 1622024 | tf_op jit(solution)/shard_map/ppermute | solution.py:1024
  65.4 21.5 %collective-permute-start.18 = (bf16[528,512]{1,0:T(8,128)(2,1)S(1)}, bf16[528,512]{1,0:T(8,128)(2,1)S(1)}, u32[]{:S(2)}, u32[]{:S(2)}) collective-permute-start(bf16[528,512]{1,0:T(8,128)(2,1)S(1)} %collective-permute-done.2.refs_7_), channel_id=1, source_target_pairs={{0,8},{8,0},{16,24},{24,16},{1,9},{9,1},{17,25},{25,17},{2,10},{10... | collective-permute-start | bytes 1622024 | tf_op jit(solution)/shard_map/ppermute | solution.py:1024
  78.4 7.8 %collective-permute-start.10 = (bf16[256,512]{1,0:T(8,128)(2,1)S(1)}, bf16[256,512]{1,0:T(8,128)(2,1)S(1)}, u32[]{:S(2)}, u32[]{:S(2)}) collective-permute-start(bf16[256,512]{1,0:T(8,128)(2,1)S(1)} %slice.196), channel_id=1, source_target_pairs={{0,1},{1,0},{2,3},{3,2},{4,5},{5,4},{6,7},{7,6},{8,9},{9,8},{10,11... | collective-permute-start | bytes 786440 | tf_op jit(solution)/shard_map/ppermute | solution.py:1016
  86.3 11.6 %collective-permute-start.19 = (bf16[528,512]{1,0:T(8,128)(2,1)S(1)}, bf16[528,512]{1,0:T(8,128)(2,1)S(1)}, u32[]{:S(2)}, u32[]{:S(2)}) collective-permute-start(bf16[528,512]{1,0:T(8,128)(2,1)S(1)} %collective-permute-done.3.refs_8_), channel_id=1, source_target_pairs={{0,8},{8,0},{16,24},{24,16},{1,9},{9,1},{17,25},{25,17},{2,10},{10... | collective-permute-start | bytes 1622024 | tf_op jit(solution)/shard_map/ppermute | solution.py:1024
  86.3 11.5 %collective-permute-start.25 = (bf16[528,512]{1,0:T(8,128)(2,1)S(1)}, bf16[528,512]{1,0:T(8,128)(2,1)S(1)}, u32[]{:S(2)}, u32[]{:S(2)}) collective-permute-start(bf16[528,512]{1,0:T(8,128)(2,1)S(1)} %collective-permute-done.5.refs_14_), channel_id=1, source_target_pairs={{0,8},{8,0},{16,24},{24,16},{1,9},{9,1},{17,25},{25,17},{2,10},{10... | collective-permute-start | bytes 1622024 | tf_op jit(solution)/shard_map/ppermute | solution.py:1024
  86.9 11.5 %collective-permute-start.20 = (bf16[528,512]{1,0:T(8,128)(2,1)S(1)}, bf16[528,512]{1,0:T(8,128)(2,1)S(1)}, u32[]{:S(2)}, u32[]{:S(2)}) collective-permute-start(bf16[528,512]{1,0:T(8,128)(2,1)S(1)} %collective-permute-done.4.refs_9_), channel_id=1, source_target_pairs={{0,8},{8,0},{16,24},{24,16},{1,9},{9,1},{17,25},{25,17},{2,10},{10... | collective-permute-start | bytes 1622024 | tf_op jit(solution)/shard_map/ppermute | solution.py:1024
  87.0 11.5 %collective-permute-start.26 = (bf16[528,512]{1,0:T(8,128)(2,1)S(1)}, bf16[528,512]{1,0:T(8,128)(2,1)S(1)}, u32[]{:S(2)}, u32[]{:S(2)}) collective-permute-start(bf16[528,512]{1,0:T(8,128)(2,1)S(1)} %collective-permute-done.7.refs_15_), channel_id=1, source_target_pairs={{0,8},{8,0},{16,24},{24,16},{1,9},{9,1},{17,25},{25,17},{2,10},{10... | collective-permute-start | bytes 1622024 | tf_op jit(solution)/shard_map/ppermute | solution.py:1024
  88.4 8.4 %collective-permute-start.12 = (bf16[256,512]{1,0:T(8,128)(2,1)S(1)}, bf16[256,512]{1,0:T(8,128)(2,1)S(1)}, u32[]{:S(2)}, u32[]{:S(2)}) collective-permute-start(bf16[256,512]{1,0:T(8,128)(2,1)S(1)} %slice.198), channel_id=1, source_target_pairs={{0,1},{1,0},{2,3},{3,2},{4,5},{5,4},{6,7},{7,6},{8,9},{9,8},{10,11... | collective-permute-start | bytes 786440 | tf_op jit(solution)/shard_map/ppermute | solution.py:1016
  96.8 7.9 %collective-permute-start.14 = (bf16[272,512]{1,0:T(8,128)(2,1)S(1)}, bf16[272,512]{1,0:T(8,128)(2,1)}, u32[]{:S(2)}, u32[]{:S(2)}) collective-permute-start(bf16[272,512]{1,0:T(8,128)(2,1)S(1)} %slice.200), channel_id=1, source_target_pairs={{0,16},{8,24},{16,0},{24,8},{1,17},{9,25},{17,1},{25,9},{2,18},{10... | collective-permute-start | bytes 835592 | tf_op jit(solution)/shard_map/ppermute | solution.py:1020
  97.8 6.9 %collective-permute-start.23 = (bf16[256,512]{1,0:T(8,128)(2,1)S(1)}, bf16[256,512]{1,0:T(8,128)(2,1)S(1)}, u32[]{:S(2)}, u32[]{:S(2)}) collective-permute-start(bf16[256,512]{1,0:T(8,128)(2,1)S(1)} %collective-permute-done.10.refs_12_), channel_id=1, source_target_pairs={{0,8},{8,0},{16,24},{24,16},{1,9},{9,1},{17,25},{25,17},{2,10},{10... | collective-permute-start | bytes 786440 | tf_op jit(solution)/shard_map/ppermute | solution.py:1024
  97.9 7.5 %collective-permute-start.24 = (bf16[256,512]{1,0:T(8,128)(2,1)S(1)}, bf16[256,512]{1,0:T(8,128)(2,1)S(1)}, u32[]{:S(2)}, u32[]{:S(2)}) collective-permute-start(bf16[256,512]{1,0:T(8,128)(2,1)S(1)} %collective-permute-done.12.refs_13_), channel_id=1, source_target_pairs={{0,8},{8,0},{16,24},{24,16},{1,9},{9,1},{17,25},{25,17},{2,10},{10... | collective-permute-start | bytes 786440 | tf_op jit(solution)/shard_map/ppermute | solution.py:1024
  98.4 12.3 %collective-permute-start.27 = (bf16[800,512]{1,0:T(8,128)(2,1)}, bf16[800,512]{1,0:T(8,128)(2,1)S(1)}, u32[]{:S(2)}, u32[]{:S(2)}) collective-permute-start(bf16[800,512]{1,0:T(8,128)(2,1)} %collective-permute-done.9.refs_16_), channel_id=1, source_target_pairs={{0,8},{8,0},{16,24},{24,16},{1,9},{9,1},{17,25},{25,17},{2,10},{10... | collective-permute-start | bytes 2457608 | tf_op jit(solution)/shard_map/ppermute | solution.py:1024
  98.5 12.3 %collective-permute-start.28 = (bf16[800,512]{1,0:T(8,128)(2,1)}, bf16[800,512]{1,0:T(8,128)(2,1)}, u32[]{:S(2)}, u32[]{:S(2)}) collective-permute-start(bf16[800,512]{1,0:T(8,128)(2,1)} %collective-permute-done.11.refs_17_), channel_id=1, source_target_pairs={{0,8},{8,0},{16,24},{24,16},{1,9},{9,1},{17,25},{25,17},{2,10},{10... | collective-permute-start | bytes 2457608 | tf_op jit(solution)/shard_map/ppermute | solution.py:1024
  104.7 5.9 %collective-permute-start.22 = (bf16[784,512]{1,0:T(8,128)(2,1)S(1)}, bf16[784,512]{1,0:T(8,128)(2,1)S(1)}, u32[]{:S(2)}, u32[]{:S(2)}) collective-permute-start(bf16[784,512]{1,0:T(8,128)(2,1)S(1)} %collective-permute-done.8.refs_11_), channel_id=1, source_target_pairs={{0,8},{8,0},{16,24},{24,16},{1,9},{9,1},{17,25},{25,17},{2,10},{10... | collective-permute-start | bytes 2408456 | tf_op jit(solution)/shard_map/ppermute | solution.py:1024
  104.8 5.9 %collective-permute-start.21 = (bf16[784,512]{1,0:T(8,128)(2,1)S(1)}, bf16[784,512]{1,0:T(8,128)(2,1)}, u32[]{:S(2)}, u32[]{:S(2)}) collective-permute-start(bf16[784,512]{1,0:T(8,128)(2,1)S(1)} %collective-permute-done.6.refs_10_), channel_id=1, source_target_pairs={{0,8},{8,0},{16,24},{24,16},{1,9},{9,1},{17,25},{25,17},{2,10},{10... | collective-permute-start | bytes 2408456 | tf_op jit(solution)/shard_map/ppermute | solution.py:1024
  105.3 2.7 collective-permute-start.29
  108.8 1.9 collective-permute-start.30
  194.6 4.7 %collective-permute-start.32 = (bf16[4,528,512]{2,1,0:T(8,128)(2,1)}, bf16[4,528,512]{2,1,0:T(8,128)(2,1)}, u32[]{:S(2)}, u32[]{:S(2)}) collective-permute-start(bf16[4,528,512]{2,1,0:T(8,128)(2,1)} %get-tuple-element.101), channel_id=1, source_target_pairs={{0,8},{8,0},{16,24},{24,16},{1,9},{9,1},{17,25},{25,17},{2,10},{10... | collective-permute-start | bytes 6488072 | tf_op jit(solution)/shard_map/ppermute | solution.py:1024
  194.7 10.8 %collective-permute-start.34 = (bf16[4,528,512]{2,1,0:T(8,128)(2,1)}, bf16[4,528,512]{2,1,0:T(8,128)(2,1)}, u32[]{:S(2)}, u32[]{:S(2)}) collective-permute-start(bf16[4,528,512]{2,1,0:T(8,128)(2,1)} %get-tuple-element.103), channel_id=1, source_target_pairs={{0,8},{8,0},{16,24},{24,16},{1,9},{9,1},{17,25},{25,17},{2,10},{10... | collective-permute-start | bytes 6488072 | tf_op jit(solution)/shard_map/ppermute | solution.py:1024
  195.2 17.1 %collective-permute-start.31 = (bf16[4,528,512]{2,1,0:T(8,128)(2,1)}, bf16[4,528,512]{2,1,0:T(8,128)(2,1)S(1)}, u32[]{:S(2)}, u32[]{:S(2)}) collective-permute-start(bf16[4,528,512]{2,1,0:T(8,128)(2,1)} %get-tuple-element.98), channel_id=1, source_target_pairs={{0,8},{8,0},{16,24},{24,16},{1,9},{9,1},{17,25},{25,17},{2,10},{10... | collective-permute-start | bytes 6488072 | tf_op jit(solution)/shard_map/ppermute | solution.py:1024
  199.3 37.1 %collective-permute-start.33 = (bf16[4,528,512]{2,1,0:T(8,128)(2,1)}, bf16[4,528,512]{2,1,0:T(8,128)(2,1)}, u32[]{:S(2)}, u32[]{:S(2)}) collective-permute-start(bf16[4,528,512]{2,1,0:T(8,128)(2,1)} %get-tuple-element.102), channel_id=1, source_target_pairs={{0,8},{8,0},{16,24},{24,16},{1,9},{9,1},{17,25},{25,17},{2,10},{10... | collective-permute-start | bytes 6488072 | tf_op jit(solution)/shard_map/ppermute | solution.py:1024
  209.8 26.0 %collective-permute-start.36 = (bf16[2,528,512]{2,1,0:T(8,128)(2,1)S(1)}, bf16[2,528,512]{2,1,0:T(8,128)(2,1)S(1)}, u32[]{:S(2)}, u32[]{:S(2)}) collective-permute-start(bf16[2,528,512]{2,1,0:T(8,128)(2,1)S(1)} %get-tuple-element.118), channel_id=1, source_target_pairs={{0,1},{1,0},{2,3},{3,2},{4,5},{5,4},{6,7},{7,6},{8,9},{9,8},{10,11... | collective-permute-start | bytes 3244040 | tf_op jit(solution)/shard_map/ppermute | solution.py:1016
  210.4 26.0 %collective-permute-start.40 = (bf16[2,528,512]{2,1,0:T(8,128)(2,1)S(1)}, bf16[2,528,512]{2,1,0:T(8,128)(2,1)S(1)}, u32[]{:S(2)}, u32[]{:S(2)}) collective-permute-start(bf16[2,528,512]{2,1,0:T(8,128)(2,1)S(1)} %get-tuple-element.119), channel_id=1, source_target_pairs={{0,16},{8,24},{16,0},{24,8},{1,17},{9,25},{17,1},{25,9},{2,18},{10... | collective-permute-start | bytes 3244040 | tf_op jit(solution)/shard_map/ppermute | solution.py:1020
  240.2 15.3 %collective-permute-start.43 = (bf16[528,512]{1,0:T(8,128)(2,1)S(1)}, bf16[528,512]{1,0:T(8,128)(2,1)S(1)}, u32[]{:S(2)}, u32[]{:S(2)}) collective-permute-start(bf16[528,512]{1,0:T(8,128)(2,1)S(1)} %get-tuple-element.128), channel_id=1, source_target_pairs={{0,1},{1,0},{2,3},{3,2},{4,5},{5,4},{6,7},{7,6},{8,9},{9,8},{10,11... | collective-permute-start | bytes 1622024 | tf_op jit(solution)/shard_map/ppermute | solution.py:1016
  241.5 15.3 %collective-permute-start.44 = (bf16[528,512]{1,0:T(8,128)(2,1)S(1)}, bf16[528,512]{1,0:T(8,128)(2,1)S(1)}, u32[]{:S(2)}, u32[]{:S(2)}) collective-permute-start(bf16[528,512]{1,0:T(8,128)(2,1)S(1)} %get-tuple-element.126), channel_id=1, source_target_pairs={{0,16},{8,24},{16,0},{24,8},{1,17},{9,25},{17,1},{25,9},{2,18},{10... | collective-permute-start | bytes 1622024 | tf_op jit(solution)/shard_map/ppermute | solution.py:1020
  242.6 24.5 %collective-permute-start.41 = (bf16[528,512]{1,0:T(8,128)(2,1)S(1)}, bf16[528,512]{1,0:T(8,128)(2,1)S(1)}, u32[]{:S(2)}, u32[]{:S(2)}) collective-permute-start(bf16[528,512]{1,0:T(8,128)(2,1)S(1)} %get-tuple-element.127), channel_id=1, source_target_pairs={{0,1},{1,0},{2,3},{3,2},{4,5},{5,4},{6,7},{7,6},{8,9},{9,8},{10,11... | collective-permute-start | bytes 1622024 | tf_op jit(solution)/shard_map/ppermute | solution.py:1016
  244.2 24.2 %collective-permute-start.42 = (bf16[528,512]{1,0:T(8,128)(2,1)S(1)}, bf16[528,512]{1,0:T(8,128)(2,1)S(1)}, u32[]{:S(2)}, u32[]{:S(2)}) collective-permute-start(bf16[528,512]{1,0:T(8,128)(2,1)S(1)} %get-tuple-element.125), channel_id=1, source_target_pairs={{0,16},{8,24},{16,0},{24,8},{1,17},{9,25},{17,1},{25,9},{2,18},{10... | collective-permute-start | bytes 1622024 | tf_op jit(solution)/shard_map/ppermute | solution.py:1020
  257.0 11.6 %collective-permute-start.45 = (bf16[528,512]{1,0:T(8,128)(2,1)S(1)}, bf16[528,512]{1,0:T(8,128)(2,1)S(1)}, u32[]{:S(2)}, u32[]{:S(2)}) collective-permute-start(bf16[528,512]{1,0:T(8,128)(2,1)S(1)} %fusion.1), channel_id=1, source_target_pairs={{0,2},{1,3},{2,4},{3,5},{4,6},{5,7},{6,0},{7,1},{8,10},{9,11},{10,... | collective-permute-start | bytes 1622024 | tf_op jit(solution)/shard_map/ppermute | solution.py:1028
  257.4 23.8 %collective-permute-start.38 = (bf16[528,512]{1,0:T(8,128)(2,1)S(1)}, bf16[528,512]{1,0:T(8,128)(2,1)S(1)}, u32[]{:S(2)}, u32[]{:S(2)}) collective-permute-start(bf16[528,512]{1,0:T(8,128)(2,1)S(1)} %get-tuple-element.122), channel_id=1, source_target_pairs={{0,1},{1,0},{2,3},{3,2},{4,5},{5,4},{6,7},{7,6},{8,9},{9,8},{10,11... | collective-permute-start | bytes 1622024 | tf_op jit(solution)/shard_map/ppermute | solution.py:1016
  258.6 22.8 %collective-permute-start.39 = (bf16[528,512]{1,0:T(8,128)(2,1)S(1)}, bf16[528,512]{1,0:T(8,128)(2,1)S(1)}, u32[]{:S(2)}, u32[]{:S(2)}) collective-permute-start(bf16[528,512]{1,0:T(8,128)(2,1)S(1)} %get-tuple-element.124), channel_id=1, source_target_pairs={{0,16},{8,24},{16,0},{24,8},{1,17},{9,25},{17,1},{25,9},{2,18},{10... | collective-permute-start | bytes 1622024 | tf_op jit(solution)/shard_map/ppermute | solution.py:1020
  268.9 12.5 %collective-permute-start.46 = (bf16[528,512]{1,0:T(8,128)(2,1)S(1)}, bf16[528,512]{1,0:T(8,128)(2,1)S(1)}, u32[]{:S(2)}, u32[]{:S(2)}) collective-permute-start(bf16[528,512]{1,0:T(8,128)(2,1)S(1)} %fusion.4), channel_id=1, source_target_pairs={{0,2},{1,3},{2,4},{3,5},{4,6},{5,7},{6,0},{7,1},{8,10},{9,11},{10,... | collective-permute-start | bytes 1622024 | tf_op jit(solution)/shard_map/ppermute | solution.py:1028
  269.0 1.3 collective-permute-start.48
  270.3 9.1 %collective-permute-start.49 = (f32[16,512]{1,0:T(8,128)S(1)}, f32[16,512]{1,0:T(8,128)S(1)}, u32[]{:S(2)}, u32[]{:S(2)}) collective-permute-start(f32[16,512]{1,0:T(8,128)S(1)} %add.211), channel_id=1, source_target_pairs={{0,1},{1,0},{2,3},{3,2},{4,5},{5,4},{6,7},{7,6},{8,9},{9,8},{10,11... | collective-permute-start | bytes 98312 | tf_op jit(solution)/shard_map/ppermute | solution.py:1016
  272.9 27.0 %collective-permute-start.35 = (bf16[528,512]{1,0:T(8,128)(2,1)S(1)}, bf16[528,512]{1,0:T(8,128)(2,1)S(1)}, u32[]{:S(2)}, u32[]{:S(2)}) collective-permute-start(bf16[528,512]{1,0:T(8,128)(2,1)S(1)} %get-tuple-element.121), channel_id=1, source_target_pairs={{0,1},{1,0},{2,3},{3,2},{4,5},{5,4},{6,7},{7,6},{8,9},{9,8},{10,11... | collective-permute-start | bytes 1622024 | tf_op jit(solution)/shard_map/ppermute | solution.py:1016
  279.4 20.5 %collective-permute-start.37 = (bf16[528,512]{1,0:T(8,128)(2,1)S(1)}, bf16[528,512]{1,0:T(8,128)(2,1)S(1)}, u32[]{:S(2)}, u32[]{:S(2)}) collective-permute-start(bf16[528,512]{1,0:T(8,128)(2,1)S(1)} %get-tuple-element.123), channel_id=1, source_target_pairs={{0,16},{8,24},{16,0},{24,8},{1,17},{9,25},{17,1},{25,9},{2,18},{10... | collective-permute-start | bytes 1622024 | tf_op jit(solution)/shard_map/ppermute | solution.py:1020
  281.2 10.0 %collective-permute-start.50 = (f32[16,512]{1,0:T(8,128)S(1)}, f32[16,512]{1,0:T(8,128)S(1)}, u32[]{:S(2)}, u32[]{:S(2)}) collective-permute-start(f32[16,512]{1,0:T(8,128)S(1)} %add.212), channel_id=1, source_target_pairs={{0,16},{8,24},{16,0},{24,8},{1,17},{9,25},{17,1},{25,9},{2,18},{10... | collective-permute-start | bytes 98312 | tf_op jit(solution)/shard_map/ppermute | solution.py:1020
  281.8 18.2 %collective-permute-start.47 = (bf16[528,512]{1,0:T(8,128)(2,1)S(1)}, bf16[528,512]{1,0:T(8,128)(2,1)S(1)}, u32[]{:S(2)}, u32[]{:S(2)}) collective-permute-start(bf16[528,512]{1,0:T(8,128)(2,1)S(1)} %fusion.7), channel_id=1, source_target_pairs={{0,2},{1,3},{2,4},{3,5},{4,6},{5,7},{6,0},{7,1},{8,10},{9,11},{10,... | collective-permute-start | bytes 1622024 | tf_op jit(solution)/shard_map/ppermute | solution.py:1028
  291.1 3.9 %collective-permute-start.51 = (f32[16,512]{1,0:T(8,128)S(1)}, f32[16,512]{1,0:T(8,128)S(1)}, u32[]{:S(2)}, u32[]{:S(2)}) collective-permute-start(f32[16,512]{1,0:T(8,128)S(1)} %add.213), channel_id=1, source_target_pairs={{0,2},{1,3},{2,0},{3,1},{4,6},{5,7},{6,4},{7,5},{8,10},{9,11},{10,... | collective-permute-start | bytes 98312 | tf_op jit(solution)/shard_map/ppermute | solution.py:1032
  295.0 4.8 %collective-permute-start.52 = (f32[16,512]{1,0:T(8,128)S(1)}, f32[16,512]{1,0:T(8,128)S(1)}, u32[]{:S(2)}, u32[]{:S(2)}) collective-permute-start(f32[16,512]{1,0:T(8,128)S(1)} %add.214), channel_id=1, source_target_pairs={{0,4},{1,5},{2,6},{3,7},{4,0},{5,1},{6,2},{7,3},{8,12},{9,13},{10,... | collective-permute-start | bytes 98312 | tf_op jit(solution)/shard_map/ppermute | solution.py:1032
  310.1 1.4 collective-permute-start.53
  312.2 3.6 %collective-permute-start.54 = (f32[8,128]{1,0:T(8,128)S(1)}, f32[8,128]{1,0:T(8,128)S(1)}, u32[]{:S(2)}, u32[]{:S(2)}) collective-permute-start(f32[8,128]{1,0:T(8,128)S(1)} %add.219), channel_id=1, source_target_pairs={{0,1},{1,0},{2,3},{3,2},{4,5},{5,4},{6,7},{7,6},{8,9},{9,8},{10,11... | collective-permute-start | bytes 12296 | tf_op jit(solution)/shard_map/ppermute | solution.py:1016
  315.8 3.6 %collective-permute-start.55 = (f32[8,128]{1,0:T(8,128)S(1)}, f32[8,128]{1,0:T(8,128)S(1)}, u32[]{:S(2)}, u32[]{:S(2)}) collective-permute-start(f32[8,128]{1,0:T(8,128)S(1)} %add.220), channel_id=1, source_target_pairs={{0,16},{8,24},{16,0},{24,8},{1,17},{9,25},{17,1},{25,9},{2,18},{10... | collective-permute-start | bytes 12296 | tf_op jit(solution)/shard_map/ppermute | solution.py:1020
  319.4 3.6 %collective-permute-start.56 = (f32[8,128]{1,0:T(8,128)S(1)}, f32[8,128]{1,0:T(8,128)S(1)}, u32[]{:S(2)}, u32[]{:S(2)}) collective-permute-start(f32[8,128]{1,0:T(8,128)S(1)} %add.221), channel_id=1, source_target_pairs={{0,2},{1,3},{2,0},{3,1},{4,6},{5,7},{6,4},{7,5},{8,10},{9,11},{10,... | collective-permute-start | bytes 12296 | tf_op jit(solution)/shard_map/ppermute | solution.py:1032
  323.0 6.1 %collective-permute-start.57 = (f32[8,128]{1,0:T(8,128)S(1)}, f32[8,128]{1,0:T(8,128)S(1)}, u32[]{:S(2)}, u32[]{:S(2)}) collective-permute-start(f32[8,128]{1,0:T(8,128)S(1)} %add.222), channel_id=1, source_target_pairs={{0,4},{1,5},{2,6},{3,7},{4,0},{5,1},{6,2},{7,3},{8,12},{9,13},{10,... | collective-permute-start | bytes 12296 | tf_op jit(solution)/shard_map/ppermute | solution.py:1032
  (30 other events, 501.6 us)
